TPU v7x, 32 devices: a whole 2x2x4 slice. The times are simulated.
32 devices in a mesh: seq: 8 (over y, x, core), fsdp: 4 (over z).
Axes of the slice: x: 2, y: 2, z: 4, core: 2. Of those that a mesh axis runs over, the one named last changes fastest.
Arguments:
- tokens: bfloat16 [4, 2048, 2048], P('fsdp', 'seq'), may hold values from -6 to 6
- segments: int32 [4, 2048], P('fsdp'), may hold values from 0 to 3, as said below
- routes: int32 [4, 2048, 8], P('fsdp', 'seq'), may hold values from 0 to 15, all different within a row; in each aligned block of 256 rows (0 to 255, 256 to 511, ..., all dimensions but the last counted through in order) at most 144 rows name the same one
- cotangent: bfloat16 [4, 2048, 2048], P('fsdp', 'seq'), may hold values from -6 to 6
- w_query: bfloat16 [2048, 2048], P(('seq', 'fsdp')), may hold values from -0.125 to 0.125
- w_key: bfloat16 [2048, 2048], P(('seq', 'fsdp')), may hold values from -0.125 to 0.125
- w_value: bfloat16 [2048, 2048], P(('seq', 'fsdp')), may hold values from -0.125 to 0.125
- w_output: bfloat16 [2048, 2048], P(('seq', 'fsdp')), may hold values from -4 to 4
- router: bfloat16 [2048, 16], P(('seq', 'fsdp')), may hold values from -0.0625 to 0.0625
- attn_gain: bfloat16 [2048], P(('seq', 'fsdp')), may hold values from 0.099609375 to 1.8984375
- moe_gain: bfloat16 [2048], P(('seq', 'fsdp')), may hold values from 0.099609375 to 1.8984375
- query_gain: bfloat16 [2048], P(('seq', 'fsdp')), may hold values from 0.099609375 to 1.8984375
- key_gain: bfloat16 [2048], P(('seq', 'fsdp')), may hold values from 0.099609375 to 1.8984375
- w_gate: bfloat16 [16, 2048, 1024], P('seq', 'fsdp'), may hold values from -0.125 to 0.125
- w_up: bfloat16 [16, 2048, 1024], P('seq', 'fsdp'), may hold values from -0.125 to 0.125
- w_down: bfloat16 [16, 1024, 2048], P('seq', 'fsdp'), may hold values from -1.5 to 1.5
Outputs:
- mixed: bfloat16 [4, 2048, 2048], P('fsdp', 'seq')
- grad_tokens: float32 [4, 2048, 2048], P('fsdp', 'seq')
- grad_query: float32 [2048, 2048], P(('seq', 'fsdp'))
- grad_key: float32 [2048, 2048], P(('seq', 'fsdp'))
- grad_value: float32 [2048, 2048], P(('seq', 'fsdp'))
- grad_output: float32 [2048, 2048], P(('seq', 'fsdp'))
- grad_router: float32 [2048, 16], P(('seq', 'fsdp'))
- grad_attn_gain: float32 [2048], P(('seq', 'fsdp'))
- grad_moe_gain: float32 [2048], P(('seq', 'fsdp'))
- grad_query_gain: float32 [2048], P(('seq', 'fsdp'))
- grad_key_gain: float32 [2048], P(('seq', 'fsdp'))
- grad_gate: float32 [16, 2048, 1024], P('seq', 'fsdp')
- grad_up: float32 [16, 2048, 1024], P('seq', 'fsdp')
- grad_down: float32 [16, 1024, 2048], P('seq', 'fsdp')
Inputs may be any that keep to these rules, and one draw needn't show every extreme that they name: `segments`: along each sequence the document numbers never fall. `routes`: each token names 8 different experts; the tokens of one device name one expert 144 times at most.
All inputs are finite; a program needn't handle non-finite values.
Results may differ from a plain program's by a relative error of at most 0.018.
Values may be sent and summed in bfloat16 or wider, within the bound.
No kernel may reach another device: no remote copies, remote signals or barrier semaphores. Data moves between devices by JAX's collectives and lax.ppermute only.
A program may use at most 384 MiB of HBM per device.

v0:
```python
from functools import partial

import jax
import jax.numpy as jnp
from jax import lax
from jax.sharding import PartitionSpec as P

D = 2048
H = 16
DH = 128
E = 16
WINDOW = 1024
CAP = 144


EPSILON = 1e-06
ROPE_BASE = 50000.0
HIGHEST = lax.Precision.HIGHEST


def matmul(left, right):
    return jnp.dot(left, right, preferred_element_type=jnp.float32)


def rms_scale(values, gain):
    return values * lax.rsqrt(jnp.mean(values * values, axis=-1, keepdims=True) + EPSILON) * gain


def rotary(values, places):
    half_size = values.shape[-1] // 2
    freqs = ROPE_BASE ** (-(jnp.arange(half_size, dtype=jnp.float32) * 2.0 / values.shape[-1]))
    angles = places[:, None] * freqs[None, :]
    cosine = jnp.cos(angles)[:, None, :]
    sine = jnp.sin(angles)[:, None, :]
    first = values[..., :half_size]
    second = values[..., half_size:]
    return jnp.concatenate(
        [first * cosine - second * sine, second * cosine + first * sine], axis=-1
    )


def prepare(projected, gain, places):
    normed = rms_scale(projected, gain)
    return rotary(normed.reshape(projected.shape[0], H, DH), places)


def gate_mix(gated, upward):
    return jax.nn.silu(gated) * upward


def window_block(
    queries, keys_pad, values_pad, seq_ids, segs_pad, block_start, block_rows, half_window
):
    key_span = block_rows + 2 * half_window
    query_blk = lax.dynamic_slice_in_dim(queries, block_start, block_rows, 0)
    key_blk = lax.dynamic_slice_in_dim(keys_pad, block_start, key_span, 0)
    value_blk = lax.dynamic_slice_in_dim(values_pad, block_start, key_span, 0)
    seg_rows = lax.dynamic_slice_in_dim(seq_ids, block_start, block_rows, 0)
    seg_keys = lax.dynamic_slice_in_dim(segs_pad, block_start, key_span, 0)
    rows_at = block_start + jnp.arange(block_rows, dtype=jnp.int32)
    keys_at = block_start - half_window + jnp.arange(key_span, dtype=jnp.int32)
    allowed = (seg_rows[:, None] == seg_keys[None, :]) & (
        jnp.abs(rows_at[:, None] - keys_at[None, :]) <= half_window
    )
    scores = jnp.einsum(
        "qhd,khd->hqk", query_blk, key_blk, preferred_element_type=jnp.float32
    ) * DH ** (-0.5)
    scores = jnp.where(allowed[None], scores, -1e30)
    return (query_blk, key_blk, value_blk, scores)


def per_device(
    tokens,
    segments,
    routes,
    cotangent,
    w_query,
    w_key,
    w_value,
    w_output,
    router,
    attn_gain,
    moe_gain,
    query_gain,
    key_gain,
    w_gate,
    w_up,
    w_down,
):
    inputs = tokens[0].astype(jnp.float32)
    tok_rows = inputs.shape[0]
    gathered = (
        lax.all_gather(w_query, ("seq", "fsdp"), axis=0, tiled=True),
        lax.all_gather(w_key, ("seq", "fsdp"), axis=0, tiled=True),
        lax.all_gather(w_value, ("seq", "fsdp"), axis=0, tiled=True),
        lax.all_gather(w_output, ("seq", "fsdp"), axis=0, tiled=True),
        lax.all_gather(router, ("seq", "fsdp"), axis=0, tiled=True),
        lax.all_gather(attn_gain, ("seq", "fsdp"), axis=0, tiled=True),
        lax.all_gather(moe_gain, ("seq", "fsdp"), axis=0, tiled=True),
        lax.all_gather(query_gain, ("seq", "fsdp"), axis=0, tiled=True),
        lax.all_gather(key_gain, ("seq", "fsdp"), axis=0, tiled=True),
    )
    full_query, full_key, full_value, full_output, full_router = (
        gathered[0],
        gathered[1],
        gathered[2],
        gathered[3],
        gathered[4],
    )
    gain_attn = gathered[5].astype(jnp.float32)
    gain_moe = gathered[6].astype(jnp.float32)
    gain_query = gathered[7].astype(jnp.float32)
    gain_key = gathered[8].astype(jnp.float32)
    places = (lax.axis_index("seq") * tok_rows + jnp.arange(tok_rows, dtype=jnp.int32)).astype(
        jnp.float32
    )
    normed = rms_scale(inputs, gain_attn)
    normed_low = normed.astype(jnp.bfloat16)
    query_pre = matmul(normed_low, full_query)
    key_pre = matmul(normed_low, full_key)
    value_low = matmul(normed_low, full_value).astype(jnp.bfloat16).reshape(tok_rows, H, DH)
    query_low = prepare(query_pre, gain_query, places).astype(jnp.bfloat16)
    key_low = prepare(key_pre, gain_key, places).astype(jnp.bfloat16)
    query_heads, key_heads, value_heads = (
        lax.all_to_all(query_low, "seq", split_axis=1, concat_axis=0, tiled=True),
        lax.all_to_all(key_low, "seq", split_axis=1, concat_axis=0, tiled=True),
        lax.all_to_all(value_low, "seq", split_axis=1, concat_axis=0, tiled=True),
    )
    seq_ids = segments[0]
    length = query_heads.shape[0]
    heads_local = query_heads.shape[1]
    block_rows = min(512, length)
    half_window = WINDOW // 2
    block_count = length // block_rows
    pad_rows = ((half_window, half_window), (0, 0), (0, 0))
    keys_pad = jnp.pad(key_heads, pad_rows)
    values_pad = jnp.pad(value_heads, pad_rows)
    segs_pad = jnp.pad(seq_ids, (half_window, half_window), constant_values=-1)

    def forward_block(block_index):
        block_start = block_index * block_rows
        query_blk, key_blk, value_blk, scores = window_block(
            query_heads,
            keys_pad,
            values_pad,
            seq_ids,
            segs_pad,
            block_start,
            block_rows,
            half_window,
        )
        peak = jnp.max(scores, axis=-1, keepdims=True)
        expos = jnp.exp(scores - peak)
        totals = jnp.sum(expos, axis=-1, keepdims=True)
        probs_low = (expos / totals).astype(jnp.bfloat16)
        attended_blk = jnp.einsum(
            "hqk,khd->qhd", probs_low, value_blk, preferred_element_type=jnp.float32
        ).astype(jnp.bfloat16)
        return (attended_blk, (peak + jnp.log(totals))[..., 0])

    attended_blocks, logsum = lax.map(forward_block, jnp.arange(block_count, dtype=jnp.int32))
    attended_heads = attended_blocks.reshape(length, heads_local, DH)
    mixed_heads = lax.all_to_all(
        attended_heads, "seq", split_axis=0, concat_axis=1, tiled=True
    ).reshape(tok_rows, H * DH)
    residual = inputs + matmul(mixed_heads, full_output)
    second = rms_scale(residual, gain_moe)
    second_low = second.astype(jnp.bfloat16)
    logits = matmul(second_low, full_router)
    router_probs = jax.nn.softmax(logits, axis=-1)
    chosen = jnp.any(routes[0][:, :, None] == jnp.arange(E, dtype=jnp.int32)[None, None, :], axis=1)
    ranks = jnp.cumsum(chosen.astype(jnp.int32), axis=0) - 1
    picked = chosen.T[:, None, :] & (
        ranks.T[:, None, :] == jnp.arange(CAP, dtype=jnp.int32)[None, :, None]
    )
    slot_tok = jnp.sum(
        jnp.where(picked, jnp.arange(tok_rows, dtype=jnp.int32)[None, None, :], 0), axis=2
    )
    slot_used = jnp.any(picked, axis=2)
    slot_gate = jnp.sum(jnp.where(picked, router_probs.T[:, None, :], 0.0), axis=2)
    flat_slots = slot_tok.reshape(-1)
    expert_rows = jnp.take(second_low, slot_tok, axis=0)
    owner_rows = lax.all_to_all(expert_rows, "seq", split_axis=0, concat_axis=1, tiled=True)
    own_gate, own_up, own_down = (
        lax.all_gather(w_gate, "fsdp", axis=1, tiled=True),
        lax.all_gather(w_up, "fsdp", axis=1, tiled=True),
        lax.all_gather(w_down, "fsdp", axis=1, tiled=True),
    )
    gated = jnp.einsum("ecd,edf->ecf", owner_rows, own_gate, preferred_element_type=jnp.float32)
    upward = jnp.einsum("ecd,edf->ecf", owner_rows, own_up, preferred_element_type=jnp.float32)
    hidden_low = gate_mix(gated, upward).astype(jnp.bfloat16)
    outputs_low = jnp.einsum(
        "ecf,efd->ecd", hidden_low, own_down, preferred_element_type=jnp.float32
    ).astype(jnp.bfloat16)
    returned = lax.all_to_all(outputs_low, "seq", split_axis=1, concat_axis=0, tiled=True)
    returned_wide = returned.astype(jnp.float32)
    expert_sum = (
        jnp.zeros((tok_rows, D), jnp.float32)
        .at[flat_slots]
        .add((returned_wide * slot_gate[:, :, None]).reshape(-1, D))
    )
    mixed = (residual + expert_sum).astype(jnp.bfloat16)[None]
    upstream = cotangent[0].astype(jnp.float32)
    slot_grads = jnp.take(upstream, slot_tok, axis=0)
    gate_grads = jnp.where(slot_used, jnp.sum(slot_grads * returned_wide, axis=-1), 0.0)
    prob_grads = jnp.sum(jnp.where(picked, gate_grads[:, :, None], 0.0), axis=1).T
    softmax_pull = jax.vjp(partial(jax.nn.softmax, axis=-1), logits)[1]
    logit_grads = softmax_pull(prob_grads)[0]
    output_grads = (slot_grads * slot_gate[:, :, None]).astype(jnp.bfloat16)
    owner_grads = lax.all_to_all(output_grads, "seq", split_axis=0, concat_axis=1, tiled=True)
    down_term = jnp.einsum(
        "ecf,ecd->efd", hidden_low, owner_grads, preferred_element_type=jnp.float32
    )
    hidden_grads = jnp.einsum(
        "ecd,efd->ecf", owner_grads, own_down, preferred_element_type=jnp.float32
    )
    mix_pull = jax.vjp(gate_mix, gated, upward)[1]
    gated_grads, upward_grads = mix_pull(hidden_grads)
    gated_low = gated_grads.astype(jnp.bfloat16)
    upward_low = upward_grads.astype(jnp.bfloat16)
    gate_term = jnp.einsum(
        "ecd,ecf->edf", owner_rows, gated_low, preferred_element_type=jnp.float32
    )
    up_term = jnp.einsum("ecd,ecf->edf", owner_rows, upward_low, preferred_element_type=jnp.float32)
    row_grads = (
        jnp.einsum("ecf,edf->ecd", gated_low, own_gate, preferred_element_type=jnp.float32)
        + jnp.einsum("ecf,edf->ecd", upward_low, own_up, preferred_element_type=jnp.float32)
    ).astype(jnp.bfloat16)
    back_rows = lax.all_to_all(row_grads, "seq", split_axis=1, concat_axis=0, tiled=True)
    grad_gate, grad_up, grad_down = (
        lax.psum_scatter(
            gate_term.astype(jnp.bfloat16), "fsdp", scatter_dimension=1, tiled=True
        ).astype(jnp.float32),
        lax.psum_scatter(
            up_term.astype(jnp.bfloat16), "fsdp", scatter_dimension=1, tiled=True
        ).astype(jnp.float32),
        lax.psum_scatter(
            down_term.astype(jnp.bfloat16), "fsdp", scatter_dimension=1, tiled=True
        ).astype(jnp.float32),
    )
    router_wide = full_router.astype(jnp.float32)
    second_grads = (
        jnp.zeros((tok_rows, D), jnp.float32)
        .at[flat_slots]
        .add(back_rows.astype(jnp.float32).reshape(-1, D))
    )
    second_grads = second_grads + jnp.dot(logit_grads, router_wide.T, precision=HIGHEST)
    router_term = jnp.dot(second_low.astype(jnp.float32).T, logit_grads, precision=HIGHEST)
    second_pull = jax.vjp(rms_scale, residual, gain_moe)[1]
    residual_part, moe_gain_term = second_pull(second_grads)
    residual_grads = upstream + residual_part
    branch_low = residual_grads.astype(jnp.bfloat16)
    output_term = matmul(mixed_heads.T, branch_low)
    head_grads = matmul(branch_low, full_output.T).astype(jnp.bfloat16).reshape(tok_rows, H, DH)
    grads_heads = lax.all_to_all(head_grads, "seq", split_axis=1, concat_axis=0, tiled=True)
    key_span = block_rows + 2 * half_window
    start_state = (
        jnp.zeros(query_heads.shape, jnp.float32),
        jnp.zeros(keys_pad.shape, jnp.float32),
        jnp.zeros(values_pad.shape, jnp.float32),
    )

    def backward_block(block_index, state):
        query_acc, key_acc, value_acc = state
        block_start = block_index * block_rows
        query_blk, key_blk, value_blk, scores = window_block(
            query_heads,
            keys_pad,
            values_pad,
            seq_ids,
            segs_pad,
            block_start,
            block_rows,
            half_window,
        )
        probs = jnp.exp(scores - logsum[block_index][..., None])
        grads_blk = lax.dynamic_slice_in_dim(grads_heads, block_start, block_rows, 0)
        value_part = jnp.einsum(
            "hqk,qhd->khd",
            probs.astype(jnp.bfloat16),
            grads_blk,
            preferred_element_type=jnp.float32,
        )
        prob_part = jnp.einsum(
            "qhd,khd->hqk", grads_blk, value_blk, preferred_element_type=jnp.float32
        )
        center = jnp.sum(probs * prob_part, axis=-1, keepdims=True)
        score_low = (probs * (prob_part - center)).astype(jnp.bfloat16)
        query_part = jnp.einsum(
            "hqk,khd->qhd", score_low, key_blk, preferred_element_type=jnp.float32
        ) * DH ** (-0.5)
        key_part = jnp.einsum(
            "hqk,qhd->khd", score_low, query_blk, preferred_element_type=jnp.float32
        ) * DH ** (-0.5)
        query_acc = lax.dynamic_update_slice_in_dim(query_acc, query_part, block_start, 0)
        key_acc = lax.dynamic_update_slice_in_dim(
            key_acc,
            lax.dynamic_slice_in_dim(key_acc, block_start, key_span, 0) + key_part,
            block_start,
            0,
        )
        value_acc = lax.dynamic_update_slice_in_dim(
            value_acc,
            lax.dynamic_slice_in_dim(value_acc, block_start, key_span, 0) + value_part,
            block_start,
            0,
        )
        return (query_acc, key_acc, value_acc)

    query_acc, key_acc, value_acc = lax.fori_loop(0, block_count, backward_block, start_state)
    query_send = query_acc.astype(jnp.bfloat16)
    key_send = key_acc[half_window : half_window + length].astype(jnp.bfloat16)
    value_send = value_acc[half_window : half_window + length].astype(jnp.bfloat16)
    query_back, key_back, value_back = (
        lax.all_to_all(query_send, "seq", split_axis=0, concat_axis=1, tiled=True),
        lax.all_to_all(key_send, "seq", split_axis=0, concat_axis=1, tiled=True),
        lax.all_to_all(value_send, "seq", split_axis=0, concat_axis=1, tiled=True),
    )
    query_pull = jax.vjp(partial(prepare, places=places), query_pre, gain_query)[1]
    query_pre_grads, query_gain_term = query_pull(query_back.astype(jnp.float32))
    key_pull = jax.vjp(partial(prepare, places=places), key_pre, gain_key)[1]
    key_pre_grads, key_gain_term = key_pull(key_back.astype(jnp.float32))
    query_pre_low = query_pre_grads.astype(jnp.bfloat16)
    key_pre_low = key_pre_grads.astype(jnp.bfloat16)
    value_back_low = value_back.reshape(tok_rows, H * DH)
    query_term = matmul(normed_low.T, query_pre_low)
    key_term = matmul(normed_low.T, key_pre_low)
    value_term = matmul(normed_low.T, value_back_low)
    normed_grads = (
        matmul(query_pre_low, full_query.T)
        + matmul(key_pre_low, full_key.T)
        + matmul(value_back_low, full_value.T)
    )
    first_pull = jax.vjp(rms_scale, inputs, gain_attn)[1]
    input_part, attn_gain_term = first_pull(normed_grads)
    grad_tokens = (residual_grads + input_part)[None]
    summed = (
        lax.psum_scatter(query_term, ("seq", "fsdp"), scatter_dimension=0, tiled=True),
        lax.psum_scatter(key_term, ("seq", "fsdp"), scatter_dimension=0, tiled=True),
        lax.psum_scatter(value_term, ("seq", "fsdp"), scatter_dimension=0, tiled=True),
        lax.psum_scatter(output_term, ("seq", "fsdp"), scatter_dimension=0, tiled=True),
        lax.psum_scatter(router_term, ("seq", "fsdp"), scatter_dimension=0, tiled=True),
        lax.psum_scatter(attn_gain_term, ("seq", "fsdp"), scatter_dimension=0, tiled=True),
        lax.psum_scatter(moe_gain_term, ("seq", "fsdp"), scatter_dimension=0, tiled=True),
        lax.psum_scatter(query_gain_term, ("seq", "fsdp"), scatter_dimension=0, tiled=True),
        lax.psum_scatter(key_gain_term, ("seq", "fsdp"), scatter_dimension=0, tiled=True),
    )
    return (
        mixed,
        grad_tokens,
        summed[0],
        summed[1],
        summed[2],
        summed[3],
        summed[4],
        summed[5],
        summed[6],
        summed[7],
        summed[8],
        grad_gate,
        grad_up,
        grad_down,
    )


def solution(mesh):
    in_specs = (
        P("fsdp", "seq", None),
        P("fsdp", None),
        P("fsdp", "seq", None),
        P("fsdp", "seq", None),
        P(("seq", "fsdp"), None),
        P(("seq", "fsdp"), None),
        P(("seq", "fsdp"), None),
        P(("seq", "fsdp"), None),
        P(("seq", "fsdp"), None),
        P(("seq", "fsdp")),
        P(("seq", "fsdp")),
        P(("seq", "fsdp")),
        P(("seq", "fsdp")),
        P("seq", "fsdp", None),
        P("seq", "fsdp", None),
        P("seq", "fsdp", None),
    )
    out_specs = (
        P("fsdp", "seq", None),
        P("fsdp", "seq", None),
        P(("seq", "fsdp"), None),
        P(("seq", "fsdp"), None),
        P(("seq", "fsdp"), None),
        P(("seq", "fsdp"), None),
        P(("seq", "fsdp"), None),
        P(("seq", "fsdp")),
        P(("seq", "fsdp")),
        P(("seq", "fsdp")),
        P(("seq", "fsdp")),
        P("seq", "fsdp", None),
        P("seq", "fsdp", None),
        P("seq", "fsdp", None),
    )
    return jax.shard_map(
        per_device, mesh=mesh, in_specs=in_specs, out_specs=out_specs, check_vma=False
    )
```

profile of v0, /device:TPU:0, one launch (start us, length us, event | category | flops | bytes accessed | tf_op | source)
XLA Modules:
  0.0 3051.5 jit_solution(15200636733246425044)
XLA Ops:
  11.6 43.0 %all-reduce.16 = (bf16[2048]{0:T(1024)(128)(2,1)S(1)}, bf16[2048]{0:T(1024)(128)(2,1)S(1)}, bf16[2048]{0:T(1024)(128)(2,1)S(1)}, bf16[2048]{0:T(1024)(128)(2,1)S(1)}) all-reduce(bf16[2048]{0:T(1024)(128)(2,1)S(1)} %dynamic-update-slice, bf16[2048]{0:T(1024)(128)(2,1)S(1)} %dynamic-update-slice.1, ...), channel_id=1, replica_groups=mesh['seq'=8,'fsdp'=4] {'seq','fsdp'}, use_global_device_ids=true, to_apply=%add.7 | all-reduce | flops 8192 | bytes 32768
  55.7 35.8 %all-gather.9.cloned.1.call-done = bf16[2048,2048]{1,0:T(8,128)(2,1)} async-done(((bf16[64,2048]{1,0:T(8,128)(2,1)}), bf16[2048,2048]{1,0:T(8,128)(2,1)}) %all-gather.9.cloned.1.call-update) | async-done | bytes 8388624 | tf_op jit(solution)/shard_map/all_gather | solution.py:95
  102.9 71.8 %all-gather.13.cloned.1.call-done = bf16[2048,2048]{1,0:T(8,128)(2,1)} async-done(((bf16[64,2048]{1,0:T(8,128)(2,1)}), bf16[2048,2048]{1,0:T(8,128)(2,1)}) %all-gather.13.cloned.1.call-update) | async-done | bytes 8388624 | tf_op jit(solution)/shard_map/all_gather | solution.py:94
  182.5 71.2 %all-gather.11.cloned.1.call-done = bf16[2048,2048]{1,0:T(8,128)(2,1)} async-done(((bf16[64,2048]{1,0:T(8,128)(2,1)}), bf16[2048,2048]{1,0:T(8,128)(2,1)}) %all-gather.11.cloned.1.call-update) | async-done | bytes 8388624 | tf_op jit(solution)/shard_map/all_gather | solution.py:93
  311.8 46.5 %while.33 = (s32[]{:T(128)}, bf16[4,512,2,128]{3,1,0,2:T(8,128)(2,1)S(1)}, f32[4,2,512]{2,1,0:T(2,128)}, s32[4]{0:T(128)S(1)}, bf16[3072,2,128]{2,0,1:T(8,128)(2...) while((s32[]{:T(128)}, ...), condition=%wide.region_6.7_spmd, body=%wide.region_3.6_spmd.sunk | while | flops 828244992 | bytes 25239832 | solution.py:161
  419.2 104.5 %all-to-all-done.4 = bf16[16,144,2048]{2,1,0:T(8,128)(2,1)} async-done(((bf16[16,144,2048]{2,1,0:T(8,128)(2,1)}), bf16[16,144,2048]{2,1,0:T(8,128)(2,1)}, u32[]{:S(2)}, u32[]{:S(2)}) %all-to-all-start.4) | async-done | bytes 9437216 | tf_op jit(solution)/shard_map/all_to_all | solution.py:183
  550.5 83.7 %all-gather.19.cloned.1.call-done = bf16[2,2048,1024]{2,1,0:T(8,128)(2,1)} async-done(((bf16[2,512,1024]{2,1,0:T(8,128)(2,1)}), bf16[2,2048,1024]{2,1,0:T(8,128)(2,1)}) %all-gather.19.cloned.1.call-update) | async-done | bytes 8388624 | tf_op jit(solution)/shard_map/all_gather | solution.py:186
  634.2 19.7 multiply_convert_fusion.3
  653.8 129.8 %all-gather.21.cloned.1.call-done = bf16[2,1024,2048]{2,1,0:T(8,128)(2,1)} async-done(((bf16[2,256,2048]{2,1,0:T(8,128)(2,1)}), bf16[2,1024,2048]{2,1,0:T(8,128)(2,1)}) %all-gather.21.cloned.1.call-update) | async-done | bytes 8388624 | tf_op jit(solution)/shard_map/all_gather | solution.py:187
  797.8 28.1 copy.192
  831.2 68.7 %all-gather = bf16[32,64,16]{1,2,0:T(8,128)(2,1)S(1)} all-gather(bf16[1,64,16]{1,2,0:T(8,128)(2,1)S(1)} %bitcast.299), channel_id=1, replica_groups=mesh['seq'=8,'fsdp'=4] {'seq','fsdp'}, dimensions={0}, use_global_device_ids=true | all-gather | bytes 67584 | tf_op jit(solution)/shard_map/all_gather | solution.py:97
  914.3 22.8 all-to-all-done.5
  952.7 17.3 fusion.39
  989.7 106.6 %all-to-all-done.6 = bf16[16,144,2048]{2,1,0:T(8,128)(2,1)} async-done(((bf16[16,144,2048]{2,1,0:T(8,128)(2,1)}), bf16[16,144,2048]{2,1,0:T(8,128)(2,1)}, u32[]{:S(2)}, u32[]{:S(2)}) %all-to-all-start.6) | async-done | bytes 9437216 | tf_op jit(solution)/shard_map/all_to_all | solution.py:210
  1105.5 21.6 multiply_convert_fusion.2
  1144.4 17.9 convolution_convert_fusion.2
  1162.4 17.7 convolution_convert_fusion.1
  1180.1 17.6 fusion.99
  1197.7 19.3 add_convert_fusion
  1217.0 18.2 copy.196
  1243.1 102.7 %all-to-all-done.7 = bf16[2,1152,2048]{2,0,1:T(2,128)(2,1)} async-done(((bf16[2,1152,2048]{2,0,1:T(2,128)(2,1)}), bf16[2,1152,2048]{2,0,1:T(2,128)(2,1)}, u32[]{:S(2)}, u32[]{:S(2)}) %all-to-all-start.7) | async-done | bytes 9437216 | tf_op jit(solution)/shard_map/all_to_all | solution.py:229
  1361.0 36.6 %scatter_fusion.1 = f32[256,2048]{1,0:T(8,128)} fusion(f32[256,2048]{1,0:T(8,128)} %fusion.85, s32[2304]{0:T(1024)S(1)} %fusion.79, f32[2304,2048]{1,0:T(8,128)} %bitcast.267), kind=kCustom, calls=%fused_computation.3 | custom fusion | flops 4718592 | bytes 56632320 | tf_op jit(solution)/shard_map/scatter-add | solution.py:245
  1445.7 198.4 %while.34 = (s32[]{:T(128)}, bf16[2048,2,128]{2,1,0:T(2,128)(2,1)}, f32[3072,2,128]{2,1,0:T(2,128)}, f32[3072,2,128]{2,1,0:T(2,128)}, bf16[3072,2,128]{2,0,1:T(8...) while((s32[]{:T(128)}, bf16[2048,2,128]{2,1,0:T(2,128)(2,1)}, ...), condition=%wide.region_24.25_spmd, body=%wide.region_22.24_spmd.sunk | while | flops 2032796672 | bytes 135328176 | solution.py:310
  1646.1 22.4 all_to_all.174
  1674.0 17.3 all-to-all-done.9
  1723.8 21.8 all_to_all.175
  1786.5 34.6 %scatter_fusion = f32[256,2048]{1,0:T(8,128)S(1)} fusion(f32[256,2048]{1,0:T(8,128)S(1)} %copy-done.2, s32[2304]{0:T(1024)S(1)} %copy-done.55, f32[2304,2048]{1,0:T(8,128)} %bitcast_multiply_fusion), kind=kCustom, calls=%fused_computation.2 | custom fusion | flops 4718592 | bytes 56632320 | tf_op jit(solution)/shard_map/scatter-add | solution.py:200
  1838.8 40.3 %all-reduce.15 = (f32[2048]{0:T(1024)S(1)}, f32[2048]{0:T(1024)S(1)}, f32[2048]{0:T(1024)S(1)}, f32[2048]{0:T(1024)S(1)}) all-reduce(f32[2048]{0:T(1024)S(1)} %get-tuple-element.459, f32[2048]{0:T(1024)S(1)} %copy-done.65, f32[2048]{0:T(1024)S(1)} %copy-done.66, ...), channel_id=7, replica_groups=mesh['seq'=8,'fsdp'=4] {'seq','fsdp'}, use_global_device_ids=true, to_apply=%region_34.35.clone | all-reduce | flops 8192 | bytes 65536
  1897.2 52.2 %reduce-scatter.17.cloned.1.call-done = f32[64,2048]{1,0:T(8,128)} async-done(((f32[2048,2048]{1,0:T(8,128)}), f32[64,2048]{1,0:T(8,128)}) %reduce-scatter.17.cloned.1.call-update) | async-done | bytes 524304 | tf_op jit(solution)/shard_map/reduce_scatter | solution.py:341
  1949.5 365.2 %reduce-scatter.11.cloned.1.call-done = f32[64,2048]{1,0:T(8,128)} async-done(((f32[2048,2048]{1,0:T(8,128)}), f32[64,2048]{1,0:T(8,128)}) %reduce-scatter.11.cloned.1.call-update) | async-done | bytes 524304 | tf_op jit(solution)/shard_map/reduce_scatter | solution.py:338
  2314.7 365.0 %reduce-scatter.13.cloned.1.call-done = f32[64,2048]{1,0:T(8,128)} async-done(((f32[2048,2048]{1,0:T(8,128)}), f32[64,2048]{1,0:T(8,128)}) %reduce-scatter.13.cloned.1.call-update) | async-done | bytes 524304 | tf_op jit(solution)/shard_map/reduce_scatter | solution.py:339
  2679.7 365.0 %reduce-scatter.15.cloned.1.call-done = f32[64,2048]{1,0:T(8,128)} async-done(((f32[2048,2048]{1,0:T(8,128)}), f32[64,2048]{1,0:T(8,128)}) %reduce-scatter.15.cloned.1.call-update) | async-done | bytes 524304 | tf_op jit(solution)/shard_map/reduce_scatter | solution.py:340
  (536 shorter events, 694.2 us)
Async XLA Ops:
  7.2 84.3 %all-gather.9.cloned.1.call-start = ((), (), s32[]{:S(2)}) async-start(), calls=%async_computation.20 | async-start | bytes 8650752 | tf_op jit(solution)/shard_map/all_gather | solution.py:95
  8.0 166.8 %all-gather.13.cloned.1.call-start = ((), (), s32[]{:S(2)}) async-start(), calls=%async_computation.22 | async-start | bytes 8650752 | tf_op jit(solution)/shard_map/all_gather | solution.py:94
  8.7 245.0 %all-gather.11.cloned.1.call-start = ((), (), s32[]{:S(2)}) async-start(), calls=%async_computation.21 | async-start | bytes 8650752 | tf_op jit(solution)/shard_map/all_gather | solution.py:93
  9.4 378.0 %all-gather.15.cloned.1.call-start = ((), (), s32[]{:S(2)}) async-start(), calls=%async_computation.23 | async-start | bytes 8650752 | tf_op jit(solution)/shard_map/all_gather | solution.py:96
  10.0 523.1 %all-gather.17.cloned.1.call-start = ((), (), s32[]{:S(2)}) async-start(), calls=%async_computation.24 | async-start | bytes 10485760 | tf_op jit(solution)/shard_map/all_gather | solution.py:185
  54.7 199.0 %copy-start.40 = (f32[2048]{0:T(1024)}, f32[2048]{0:T(1024)S(1)}, u32[]{:S(2)}) copy-start(f32[2048]{0:T(1024)S(1)} %convert_element_type.205) | copy-start | bytes 24580
  54.7 125.9 %copy-start.48 = (f32[2048]{0:T(1024)}, f32[2048]{0:T(1024)S(1)}, u32[]{:S(2)}) copy-start(f32[2048]{0:T(1024)S(1)} %convert_element_type.210) | copy-start | bytes 24580
  54.7 204.9 %copy-start.50 = (f32[2048]{0:T(1024)}, f32[2048]{0:T(1024)S(1)}, u32[]{:S(2)}) copy-start(f32[2048]{0:T(1024)S(1)} %convert_element_type.208) | copy-start | bytes 24580
  55.1 198.6 %copy-start.59 = (f32[256]{0:T(256)}, f32[256]{0:T(256)S(1)}, u32[]{:S(2)}) copy-start(f32[256]{0:T(256)S(1)} %fusion.80) | copy-start | bytes 3076
  55.6 207.1 %copy-start.27 = (f32[256,64]{1,0:T(8,128)}, f32[256,64]{1,0:T(8,128)S(1)}, u32[]{:S(2)}) copy-start(f32[256,64]{1,0:T(8,128)S(1)} %get-tuple-element.535) | copy-start | bytes 196612
  55.7 207.1 %copy-start.29 = (f32[256,64]{1,0:T(8,128)}, f32[256,64]{1,0:T(8,128)S(1)}, u32[]{:S(2)}) copy-start(f32[256,64]{1,0:T(8,128)S(1)} %get-tuple-element.536) | copy-start | bytes 196612
  98.5 168.6 %all-to-all-start = ((bf16[256,16,128]{2,0,1:T(8,128)(2,1)}), bf16[256,16,128]{2,0,1:T(8,128)(2,1)}, u32[]{:S(2)}, u32[]{:S(2)}) async-start(bf16[256,16,128]{2,0,1:T(8,128)(2,1)} %bitcast.244), calls=%async_computation | async-start | bytes 2097152 | tf_op jit(solution)/shard_map/all_to_all | solution.py:127
  267.1 22.2 all-to-all-start.1
  289.2 19.6 all-to-all-start.2
  292.8 341.4 %all-gather.19.cloned.1.call-start = ((), (), s32[]{:S(2)}) async-start(), calls=%async_computation.25 | async-start | bytes 10485760 | tf_op jit(solution)/shard_map/all_gather | solution.py:186
  367.8 18.9 all-to-all-start.3
  372.1 459.0 %copy-start.38 = (s32[16,144]{1,0:T(8,128)}, s32[16,144]{1,0:T(8,128)S(1)}, u32[]{:S(2)}) copy-start(s32[16,144]{1,0:T(8,128)S(1)} %select_reduce_fusion.2) | copy-start | bytes 27652
  413.5 110.3 %all-to-all-start.4 = ((bf16[16,144,2048]{2,1,0:T(8,128)(2,1)}), bf16[16,144,2048]{2,1,0:T(8,128)(2,1)}, u32[]{:S(2)}, u32[]{:S(2)}) async-start(bf16[16,144,2048]{2,1,0:T(8,128)(2,1)} %broadcast_select_fusion), calls=%async_computation.4 | async-start | bytes 18874368 | tf_op jit(solution)/shard_map/all_to_all | solution.py:183
  418.5 365.1 %all-gather.21.cloned.1.call-start = ((), (), s32[]{:S(2)}) async-start(), calls=%async_computation.26 | async-start | bytes 10485760 | tf_op jit(solution)/shard_map/all_gather | solution.py:187
  825.9 111.2 %all-to-all-start.5 = ((bf16[2,1152,2048]{2,0,1:T(2,128)(2,1)}), bf16[2,1152,2048]{2,0,1:T(2,128)(2,1)}, u32[]{:S(2)}, u32[]{:S(2)}) async-start(bf16[2,1152,2048]{2,0,1:T(2,128)(2,1)} %copy.192), calls=%async_computation.5 | async-start | bytes 18874368 | tf_op jit(solution)/shard_map/all_to_all | solution.py:195
  981.8 114.5 %all-to-all-start.6 = ((bf16[16,144,2048]{2,1,0:T(8,128)(2,1)}), bf16[16,144,2048]{2,1,0:T(8,128)(2,1)}, u32[]{:S(2)}, u32[]{:S(2)}) async-start(bf16[16,144,2048]{2,1,0:T(8,128)(2,1)} %multiply_convert_fusion.1), calls=%async_computation.6 | async-start | bytes 18874368 | tf_op jit(solution)/shard_map/all_to_all | solution.py:210
  986.9 798.2 %reduce-scatter.25.cloned.1.call-start = ((), (), s32[]{:S(2)}) async-start(), calls=%async_computation.34 | async-start | bytes 1081344
  989.7 895.2 %reduce-scatter.19.cloned.1.call-start = ((), (), s32[]{:S(2)}) async-start(), calls=%async_computation.31 | async-start | bytes 10485760 | tf_op jit(solution)/shard_map/reduce_scatter | solution.py:231
  1144.2 744.8 %reduce-scatter.21.cloned.1.call-start = ((), (), s32[]{:S(2)}) async-start(), calls=%async_computation.32 | async-start | bytes 10485760 | tf_op jit(solution)/shard_map/reduce_scatter | solution.py:234
  1162.3 730.8 %reduce-scatter.23.cloned.1.call-start = ((), (), s32[]{:S(2)}) async-start(), calls=%async_computation.33 | async-start | bytes 10485760 | tf_op jit(solution)/shard_map/reduce_scatter | solution.py:237
  1235.3 110.5 %all-to-all-start.7 = ((bf16[2,1152,2048]{2,0,1:T(2,128)(2,1)}), bf16[2,1152,2048]{2,0,1:T(2,128)(2,1)}, u32[]{:S(2)}, u32[]{:S(2)}) async-start(bf16[2,1152,2048]{2,0,1:T(2,128)(2,1)} %copy.196), calls=%async_computation.7 | async-start | bytes 18874368 | tf_op jit(solution)/shard_map/all_to_all | solution.py:229
  1240.5 709.0 %reduce-scatter.17.cloned.1.call-start = ((), (), s32[]{:S(2)}) async-start(), calls=%async_computation.30 | async-start | bytes 17301504 | tf_op jit(solution)/shard_map/reduce_scatter | solution.py:341
  1419.2 19.1 all-to-all-start.8
  1668.5 22.8 all-to-all-start.9
  1672.0 642.6 %reduce-scatter.11.cloned.1.call-start = ((), (), s32[]{:S(2)}) async-start(), calls=%async_computation.27 | async-start | bytes 17301504 | tf_op jit(solution)/shard_map/reduce_scatter | solution.py:338
  1706.6 973.1 %reduce-scatter.13.cloned.1.call-start = ((), (), s32[]{:S(2)}) async-start(), calls=%async_computation.28 | async-start | bytes 17301504 | tf_op jit(solution)/shard_map/reduce_scatter | solution.py:339
  1721.8 1322.9 %reduce-scatter.15.cloned.1.call-start = ((), (), s32[]{:S(2)}) async-start(), calls=%async_computation.29 | async-start | bytes 17301504 | tf_op jit(solution)/shard_map/reduce_scatter | solution.py:340
  (102 other events, 1360.7 us)
Sparse Core Ops, SparseCore 0:
  11.0 80.4 all-gather.8
  94.4 80.2 all-gather.12
  177.7 75.9 all-gather.10
  256.5 79.0 all-gather.14
  337.0 147.8 all-gather.16
  486.3 147.8 all-gather.18
  635.7 147.8 all-gather.20
  990.0 136.6 reduce-scatter.24
  1144.3 141.1 reduce-scatter.18
  1287.8 145.1 reduce-scatter.20
  1435.6 145.1 reduce-scatter.22
  1583.6 365.8 reduce-scatter.16
  1952.5 362.1 reduce-scatter.10
  2317.5 362.1 reduce-scatter.12
  2682.5 362.1 reduce-scatter.14
where the time goes:
time: 3060 us; the launch traced here: 3050 us
  waiting for transfers between devices  1950 us (64%)
  matrix products  356 us (12%)
  local copies, waits for them, and re-layouts  280 us (9%)
  other arithmetic  200 us (7%)
  blocking collectives  196 us (6%)
  starting transfers between devices  45.6 us (1%)
    reduce_scatter x1, waiting for transfers between devices, per_device(): lax.psum_scatter(query_term, ('seq', 'fsdp'), scatter_dimension=0, tiled=...  365 us
    reduce_scatter x1, waiting for transfers between devices, per_device(): lax.psum_scatter(key_term, ('seq', 'fsdp'), scatter_dimension=0, tiled=True)  365 us
    reduce_scatter x1, waiting for transfers between devices, per_device(): lax.psum_scatter(value_term, ('seq', 'fsdp'), scatter_dimension=0, tiled=...  365 us
    all_gather x1, waiting for transfers between devices, per_device(): lax.all_gather(w_down, 'fsdp', axis=1, tiled=True)  130 us
    all_to_all x1, waiting for transfers between devices, per_device(): lax.all_to_all(output_grads, 'seq', split_axis=0, concat_axis=1, tiled=True)  107 us
    all_to_all x1, waiting for transfers between devices, per_device(): lax.all_to_all(expert_rows, 'seq', split_axis=0, concat_axis=1, tiled=True)  105 us
    all_to_all x1, waiting for transfers between devices, per_device(): lax.all_to_all(row_grads, 'seq', split_axis=1, concat_axis=0, tiled=True)  103 us
    all_gather x1, waiting for transfers between devices, per_device(): lax.all_gather(w_up, 'fsdp', axis=1, tiled=True)  83.7 us
  transfers between devices with their start and end apart: 25, of which 18 were waited for; matrix products, arithmetic and copies ran while one was open for 24% of the time, Pallas kernels for 0%

commit v1 on v0

v1 whole, which is shorter than its diff:
```python
from functools import partial

import jax
import jax.numpy as jnp
from jax import lax
from jax.experimental import pallas as pl
from jax.experimental.pallas import tpu as pltpu
from jax.sharding import PartitionSpec as P

D = 2048
H = 16
DH = 128
E = 16
WINDOW = 1024
CAP = 144

EPSILON = 1e-06
ROPE_BASE = 50000.0
HIGHEST = lax.Precision.HIGHEST
BF16 = jnp.bfloat16
F32 = jnp.float32
MIB = 1024 * 1024


def matmul(left, right):
    return jnp.dot(left, right, preferred_element_type=F32)


def matmul_t(left, right):
    return lax.dot_general(left, right, (((1,), (1,)), ((), ())), preferred_element_type=F32)


def t_matmul(left, right):
    return lax.dot_general(left, right, (((0,), (0,)), ((), ())), preferred_element_type=F32)


def rms_factor(values):
    return lax.rsqrt(jnp.mean(values * values, axis=-1, keepdims=True) + EPSILON)


def swap(values, axis, size, mask):
    return lax.ppermute(values, axis, [(i, i ^ mask) for i in range(size)])


def high_bit(number):
    return 1 << (number.bit_length() - 1)


def low_bit(number):
    return number & -number


def gather_pieces(values, axis, size):
    rows = values.shape[0] // 2
    pieces = {0: (values[:rows], values[rows:])}
    for r in range(2, size, 2):
        if r == low_bit(r):
            whole = swap(values, axis, size, r)
            pieces[r] = (whole[:rows], whole[rows:])
        else:
            up, down = high_bit(r), low_bit(r)
            pieces[r] = (
                swap(pieces[r ^ up][0], axis, size, up),
                swap(pieces[r ^ down][1], axis, size, down),
            )
    for r in range(0, size, 2):
        if r == low_bit(r) or r == 0:
            whole = swap(jnp.concatenate(pieces[r], 0), axis, size, 1)
            pieces[r + 1] = (whole[:rows], whole[rows:])
        else:
            pieces[r + 1] = tuple(swap(half, axis, size, 1) for half in pieces[r])
    return pieces


def place_pieces(pieces, me, size):
    half_rows, columns = pieces[0][0].shape
    whole = jnp.zeros((size * 2 * half_rows, columns), pieces[0][0].dtype)
    for r in range(size):
        for k in range(2):
            at = ((me ^ r) * 2 + k) * half_rows
            whole = lax.dynamic_update_slice_in_dim(whole, pieces[r][k], at, 0)
    return whole


def gather_seq(values, me, size):
    return place_pieces(gather_pieces(values, "seq", size), me, size)


def scatter_sum(chunk_of, axis, size):
    sums = {}
    for r in range(0, size, 2):
        sums[r] = chunk_of(r).astype(F32) + swap(chunk_of(r + 1), axis, size, 1).astype(F32)
    rows = sums[0].shape[0] // 2
    sums = {r: [value[:rows], value[rows:]] for r, value in sums.items()}
    for r in range(size - 2, 0, -2):
        if r == low_bit(r):
            whole = jnp.concatenate([half.astype(BF16) for half in sums[r]], 0)
            got = swap(whole, axis, size, r).astype(F32)
            sums[0] = [sums[0][0] + got[:rows], sums[0][1] + got[rows:]]
        else:
            up, down = high_bit(r), low_bit(r)
            sums[r ^ up][0] += swap(sums[r][0].astype(BF16), axis, size, up).astype(F32)
            sums[r ^ down][1] += swap(sums[r][1].astype(BF16), axis, size, down).astype(F32)
    return jnp.concatenate(sums[0], 0)


def sum_all(values, axis, size):
    mask = 1
    while mask < size:
        values = values + swap(values, axis, size, mask)
        mask *= 2
    return values


def gather_expert_cols(weight, me, size):
    experts, part, hidden = weight.shape
    half = size // 2
    mine = lax.dynamic_slice_in_dim(weight, (me // half) * (hidden // 2), hidden // 2, 2)
    theirs = lax.dynamic_slice_in_dim(weight, (1 - me // half) * (hidden // 2), hidden // 2, 2)
    pieces = {0: mine, half: swap(theirs, "fsdp", size, half)}
    for r in range(1, half):
        up = high_bit(r)
        for base in (0, half):
            pieces[r | base] = swap(pieces[(r ^ up) | base], "fsdp", size, up)
    whole = jnp.zeros((experts, size, part, hidden // 2), weight.dtype)
    for r in range(size):
        whole = lax.dynamic_update_slice_in_dim(whole, pieces[r][:, None], me ^ r, 1)
    return whole.reshape(experts, size * part, hidden // 2)


def gather_expert_rows(weight, me, size):
    experts, part, columns = weight.shape
    half = size // 2
    pieces = {0: weight}
    for r in range(1, half):
        up = high_bit(r)
        pieces[r] = swap(pieces[r ^ up], "fsdp", size, up)
    whole = jnp.zeros((experts, half, part, columns), weight.dtype)
    for r in range(half):
        whole = lax.dynamic_update_slice_in_dim(whole, pieces[r][:, None], (me ^ r) % half, 1)
    return whole.reshape(experts, half * part, columns)


def scatter_expert_cols(partial_sum, me, size):
    experts, depth, hidden_half = partial_sum.shape
    half = size // 2
    parts = partial_sum.reshape(experts, size, depth // size, hidden_half)

    def chunk(r):
        return lax.dynamic_index_in_dim(parts, me ^ r, 1, keepdims=False)

    sums = {r: chunk(r) for r in range(size)}
    for r in range(half - 1, 0, -1):
        up = high_bit(r)
        for base in (half, 0):
            got = swap(sums[r | base].astype(BF16), "fsdp", size, up)
            sums[(r ^ up) | base] += got.astype(F32)
    got = swap(sums[half].astype(BF16), "fsdp", size, half).astype(F32)
    first = me // half == 0
    return jnp.concatenate(
        [jnp.where(first, sums[0], got), jnp.where(first, got, sums[0])], axis=-1
    )


def scatter_expert_rows(partial_sum, me, size):
    experts, hidden_half, columns = partial_sum.shape
    half = size // 2
    parts = partial_sum.reshape(experts, half, hidden_half // half, columns)
    sums = {
        r: lax.dynamic_index_in_dim(parts, (me ^ r) % half, 1, keepdims=False) for r in range(half)
    }
    for r in range(half - 1, 0, -1):
        up = high_bit(r)
        sums[r ^ up] += swap(sums[r].astype(BF16), "fsdp", size, up).astype(F32)
    return sums[0]


def allowed_keys(seg_row, seg_col, first_query, first_key, rows, span, half_window):
    query_at = first_query + lax.broadcasted_iota(jnp.int32, (span, rows), 1)
    key_at = first_key + lax.broadcasted_iota(jnp.int32, (span, rows), 0)
    return (jnp.abs(query_at - key_at) <= half_window) & (seg_col == seg_row)


def first_key_of(block, rows, span, length):
    start = jnp.clip(block * rows - (span - rows) // 2, 0, length - span)
    return pl.multiple_of(start, rows)


def forward_kernel(span, q_ref, k_ref, v_ref, seg_row_ref, seg_col_ref, o_ref, lse_ref):
    block = pl.program_id(1)
    rows, length = q_ref.shape[0], k_ref.shape[0]
    first_key = first_key_of(block, rows, span, length)
    keys = k_ref[pl.ds(first_key, span), :]
    values = v_ref[pl.ds(first_key, span), :]
    scores = matmul_t(keys, q_ref[...]) * DH ** (-0.5)
    allowed = allowed_keys(
        seg_row_ref[...],
        seg_col_ref[pl.ds(first_key, span), :],
        block * rows,
        first_key,
        rows,
        span,
        WINDOW // 2,
    )
    scores = jnp.where(allowed, scores, -1e30)
    peak = jnp.max(scores, axis=0, keepdims=True)
    expos = jnp.exp(scores - peak)
    totals = jnp.sum(expos, axis=0, keepdims=True)
    probs = (expos * (1.0 / totals)).astype(BF16)
    o_ref[...] = t_matmul(values, probs).T.astype(BF16)
    lse_ref[...] = (peak + jnp.log(totals))[None]


def backward_kernel(
    span,
    q_ref,
    k_ref,
    v_ref,
    do_ref,
    lse_ref,
    seg_row_ref,
    seg_col_ref,
    dq_ref,
    dk_ref,
    dv_ref,
    dk_sum,
    dv_sum,
):
    block = pl.program_id(1)
    rows, length = q_ref.shape[0], k_ref.shape[0]

    @pl.when(block == 0)
    def _():
        dk_sum[...] = jnp.zeros_like(dk_sum)
        dv_sum[...] = jnp.zeros_like(dv_sum)

    first_key = first_key_of(block, rows, span, length)
    at = pl.ds(first_key, span)
    keys = k_ref[at, :]
    values = v_ref[at, :]
    queries = q_ref[...]
    grads = do_ref[...]
    scores = matmul_t(keys, queries) * DH ** (-0.5)
    allowed = allowed_keys(
        seg_row_ref[...],
        seg_col_ref[at, :],
        block * rows,
        first_key,
        rows,
        span,
        WINDOW // 2,
    )
    probs = jnp.where(allowed, jnp.exp(scores - lse_ref[0]), 0.0)
    dv_sum[at, :] += matmul(probs.astype(BF16), grads)
    prob_grads = matmul_t(values, grads)
    center = jnp.sum(probs * prob_grads, axis=0, keepdims=True)
    score_grads = (probs * (prob_grads - center)).astype(BF16)
    dk_sum[at, :] += matmul(score_grads, queries)
    dq_ref[...] = (t_matmul(keys, score_grads) * DH ** (-0.5)).T.astype(BF16)

    @pl.when(block == length // rows - 1)
    def _():
        dk_ref[...] = (dk_sum[...] * DH ** (-0.5)).astype(BF16)
        dv_ref[...] = dv_sum[...].astype(BF16)


def attention_sizes(length):
    rows = 256
    return rows, min(length, rows + WINDOW)


def attention_forward(queries, keys, values, seg_row, seg_col):
    length, columns = queries.shape
    heads = columns // DH
    rows, span = attention_sizes(length)
    block = pl.BlockSpec((rows, DH), lambda h, i: (i, h))
    whole = pl.BlockSpec((length, DH), lambda h, i: (0, h))
    return pl.pallas_call(
        partial(forward_kernel, span),
        grid=(heads, length // rows),
        in_specs=[
            block,
            whole,
            whole,
            pl.BlockSpec((1, rows), lambda h, i: (0, i)),
            pl.BlockSpec((length, 1), lambda h, i: (0, 0)),
        ],
        out_specs=[block, pl.BlockSpec((1, 1, rows), lambda h, i: (h, 0, i))],
        out_shape=[
            jax.ShapeDtypeStruct((length, columns), BF16),
            jax.ShapeDtypeStruct((heads, 1, length), F32),
        ],
        compiler_params=pltpu.CompilerParams(vmem_limit_bytes=48 * MIB),
        cost_estimate=pl.CostEstimate(
            flops=4 * heads * length * span * DH,
            bytes_accessed=8 * length * columns,
            transcendentals=heads * length * span,
        ),
        name="attend",
    )(queries, keys, values, seg_row, seg_col)


def attention_backward(queries, keys, values, grads, lse, seg_row, seg_col):
    length, columns = queries.shape
    heads = columns // DH
    rows, span = attention_sizes(length)
    block = pl.BlockSpec((rows, DH), lambda h, i: (i, h))
    whole = pl.BlockSpec((length, DH), lambda h, i: (0, h))
    shape = jax.ShapeDtypeStruct((length, columns), BF16)
    return pl.pallas_call(
        partial(backward_kernel, span),
        grid=(heads, length // rows),
        in_specs=[
            block,
            whole,
            whole,
            block,
            pl.BlockSpec((1, 1, rows), lambda h, i: (h, 0, i)),
            pl.BlockSpec((1, rows), lambda h, i: (0, i)),
            pl.BlockSpec((length, 1), lambda h, i: (0, 0)),
        ],
        out_specs=[block, whole, whole],
        out_shape=[shape, shape, shape],
        scratch_shapes=[pltpu.VMEM((length, DH), F32), pltpu.VMEM((length, DH), F32)],
        compiler_params=pltpu.CompilerParams(vmem_limit_bytes=48 * MIB),
        cost_estimate=pl.CostEstimate(
            flops=10 * heads * length * span * DH,
            bytes_accessed=14 * length * columns,
            transcendentals=heads * length * span,
        ),
        name="attend_back",
    )(queries, keys, values, grads, lse, seg_row, seg_col)


def rotate(values, cosine, sine, heads):
    half = DH // 2
    shaped = values.reshape(values.shape[0], heads, DH)
    first, second = shaped[..., :half], shaped[..., half:]
    cosine, sine = cosine[:, None, :], sine[:, None, :]
    return jnp.concatenate(
        [first * cosine - second * sine, second * cosine + first * sine], axis=-1
    ).reshape(values.shape)


def per_device(
    S,
    F,
    tokens,
    segments,
    routes,
    cotangent,
    w_query,
    w_key,
    w_value,
    w_output,
    router,
    attn_gain,
    moe_gain,
    query_gain,
    key_gain,
    w_gate,
    w_up,
    w_down,
):
    s = lax.axis_index("seq")
    f = lax.axis_index("fsdp")
    T = tokens.shape[1]
    L = S * T
    heads = H // S
    C = heads * DH
    experts = E // S
    part = w_query.shape[0]
    half_f = F // 2

    stacked = jnp.stack([w_query, w_key, w_value], 1).reshape(part, 3, S, C)
    stacked = stacked.transpose(2, 0, 1, 3).reshape(S, part, 3 * C)
    crossed = lax.all_to_all(stacked, "seq", split_axis=0, concat_axis=0, tiled=True)
    w_qkv = lax.all_gather(crossed, "fsdp", axis=1, tiled=True).reshape(D, 3 * C)
    small = jnp.concatenate(
        [router, attn_gain[:, None], moe_gain[:, None], query_gain[:, None], key_gain[:, None]], 1
    )
    small = lax.all_gather(small, ("seq", "fsdp"), axis=0, tiled=True)
    full_router = small[:, :E]
    gains = small[:, E:].astype(F32)
    gain_attn, gain_moe = gains[:, 0], gains[:, 1]
    gain_query = lax.dynamic_slice_in_dim(gains[:, 2], s * C, C, 0)
    gain_key = lax.dynamic_slice_in_dim(gains[:, 3], s * C, C, 0)

    tokens_low = tokens[0]
    inputs = tokens_low.astype(F32)
    tokens_all = gather_seq(tokens_low, s, S).astype(F32)
    normed_all = (tokens_all * rms_factor(tokens_all) * gain_attn).astype(BF16)

    full_output = lax.all_gather(w_output, ("seq", "fsdp"), axis=0, tiled=True)
    own_gate = gather_expert_cols(w_gate, f, F)
    own_up = gather_expert_cols(w_up, f, F)
    own_down = gather_expert_rows(w_down, f, F)
    routes_low = routes[0].reshape(1, -1)
    routes_both = jnp.concatenate([routes_low, swap(routes_low, "fsdp", F, half_f)], 0)
    routes_all = lax.all_gather(routes_both, "seq", axis=1).reshape(2 * S, T, -1)
    upstream_low = cotangent[0]
    upstream_all = jnp.stack(
        [
            lax.all_gather(upstream_low, "seq", axis=0),
            lax.all_gather(swap(upstream_low, "fsdp", F, half_f), "seq", axis=0),
        ],
        0,
    ).reshape(2 * S, T, D)

    places = jnp.arange(L, dtype=jnp.int32).astype(F32)
    freqs = ROPE_BASE ** (-(jnp.arange(DH // 2, dtype=F32) * 2.0 / DH))
    angles = places[:, None] * freqs[None, :]
    cosine, sine = jnp.cos(angles), jnp.sin(angles)
    query_pre = matmul(normed_all, w_qkv[:, :C])
    key_pre = matmul(normed_all, w_qkv[:, C : 2 * C])
    value_low = matmul(normed_all, w_qkv[:, 2 * C :]).astype(BF16)
    squares = jnp.stack([jnp.sum(query_pre**2, -1), jnp.sum(key_pre**2, -1)], 0)
    factors = lax.rsqrt(sum_all(squares, "seq", S) / D + EPSILON)
    query_n = query_pre * factors[0][:, None]
    key_n = key_pre * factors[1][:, None]
    query_low = rotate(query_n * gain_query, cosine, sine, heads).astype(BF16)
    key_low = rotate(key_n * gain_key, cosine, sine, heads).astype(BF16)
    seg_row = segments
    seg_col = segments.reshape(L, 1)
    attended, lse = attention_forward(query_low, key_low, value_low, seg_row, seg_col)
    attended_rows = (
        lax.all_to_all(attended.reshape(S, T, C), "seq", split_axis=0, concat_axis=0, tiled=True)
        .transpose(1, 0, 2)
        .reshape(T, D)
    )
    residual = inputs + matmul(attended_rows, full_output)

    moe_factor = rms_factor(residual)
    residual_n = residual * moe_factor
    second_low = (residual_n * gain_moe).astype(BF16)
    logits = matmul(second_low, full_router)
    router_probs = jax.nn.softmax(logits, axis=-1)
    partner_low = swap(second_low, "fsdp", F, half_f)
    second_all = jnp.stack(
        [gather_seq(second_low, s, S), gather_seq(partner_low, s, S)], 0
    ).reshape(2 * S, T, D)
    probs_all = jax.nn.softmax(matmul(second_all.reshape(2 * L, D), full_router), axis=-1)
    expert_ids = s * experts + jnp.arange(experts, dtype=jnp.int32)
    chosen = jnp.any(routes_all[None] == expert_ids[:, None, None, None], axis=-1)
    gates = lax.dynamic_slice_in_dim(probs_all, s * experts, experts, 1)
    gates = gates.T.reshape(experts, 2 * S, T)
    ranks = jnp.cumsum(chosen.astype(jnp.int32), axis=-1) - 1
    picked = chosen[:, :, None, :] & (
        ranks[:, :, None, :] == jnp.arange(CAP, dtype=jnp.int32)[None, None, :, None]
    )
    picks = picked.astype(BF16)
    slot_gate = jnp.sum(jnp.where(picked, gates[:, :, None, :], 0.0), axis=-1)
    out_sum = 0.0
    row_sum = 0.0
    gate_grad_parts = []
    down_terms, gate_terms, up_terms = [], [], []
    for e in range(experts):
        rows = jnp.einsum("bct,btd->bcd", picks[e], second_all, preferred_element_type=F32)
        rows = rows.astype(BF16).reshape(-1, D)
        ups = jnp.einsum("bct,btd->bcd", picks[e], upstream_all, preferred_element_type=F32)
        ups = ups.astype(BF16).reshape(-1, D)
        gate_col = slot_gate[e].reshape(-1, 1)
        gated = matmul(rows, own_gate[e])
        upward = matmul(rows, own_up[e])
        sig = jax.nn.sigmoid(gated)
        silu = gated * sig
        hidden = silu * upward
        hidden_gate = (hidden * gate_col).astype(BF16)
        hidden_pull = matmul_t(ups, own_down[e])
        slot_grads = jnp.sum(hidden * hidden_pull, axis=-1).reshape(2 * S, CAP)
        gate_grad_parts.append(
            jnp.sum(jnp.where(picked[e], slot_grads[:, :, None], 0.0), axis=1)
        )
        hidden_grads = hidden_pull * gate_col
        gated_low = (hidden_grads * upward * sig * (1.0 + gated * (1.0 - sig))).astype(BF16)
        upward_low = (hidden_grads * silu).astype(BF16)
        outs = matmul(hidden_gate, own_down[e]).astype(BF16).reshape(2 * S, CAP, D)
        out_sum += jnp.einsum("bct,bcd->btd", picks[e], outs, preferred_element_type=F32)
        backs = matmul_t(gated_low, own_gate[e]) + matmul_t(upward_low, own_up[e])
        backs = backs.astype(BF16).reshape(2 * S, CAP, D)
        row_sum += jnp.einsum("bct,bcd->btd", picks[e], backs, preferred_element_type=F32)
        down_terms.append(t_matmul(hidden_gate, ups))
        gate_terms.append(t_matmul(rows, gated_low))
        up_terms.append(t_matmul(rows, upward_low))
    row_sum = row_sum.astype(BF16).reshape(2, S, T, D)
    out_sum = out_sum.astype(BF16).reshape(2, S, T, D)

    def chunk(values, which):
        return lambda r: lax.dynamic_index_in_dim(values[which], s ^ r, 0, keepdims=False)

    def both(values):
        other = scatter_sum(chunk(values, 1), "seq", S).astype(BF16)
        own = scatter_sum(chunk(values, 0), "seq", S)
        return own + swap(other, "fsdp", F, half_f).astype(F32)

    gate_grads = jnp.stack(gate_grad_parts, -1).reshape(2, S, T, experts)
    gate_grads = lax.all_to_all(
        gate_grads.transpose(1, 0, 2, 3).reshape(S, -1), "seq", split_axis=0, concat_axis=0, tiled=True
    ).reshape(S, 2, T * experts)
    gate_grads = gate_grads[:, 0] + swap(gate_grads[:, 1], "fsdp", F, half_f)
    gate_grads = gate_grads.reshape(S, T, experts).transpose(1, 0, 2).reshape(T, E)
    row_grads = both(row_sum)
    mixed = (residual + both(out_sum)).astype(BF16)[None]
    grad_gate = scatter_expert_cols(jnp.stack(gate_terms, 0), f, F)
    grad_up = scatter_expert_cols(jnp.stack(up_terms, 0), f, F)
    grad_down = scatter_expert_rows(jnp.stack(down_terms, 0), f, F)

    upstream = upstream_low.astype(F32)
    logit_grads = router_probs * (
        gate_grads - jnp.sum(router_probs * gate_grads, axis=-1, keepdims=True)
    )
    router_wide = full_router.astype(F32)
    second_grads = row_grads + jnp.dot(logit_grads, router_wide.T, precision=HIGHEST)
    router_term = jnp.dot(second_low.astype(F32).T, logit_grads, precision=HIGHEST)
    moe_gain_term = jnp.sum(second_grads * residual_n, axis=0)
    pulled = second_grads * gain_moe
    residual_grads = upstream + moe_factor * (
        pulled - residual_n * jnp.mean(pulled * residual_n, axis=-1, keepdims=True)
    )
    branch_low = residual_grads.astype(BF16)

    branch_all = gather_seq(branch_low, s, S)
    own_output = lax.dynamic_slice_in_dim(full_output, s * C, C, 0)
    head_grads = matmul_t(branch_all, own_output).astype(BF16)
    output_term = t_matmul(attended, branch_all)
    query_back, key_back, value_back = attention_backward(
        query_low, key_low, value_low, head_grads, lse, seg_row, seg_col
    )
    query_turned = rotate(query_back.astype(F32), cosine, -sine, heads)
    key_turned = rotate(key_back.astype(F32), cosine, -sine, heads)
    query_gain_term = jnp.sum(query_turned * query_n, axis=0)
    key_gain_term = jnp.sum(key_turned * key_n, axis=0)
    query_pulled = query_turned * gain_query
    key_pulled = key_turned * gain_key
    means = jnp.stack([jnp.sum(query_pulled * query_n, -1), jnp.sum(key_pulled * key_n, -1)], 0)
    means = sum_all(means, "seq", S) / D
    query_pre_low = (factors[0][:, None] * (query_pulled - query_n * means[0][:, None])).astype(BF16)
    key_pre_low = (factors[1][:, None] * (key_pulled - key_n * means[1][:, None])).astype(BF16)
    pre_low = jnp.concatenate([query_pre_low, key_pre_low, value_back], 1)
    normed_parts = matmul_t(pre_low, w_qkv).astype(BF16).reshape(1, S, T, D)
    normed_grads = scatter_sum(chunk(normed_parts, 0), "seq", S)
    qkv_term = t_matmul(normed_all, pre_low).astype(BF16)
    qkv_term = lax.psum_scatter(
        qkv_term.reshape(S, F, part, 3 * C), "fsdp", scatter_dimension=1, tiled=True
    ).reshape(S, part, 3 * C)
    qkv_term = lax.all_to_all(qkv_term, "seq", split_axis=0, concat_axis=0, tiled=True)
    qkv_term = qkv_term.reshape(S, part, 3, C).transpose(2, 1, 0, 3).reshape(3, part, D).astype(F32)
    grad_output = lax.psum_scatter(
        output_term.astype(BF16), "fsdp", scatter_dimension=0, tiled=True
    ).astype(F32)
    head_gains = lax.psum_scatter(
        jnp.stack([query_gain_term, key_gain_term], 1), "fsdp", scatter_dimension=0, tiled=True
    )
    attn_factor = rms_factor(inputs)
    inputs_n = inputs * attn_factor
    attn_gain_term = jnp.sum(normed_grads * inputs_n, axis=0)
    attn_pulled = normed_grads * gain_attn
    grad_tokens = residual_grads + attn_factor * (
        attn_pulled - inputs_n * jnp.mean(attn_pulled * inputs_n, axis=-1, keepdims=True)
    )
    gain_terms = jnp.concatenate([router_term, moe_gain_term[:, None], attn_gain_term[:, None]], 1)
    gain_terms = lax.psum_scatter(gain_terms, ("seq", "fsdp"), scatter_dimension=0, tiled=True)
    return (
        mixed,
        grad_tokens[None],
        qkv_term[0],
        qkv_term[1],
        qkv_term[2],
        grad_output,
        gain_terms[:, :E],
        gain_terms[:, E + 1],
        gain_terms[:, E],
        head_gains[:, 0],
        head_gains[:, 1],
        grad_gate,
        grad_up,
        grad_down,
    )


def solution(mesh):
    tokens_spec = P("fsdp", "seq", None)
    rows_spec = P(("seq", "fsdp"), None)
    gain_spec = P(("seq", "fsdp"))
    expert_spec = P("seq", "fsdp", None)
    in_specs = (
        (tokens_spec, P("fsdp", None), tokens_spec, tokens_spec)
        + (rows_spec,) * 5
        + (gain_spec,) * 4
        + (expert_spec,) * 3
    )
    out_specs = (tokens_spec,) * 2 + (rows_spec,) * 5 + (gain_spec,) * 4 + (expert_spec,) * 3
    return jax.shard_map(
        partial(per_device, mesh.shape["seq"], mesh.shape["fsdp"]),
        mesh=mesh,
        in_specs=in_specs,
        out_specs=out_specs,
        check_vma=False,
    )
```

time: 3060 us -> 1770 us (0.58)
  waiting for transfers between devices: 1950 us -> 727 us
  blocking collectives: 196 us -> 114 us
  local copies, waits for them, and re-layouts: 280 us -> 218 us
  Pallas kernels: 0 us -> 49.7 us
  starting transfers between devices: 45.6 us -> 87.4 us
    reduce_scatter x7 -> x2, waiting for transfers between devices: 1150 us -> 0.02 us  [the longest x1 0.02 us: per_device(): lax.psum_scatter(qkv_term.reshape(S, F, part, 3 * C), 'fsdp', scatter_dim...]
    ppermute x0 -> x102, waiting for transfers between devices: none -> 614 us  [swap(): return lax.ppermute(values, axis, [(i, i ^ mask) for i in range(size)])]
    all_to_all x10 -> x3, waiting for transfers between devices: 411 us -> 0.01 us  [the longest x1 0.01 us: per_device(): lax.all_to_all(attended.reshape(S, T, C), 'seq', split_axis=0, concat_axi...]
    all_gather x7 -> x4, waiting for transfers between devices: 392 us -> 0.04 us  [the longest x1 0.02 us: per_device(): lax.all_gather(upstream_low, 'seq', axis=0)]
    unnamed x16 -> x10, waiting for transfers between devices: 4.06 us -> 113 us
    unnamed x2 -> x0, blocking collectives: 83.3 us -> none
    convert_element_type x6 -> x1, local copies, waits for them, and re-layouts: 78 us -> 2.52 us  [per_device(): qkv_term.reshape(S, part, 3, C).transpose(2, 1, 0, 3).reshape(3, part, D)]
    ppermute x0 -> x102, starting transfers between devices: none -> 75.1 us  [swap(): return lax.ppermute(values, axis, [(i, i ^ mask) for i in range(size)])]
  transfers between devices with their start and end apart: 25 -> 113, of which waited for: 18 -> 37; matrix products, arithmetic and copies ran while one was open for 24% -> 25% of each run, Pallas kernels for 0% -> 3%
where the time goes in v1:
time: 1770 us; the launch traced here: 1760 us
  waiting for transfers between devices  727 us (41%)
  matrix products  367 us (21%)
  local copies, waits for them, and re-layouts  218 us (12%)
  other arithmetic  181 us (10%)
  blocking collectives  114 us (6%)
  starting transfers between devices  87.4 us (5%)
  Pallas kernels  49.7 us (3%)
    ppermute x102, waiting for transfers between devices, swap(): return lax.ppermute(values, axis, [(i, i ^ mask) for i in range(size)])  614 us
    unnamed x10, waiting for transfers between devices  113 us
    dot_general x12, matrix products, matmul(): return jnp.dot(left, right, preferred_element_type=F32)  96.6 us
    all_gather x1, blocking collectives, per_device(): small = lax.all_gather(small, ('seq', 'fsdp'), axis=0, tiled=True)  86.8 us
    dot_general x8, matrix products, matmul_t(): lax.dot_general(left, right, (((1,), (1,)), ((), ())), preferred_element_...  86.7 us
    ppermute x102, starting transfers between devices, swap(): return lax.ppermute(values, axis, [(i, i ^ mask) for i in range(size)])  75.1 us
    dot_general x8, matrix products, t_matmul(): lax.dot_general(left, right, (((0,), (0,)), ((), ())), preferred_element_...  57.9 us
    unnamed x304, local copies, waits for them, and re-layouts  40.8 us
  transfers between devices with their start and end apart: 113, of which 37 were waited for; matrix products, arithmetic and copies ran while one was open for 25% of the time, Pallas kernels for 3%

profile of v1, /device:TPU:0, one launch (start us, length us, event | category | flops | bytes accessed | tf_op | source)
XLA Modules:
  0.0 1761.0 jit_solution(7538041040211149035)
XLA Ops:
  15.0 18.0 %all_to_all.24 = bf16[8,64,768]{2,1,0:T(8,128)(2,1)} all-to-all(bf16[8,64,768]{2,1,0:T(8,128)(2,1)} %reshape.498), channel_id=1, replica_groups=mesh['seq'=8,'fsdp'=4] {'seq'}, dimensions={0} | all-to-all | bytes 1572864 | tf_op jit(solution)/shard_map/all_to_all | solution.py:377
  36.8 92.8 %collective-permute-done.56 = bf16[256,2048]{1,0:T(8,128)(2,1)S(1)} collective-permute-done((bf16[256,2048]{1,0:T(8,128)(2,1)S(1)}, bf16[256,2048]{1,0:T(8,128)(2,1)S(1)}, u32[]{:S(2)}, u32[]{:S(2)}) %collective-permute-start.56) | collective-permute-done | bytes 1048608 | tf_op jit(solution)/shard_map/ppermute | solution.py:42
  143.6 86.8 %all-gather.2 = bf16[32,64,20]{1,2,0:T(8,128)(2,1)S(1)} all-gather(bf16[1,64,20]{1,2,0:T(8,128)(2,1)S(1)} %bitcast.708), channel_id=1, replica_groups=mesh['seq'=8,'fsdp'=4] {'seq','fsdp'}, dimensions={0}, use_global_device_ids=true | all-gather | bytes 84480 | tf_op jit(solution)/shard_map/all_gather | solution.py:382
  290.0 65.4 %collective-permute-done.33 = bf16[2,512,512]{2,1,0:T(8,128)(2,1)S(1)} collective-permute-done((bf16[2,512,512]{2,1,0:T(8,128)(2,1)}, bf16[2,512,512]{2,1,0:T(8,128)(2,1)S(1)}, u32[]{:S(2)}, u32[]{:S(2)}) %collective-permute-start.33) | collective-permute-done | bytes 1048608 | tf_op jit(solution)/shard_map/ppermute | solution.py:42
  357.4 20.2 %collective-permute-done.36 = bf16[2,512,512]{2,1,0:T(8,128)(2,1)S(1)} collective-permute-done((bf16[2,512,512]{2,1,0:T(8,128)(2,1)}, bf16[2,512,512]{2,1,0:T(8,128)(2,1)S(1)}, u32[]{:S(2)}, u32[]{:S(2)}) %collective-permute-start.36) | collective-permute-done | bytes 1048608 | tf_op jit(solution)/shard_map/ppermute | solution.py:42
  397.8 33.8 %collective-permute-done.34 = bf16[2,512,512]{2,1,0:T(8,128)(2,1)S(1)} collective-permute-done((bf16[2,512,512]{2,1,0:T(8,128)(2,1)S(1)}, bf16[2,512,512]{2,1,0:T(8,128)(2,1)S(1)}, u32[]{:S(2)}, u32[]{:S(2)}) %collective-permute-start.34) | collective-permute-done | bytes 1048608 | tf_op jit(solution)/shard_map/ppermute | solution.py:42
  431.6 22.8 %collective-permute-done.37 = bf16[2,512,512]{2,1,0:T(8,128)(2,1)S(1)} collective-permute-done((bf16[2,512,512]{2,1,0:T(8,128)(2,1)S(1)}, bf16[2,512,512]{2,1,0:T(8,128)(2,1)S(1)}, u32[]{:S(2)}, u32[]{:S(2)}) %collective-permute-start.37) | collective-permute-done | bytes 1048608 | tf_op jit(solution)/shard_map/ppermute | solution.py:42
  535.2 21.6 %attend.1 = (bf16[2048,256]{1,0:T(8,128)(2,1)S(1)}, f32[2,1,2048]{2,1,0:T(1,128)S(1)}) custom-call(bf16[2048,256]{1,0:T(8,128)(2,1)S(1)} %bitcast.590, bf16[2048,256]{1,0:T(8,128)(2,1)S(1)} %bitcast.588, bf16[2048,256]{1,0:T(8,128)(2,1)S(1)} %convolution_convert_fusion.10.v_ref, s32[1,2048]{1,0:T(1,128)S(1)} %copy-done.7, s32[2048,1]{1,0:T(8,128)S(1)} %copy.113.seg_col_ref), custom_call_target="tpu_custom_call" | custom-call | flops 2684354560 | bytes 4194304 | tf_op jit(solution)/shard_map/attend/pallas_call | solution.py:278
  562.4 14.0 pad_maximum_fusion.1
  615.0 19.1 %collective-permute-done.14 = bf16[256,2048]{1,0:T(8,128)(2,1)S(1)} collective-permute-done((bf16[256,2048]{1,0:T(8,128)(2,1)S(1)}, bf16[256,2048]{1,0:T(8,128)(2,1)S(1)}, u32[]{:S(2)}, u32[]{:S(2)}) %collective-permute-start.14) | collective-permute-done | bytes 1048608 | tf_op jit(solution)/shard_map/ppermute | solution.py:42
  639.0 20.4 %collective-permute-done.22 = bf16[256,2048]{1,0:T(8,128)(2,1)} collective-permute-done((bf16[256,2048]{1,0:T(8,128)(2,1)S(1)}, bf16[256,2048]{1,0:T(8,128)(2,1)}, u32[]{:S(2)}, u32[]{:S(2)}) %collective-permute-start.22) | collective-permute-done | bytes 1048608 | tf_op jit(solution)/shard_map/ppermute | solution.py:42
  666.7 18.1 %collective-permute-done.24 = bf16[256,2048]{1,0:T(8,128)(2,1)S(1)} collective-permute-done((bf16[256,2048]{1,0:T(8,128)(2,1)}, bf16[256,2048]{1,0:T(8,128)(2,1)S(1)}, u32[]{:S(2)}, u32[]{:S(2)}) %collective-permute-start.24) | collective-permute-done | bytes 1048608 | tf_op jit(solution)/shard_map/ppermute | solution.py:42
  755.5 12.5 fusion.4
  791.7 12.7 copy.130
  804.4 12.8 fusion.187
  853.8 12.6 multiply_reduce_fusion.1
  866.4 12.4 copy.129
  934.1 17.1 fusion.136
  951.2 19.6 %add_convert_fusion = bf16[16,256,2048]{2,1,0:T(8,128)(2,1)} fusion(f32[16,256,2048]{2,1,0:T(8,128)} %fusion.136, bf16[16,144,2048]{2,1,0:T(8,128)(2,1)} %bitcast.627, pred[2,16,144,256]{3,2,1,0:T(8,128)(4,1)S(1)} %copy-done.10), kind=kOutput, calls=%fused_computation | convolution fusion | flops 2432696320 | bytes 60358656 | tf_op jit(solution)/shard_map/bct,bcd->btd/dot_general | solution.py:481
  991.8 17.1 fusion.137
  1025.7 21.2 %add_convert_fusion.1 = bf16[16,256,2048]{2,1,0:T(8,128)(2,1)} fusion(f32[16,256,2048]{2,1,0:T(8,128)} %fusion.137, bf16[16,144,2048]{2,1,0:T(8,128)(2,1)} %bitcast.626, pred[2,16,144,256]{3,2,1,0:T(8,128)(4,1)S(1)} %copy-done.10), kind=kOutput, calls=%fused_computation.1 | convolution fusion | flops 2432696320 | bytes 60358656 | tf_op jit(solution)/shard_map/bct,bcd->btd/dot_general | solution.py:478
  1125.1 52.0 %collective-permute-done.99 = bf16[2,512,512]{1,2,0:T(8,128)(2,1)S(1)} collective-permute-done((bf16[2,512,512]{1,2,0:T(8,128)(2,1)}, bf16[2,512,512]{1,2,0:T(8,128)(2,1)S(1)}, u32[]{:S(2)}, u32[]{:S(2)}) %collective-permute-start.99) | collective-permute-done | bytes 1048608 | tf_op jit(solution)/shard_map/ppermute | solution.py:42
  1180.1 41.2 %collective-permute-done.96 = bf16[2,512,512]{1,2,0:T(8,128)(2,1)S(1)} collective-permute-done((bf16[2,512,512]{1,2,0:T(8,128)(2,1)}, bf16[2,512,512]{1,2,0:T(8,128)(2,1)S(1)}, u32[]{:S(2)}, u32[]{:S(2)}) %collective-permute-start.96) | collective-permute-done | bytes 1048608 | tf_op jit(solution)/shard_map/ppermute | solution.py:42
  1261.7 16.7 collective-permute-done.69
  1290.2 20.0 %collective-permute-done.61 = bf16[256,2048]{1,0:T(8,128)(2,1)S(1)} collective-permute-done((bf16[256,2048]{1,0:T(8,128)(2,1)S(1)}, bf16[256,2048]{1,0:T(8,128)(2,1)S(1)}, u32[]{:S(2)}, u32[]{:S(2)}) %collective-permute-start.61) | collective-permute-done | bytes 1048608 | tf_op jit(solution)/shard_map/ppermute | solution.py:42
  1311.3 22.9 %collective-permute-done.73 = bf16[256,2048]{1,0:T(8,128)(2,1)S(1)} collective-permute-done((bf16[256,2048]{1,0:T(8,128)(2,1)S(1)}, bf16[256,2048]{1,0:T(8,128)(2,1)S(1)}, u32[]{:S(2)}, u32[]{:S(2)}) %collective-permute-start.73) | collective-permute-done | bytes 1048608 | tf_op jit(solution)/shard_map/ppermute | solution.py:42
  1340.8 22.6 %collective-permute-done.76 = bf16[256,2048]{1,0:T(8,128)(2,1)S(1)} collective-permute-done((bf16[256,2048]{1,0:T(8,128)(2,1)S(1)}, bf16[256,2048]{1,0:T(8,128)(2,1)S(1)}, u32[]{:S(2)}, u32[]{:S(2)}) %collective-permute-start.76) | collective-permute-done | bytes 1048608 | tf_op jit(solution)/shard_map/ppermute | solution.py:42
  1381.3 13.3 collective-permute-done.81
  1403.6 28.1 %attend_back.1 = (bf16[2048,256]{1,0:T(8,128)(2,1)S(1)}, bf16[2048,256]{1,0:T(8,128)(2,1)S(1)}, bf16[2048,256]{1,0:T(8,128)(2,1)S(1)}) custom-call(bf16[2048,256]{1,0:T(8,128)(2,1)S(1)} %bitcast.591, bf16[2048,256]{1,0:T(8,128)(2,1)S(1)} %bitcast.589, bf16[2048,256]{1,0:T(8,128)(2,1)} %copy-done.8, bf16[2048,256]{1,0:T(8,128)(2,1)} %convolution_convert_fusion.9.do_ref, ...), custom_call_target="tpu_custom_call" | custom-call | flops 6710886400 | bytes 7340032 | tf_op jit(solution)/shard_map/attend_back/pallas_call | solution.py:310
  1534.4 25.9 %collective-permute-done.90 = bf16[128,2048]{1,0:T(8,128)(2,1)S(1)} collective-permute-done((bf16[128,2048]{1,0:T(8,128)(2,1)S(1)}, bf16[128,2048]{1,0:T(8,128)(2,1)S(1)}, u32[]{:S(2)}, u32[]{:S(2)}) %collective-permute-start.90) | collective-permute-done | bytes 524320 | tf_op jit(solution)/shard_map/ppermute | solution.py:42
  1597.7 27.4 %collective-permute-done.55 = bf16[256,2048]{1,0:T(8,128)(2,1)} collective-permute-done((bf16[256,2048]{1,0:T(8,128)(2,1)}, bf16[256,2048]{1,0:T(8,128)(2,1)}, u32[]{:S(2)}, u32[]{:S(2)}) %collective-permute-start.55) | collective-permute-done | bytes 1048608 | tf_op jit(solution)/shard_map/ppermute | solution.py:42
  1630.4 112.2 %reduce-scatter.13.cloned.1.call-done = f32[64,18]{1,0:T(8,128)} async-done(((f32[2048,18]{1,0:T(8,128)}), f32[64,18]{1,0:T(8,128)}) %reduce-scatter.13.cloned.1.call-update) | async-done | bytes 4624
  (823 shorter events, 790.5 us)
Async XLA Ops:
  7.2 465.7 %all-gather.8.cloned.1.call-start = ((), (), s32[]{:S(2)}) async-start(), calls=%async_computation.8 | async-start | bytes 3932160 | tf_op jit(solution)/shard_map/all_gather | solution.py:378
  33.0 529.4 %all-gather.12.cloned.1.call-start = ((), (), s32[]{:S(2)}) async-start(), calls=%async_computation.10 | async-start | bytes 9437184 | tf_op jit(solution)/shard_map/all_gather | solution.py:404
  33.7 528.7 %all-gather.14.cloned.1.call-start = ((), (), s32[]{:S(2)}) async-start(), calls=%async_computation.13 | async-start | bytes 9437184 | tf_op jit(solution)/shard_map/all_gather | solution.py:405
  33.8 95.8 %collective-permute-start.56 = (bf16[256,2048]{1,0:T(8,128)(2,1)S(1)}, bf16[256,2048]{1,0:T(8,128)(2,1)S(1)}, u32[]{:S(2)}, u32[]{:S(2)}) collective-permute-start(bf16[256,2048]{1,0:T(8,128)(2,1)S(1)} %bitcast.634), channel_id=1, source_target_pairs={{0,2},{1,3},{2,0},{3,1},{4,6},{5,7},{6,4},{7,5},{8,10},{9,11},{10,... | collective-permute-start | bytes 3145736 | tf_op jit(solution)/shard_map/ppermute | solution.py:42
  130.6 470.0 %all-gather.10.cloned.1.call-start = ((), (), s32[]{:S(2)}) async-start(), calls=%async_computation.9 | async-start | bytes 8650752 | tf_op jit(solution)/shard_map/all_gather | solution.py:394
  130.6 153.1 %collective-permute-start.1 = (bf16[256,2048]{1,0:T(8,128)(2,1)S(1)}, bf16[256,2048]{1,0:T(8,128)(2,1)}, u32[]{:S(2)}, u32[]{:S(2)}) collective-permute-start(bf16[256,2048]{1,0:T(8,128)(2,1)S(1)} %bitcast.606), channel_id=1, source_target_pairs={{0,8},{4,12},{8,0},{12,4},{16,24},{20,28},{24,16},{28,20},{1,9},{5... | collective-permute-start | bytes 3145736 | tf_op jit(solution)/shard_map/ppermute | solution.py:42
  131.6 249.0 %collective-permute-start.3 = (bf16[256,2048]{1,0:T(8,128)(2,1)S(1)}, bf16[256,2048]{1,0:T(8,128)(2,1)}, u32[]{:S(2)}, u32[]{:S(2)}) collective-permute-start(bf16[256,2048]{1,0:T(8,128)(2,1)S(1)} %bitcast.607), channel_id=1, source_target_pairs={{0,16},{4,20},{8,24},{12,28},{16,0},{20,4},{24,8},{28,12},{1,17},{... | collective-permute-start | bytes 3145736 | tf_op jit(solution)/shard_map/ppermute | solution.py:42
  133.4 141.4 %collective-permute-start = (bf16[256,2048]{1,0:T(8,128)(2,1)}, bf16[256,2048]{1,0:T(8,128)(2,1)}, u32[]{:S(2)}, u32[]{:S(2)}) collective-permute-start(bf16[256,2048]{1,0:T(8,128)(2,1)} %pad_maximum_fusion.10), channel_id=1, source_target_pairs={{0,4},{4,0},{8,12},{12,8},{16,20},{20,16},{24,28},{28,24},{1,5},{5... | collective-permute-start | bytes 3145736 | tf_op jit(solution)/shard_map/ppermute | solution.py:42
  133.6 123.1 %collective-permute-start.12 = (s32[1,2048]{1,0:T(1,128)S(1)}, s32[1,2048]{1,0:T(1,128)S(1)}, u32[]{:S(2)}, u32[]{:S(2)}) collective-permute-start(s32[1,2048]{1,0:T(1,128)S(1)} %reshape_squeeze.2), channel_id=1, source_target_pairs={{0,2},{1,3},{2,0},{3,1},{4,6},{5,7},{6,4},{7,5},{8,10},{9,11},{10,... | collective-permute-start | bytes 24584 | tf_op jit(solution)/shard_map/ppermute | solution.py:42
  138.9 139.7 %collective-permute-start.35 = (bf16[2,512,512]{2,1,0:T(8,128)(2,1)}, bf16[2,512,512]{2,1,0:T(8,128)(2,1)}, u32[]{:S(2)}, u32[]{:S(2)}) collective-permute-start(bf16[2,512,512]{2,1,0:T(8,128)(2,1)} %get-tuple-element.107), channel_id=1, source_target_pairs={{0,1},{1,0},{2,3},{3,2},{4,5},{5,4},{6,7},{7,6},{8,9},{9,8},{10,11... | collective-permute-start | bytes 3145736 | tf_op jit(solution)/shard_map/ppermute | solution.py:42
  274.7 80.6 %collective-permute-start.33 = (bf16[2,512,512]{2,1,0:T(8,128)(2,1)}, bf16[2,512,512]{2,1,0:T(8,128)(2,1)S(1)}, u32[]{:S(2)}, u32[]{:S(2)}) collective-permute-start(bf16[2,512,512]{2,1,0:T(8,128)(2,1)} %constant_dynamic-slice_fusion.3), channel_id=1, source_target_pairs={{0,2},{1,3},{2,0},{3,1},{4,6},{5,7},{6,4},{7,5},{8,10},{9,11},{10,... | collective-permute-start | bytes 3145736 | tf_op jit(solution)/shard_map/ppermute | solution.py:42
  278.5 99.1 %collective-permute-start.36 = (bf16[2,512,512]{2,1,0:T(8,128)(2,1)}, bf16[2,512,512]{2,1,0:T(8,128)(2,1)S(1)}, u32[]{:S(2)}, u32[]{:S(2)}) collective-permute-start(bf16[2,512,512]{2,1,0:T(8,128)(2,1)} %constant_dynamic-slice_fusion.1), channel_id=1, source_target_pairs={{0,2},{1,3},{2,0},{3,1},{4,6},{5,7},{6,4},{7,5},{8,10},{9,11},{10,... | collective-permute-start | bytes 3145736 | tf_op jit(solution)/shard_map/ppermute | solution.py:42
  283.7 106.6 %collective-permute-start.38 = (bf16[2,256,2048]{2,1,0:T(8,128)(2,1)S(1)}, bf16[2,256,2048]{2,1,0:T(8,128)(2,1)S(1)}, u32[]{:S(2)}, u32[]{:S(2)}) collective-permute-start(bf16[2,256,2048]{2,1,0:T(8,128)(2,1)S(1)} %copy-done.62), channel_id=1, source_target_pairs={{0,1},{1,0},{2,3},{3,2},{4,5},{5,4},{6,7},{7,6},{8,9},{9,8},{10,11... | collective-permute-start | bytes 6291464 | tf_op jit(solution)/shard_map/ppermute | solution.py:42
  287.7 94.9 %collective-permute-start.2 = (bf16[256,2048]{1,0:T(8,128)(2,1)}, bf16[256,2048]{1,0:T(8,128)(2,1)S(1)}, u32[]{:S(2)}, u32[]{:S(2)}) collective-permute-start(bf16[256,2048]{1,0:T(8,128)(2,1)} %collective-permute-done.1), channel_id=1, source_target_pairs={{0,4},{4,0},{8,12},{12,8},{16,20},{20,16},{24,28},{28,24},{1,5},{5... | collective-permute-start | bytes 3145736 | tf_op jit(solution)/shard_map/ppermute | solution.py:42
  382.6 74.9 %collective-permute-start.7 = (bf16[128,2048]{1,0:T(8,128)(2,1)S(1)}, bf16[128,2048]{1,0:T(8,128)(2,1)S(1)}, u32[]{:S(2)}, u32[]{:S(2)}) collective-permute-start(bf16[128,2048]{1,0:T(8,128)(2,1)S(1)} %collective-permute-done.5), channel_id=1, source_target_pairs={{0,4},{4,0},{8,12},{12,8},{16,20},{20,16},{24,28},{28,24},{1,5},{5... | collective-permute-start | bytes 1572872 | tf_op jit(solution)/shard_map/ppermute | solution.py:42
  980.3 97.8 %collective-permute-start.57 = (bf16[256,2048]{1,0:T(8,128)(2,1)}, bf16[256,2048]{1,0:T(8,128)(2,1)S(1)}, u32[]{:S(2)}, u32[]{:S(2)}) collective-permute-start(bf16[256,2048]{1,0:T(8,128)(2,1)} %get-tuple-element.148), channel_id=1, source_target_pairs={{0,4},{4,0},{8,12},{12,8},{16,20},{20,16},{24,28},{28,24},{1,5},{5... | collective-permute-start | bytes 3145736 | tf_op jit(solution)/shard_map/ppermute | solution.py:42
  980.5 104.6 %collective-permute-start.58 = (bf16[256,2048]{1,0:T(8,128)(2,1)}, bf16[256,2048]{1,0:T(8,128)(2,1)}, u32[]{:S(2)}, u32[]{:S(2)}) collective-permute-start(bf16[256,2048]{1,0:T(8,128)(2,1)} %get-tuple-element.151), channel_id=1, source_target_pairs={{0,4},{4,0},{8,12},{12,8},{16,20},{20,16},{24,28},{28,24},{1,5},{5... | collective-permute-start | bytes 3145736 | tf_op jit(solution)/shard_map/ppermute | solution.py:42
  980.9 104.4 %collective-permute-start.59 = (bf16[256,2048]{1,0:T(8,128)(2,1)}, bf16[256,2048]{1,0:T(8,128)(2,1)}, u32[]{:S(2)}, u32[]{:S(2)}) collective-permute-start(bf16[256,2048]{1,0:T(8,128)(2,1)} %get-tuple-element.150), channel_id=1, source_target_pairs={{0,4},{4,0},{8,12},{12,8},{16,20},{20,16},{24,28},{28,24},{1,5},{5... | collective-permute-start | bytes 3145736 | tf_op jit(solution)/shard_map/ppermute | solution.py:42
  981.0 105.9 %collective-permute-start.62 = (bf16[256,2048]{1,0:T(8,128)(2,1)}, bf16[256,2048]{1,0:T(8,128)(2,1)}, u32[]{:S(2)}, u32[]{:S(2)}) collective-permute-start(bf16[256,2048]{1,0:T(8,128)(2,1)} %get-tuple-element.149), channel_id=1, source_target_pairs={{0,4},{4,0},{8,12},{12,8},{16,20},{20,16},{24,28},{28,24},{1,5},{5... | collective-permute-start | bytes 3145736 | tf_op jit(solution)/shard_map/ppermute | solution.py:42
  988.4 74.7 %all-to-all-start.2 = ((f32[8,1,1024]{2,1,0:T(1,128)}), f32[8,1,1024]{2,1,0:T(1,128)S(1)}, u32[]{:S(2)}, u32[]{:S(2)}) async-start(f32[8,1,1024]{2,1,0:T(1,128)} %copy.120), calls=%async_computation.2 | async-start | bytes 65536 | tf_op jit(solution)/shard_map/all_to_all | solution.py:497
  991.7 578.8 %reduce-scatter.15.cloned.1.call-start = ((), (), s32[]{:S(2)}) async-start(), calls=%async_computation.15 | async-start | bytes 163840
  1106.0 344.5 %collective-permute-start.101 = (bf16[2,256,2048]{2,1,0:T(8,128)(2,1)}, bf16[2,256,2048]{2,1,0:T(8,128)(2,1)}, u32[]{:S(2)}, u32[]{:S(2)}) collective-permute-start(bf16[2,256,2048]{2,1,0:T(8,128)(2,1)} %fusion.53), channel_id=1, source_target_pairs={{0,1},{1,0},{2,3},{3,2},{4,5},{5,4},{6,7},{7,6},{8,9},{9,8},{10,11... | collective-permute-start | bytes 6291464 | tf_op jit(solution)/shard_map/ppermute | solution.py:42
  1113.9 383.2 %collective-permute-start.98 = (bf16[2,512,512]{1,2,0:T(8,128)(2,1)}, bf16[2,512,512]{1,2,0:T(8,128)(2,1)}, u32[]{:S(2)}, u32[]{:S(2)}) collective-permute-start(bf16[2,512,512]{1,2,0:T(8,128)(2,1)} %get-tuple-element.124), channel_id=1, source_target_pairs={{0,1},{1,0},{2,3},{3,2},{4,5},{5,4},{6,7},{7,6},{8,9},{9,8},{10,11... | collective-permute-start | bytes 3145736 | tf_op jit(solution)/shard_map/ppermute | solution.py:42
  1114.7 106.6 %collective-permute-start.96 = (bf16[2,512,512]{1,2,0:T(8,128)(2,1)}, bf16[2,512,512]{1,2,0:T(8,128)(2,1)S(1)}, u32[]{:S(2)}, u32[]{:S(2)}) collective-permute-start(bf16[2,512,512]{1,2,0:T(8,128)(2,1)} %get-tuple-element.127), channel_id=1, source_target_pairs={{0,1},{1,0},{2,3},{3,2},{4,5},{5,4},{6,7},{7,6},{8,9},{9,8},{10,11... | collective-permute-start | bytes 3145736 | tf_op jit(solution)/shard_map/ppermute | solution.py:42
  1117.0 112.8 %collective-permute-start.60 = (bf16[128,2048]{1,0:T(8,128)(2,1)}, bf16[128,2048]{1,0:T(8,128)(2,1)}, u32[]{:S(2)}, u32[]{:S(2)}) collective-permute-start(bf16[128,2048]{1,0:T(8,128)(2,1)} %get-tuple-element.209), channel_id=1, source_target_pairs={{0,8},{4,12},{8,0},{12,4},{16,24},{20,28},{24,16},{28,20},{1,9},{5... | collective-permute-start | bytes 1572872 | tf_op jit(solution)/shard_map/ppermute | solution.py:42
  1366.1 131.4 %collective-permute-start.95 = (bf16[2,512,512]{1,2,0:T(8,128)(2,1)}, bf16[2,512,512]{1,2,0:T(8,128)(2,1)}, u32[]{:S(2)}, u32[]{:S(2)}) collective-permute-start(bf16[2,512,512]{1,2,0:T(8,128)(2,1)} %get-tuple-element.126), channel_id=1, source_target_pairs={{0,1},{1,0},{2,3},{3,2},{4,5},{5,4},{6,7},{7,6},{8,9},{9,8},{10,11... | collective-permute-start | bytes 3145736 | tf_op jit(solution)/shard_map/ppermute | solution.py:42
  1394.7 102.8 %collective-permute-start.100 = (bf16[2,512,512]{1,2,0:T(8,128)(2,1)}, bf16[2,512,512]{1,2,0:T(8,128)(2,1)}, u32[]{:S(2)}, u32[]{:S(2)}) collective-permute-start(bf16[2,512,512]{1,2,0:T(8,128)(2,1)} %fusion.64), channel_id=1, source_target_pairs={{0,2},{1,3},{2,0},{3,1},{4,6},{5,7},{6,4},{7,5},{8,10},{9,11},{10,... | collective-permute-start | bytes 3145736 | tf_op jit(solution)/shard_map/ppermute | solution.py:42
  1396.5 101.5 %collective-permute-start.97 = (bf16[2,512,512]{1,2,0:T(8,128)(2,1)}, bf16[2,512,512]{1,2,0:T(8,128)(2,1)}, u32[]{:S(2)}, u32[]{:S(2)}) collective-permute-start(bf16[2,512,512]{1,2,0:T(8,128)(2,1)} %fusion.76), channel_id=1, source_target_pairs={{0,2},{1,3},{2,0},{3,1},{4,6},{5,7},{6,4},{7,5},{8,10},{9,11},{10,... | collective-permute-start | bytes 3145736 | tf_op jit(solution)/shard_map/ppermute | solution.py:42
  1458.9 113.8 %reduce-scatter.11.cloned.1.call-start = ((), (), s32[]{:S(2)}) async-start(), calls=%async_computation.12 | async-start | bytes 1310720 | tf_op jit(solution)/shard_map/reduce_scatter | solution.py:548
  1469.5 123.8 %reduce-scatter.9.cloned.1.call-start = ((), (), s32[]{:S(2)}) async-start(), calls=%async_computation.11 | async-start | bytes 3932160 | tf_op jit(solution)/shard_map/reduce_scatter | solution.py:543
  1493.4 249.2 %reduce-scatter.13.cloned.1.call-start = ((), (), s32[]{:S(2)}) async-start(), calls=%async_computation.14 | async-start | bytes 1081344
  1593.3 152.9 %all-to-all-start.3 = ((bf16[8,64,768]{2,1,0:T(8,128)(2,1)}), bf16[8,64,768]{2,1,0:T(8,128)(2,1)}, u32[]{:S(2)}, u32[]{:S(2)}) async-start(bf16[8,64,768]{2,1,0:T(8,128)(2,1)} %bitcast.667), calls=%async_computation.4 | async-start | bytes 1572864 | tf_op jit(solution)/shard_map/all_to_all | solution.py:546
  (223 other events, 5752.3 us)
Sparse Core Ops, SparseCore 0:
  33.1 99.6 all-gather.7
  134.6 64.9 all-gather.11
  201.5 54.5 all-gather.13
  258.9 182.4 all-gather.9
  1459.0 31.8 reduce-scatter.14
  1493.1 24.4 reduce-scatter.10
  1519.9 66.4 reduce-scatter.8
  1593.4 149.2 reduce-scatter.12

commit v2 on v1

v2 whole, which is shorter than its diff:
```python
from functools import partial

import jax
import jax.numpy as jnp
from jax import lax
from jax.experimental import pallas as pl
from jax.experimental.pallas import tpu as pltpu
from jax.sharding import PartitionSpec as P

D = 2048
H = 16
DH = 128
E = 16
WINDOW = 1024
CAP = 144

EPSILON = 1e-06
ROPE_BASE = 50000.0
HIGHEST = lax.Precision.HIGHEST
BF16 = jnp.bfloat16
F32 = jnp.float32
MIB = 1024 * 1024


def matmul(left, right):
    return jnp.dot(left, right, preferred_element_type=F32)


def matmul_t(left, right):
    return lax.dot_general(left, right, (((1,), (1,)), ((), ())), preferred_element_type=F32)


def t_matmul(left, right):
    return lax.dot_general(left, right, (((0,), (0,)), ((), ())), preferred_element_type=F32)


def rms_factor(values):
    return lax.rsqrt(jnp.mean(values * values, axis=-1, keepdims=True) + EPSILON)


def swap(values, axis, size, mask):
    return lax.ppermute(values, axis, [(i, i ^ mask) for i in range(size)])


def high_bit(number):
    return 1 << (number.bit_length() - 1)


def low_bit(number):
    return number & -number


def after(values, *others):
    return lax.optimization_barrier((values, others))[0]


def gather_seq(values, size):
    rows = values.shape[0] // 2
    pieces = {0: values}
    for r in range(2, size, 2):
        if r == low_bit(r):
            pieces[r] = swap(values, "seq", size, r)
        else:
            up, down = high_bit(r), low_bit(r)
            pieces[r] = jnp.concatenate(
                [
                    swap(pieces[r ^ up][:rows], "seq", size, up),
                    swap(pieces[r ^ down][rows:], "seq", size, down),
                ],
                0,
            )
    even = jnp.concatenate([pieces[r] for r in range(0, size, 2)], 0)
    return even, swap(even, "seq", size, 1)


def relative(blocks, me):
    size = blocks.shape[0]
    order = list(range(0, size, 2)) + list(range(1, size, 2))
    return jnp.concatenate([lax.dynamic_slice_in_dim(blocks, me ^ r, 1, 0) for r in order], 0)


def absolute(blocks, me):
    size = blocks.shape[0]
    places = [((me ^ j) // 2) + ((me ^ j) % 2) * (size // 2) for j in range(size)]
    return jnp.concatenate([lax.dynamic_slice_in_dim(blocks, at, 1, 0) for at in places], 0)


def scatter_sum(even, odd, size):
    got = swap(odd, "seq", size, 1)
    rows = even.shape[0] // (size // 2)
    half = rows // 2

    def part(r, first, count):
        at = slice(r // 2 * rows + first, r // 2 * rows + first + count)
        return even[at].astype(F32) + got[at].astype(F32)

    sums = {r: [part(r, 0, half), part(r, half, half)] for r in range(0, size, 2)}
    for r in range(size - 2, 0, -2):
        if r == low_bit(r):
            whole = jnp.concatenate([value.astype(BF16) for value in sums[r]], 0)
            come = swap(whole, "seq", size, r).astype(F32)
            sums[0] = [sums[0][0] + come[:half], sums[0][1] + come[half:]]
        else:
            up, down = high_bit(r), low_bit(r)
            sums[r ^ up][0] += swap(sums[r][0].astype(BF16), "seq", size, up).astype(F32)
            sums[r ^ down][1] += swap(sums[r][1].astype(BF16), "seq", size, down).astype(F32)
    return jnp.concatenate(sums[0], 0)


def sum_all(values, axis, size):
    mask = 1
    while mask < size:
        values = values + swap(values, axis, size, mask)
        mask *= 2
    return values


def ring_pieces(values, size):
    pieces = [values]
    for _ in range(1, size):
        pieces.append(lax.ppermute(pieces[-1], "fsdp", [(i, (i + 1) % size) for i in range(size)]))
    return pieces


def place_ring(pieces, me, axis):
    size = len(pieces)
    shape = pieces[0].shape
    whole = jnp.zeros(shape[:axis] + (size,) + shape[axis:], pieces[0].dtype)
    for k, piece in enumerate(pieces):
        at = lax.rem(me + size - k, size)
        whole = lax.dynamic_update_slice_in_dim(whole, jnp.expand_dims(piece, axis), at, axis)
    return whole


def near_swaps(pieces, base, size, dep):
    for r in range(1, size // 2):
        up = high_bit(r)
        pieces[base + r] = swap(after(pieces[base + (r ^ up)], dep), "fsdp", size, up)
        dep = pieces[base + r]
    return dep


def place_swapped(pieces, me, experts_first):
    size = len(pieces)
    experts, part, columns = pieces[0].shape
    whole = jnp.zeros((experts, size, part, columns), pieces[0].dtype)
    for r in range(size):
        at = (me ^ r) % size
        whole = lax.dynamic_update_slice_in_dim(whole, pieces[r][:, None], at, 1)
    return whole.reshape(experts, size * part, columns)


def scatter_expert_cols(partial_sum, me, size, dep):
    experts, depth, hidden_half = partial_sum.shape
    half = size // 2
    parts = partial_sum.reshape(experts, size, depth // size, hidden_half)
    sums = {
        r: lax.dynamic_index_in_dim(parts, me ^ r, 1, keepdims=False).astype(F32)
        for r in range(size)
    }
    for r in range(half - 1, 0, -1):
        up = high_bit(r)
        for base in (half, 0):
            got = swap(after(sums[r | base].astype(BF16), dep), "fsdp", size, up)
            sums[(r ^ up) | base] += got.astype(F32)
            dep = got
    got = swap(after(sums[half].astype(BF16), dep), "fsdp", size, half)
    dep, got = got, got.astype(F32)
    first = me // half == 0
    return jnp.concatenate(
        [jnp.where(first, sums[0], got), jnp.where(first, got, sums[0])], axis=-1
    ), dep


def scatter_expert_rows(partial_sum, me, size, dep):
    experts, hidden_half, columns = partial_sum.shape
    half = size // 2
    parts = partial_sum.reshape(experts, half, hidden_half // half, columns)
    sums = {
        r: lax.dynamic_index_in_dim(parts, (me ^ r) % half, 1, keepdims=False).astype(F32)
        for r in range(half)
    }
    for r in range(half - 1, 0, -1):
        up = high_bit(r)
        dep = swap(after(sums[r].astype(BF16), dep), "fsdp", size, up)
        sums[r ^ up] += dep.astype(F32)
    return sums[0], dep


def scatter_rows(partial_sum, me, size):
    sums = {
        r: lax.dynamic_index_in_dim(partial_sum, me ^ r, 0, keepdims=False).astype(F32)
        for r in range(size)
    }
    mask = 1
    while mask < size:
        stay = [r for r in sums if not r & mask]
        moved = jnp.stack([sums[r | mask].astype(BF16) for r in stay], 0)
        got = swap(moved, "fsdp", size, mask).astype(F32)
        sums = {r: sums[r] + got[i] for i, r in enumerate(stay)}
        mask *= 2
    return sums[0]


def allowed_keys(seg_row, seg_col, first_query, first_key, rows, span, half_window):
    query_at = first_query + lax.broadcasted_iota(jnp.int32, (span, rows), 1)
    key_at = first_key + lax.broadcasted_iota(jnp.int32, (span, rows), 0)
    return (jnp.abs(query_at - key_at) <= half_window) & (seg_col == seg_row)


def first_key_of(block, rows, span, length):
    start = jnp.clip(block * rows - (span - rows) // 2, 0, length - span)
    return pl.multiple_of(start, rows)


def forward_kernel(span, q_ref, k_ref, v_ref, seg_row_ref, seg_col_ref, o_ref, lse_ref):
    block = pl.program_id(1)
    rows, length = q_ref.shape[0], k_ref.shape[0]
    first_key = first_key_of(block, rows, span, length)
    keys = k_ref[pl.ds(first_key, span), :]
    values = v_ref[pl.ds(first_key, span), :]
    scores = matmul_t(keys, q_ref[...]) * DH ** (-0.5)
    allowed = allowed_keys(
        seg_row_ref[...],
        seg_col_ref[pl.ds(first_key, span), :],
        block * rows,
        first_key,
        rows,
        span,
        WINDOW // 2,
    )
    scores = jnp.where(allowed, scores, -1e30)
    peak = jnp.max(scores, axis=0, keepdims=True)
    expos = jnp.exp(scores - peak)
    totals = jnp.sum(expos, axis=0, keepdims=True)
    probs = (expos * (1.0 / totals)).astype(BF16)
    o_ref[...] = t_matmul(values, probs).T.astype(BF16)
    lse_ref[...] = (peak + jnp.log(totals))[None]


def backward_kernel(
    span,
    q_ref,
    k_ref,
    v_ref,
    do_ref,
    lse_ref,
    seg_row_ref,
    seg_col_ref,
    dq_ref,
    dk_ref,
    dv_ref,
    dk_sum,
    dv_sum,
):
    block = pl.program_id(1)
    rows, length = q_ref.shape[0], k_ref.shape[0]

    @pl.when(block == 0)
    def _():
        dk_sum[...] = jnp.zeros_like(dk_sum)
        dv_sum[...] = jnp.zeros_like(dv_sum)

    first_key = first_key_of(block, rows, span, length)
    at = pl.ds(first_key, span)
    keys = k_ref[at, :]
    values = v_ref[at, :]
    queries = q_ref[...]
    grads = do_ref[...]
    scores = matmul_t(keys, queries) * DH ** (-0.5)
    allowed = allowed_keys(
        seg_row_ref[...],
        seg_col_ref[at, :],
        block * rows,
        first_key,
        rows,
        span,
        WINDOW // 2,
    )
    probs = jnp.where(allowed, jnp.exp(scores - lse_ref[0]), 0.0)
    dv_sum[at, :] += matmul(probs.astype(BF16), grads)
    prob_grads = matmul_t(values, grads)
    center = jnp.sum(probs * prob_grads, axis=0, keepdims=True)
    score_grads = (probs * (prob_grads - center)).astype(BF16)
    dk_sum[at, :] += matmul(score_grads, queries)
    dq_ref[...] = (t_matmul(keys, score_grads) * DH ** (-0.5)).T.astype(BF16)

    @pl.when(block == length // rows - 1)
    def _():
        dk_ref[...] = (dk_sum[...] * DH ** (-0.5)).astype(BF16)
        dv_ref[...] = dv_sum[...].astype(BF16)


def attention_sizes(length):
    rows = 256
    return rows, min(length, rows + WINDOW)


def attention_forward(queries, keys, values, seg_row, seg_col):
    length, columns = queries.shape
    heads = columns // DH
    rows, span = attention_sizes(length)
    block = pl.BlockSpec((rows, DH), lambda h, i: (i, h))
    whole = pl.BlockSpec((length, DH), lambda h, i: (0, h))
    return pl.pallas_call(
        partial(forward_kernel, span),
        grid=(heads, length // rows),
        in_specs=[
            block,
            whole,
            whole,
            pl.BlockSpec((1, rows), lambda h, i: (0, i)),
            pl.BlockSpec((length, 1), lambda h, i: (0, 0)),
        ],
        out_specs=[block, pl.BlockSpec((1, 1, rows), lambda h, i: (h, 0, i))],
        out_shape=[
            jax.ShapeDtypeStruct((length, columns), BF16),
            jax.ShapeDtypeStruct((heads, 1, length), F32),
        ],
        compiler_params=pltpu.CompilerParams(vmem_limit_bytes=48 * MIB),
        cost_estimate=pl.CostEstimate(
            flops=4 * heads * length * span * DH,
            bytes_accessed=8 * length * columns,
            transcendentals=heads * length * span,
        ),
        name="attend",
    )(queries, keys, values, seg_row, seg_col)


def attention_backward(queries, keys, values, grads, lse, seg_row, seg_col):
    length, columns = queries.shape
    heads = columns // DH
    rows, span = attention_sizes(length)
    block = pl.BlockSpec((rows, DH), lambda h, i: (i, h))
    whole = pl.BlockSpec((length, DH), lambda h, i: (0, h))
    shape = jax.ShapeDtypeStruct((length, columns), BF16)
    return pl.pallas_call(
        partial(backward_kernel, span),
        grid=(heads, length // rows),
        in_specs=[
            block,
            whole,
            whole,
            block,
            pl.BlockSpec((1, 1, rows), lambda h, i: (h, 0, i)),
            pl.BlockSpec((1, rows), lambda h, i: (0, i)),
            pl.BlockSpec((length, 1), lambda h, i: (0, 0)),
        ],
        out_specs=[block, whole, whole],
        out_shape=[shape, shape, shape],
        scratch_shapes=[pltpu.VMEM((length, DH), F32), pltpu.VMEM((length, DH), F32)],
        compiler_params=pltpu.CompilerParams(vmem_limit_bytes=48 * MIB),
        cost_estimate=pl.CostEstimate(
            flops=10 * heads * length * span * DH,
            bytes_accessed=14 * length * columns,
            transcendentals=heads * length * span,
        ),
        name="attend_back",
    )(queries, keys, values, grads, lse, seg_row, seg_col)


def qkv_kernel(
    me_ref, even_ref, odd_ref, weight_ref, gain_ref, normed_ref, q_ref, k_ref, v_ref, square_ref
):
    turned = me_ref[0] % 2 == 1
    rows = even_ref.shape[0]
    columns = q_ref.shape[1]
    first, second = even_ref[...], odd_ref[...]
    blocks = (jnp.where(turned, second, first), jnp.where(turned, first, second))
    for k, block in enumerate(blocks):
        at = pl.ds(k * rows, rows)
        wide = block.astype(F32)
        normed = (wide * rms_factor(wide) * gain_ref[...]).astype(BF16)
        normed_ref[at, :] = normed
        pre = matmul(normed, weight_ref[...])
        q_ref[at, :] = pre[:, :columns]
        k_ref[at, :] = pre[:, columns : 2 * columns]
        v_ref[at, :] = pre[:, 2 * columns :].astype(BF16)
        for j in range(2):
            squares = 0.0
            for c in range(j * columns, (j + 1) * columns, DH):
                squares += pre[:, c : c + DH] * pre[:, c : c + DH]
            square_ref[j : j + 1, at] = jnp.sum(squares.T, axis=0, keepdims=True)


def project(even, odd, weight, gain, me, rows):
    pairs = even.shape[0] // rows
    length = 2 * even.shape[0]
    depth, columns = weight.shape[0], weight.shape[1] // 3
    token = pl.BlockSpec((rows, depth), lambda i, me: (i, 0))

    def placed(shape):
        return pl.BlockSpec(shape, lambda i, me: (i ^ (me[0] // 2), 0))

    head = jax.ShapeDtypeStruct((length, columns), F32)
    return pl.pallas_call(
        qkv_kernel,
        grid_spec=pltpu.PrefetchScalarGridSpec(
            num_scalar_prefetch=1,
            grid=(pairs,),
            in_specs=[
                token,
                token,
                pl.BlockSpec(weight.shape, lambda i, me: (0, 0)),
                pl.BlockSpec((1, depth), lambda i, me: (0, 0)),
            ],
            out_specs=[
                placed((2 * rows, depth)),
                placed((2 * rows, columns)),
                placed((2 * rows, columns)),
                placed((2 * rows, columns)),
                pl.BlockSpec((2, 2 * rows), lambda i, me: (0, i ^ (me[0] // 2))),
            ],
        ),
        out_shape=[
            jax.ShapeDtypeStruct((length, depth), BF16),
            head,
            head,
            jax.ShapeDtypeStruct((length, columns), BF16),
            jax.ShapeDtypeStruct((2, length), F32),
        ],
        compiler_params=pltpu.CompilerParams(vmem_limit_bytes=48 * MIB),
        cost_estimate=pl.CostEstimate(
            flops=6 * length * depth * columns,
            bytes_accessed=length * (4 * depth + 10 * columns) + 6 * depth * columns,
            transcendentals=length,
        ),
        name="project",
    )(me, even, odd, weight, gain)


def expert_kernel(
    first_ref,
    xa_ref,
    xb_ref,
    ua_ref,
    ub_ref,
    ra_ref,
    rb_ref,
    wg_ref,
    wu_ref,
    wd_ref,
    router_ref,
    *refs,
):
    ya_ref, yb_ref, za_ref, zb_ref, ga_ref, gb_ref, xc_ref, uc_ref, dg_ref, du_ref, hid_ref = refs[-11:]
    experts = wg_ref.shape[0]
    rows = xa_ref.shape[0]
    slot = lax.broadcasted_iota(jnp.int32, (CAP, rows), 0)
    blocks = (
        (xa_ref, ua_ref, ra_ref, ya_ref, za_ref, ga_ref),
        (xb_ref, ub_ref, rb_ref, yb_ref, zb_ref, gb_ref),
    )
    picks = []
    for k, (x_ref, u_ref, rank_ref, _, _, _) in enumerate(blocks):
        hits = jnp.concatenate([slot == rank_ref[0, e : e + 1, :] for e in range(experts)], 0)
        pick = hits.astype(F32).astype(BF16)
        picks.append(pick)
        x_rows = matmul(pick, x_ref[...]).astype(BF16)
        u_rows = matmul(pick, u_ref[...]).astype(BF16)
        for e in range(experts):
            xc_ref[e, k * CAP : (k + 1) * CAP, :] = x_rows[e * CAP : (e + 1) * CAP]
            uc_ref[e, k * CAP : (k + 1) * CAP, :] = u_rows[e * CAP : (e + 1) * CAP]
    outs, backs, gate_grads = [], [], []
    for e in range(experts):
        x_rows, u_rows = xc_ref[e], uc_ref[e]
        logits = matmul(x_rows, router_ref[...])
        lane = lax.broadcasted_iota(jnp.int32, logits.shape, 1)
        logits = jnp.where(lane < E, logits, -1e30)
        expos = jnp.exp(logits - jnp.max(logits, axis=-1, keepdims=True))
        own = jnp.sum(jnp.where(lane == first_ref[0] + e, expos, 0.0), axis=-1, keepdims=True)
        gate = own / jnp.sum(expos, axis=-1, keepdims=True)
        gated = matmul(x_rows, wg_ref[e])
        upward = matmul(x_rows, wu_ref[e])
        pulled = matmul_t(u_rows, wd_ref[e])
        sig = jax.nn.sigmoid(gated)
        silu = gated * sig
        hidden = silu * upward
        gate_grads.append(jnp.sum(hidden * pulled, axis=-1, keepdims=True))
        hidden_gate = (hidden * gate).astype(BF16)
        hidden_grads = pulled * gate
        gated_low = (hidden_grads * upward * sig * (1.0 + gated * (1.0 - sig))).astype(BF16)
        upward_low = (hidden_grads * silu).astype(BF16)
        hid_ref[e] = hidden_gate
        dg_ref[e] = gated_low
        du_ref[e] = upward_low
        outs.append(matmul(hidden_gate, wd_ref[e]).astype(BF16))
        backs.append(
            (matmul_t(gated_low, wg_ref[e]) + matmul_t(upward_low, wu_ref[e])).astype(BF16)
        )
    for k, (_, _, rank_ref, y_ref, z_ref, g_ref) in enumerate(blocks):
        at = slice(k * CAP, (k + 1) * CAP)
        y_ref[...] = t_matmul(picks[k], jnp.concatenate([v[at] for v in outs], 0)).astype(BF16)
        z_ref[...] = t_matmul(picks[k], jnp.concatenate([v[at] for v in backs], 0)).astype(BF16)
        for e in range(experts):
            hit = slot == rank_ref[0, e : e + 1, :]
            g_ref[0, e : e + 1, :] = jnp.sum(
                jnp.where(hit, gate_grads[e][at], 0.0), axis=0, keepdims=True
            )


def run_experts(x, u, ranks, weights, router, first, which, compact):
    experts, depth, hidden = weights[0].shape
    rows = ranks[0].shape[2]
    steps = x[0].shape[0] // rows
    token = pl.BlockSpec((rows, depth), lambda i: (i, 0))
    rank = pl.BlockSpec((1, experts, rows), lambda i: (i, 0, 0))

    def whole(array):
        return pl.BlockSpec(
            array.shape, lambda i: (0,) * array.ndim, pipeline_mode=pl.Buffered(1)
        )

    def slots(columns):
        return pl.BlockSpec((experts, 2 * CAP, columns), lambda i: (0, i + which * steps, 0))

    shape = jax.ShapeDtypeStruct
    tokens = shape(x[0].shape, BF16)
    gates = shape((steps, experts, rows), F32)
    count = 4 * steps * CAP
    wide = shape((experts, count, depth), BF16)
    narrow = shape((experts, count, hidden), BF16)
    inputs = [first, *x, *u, *ranks, *weights, router]
    return pl.pallas_call(
        expert_kernel,
        grid=(steps,),
        in_specs=[pl.BlockSpec(memory_space=pltpu.SMEM)]
        + [token] * 4
        + [rank] * 2
        + [whole(w) for w in weights]
        + [whole(router)]
        + [pl.BlockSpec(memory_space=pl.ANY)] * len(compact),
        out_specs=[token] * 4 + [rank] * 2 + [slots(depth)] * 2 + [slots(hidden)] * 3,
        out_shape=[tokens] * 4 + [gates] * 2 + [wide] * 2 + [narrow] * 3,
        input_output_aliases={len(inputs) + i: 6 + i for i in range(len(compact))},
        compiler_params=pltpu.CompilerParams(vmem_limit_bytes=60 * MIB),
        cost_estimate=pl.CostEstimate(
            flops=4 * steps * CAP * experts * depth * (7 * hidden + 2 * rows),
            bytes_accessed=40 * MIB,
            transcendentals=2 * steps * CAP * experts * hidden,
        ),
        name="experts",
    )(*inputs, *compact)


def rotate(values, cosine, sine, heads):
    half = DH // 2
    shaped = values.reshape(values.shape[0], heads, DH)
    first, second = shaped[..., :half], shaped[..., half:]
    cosine, sine = cosine[:, None, :], sine[:, None, :]
    return jnp.concatenate(
        [first * cosine - second * sine, second * cosine + first * sine], axis=-1
    ).reshape(values.shape)


def per_device(
    S,
    F,
    tokens,
    segments,
    routes,
    cotangent,
    w_query,
    w_key,
    w_value,
    w_output,
    router,
    attn_gain,
    moe_gain,
    query_gain,
    key_gain,
    w_gate,
    w_up,
    w_down,
):
    s = lax.axis_index("seq")
    f = lax.axis_index("fsdp")
    T = tokens.shape[1]
    L = S * T
    heads = H // S
    C = heads * DH
    experts = E // S
    part = w_query.shape[0]
    half_f = F // 2
    hidden_half = w_gate.shape[2] // 2

    tokens_low = tokens[0]
    inputs = tokens_low.astype(F32)
    small = jnp.concatenate(
        [
            router.reshape(-1),
            attn_gain,
            moe_gain,
            query_gain,
            key_gain,
            routes[0].astype(BF16).reshape(-1),
        ]
    )
    small = lax.all_gather(small, ("seq", "fsdp"), axis=0, tiled=False).reshape(S, F, -1)
    tokens_even, tokens_odd = gather_seq(tokens_low, S)

    stacked = jnp.stack([w_query, w_key, w_value], 1).reshape(part, 3, S, C)
    stacked = stacked.transpose(2, 0, 1, 3).reshape(S, part, 3 * C)
    crossed = lax.all_to_all(stacked, "seq", split_axis=0, concat_axis=0, tiled=True)
    output_ring = ring_pieces(w_output, F)
    own_output = place_ring(output_ring, f, 0).reshape(C, D)
    qkv_ring = ring_pieces(after(crossed, output_ring[-1]), F)
    w_qkv = place_ring(qkv_ring, f, 1).reshape(D, 3 * C)

    full_router = small[:, :, : part * E].reshape(D, E)
    gains = [
        small[:, :, part * (E + i) : part * (E + i + 1)].reshape(D).astype(F32) for i in range(4)
    ]
    gain_attn, gain_moe = gains[0], gains[1]
    gain_query = lax.dynamic_slice_in_dim(gains[2], s * C, C, 0)
    gain_key = lax.dynamic_slice_in_dim(gains[3], s * C, C, 0)
    route_part = small[:, :, part * (E + 4) :].reshape(S, F, T, -1)
    expert_ids = s * experts + jnp.arange(experts, dtype=jnp.int32)

    def ranks_of(index):
        named = lax.dynamic_index_in_dim(route_part, index, 1, keepdims=False)
        named = relative(named, s).astype(jnp.int32)
        chosen = jnp.any(named[:, None] == expert_ids[None, :, None, None], axis=-1)
        ranks = jnp.cumsum(chosen.astype(jnp.int32), axis=-1) - 1
        ranks = jnp.where(chosen, ranks, -1)
        return ranks[: S // 2], ranks[S // 2 :]

    def split_hidden(weight):
        mine = lax.dynamic_slice_in_dim(weight, (f // half_f) * hidden_half, hidden_half, 2)
        other = lax.dynamic_slice_in_dim(weight, (1 - f // half_f) * hidden_half, hidden_half, 2)
        return mine, other

    gate_pieces, up_pieces, down_pieces = {}, {}, {0: w_down}
    gate_pieces[0], gate_other = split_hidden(w_gate)
    up_pieces[0], up_other = split_hidden(w_up)
    gate_pieces[half_f] = swap(after(gate_other, qkv_ring[-2]), "fsdp", F, half_f)
    up_pieces[half_f] = swap(after(up_other, gate_pieces[half_f]), "fsdp", F, half_f)
    upstream_low = cotangent[0]
    partner_up = swap(after(upstream_low, up_pieces[half_f]), "fsdp", F, half_f)
    dep = near_swaps(gate_pieces, 0, F, qkv_ring[-1])
    dep = near_swaps(up_pieces, 0, F, dep)
    dep = near_swaps(gate_pieces, half_f, F, dep)
    dep = near_swaps(up_pieces, half_f, F, dep)
    dep = near_swaps(down_pieces, 0, F, dep)
    own_gate = place_swapped(gate_pieces, f, experts)
    own_up = place_swapped(up_pieces, f, experts)
    own_down = place_swapped(down_pieces, f, experts)

    own_up_even, own_up_odd = gather_seq(after(upstream_low, tokens_even), S)
    out_even, out_odd = gather_seq(after(own_output, own_up_even), S)
    other_up_even, other_up_odd = gather_seq(after(partner_up, out_even), S)

    me = s.reshape(1).astype(jnp.int32)
    normed_all, query_pre, key_pre, value_low, squares = project(
        tokens_even, tokens_odd, w_qkv, gain_attn[None], me, T
    )
    places = jnp.arange(L, dtype=jnp.int32).astype(F32)
    freqs = ROPE_BASE ** (-(jnp.arange(DH // 2, dtype=F32) * 2.0 / DH))
    angles = places[:, None] * freqs[None, :]
    cosine, sine = jnp.cos(angles), jnp.sin(angles)
    factors = lax.rsqrt(sum_all(squares, "seq", S) / D + EPSILON)
    query_n = query_pre * factors[0][:, None]
    key_n = key_pre * factors[1][:, None]
    query_low = rotate(query_n * gain_query, cosine, sine, heads).astype(BF16)
    key_low = rotate(key_n * gain_key, cosine, sine, heads).astype(BF16)
    seg_row = segments
    seg_col = segments.reshape(L, 1)
    attended, lse = attention_forward(query_low, key_low, value_low, seg_row, seg_col)
    attended_blocks = attended.reshape(S, T, C)
    come = lax.all_to_all(attended_blocks, "seq", split_axis=0, concat_axis=0, tiled=True)
    come = relative(come, s).transpose(1, 0, 2).reshape(T, D)
    residual = inputs + matmul(come[:, : D // 2], out_even) + matmul(come[:, D // 2 :], out_odd)

    moe_factor = rms_factor(residual)
    residual_n = residual * moe_factor
    second_low = (residual_n * gain_moe).astype(BF16)
    partner_low = swap(second_low, "fsdp", F, half_f)
    own_x = gather_seq(second_low, S)
    other_x = gather_seq(after(partner_low, own_x[0]), S)
    logits = matmul(second_low, full_router)
    router_probs = jax.nn.softmax(logits, axis=-1)
    expert_weights = (own_gate, own_up, own_down)
    wide_router = jnp.pad(full_router, ((0, 0), (0, 128 - E)))
    first = (s * experts).reshape(1).astype(jnp.int32)
    own_parts = run_experts(
        own_x, (own_up_even, own_up_odd), ranks_of(f), expert_weights, wide_router, first, 0, ()
    )
    other_parts = run_experts(
        other_x,
        (other_up_even, other_up_odd),
        ranks_of(f ^ half_f),
        expert_weights,
        wide_router,
        first,
        1,
        own_parts[6:],
    )
    x_rows, u_rows, gated_low, upward_low, hidden_gate = other_parts[6:]
    own_rows = scatter_sum(own_parts[2], own_parts[3], S)
    other_rows = scatter_sum(other_parts[2], other_parts[3], S).astype(BF16)
    back_rows = swap(other_rows, "fsdp", F, half_f)
    row_grads = own_rows + back_rows.astype(F32)

    def to_home(even, odd):
        return absolute(jnp.concatenate([even, odd], 0).transpose(0, 2, 1), s)

    gate_grads = jnp.stack(
        [to_home(own_parts[4], own_parts[5]), to_home(other_parts[4], other_parts[5])], 1
    )
    gate_grads = lax.all_to_all(
        gate_grads.reshape(S, -1), "seq", split_axis=0, concat_axis=0, tiled=True
    ).reshape(S, 2, T * experts)
    gate_grads = gate_grads[:, 0] + swap(gate_grads[:, 1], "fsdp", F, half_f)
    gate_grads = gate_grads.reshape(S, T, experts).transpose(1, 0, 2).reshape(T, E)

    down_term = jnp.stack([t_matmul(hidden_gate[e], u_rows[e]) for e in range(experts)], 0)
    gate_term = jnp.stack([t_matmul(x_rows[e], gated_low[e]) for e in range(experts)], 0)
    up_term = jnp.stack([t_matmul(x_rows[e], upward_low[e]) for e in range(experts)], 0)
    grad_down, dep = scatter_expert_rows(down_term.astype(BF16), f, F, own_rows)
    grad_gate, dep = scatter_expert_cols(gate_term.astype(BF16), f, F, back_rows)
    grad_up, dep = scatter_expert_cols(up_term.astype(BF16), f, F, dep)

    upstream = upstream_low.astype(F32)
    logit_grads = router_probs * (
        gate_grads - jnp.sum(router_probs * gate_grads, axis=-1, keepdims=True)
    )
    router_wide = full_router.astype(F32)
    second_grads = row_grads + jnp.dot(logit_grads, router_wide.T, precision=HIGHEST)
    router_term = jnp.dot(second_low.astype(F32).T, logit_grads, precision=HIGHEST)
    moe_gain_term = jnp.sum(second_grads * residual_n, axis=0)
    pulled = second_grads * gain_moe
    residual_grads = upstream + moe_factor * (
        pulled - residual_n * jnp.mean(pulled * residual_n, axis=-1, keepdims=True)
    )
    branch_low = residual_grads.astype(BF16)

    branch_even, branch_odd = gather_seq(branch_low, S)
    head_grads = jnp.concatenate(
        [matmul_t(branch_even, own_output), matmul_t(branch_odd, own_output)], 0
    ).astype(BF16)
    head_grads = absolute(head_grads.reshape(S, T, C), s).reshape(L, C)
    attended_rel = relative(attended_blocks, s).reshape(2, L // 2, C)
    output_term = t_matmul(attended_rel[0], branch_even) + t_matmul(attended_rel[1], branch_odd)
    query_back, key_back, value_back = attention_backward(
        query_low, key_low, value_low, head_grads, lse, seg_row, seg_col
    )
    own_outs = scatter_sum(own_parts[0], after(own_parts[1], branch_even), S)
    other_outs = scatter_sum(other_parts[0], after(other_parts[1], own_outs), S).astype(BF16)
    other_outs = swap(other_outs, "fsdp", F, half_f).astype(F32)
    mixed = (residual + own_outs + other_outs).astype(BF16)[None]
    query_turned = rotate(query_back.astype(F32), cosine, -sine, heads)
    key_turned = rotate(key_back.astype(F32), cosine, -sine, heads)
    query_gain_term = jnp.sum(query_turned * query_n, axis=0)
    key_gain_term = jnp.sum(key_turned * key_n, axis=0)
    query_pulled = query_turned * gain_query
    key_pulled = key_turned * gain_key
    means = jnp.stack([jnp.sum(query_pulled * query_n, -1), jnp.sum(key_pulled * key_n, -1)], 0)
    means = sum_all(means, "seq", S) / D
    query_pre_low = (factors[0][:, None] * (query_pulled - query_n * means[0][:, None])).astype(BF16)
    key_pre_low = (factors[1][:, None] * (key_pulled - key_n * means[1][:, None])).astype(BF16)
    pre_low = jnp.concatenate([query_pre_low, key_pre_low, value_back], 1)
    pre_rel = relative(pre_low.reshape(S, T, 3 * C), s).reshape(2, L // 2, 3 * C)
    normed_grads = scatter_sum(
        matmul_t(pre_rel[0], w_qkv).astype(BF16), matmul_t(pre_rel[1], w_qkv).astype(BF16), S
    )

    def weight_sum(grads):
        term = t_matmul(normed_all, grads).astype(BF16)
        term = term.reshape(S, F, part, -1).transpose(1, 0, 2, 3)
        return scatter_rows(term, f, F).astype(BF16)

    value_term = weight_sum(value_back)
    turned_term = weight_sum(pre_low[:, : 2 * C])
    qkv_term = jnp.concatenate([turned_term, value_term], -1)
    qkv_term = lax.all_to_all(qkv_term, "seq", split_axis=0, concat_axis=0, tiled=True)
    qkv_term = qkv_term.reshape(S, part, 3, C).transpose(2, 1, 0, 3).reshape(3, part, D).astype(F32)
    grad_output = scatter_rows(output_term.astype(BF16).reshape(F, part, D), f, F)
    head_gains = lax.psum_scatter(
        jnp.stack([query_gain_term, key_gain_term], 1), "fsdp", scatter_dimension=0, tiled=True
    )
    attn_factor = rms_factor(inputs)
    inputs_n = inputs * attn_factor
    attn_gain_term = jnp.sum(normed_grads * inputs_n, axis=0)
    attn_pulled = normed_grads * gain_attn
    grad_tokens = residual_grads + attn_factor * (
        attn_pulled - inputs_n * jnp.mean(attn_pulled * inputs_n, axis=-1, keepdims=True)
    )
    gain_terms = jnp.concatenate([router_term, moe_gain_term[:, None], attn_gain_term[:, None]], 1)
    gain_terms = lax.psum_scatter(gain_terms, ("seq", "fsdp"), scatter_dimension=0, tiled=True)
    return (
        mixed,
        grad_tokens[None],
        qkv_term[0],
        qkv_term[1],
        qkv_term[2],
        grad_output,
        gain_terms[:, :E],
        gain_terms[:, E + 1],
        gain_terms[:, E],
        head_gains[:, 0],
        head_gains[:, 1],
        grad_gate,
        grad_up,
        grad_down,
    )


def solution(mesh):
    tokens_spec = P("fsdp", "seq", None)
    rows_spec = P(("seq", "fsdp"), None)
    gain_spec = P(("seq", "fsdp"))
    expert_spec = P("seq", "fsdp", None)
    in_specs = (
        (tokens_spec, P("fsdp", None), tokens_spec, tokens_spec)
        + (rows_spec,) * 5
        + (gain_spec,) * 4
        + (expert_spec,) * 3
    )
    out_specs = (tokens_spec,) * 2 + (rows_spec,) * 5 + (gain_spec,) * 4 + (expert_spec,) * 3
    return jax.shard_map(
        partial(per_device, mesh.shape["seq"], mesh.shape["fsdp"]),
        mesh=mesh,
        in_specs=in_specs,
        out_specs=out_specs,
        check_vma=False,
    )
```

time: 1770 us -> 1480 us (0.84)
  matrix products: 367 us -> 94.4 us
  Pallas kernels: 49.7 us -> 179 us
  waiting for transfers between devices: 727 us -> 644 us
  blocking collectives: 114 us -> 71.3 us
  other arithmetic: 181 us -> 147 us
  starting transfers between devices: 87.4 us -> 109 us
  local copies, waits for them, and re-layouts: 218 us -> 200 us
    pallas_call x0 -> x3, Pallas kernels: none -> 129 us  [the longest x2 116 us: run_experts(): pl.pallas_call(expert_kernel, grid=(steps,), in_specs=[pl.BlockSpec(memor...]
    dot_general x8 -> x0, matrix products: 123 us -> none  [the longest x2 38.3 us: per_device(): jnp.einsum('bct,bcd->btd', picks[e], outs, preferred_element_type=F32)]
    ppermute x102 -> x91, waiting for transfers between devices: 614 us -> 492 us  [swap(): return lax.ppermute(values, axis, [(i, i ^ mask) for i in range(size)])]
    dot_general x12 -> x3, matrix products: 96.6 us -> 9.67 us  [matmul(): return jnp.dot(left, right, preferred_element_type=F32)]
    dot_general x8 -> x4, matrix products: 86.7 us -> 12.7 us  [matmul_t(): lax.dot_general(left, right, (((1,), (1,)), ((), ())), preferred_element_...]
    slice x32 -> x21, local copies, waits for them, and re-layouts: 39.2 us -> 4.3 us  [the longest x7 1.47 us: gather_seq(): pieces[r ^ up][:rows]]
    all_gather x2 -> x1, blocking collectives: 96.1 us -> 71.3 us  [per_device(): lax.all_gather(small, ('seq', 'fsdp'), axis=0, tiled=False)]
    add x9 -> x5, other arithmetic: 38.8 us -> 14.2 us  [the longest x3 8.07 us: scatter_sum(): sums[0] = [sums[0][0] + come[:half], sums[0][1] + come[half:]]]
  transfers between devices with their start and end apart: 113 -> 103, of which waited for: 37 -> 44; matrix products, arithmetic and copies ran while one was open for 25% -> 29% of each run, Pallas kernels for 3% -> 12%
where the time goes in v2:
time: 1480 us; the launch traced here: 1460 us
  waiting for transfers between devices  644 us (44%)
  local copies, waits for them, and re-layouts  200 us (14%)
  Pallas kernels  179 us (12%)
  other arithmetic  147 us (10%)
  starting transfers between devices  109 us (7%)
  matrix products  94.4 us (6%)
  blocking collectives  71.3 us (5%)
  between operations  19.4 us (1%)
    ppermute x91, waiting for transfers between devices, swap(): return lax.ppermute(values, axis, [(i, i ^ mask) for i in range(size)])  492 us
    unnamed x4, waiting for transfers between devices  133 us
    pallas_call x2, Pallas kernels, run_experts(): pl.pallas_call(expert_kernel, grid=(steps,), in_specs=[pl.BlockSpec(memor...  116 us
    ppermute x91, starting transfers between devices, swap(): return lax.ppermute(values, axis, [(i, i ^ mask) for i in range(size)])  90.3 us
    all_gather x1, blocking collectives, per_device(): lax.all_gather(small, ('seq', 'fsdp'), axis=0, tiled=False)  71.3 us
    dot_general x10, matrix products, t_matmul(): lax.dot_general(left, right, (((0,), (0,)), ((), ())), preferred_element_...  66.1 us
    unnamed x373, local copies, waits for them, and re-layouts  64.7 us
    another operation x12, local copies, waits for them, and re-layouts  36 us
  transfers between devices with their start and end apart: 103, of which 44 were waited for; matrix products, arithmetic and copies ran while one was open for 29% of the time, Pallas kernels for 12%

profile of v2, /device:TPU:0, one launch (start us, length us, event | category | flops | bytes accessed | tf_op | source)
XLA Modules:
  0.0 1463.8 jit_solution(15712650864991136334)
XLA Ops:
  27.1 71.3 %all-gather.1 = bf16[32,1,3328]{2,1,0:T(2,128)(2,1)S(1)} all-gather(bf16[1,1,3328]{2,1,0:T(2,128)(2,1)S(1)} %reshape.637), channel_id=2, replica_groups=mesh['seq'=8,'fsdp'=4] {'seq','fsdp'}, dimensions={0}, use_global_device_ids=true | all-gather | bytes 219648 | tf_op jit(solution)/shard_map/all_gather | solution.py:599
  167.6 20.9 %collective-permute-done.14 = bf16[256,2048]{1,0:T(8,128)(2,1)S(1)} collective-permute-done((bf16[256,2048]{1,0:T(8,128)(2,1)S(1)}, bf16[256,2048]{1,0:T(8,128)(2,1)S(1)}, u32[]{:S(2)}, u32[]{:S(2)}) %collective-permute-start.14) | collective-permute-done | bytes 1048608 | tf_op jit(solution)/shard_map/ppermute | solution.py:42
  191.6 10.6 collective-permute-done.16
  215.2 12.0 collective-permute-done.19
  232.8 13.1 project.1
  279.8 21.4 %attend.1 = (bf16[2048,256]{1,0:T(8,128)(2,1)S(1)}, f32[2,1,2048]{2,1,0:T(1,128)S(1)}) custom-call(bf16[2048,256]{1,0:T(8,128)(2,1)S(1)} %bitcast.484, bf16[2048,256]{1,0:T(8,128)(2,1)S(1)} %bitcast.482, bf16[2048,256]{1,0:T(8,128)(2,1)S(1)} %copy-done.11, s32[1,2048]{1,0:T(1,128)S(1)} %copy-done.9, s32[2048,1]{1,0:T(8,128)S(1)} %copy.309.seg_col_ref), custom_call_target="tpu_custom_call" | custom-call | flops 2684354560 | bytes 4194304 | tf_op jit(solution)/shard_map/attend/pallas_call | solution.py:305
  335.2 27.9 %collective-permute-done.33 = bf16[2,512,512]{2,1,0:T(8,128)(2,1)} collective-permute-done((bf16[2,512,512]{2,1,0:T(8,128)(2,1)}, bf16[2,512,512]{2,1,0:T(8,128)(2,1)}, u32[]{:S(2)}, u32[]{:S(2)}) %collective-permute-start.33) | collective-permute-done | bytes 1048608 | tf_op jit(solution)/shard_map/ppermute | solution.py:42
  376.3 35.1 %collective-permute-done.47 = bf16[256,2048]{1,0:T(8,128)(2,1)S(1)} collective-permute-done((bf16[256,2048]{1,0:T(8,128)(2,1)S(1)}, bf16[256,2048]{1,0:T(8,128)(2,1)S(1)}, u32[]{:S(2)}, u32[]{:S(2)}) %collective-permute-start.47) | collective-permute-done | bytes 1048608 | tf_op jit(solution)/shard_map/ppermute | solution.py:42
  416.4 31.2 %collective-permute-done.26 = bf16[128,2048]{1,0:T(8,128)(2,1)S(1)} collective-permute-done((bf16[128,2048]{1,0:T(8,128)(2,1)S(1)}, bf16[128,2048]{1,0:T(8,128)(2,1)S(1)}, u32[]{:S(2)}, u32[]{:S(2)}) %collective-permute-start.26) | collective-permute-done | bytes 524320 | tf_op jit(solution)/shard_map/ppermute | solution.py:42
  477.0 41.7 %collective-permute-done.41 = bf16[256,2048]{1,0:T(8,128)(2,1)S(1)} collective-permute-done((bf16[256,2048]{1,0:T(8,128)(2,1)}, bf16[256,2048]{1,0:T(8,128)(2,1)S(1)}, u32[]{:S(2)}, u32[]{:S(2)}) %collective-permute-start.41) | collective-permute-done | bytes 1048608 | tf_op jit(solution)/shard_map/ppermute | solution.py:42
  524.3 18.3 %collective-permute-done.42 = bf16[256,2048]{1,0:T(8,128)(2,1)S(1)} collective-permute-done((bf16[256,2048]{1,0:T(8,128)(2,1)S(1)}, bf16[256,2048]{1,0:T(8,128)(2,1)S(1)}, u32[]{:S(2)}, u32[]{:S(2)}) %collective-permute-start.42) | collective-permute-done | bytes 1048608 | tf_op jit(solution)/shard_map/ppermute | solution.py:42
  560.8 58.1 %experts.2 = (bf16[1024,2048]{1,0:T(8,128)(2,1)}, bf16[1024,2048]{1,0:T(8,128)(2,1)}, bf16[1024,2048]{1,0:T(8,128)(2,1)}, bf16[1024,2048]{1,0:T(8,128)(2,1)}, f3...) custom-call(s32[1]{0:T(128)} %bitcast.25.first_ref, ...), custom_call_target="tpu_custom_call" | custom-call | flops 38654705664 | bytes 41943040 | tf_op jit(solution)/shard_map/experts/pallas_call | solution.py:524
  621.0 58.2 %experts.3 = (bf16[1024,2048]{1,0:T(8,128)(2,1)}, bf16[1024,2048]{1,0:T(8,128)(2,1)}, bf16[1024,2048]{1,0:T(8,128)(2,1)}, bf16[1024,2048]{1,0:T(8,128)(2,1)}, f3...) custom-call(s32[1]{0:T(128)} %bitcast.25.first_ref, ...), custom_call_target="tpu_custom_call", output_to_operand_aliasing={{6}: (11, {}), {7}: (12, {}), {8}: (13, {}), {9}: (14, {}),... | custom-call | flops 38654705664 | bytes 41943040 | tf_op jit(solution)/shard_map/experts/pallas_call | solution.py:524
  685.8 15.7 %slice_bitcast_fusion = (bf16[2048,2304]{0,1:T(8,128)(2,1)}, bf16[2048,2304]{0,1:T(8,128)(2,1)}) fusion(bf16[2,2304,2048]{2,1,0:T(8,128)(2,1)} %get-tuple-element.110), kind=kLoop, calls=%fused_computation.6 | loop fusion | bytes 37748736 | tf_op jit(solution)/shard_map/dot_general | solution.py:34
  701.4 12.4 copy.386
  736.5 12.1 copy.385
  748.6 9.6 convert_bitcast_fusion.3
  758.2 9.1 fusion.15
  814.2 15.4 %collective-permute-done.57 = bf16[256,2048]{1,0:T(8,128)(2,1)S(1)} collective-permute-done((bf16[256,2048]{1,0:T(8,128)(2,1)S(1)}, bf16[256,2048]{1,0:T(8,128)(2,1)S(1)}, u32[]{:S(2)}, u32[]{:S(2)}) %collective-permute-start.57) | collective-permute-done | bytes 1048608 | tf_op jit(solution)/shard_map/ppermute | solution.py:42
  838.3 12.8 collective-permute-done.40
  856.8 24.1 %collective-permute-done.58 = bf16[256,2048]{1,0:T(8,128)(2,1)} collective-permute-done((bf16[256,2048]{1,0:T(8,128)(2,1)}, bf16[256,2048]{1,0:T(8,128)(2,1)}, u32[]{:S(2)}, u32[]{:S(2)}) %collective-permute-start.58) | collective-permute-done | bytes 1048608 | tf_op jit(solution)/shard_map/ppermute | solution.py:42
  898.2 12.9 collective-permute-done.60
  939.1 11.9 collective-permute-done.91
  955.7 44.2 %collective-permute-done.92 = bf16[2,512,512]{1,2,0:T(8,128)(2,1)S(1)} collective-permute-done((bf16[2,512,512]{1,2,0:T(8,128)(2,1)S(1)}, bf16[2,512,512]{1,2,0:T(8,128)(2,1)S(1)}, u32[]{:S(2)}, u32[]{:S(2)}) %collective-permute-start.92) | collective-permute-done | bytes 1048608 | tf_op jit(solution)/shard_map/ppermute | solution.py:42
  1008.6 16.4 %collective-permute-done.71 = bf16[256,2048]{1,0:T(8,128)(2,1)S(1)} collective-permute-done((bf16[256,2048]{1,0:T(8,128)(2,1)S(1)}, bf16[256,2048]{1,0:T(8,128)(2,1)S(1)}, u32[]{:S(2)}, u32[]{:S(2)}) %collective-permute-start.71) | collective-permute-done | bytes 1048608 | tf_op jit(solution)/shard_map/ppermute | solution.py:42
  1032.9 34.1 %collective-permute-done.94 = bf16[2,512,512]{1,2,0:T(8,128)(2,1)S(1)} collective-permute-done((bf16[2,512,512]{1,2,0:T(8,128)(2,1)S(1)}, bf16[2,512,512]{1,2,0:T(8,128)(2,1)S(1)}, u32[]{:S(2)}, u32[]{:S(2)}) %collective-permute-start.94) | collective-permute-done | bytes 1048608 | tf_op jit(solution)/shard_map/ppermute | solution.py:42
  1079.5 27.8 %attend_back.1 = (bf16[2048,256]{1,0:T(8,128)(2,1)S(1)}, bf16[2048,256]{1,0:T(8,128)(2,1)S(1)}, bf16[2048,256]{1,0:T(8,128)(2,1)S(1)}) custom-call(bf16[2048,256]{1,0:T(8,128)(2,1)S(1)} %bitcast.485, bf16[2048,256]{1,0:T(8,128)(2,1)S(1)} %bitcast.483, bf16[2048,256]{1,0:T(8,128)(2,1)} %copy-done.10, bf16[2048,256]{1,0:T(8,128)(2,1)} %bitcast.579, ...), custom_call_target="tpu_custom_call" | custom-call | flops 6710886400 | bytes 7340032 | tf_op jit(solution)/shard_map/attend_back/pallas_call | solution.py:337
  1180.3 9.1 collective-permute-done.88
  1189.6 11.0 collective-permute-done.86
  1240.1 15.8 %collective-permute-done.85 = bf16[1,8,64,512]{3,2,1,0:T(8,128)(2,1)S(1)} collective-permute-done((bf16[1,8,64,512]{3,2,1,0:T(8,128)(2,1)S(1)}, bf16[1,8,64,512]{3,2,1,0:T(8,128)(2,1)S(1)}, u32[]{:S(2)}, u32[]{:S(2)}) %collective-permute-start.85) | collective-permute-done | bytes 524320 | tf_op jit(solution)/shard_map/ppermute | solution.py:42
  1300.7 11.6 collective-permute-done.81
  1324.9 127.6 %reduce-scatter.7.cloned.1.call-done = f32[64,18]{1,0:T(8,128)} async-done(((f32[2048,18]{1,0:T(8,128)}), f32[64,18]{1,0:T(8,128)}) %reduce-scatter.7.cloned.1.call-update) | async-done | bytes 4624
  (838 shorter events, 591.1 us)
Async XLA Ops:
  8.0 130.4 %collective-permute-start = (bf16[256,2048]{1,0:T(8,128)(2,1)}, bf16[256,2048]{1,0:T(8,128)(2,1)S(1)}, u32[]{:S(2)}, u32[]{:S(2)}) collective-permute-start(bf16[256,2048]{1,0:T(8,128)(2,1)} %bitcast.487), channel_id=1, source_target_pairs={{0,8},{4,12},{8,0},{12,4},{16,24},{20,28},{24,16},{28,20},{1,9},{5... | collective-permute-start | bytes 3145736 | tf_op jit(solution)/shard_map/ppermute | solution.py:42
  11.0 135.9 %collective-permute-start.1 = (bf16[256,2048]{1,0:T(8,128)(2,1)}, bf16[256,2048]{1,0:T(8,128)(2,1)}, u32[]{:S(2)}, u32[]{:S(2)}) collective-permute-start(bf16[256,2048]{1,0:T(8,128)(2,1)} %bitcast.488), channel_id=1, source_target_pairs={{0,16},{4,20},{8,24},{12,28},{16,0},{20,4},{24,8},{28,12},{1,17},{... | collective-permute-start | bytes 3145736 | tf_op jit(solution)/shard_map/ppermute | solution.py:42
  19.4 121.2 %all-to-all-start = ((bf16[8,64,768]{2,1,0:T(8,128)(2,1)}), bf16[8,64,768]{2,1,0:T(8,128)(2,1)}, u32[]{:S(2)}, u32[]{:S(2)}) async-start(bf16[8,64,768]{2,1,0:T(8,128)(2,1)} %reshape.576), calls=%async_computation | async-start | bytes 1572864 | tf_op jit(solution)/shard_map/all_to_all | solution.py:604
  23.8 102.7 %collective-permute-start.5 = (bf16[64,2048]{1,0:T(8,128)(2,1)}, bf16[64,2048]{1,0:T(8,128)(2,1)}, u32[]{:S(2)}, u32[]{:S(2)}) collective-permute-start(bf16[64,2048]{1,0:T(8,128)(2,1)} %param.23), channel_id=1, source_target_pairs={{0,1},{1,2},{2,3},{3,0},{4,5},{5,6},{6,7},{7,4},{8,9},{9,10},{10,1... | collective-permute-start | bytes 786440 | tf_op jit(solution)/shard_map/ppermute | solution.py:121
  158.1 74.7 %collective-permute-start.4 = (bf16[1024,2048]{1,0:T(8,128)(2,1)}, bf16[1024,2048]{1,0:T(8,128)(2,1)}, u32[]{:S(2)}, u32[]{:S(2)}) collective-permute-start(bf16[1024,2048]{1,0:T(8,128)(2,1)} %constant_dynamic-update-slice_fusion.even_ref), channel_id=1, source_target_pairs={{0,4},{4,0},{8,12},{12,8},{16,20},{20,16},{24,28},{28,24},{1,5},{5... | collective-permute-start | bytes 12582920 | tf_op jit(solution)/shard_map/ppermute | solution.py:42
  209.4 103.3 %collective-permute-start.30 = (bf16[2,512,512]{2,1,0:T(8,128)(2,1)}, bf16[2,512,512]{2,1,0:T(8,128)(2,1)}, u32[]{:S(2)}, u32[]{:S(2)}) collective-permute-start(bf16[2,512,512]{2,1,0:T(8,128)(2,1)} %constant_dynamic-slice_fusion.44), channel_id=1, source_target_pairs={{0,2},{1,3},{2,0},{3,1},{4,6},{5,7},{6,4},{7,5},{8,10},{9,11},{10,... | collective-permute-start | bytes 3145736 | tf_op jit(solution)/shard_map/ppermute | solution.py:42
  212.9 103.6 %collective-permute-start.29 = (bf16[2,512,512]{2,1,0:T(8,128)(2,1)}, bf16[2,512,512]{2,1,0:T(8,128)(2,1)}, u32[]{:S(2)}, u32[]{:S(2)}) collective-permute-start(bf16[2,512,512]{2,1,0:T(8,128)(2,1)} %get-tuple-element.76), channel_id=1, source_target_pairs={{0,1},{1,0},{2,3},{3,2},{4,5},{5,4},{6,7},{7,6},{8,9},{9,8},{10,11... | collective-permute-start | bytes 3145736 | tf_op jit(solution)/shard_map/ppermute | solution.py:42
  253.6 68.4 %collective-permute-start.22 = (bf16[1024,2048]{1,0:T(8,128)(2,1)}, bf16[1024,2048]{1,0:T(8,128)(2,1)}, u32[]{:S(2)}, u32[]{:S(2)}) collective-permute-start(bf16[1024,2048]{1,0:T(8,128)(2,1)} %constant_dynamic-update-slice_fusion.18), channel_id=1, source_target_pairs={{0,4},{4,0},{8,12},{12,8},{16,20},{20,16},{24,28},{28,24},{1,5},{5... | collective-permute-start | bytes 12582920 | tf_op jit(solution)/shard_map/ppermute | solution.py:42
  312.7 50.4 %collective-permute-start.33 = (bf16[2,512,512]{2,1,0:T(8,128)(2,1)}, bf16[2,512,512]{2,1,0:T(8,128)(2,1)}, u32[]{:S(2)}, u32[]{:S(2)}) collective-permute-start(bf16[2,512,512]{2,1,0:T(8,128)(2,1)} %constant_dynamic-slice_fusion.42), channel_id=1, source_target_pairs={{0,2},{1,3},{2,0},{3,1},{4,6},{5,7},{6,4},{7,5},{8,10},{9,11},{10,... | collective-permute-start | bytes 3145736 | tf_op jit(solution)/shard_map/ppermute | solution.py:42
  368.7 188.2 %collective-permute-start.28 = (bf16[1024,2048]{1,0:T(8,128)(2,1)}, bf16[1024,2048]{1,0:T(8,128)(2,1)S(1)}, u32[]{:S(2)}, u32[]{:S(2)}) collective-permute-start(bf16[1024,2048]{1,0:T(8,128)(2,1)} %copy-done.100), channel_id=1, source_target_pairs={{0,4},{4,0},{8,12},{12,8},{16,20},{20,16},{24,28},{28,24},{1,5},{5... | collective-permute-start | bytes 12582920 | tf_op jit(solution)/shard_map/ppermute | solution.py:42
  447.7 109.2 %collective-permute-start.27 = (bf16[1024,2048]{1,0:T(8,128)(2,1)S(1)}, bf16[1024,2048]{1,0:T(8,128)(2,1)S(1)}, u32[]{:S(2)}, u32[]{:S(2)}) collective-permute-start(bf16[1024,2048]{1,0:T(8,128)(2,1)S(1)} %constant_dynamic-update-slice_fusion.23.xa_ref), channel_id=1, source_target_pairs={{0,4},{4,0},{8,12},{12,8},{16,20},{20,16},{24,28},{28,24},{1,5},{5... | collective-permute-start | bytes 12582920 | tf_op jit(solution)/shard_map/ppermute | solution.py:42
  451.4 72.6 %collective-permute-start.35 = (bf16[2,256,2048]{2,1,0:T(8,128)(2,1)S(1)}, bf16[2,256,2048]{2,1,0:T(8,128)(2,1)S(1)}, u32[]{:S(2)}, u32[]{:S(2)}) collective-permute-start(bf16[2,256,2048]{2,1,0:T(8,128)(2,1)S(1)} %copy-done.69), channel_id=1, source_target_pairs={{0,1},{1,0},{2,3},{3,2},{4,5},{5,4},{6,7},{7,6},{8,9},{9,8},{10,11... | collective-permute-start | bytes 6291464 | tf_op jit(solution)/shard_map/ppermute | solution.py:42
  453.4 65.3 %collective-permute-start.41 = (bf16[256,2048]{1,0:T(8,128)(2,1)}, bf16[256,2048]{1,0:T(8,128)(2,1)S(1)}, u32[]{:S(2)}, u32[]{:S(2)}) collective-permute-start(bf16[256,2048]{1,0:T(8,128)(2,1)} %get-tuple-element.223), channel_id=1, source_target_pairs={{0,2},{1,3},{2,0},{3,1},{4,6},{5,7},{6,4},{7,5},{8,10},{9,11},{10,... | collective-permute-start | bytes 3145736 | tf_op jit(solution)/shard_map/ppermute | solution.py:42
  524.0 97.0 %collective-permute-start.52 = (bf16[1024,2048]{1,0:T(8,128)(2,1)}, bf16[1024,2048]{1,0:T(8,128)(2,1)}, u32[]{:S(2)}, u32[]{:S(2)}) collective-permute-start(bf16[1024,2048]{1,0:T(8,128)(2,1)} %constant_dynamic-update-slice_fusion.41.ua_ref), channel_id=1, source_target_pairs={{0,4},{4,0},{8,12},{12,8},{16,20},{20,16},{24,28},{28,24},{1,5},{5... | collective-permute-start | bytes 12582920 | tf_op jit(solution)/shard_map/ppermute | solution.py:42
  556.9 64.1 %collective-permute-start.46 = (bf16[1024,2048]{1,0:T(8,128)(2,1)}, bf16[1024,2048]{1,0:T(8,128)(2,1)}, u32[]{:S(2)}, u32[]{:S(2)}) collective-permute-start(bf16[1024,2048]{1,0:T(8,128)(2,1)} %constant_dynamic-update-slice_fusion.36.xa_ref), channel_id=1, source_target_pairs={{0,4},{4,0},{8,12},{12,8},{16,20},{20,16},{24,28},{28,24},{1,5},{5... | collective-permute-start | bytes 12582920 | tf_op jit(solution)/shard_map/ppermute | solution.py:42
  618.9 163.8 %collective-permute-start.36 = (bf16[1024,2048]{1,0:T(8,128)(2,1)}, bf16[1024,2048]{1,0:T(8,128)(2,1)}, u32[]{:S(2)}, u32[]{:S(2)}) collective-permute-start(bf16[1024,2048]{1,0:T(8,128)(2,1)} %get-tuple-element.86), channel_id=1, source_target_pairs={{0,4},{4,0},{8,12},{12,8},{16,20},{20,16},{24,28},{28,24},{1,5},{5... | collective-permute-start | bytes 12582920 | tf_op jit(solution)/shard_map/ppermute | solution.py:42
  681.7 94.0 %all-to-all-start.2 = ((f32[8,1,1024]{2,1,0:T(1,128)}), f32[8,1,1024]{2,1,0:T(1,128)S(1)}, u32[]{:S(2)}, u32[]{:S(2)}) async-start(f32[8,1,1024]{2,1,0:T(1,128)} %copy.345), calls=%async_computation.2 | async-start | bytes 65536 | tf_op jit(solution)/shard_map/all_to_all | solution.py:710
  685.2 460.7 %reduce-scatter.9.cloned.1.call-start = ((), (), s32[]{:S(2)}) async-start(), calls=%async_computation.7 | async-start | bytes 163840
  685.2 226.7 %collective-permute-start.69 = (bf16[1024,2048]{1,0:T(8,128)(2,1)}, bf16[1024,2048]{1,0:T(8,128)(2,1)}, u32[]{:S(2)}, u32[]{:S(2)}) collective-permute-start(bf16[1024,2048]{1,0:T(8,128)(2,1)} %get-tuple-element.104), channel_id=1, source_target_pairs={{0,4},{4,0},{8,12},{12,8},{16,20},{20,16},{24,28},{28,24},{1,5},{5... | collective-permute-start | bytes 12582920 | tf_op jit(solution)/shard_map/ppermute | solution.py:42
  685.7 90.3 %collective-permute-start.53 = (bf16[1024,2048]{1,0:T(8,128)(2,1)}, bf16[1024,2048]{1,0:T(8,128)(2,1)}, u32[]{:S(2)}, u32[]{:S(2)}) collective-permute-start(bf16[1024,2048]{1,0:T(8,128)(2,1)} %get-tuple-element.96), channel_id=1, source_target_pairs={{0,4},{4,0},{8,12},{12,8},{16,20},{20,16},{24,28},{28,24},{1,5},{5... | collective-permute-start | bytes 12582920 | tf_op jit(solution)/shard_map/ppermute | solution.py:42
  838.0 163.4 %collective-permute-start.96 = (bf16[2,256,2048]{2,1,0:T(8,128)(2,1)}, bf16[2,256,2048]{2,1,0:T(8,128)(2,1)}, u32[]{:S(2)}, u32[]{:S(2)}) collective-permute-start(bf16[2,256,2048]{2,1,0:T(8,128)(2,1)} %fusion.43), channel_id=1, source_target_pairs={{0,1},{1,0},{2,3},{3,2},{4,5},{5,4},{6,7},{7,6},{8,9},{9,8},{10,11... | collective-permute-start | bytes 6291464 | tf_op jit(solution)/shard_map/ppermute | solution.py:42
  931.5 136.2 %collective-permute-start.64 = (bf16[1024,2048]{1,0:T(8,128)(2,1)}, bf16[1024,2048]{1,0:T(8,128)(2,1)}, u32[]{:S(2)}, u32[]{:S(2)}) collective-permute-start(bf16[1024,2048]{1,0:T(8,128)(2,1)} %get-tuple-element.101), channel_id=1, source_target_pairs={{0,4},{4,0},{8,12},{12,8},{16,20},{20,16},{24,28},{28,24},{1,5},{5... | collective-permute-start | bytes 12582920 | tf_op jit(solution)/shard_map/ppermute | solution.py:42
  951.0 122.0 %collective-permute-start.75 = (bf16[1024,2048]{1,0:T(8,128)(2,1)S(1)}, bf16[1024,2048]{1,0:T(8,128)(2,1)S(1)}, u32[]{:S(2)}, u32[]{:S(2)}) collective-permute-start(bf16[1024,2048]{1,0:T(8,128)(2,1)S(1)} %copy-done.99), channel_id=1, source_target_pairs={{0,4},{4,0},{8,12},{12,8},{16,20},{20,16},{24,28},{28,24},{1,5},{5... | collective-permute-start | bytes 12582920 | tf_op jit(solution)/shard_map/ppermute | solution.py:42
  951.0 48.9 %collective-permute-start.92 = (bf16[2,512,512]{1,2,0:T(8,128)(2,1)S(1)}, bf16[2,512,512]{1,2,0:T(8,128)(2,1)S(1)}, u32[]{:S(2)}, u32[]{:S(2)}) collective-permute-start(bf16[2,512,512]{1,2,0:T(8,128)(2,1)S(1)} %fusion.52), channel_id=1, source_target_pairs={{0,2},{1,3},{2,0},{3,1},{4,6},{5,7},{6,4},{7,5},{8,10},{9,11},{10,... | collective-permute-start | bytes 3145736 | tf_op jit(solution)/shard_map/ppermute | solution.py:42
  954.1 54.2 %collective-permute-start.73 = (bf16[256,2048]{1,0:T(8,128)(2,1)S(1)}, bf16[256,2048]{1,0:T(8,128)(2,1)S(1)}, u32[]{:S(2)}, u32[]{:S(2)}) collective-permute-start(bf16[256,2048]{1,0:T(8,128)(2,1)S(1)} %pad_maximum_fusion.20), channel_id=1, source_target_pairs={{0,8},{4,12},{8,0},{12,4},{16,24},{20,28},{24,16},{28,20},{1,9},{5... | collective-permute-start | bytes 3145736 | tf_op jit(solution)/shard_map/ppermute | solution.py:42
  1029.4 289.8 %collective-permute-start.74 = (bf16[256,2048]{1,0:T(8,128)(2,1)}, bf16[256,2048]{1,0:T(8,128)(2,1)}, u32[]{:S(2)}, u32[]{:S(2)}) collective-permute-start(bf16[256,2048]{1,0:T(8,128)(2,1)} %pad_maximum_fusion.21), channel_id=1, source_target_pairs={{0,2},{1,3},{2,0},{3,1},{4,6},{5,7},{6,4},{7,5},{8,10},{9,11},{10,... | collective-permute-start | bytes 3145736 | tf_op jit(solution)/shard_map/ppermute | solution.py:42
  1067.1 140.8 %collective-permute-start.95 = (bf16[2,512,512]{1,2,0:T(8,128)(2,1)}, bf16[2,512,512]{1,2,0:T(8,128)(2,1)}, u32[]{:S(2)}, u32[]{:S(2)}) collective-permute-start(bf16[2,512,512]{1,2,0:T(8,128)(2,1)} %fusion.51), channel_id=1, source_target_pairs={{0,2},{1,3},{2,0},{3,1},{4,6},{5,7},{6,4},{7,5},{8,10},{9,11},{10,... | collective-permute-start | bytes 3145736 | tf_op jit(solution)/shard_map/ppermute | solution.py:42
  1071.0 103.6 %collective-permute-start.67 = (bf16[128,2048]{1,0:T(8,128)(2,1)}, bf16[128,2048]{1,0:T(8,128)(2,1)}, u32[]{:S(2)}, u32[]{:S(2)}) collective-permute-start(bf16[128,2048]{1,0:T(8,128)(2,1)} %get-tuple-element.244), channel_id=1, source_target_pairs={{0,16},{4,20},{8,24},{12,28},{16,0},{20,4},{24,8},{28,12},{1,17},{... | collective-permute-start | bytes 1572872 | tf_op jit(solution)/shard_map/ppermute | solution.py:42
  1071.9 102.8 %collective-permute-start.65 = (bf16[128,2048]{1,0:T(8,128)(2,1)}, bf16[128,2048]{1,0:T(8,128)(2,1)}, u32[]{:S(2)}, u32[]{:S(2)}) collective-permute-start(bf16[128,2048]{1,0:T(8,128)(2,1)} %get-tuple-element.245), channel_id=1, source_target_pairs={{0,8},{4,12},{8,0},{12,4},{16,24},{20,28},{24,16},{28,20},{1,9},{5... | collective-permute-start | bytes 1572872 | tf_op jit(solution)/shard_map/ppermute | solution.py:42
  1168.1 65.5 %collective-permute-start.79 = (bf16[1024,2048]{1,0:T(8,128)(2,1)}, bf16[1024,2048]{1,0:T(8,128)(2,1)}, u32[]{:S(2)}, u32[]{:S(2)}) collective-permute-start(bf16[1024,2048]{1,0:T(8,128)(2,1)} %convolution_convert_fusion), channel_id=1, source_target_pairs={{0,4},{4,0},{8,12},{12,8},{16,20},{20,16},{24,28},{28,24},{1,5},{5... | collective-permute-start | bytes 12582920 | tf_op jit(solution)/shard_map/ppermute | solution.py:42
  1200.7 80.8 %collective-permute-start.68 = (bf16[256,2048]{1,0:T(8,128)(2,1)}, bf16[256,2048]{1,0:T(8,128)(2,1)}, u32[]{:S(2)}, u32[]{:S(2)}) collective-permute-start(bf16[256,2048]{1,0:T(8,128)(2,1)} %pad_maximum_fusion.18), channel_id=1, source_target_pairs={{0,8},{4,12},{8,0},{12,4},{16,24},{20,28},{24,16},{28,20},{1,9},{5... | collective-permute-start | bytes 3145736 | tf_op jit(solution)/shard_map/ppermute | solution.py:42
  1262.9 189.6 %reduce-scatter.7.cloned.1.call-start = ((), (), s32[]{:S(2)}) async-start(), calls=%async_computation.6 | async-start | bytes 1081344
  (213 other events, 4535.7 us)
Sparse Core Ops, SparseCore 0:
  1127.2 18.5 reduce-scatter.8
Sparse Core Ops, SparseCore 1:
  1319.2 133.1 reduce-scatter.6

commit v3 on v2

--- a/solution.py
+++ b/solution.py
@@ -85,8 +85,7 @@
     return jnp.concatenate([lax.dynamic_slice_in_dim(blocks, at, 1, 0) for at in places], 0)
 
 
-def scatter_sum(even, odd, size):
-    got = swap(odd, "seq", size, 1)
+def scatter_sum(even, got, size):
     rows = even.shape[0] // (size // 2)
     half = rows // 2
 
@@ -132,59 +131,49 @@
     return whole
 
 
-def near_swaps(pieces, base, size, dep):
+def near_swaps(pieces, base, size):
     for r in range(1, size // 2):
         up = high_bit(r)
-        pieces[base + r] = swap(after(pieces[base + (r ^ up)], dep), "fsdp", size, up)
-        dep = pieces[base + r]
-    return dep
-
-
-def place_swapped(pieces, me, experts_first):
-    size = len(pieces)
-    experts, part, columns = pieces[0].shape
-    whole = jnp.zeros((experts, size, part, columns), pieces[0].dtype)
-    for r in range(size):
-        at = (me ^ r) % size
-        whole = lax.dynamic_update_slice_in_dim(whole, pieces[r][:, None], at, 1)
-    return whole.reshape(experts, size * part, columns)
-
-
-def scatter_expert_cols(partial_sum, me, size, dep):
-    experts, depth, hidden_half = partial_sum.shape
-    half = size // 2
-    parts = partial_sum.reshape(experts, size, depth // size, hidden_half)
-    sums = {
-        r: lax.dynamic_index_in_dim(parts, me ^ r, 1, keepdims=False).astype(F32)
-        for r in range(size)
-    }
-    for r in range(half - 1, 0, -1):
-        up = high_bit(r)
-        for base in (half, 0):
-            got = swap(after(sums[r | base].astype(BF16), dep), "fsdp", size, up)
-            sums[(r ^ up) | base] += got.astype(F32)
-            dep = got
-    got = swap(after(sums[half].astype(BF16), dep), "fsdp", size, half)
-    dep, got = got, got.astype(F32)
-    first = me // half == 0
-    return jnp.concatenate(
-        [jnp.where(first, sums[0], got), jnp.where(first, got, sums[0])], axis=-1
-    ), dep
-
-
-def scatter_expert_rows(partial_sum, me, size, dep):
-    experts, hidden_half, columns = partial_sum.shape
-    half = size // 2
-    parts = partial_sum.reshape(experts, half, hidden_half // half, columns)
-    sums = {
-        r: lax.dynamic_index_in_dim(parts, (me ^ r) % half, 1, keepdims=False).astype(F32)
-        for r in range(half)
-    }
-    for r in range(half - 1, 0, -1):
-        up = high_bit(r)
-        dep = swap(after(sums[r].astype(BF16), dep), "fsdp", size, up)
-        sums[r ^ up] += dep.astype(F32)
-    return sums[0], dep
+        pieces[base + r] = swap(pieces[base + (r ^ up)], "fsdp", size, up)
+
+
+def gather_small(values, seq_size, fsdp_size, s, f):
+    count = seq_size * fsdp_size
+    whole = values[None]
+    for axis, size in (("seq", seq_size), ("fsdp", fsdp_size)):
+        mask = 1
+        while mask < size:
+            whole = jnp.concatenate([whole, swap(whole, axis, size, mask)], 0)
+            mask *= 2
+    index = jnp.arange(count, dtype=jnp.int32)
+    source = ((index % fsdp_size) ^ f) * seq_size + ((index // fsdp_size) ^ s)
+    pick = (source[:, None] == index[None, :]).astype(values.dtype)
+    return matmul(pick, whole).astype(values.dtype)
+
+
+def sum_near(send, keep, size, dep):
+    got = after(swap(send, "fsdp", size, 1), dep)
+    sums = {2 * k: keep[k].astype(F32) + got[k].astype(F32) for k in range(size // 2)}
+    mask = 2
+    while mask < size // 2:
+        stay = [r for r in sums if not r & mask]
+        moved = jnp.stack([sums[r | mask].astype(BF16) for r in stay], 0)
+        got = swap(moved, "fsdp", size, mask)
+        sums = {r: sums[r] + got[i].astype(F32) for i, r in enumerate(stay)}
+        mask *= 2
+    return sums
+
+
+def scatter_down(terms, half, size, dep):
+    sums = {r: terms[r].astype(F32) for r in range(half)}
+    mask = 1
+    while mask < half:
+        stay = [r for r in sums if not r & mask]
+        moved = terms[1::2] if mask == 1 else jnp.stack([sums[r | mask].astype(BF16) for r in stay])
+        got = after(swap(moved, "fsdp", size, mask), dep)
+        sums = {r: sums[r] + got[i].astype(F32) for i, r in enumerate(stay)}
+        mask *= 2
+    return sums[0]
 
 
 def scatter_rows(partial_sum, me, size):
@@ -429,23 +418,30 @@
     )(me, even, odd, weight, gain)
 
 
-def expert_kernel(
-    first_ref,
-    xa_ref,
-    xb_ref,
-    ua_ref,
-    ub_ref,
-    ra_ref,
-    rb_ref,
-    wg_ref,
-    wu_ref,
-    wd_ref,
-    router_ref,
-    *refs,
-):
-    ya_ref, yb_ref, za_ref, zb_ref, ga_ref, gb_ref, xc_ref, uc_ref, dg_ref, du_ref, hid_ref = refs[-11:]
-    experts = wg_ref.shape[0]
+def expert_kernel(pieces, first_ref, xa_ref, xb_ref, ua_ref, ub_ref, ra_ref, rb_ref, router_ref, *refs):
+    weight_refs = refs[: sum(pieces)]
+    (ya_ref, yb_ref, za_ref, zb_ref, ga_ref, gb_ref, xc_ref, uc_ref, dg_ref, hid_ref) = refs[-13:-3]
+    wi_ref, wd_ref, sems = refs[-3:]
+    experts, _, hidden = hid_ref.shape
     rows = xa_ref.shape[0]
+
+    @pl.when(pl.program_id(0) == 0)
+    def _():
+        copies = []
+        for r, ref in enumerate(weight_refs[: pieces[0]]):
+            part = ref.shape[1]
+            at = pl.ds(pl.multiple_of((first_ref[1] ^ r) * part, part), part)
+            copies.append(pltpu.make_async_copy(ref, wi_ref.at[:, at, :], sems.at[r]))
+        for r, ref in enumerate(weight_refs[pieces[0] :]):
+            part = ref.shape[1]
+            place = lax.rem(first_ref[1] ^ r, pieces[1])
+            at = pl.ds(pl.multiple_of(place * part, part), part)
+            copies.append(pltpu.make_async_copy(ref, wd_ref.at[:, at, :], sems.at[pieces[0] + r]))
+        for copy in copies:
+            copy.start()
+        for copy in copies:
+            copy.wait()
+
     slot = lax.broadcasted_iota(jnp.int32, (CAP, rows), 0)
     blocks = (
         (xa_ref, ua_ref, ra_ref, ya_ref, za_ref, ga_ref),
@@ -470,24 +466,20 @@
         expos = jnp.exp(logits - jnp.max(logits, axis=-1, keepdims=True))
         own = jnp.sum(jnp.where(lane == first_ref[0] + e, expos, 0.0), axis=-1, keepdims=True)
         gate = own / jnp.sum(expos, axis=-1, keepdims=True)
-        gated = matmul(x_rows, wg_ref[e])
-        upward = matmul(x_rows, wu_ref[e])
+        gated = matmul(x_rows, wi_ref[e, :, :hidden])
+        upward = matmul(x_rows, wi_ref[e, :, hidden:])
         pulled = matmul_t(u_rows, wd_ref[e])
         sig = jax.nn.sigmoid(gated)
         silu = gated * sig
-        hidden = silu * upward
-        gate_grads.append(jnp.sum(hidden * pulled, axis=-1, keepdims=True))
-        hidden_gate = (hidden * gate).astype(BF16)
+        acts = silu * upward
+        gate_grads.append(jnp.sum(acts * pulled, axis=-1, keepdims=True))
+        hidden_gate = (acts * gate).astype(BF16)
         hidden_grads = pulled * gate
-        gated_low = (hidden_grads * upward * sig * (1.0 + gated * (1.0 - sig))).astype(BF16)
-        upward_low = (hidden_grads * silu).astype(BF16)
         hid_ref[e] = hidden_gate
-        dg_ref[e] = gated_low
-        du_ref[e] = upward_low
+        dg_ref[e, :, :hidden] = (hidden_grads * upward * sig * (1.0 + gated * (1.0 - sig))).astype(BF16)
+        dg_ref[e, :, hidden:] = (hidden_grads * silu).astype(BF16)
         outs.append(matmul(hidden_gate, wd_ref[e]).astype(BF16))
-        backs.append(
-            (matmul_t(gated_low, wg_ref[e]) + matmul_t(upward_low, wu_ref[e])).astype(BF16)
-        )
+        backs.append(matmul_t(dg_ref[e], wi_ref[e]).astype(BF16))
     for k, (_, _, rank_ref, y_ref, z_ref, g_ref) in enumerate(blocks):
         at = slice(k * CAP, (k + 1) * CAP)
         y_ref[...] = t_matmul(picks[k], jnp.concatenate([v[at] for v in outs], 0)).astype(BF16)
@@ -499,17 +491,15 @@
             )
 
 
-def run_experts(x, u, ranks, weights, router, first, which, compact):
-    experts, depth, hidden = weights[0].shape
+def run_experts(x, u, ranks, in_pieces, down_pieces, router, places, which, compact):
+    experts, part, hidden = in_pieces[0].shape
+    hidden //= 2
+    depth = part * len(in_pieces)
     rows = ranks[0].shape[2]
     steps = x[0].shape[0] // rows
     token = pl.BlockSpec((rows, depth), lambda i: (i, 0))
     rank = pl.BlockSpec((1, experts, rows), lambda i: (i, 0, 0))
-
-    def whole(array):
-        return pl.BlockSpec(
-            array.shape, lambda i: (0,) * array.ndim, pipeline_mode=pl.Buffered(1)
-        )
+    anywhere = pl.BlockSpec(memory_space=pl.ANY)
 
     def slots(columns):
         return pl.BlockSpec((experts, 2 * CAP, columns), lambda i: (0, i + which * steps, 0))
@@ -519,28 +509,70 @@
     gates = shape((steps, experts, rows), F32)
     count = 4 * steps * CAP
     wide = shape((experts, count, depth), BF16)
-    narrow = shape((experts, count, hidden), BF16)
-    inputs = [first, *x, *u, *ranks, *weights, router]
+    pieces = (len(in_pieces), len(down_pieces))
+    inputs = [places, *x, *u, *ranks, router, *in_pieces, *down_pieces]
     return pl.pallas_call(
-        expert_kernel,
+        partial(expert_kernel, pieces),
         grid=(steps,),
         in_specs=[pl.BlockSpec(memory_space=pltpu.SMEM)]
         + [token] * 4
         + [rank] * 2
-        + [whole(w) for w in weights]
-        + [whole(router)]
-        + [pl.BlockSpec(memory_space=pl.ANY)] * len(compact),
-        out_specs=[token] * 4 + [rank] * 2 + [slots(depth)] * 2 + [slots(hidden)] * 3,
-        out_shape=[tokens] * 4 + [gates] * 2 + [wide] * 2 + [narrow] * 3,
+        + [pl.BlockSpec(router.shape, lambda i: (0, 0), pipeline_mode=pl.Buffered(1))]
+        + [anywhere] * (sum(pieces) + len(compact)),
+        out_specs=[token] * 4 + [rank] * 2 + [slots(depth)] * 2 + [slots(2 * hidden), slots(hidden)],
+        out_shape=[tokens] * 4
+        + [gates] * 2
+        + [wide] * 2
+        + [shape((experts, count, 2 * hidden), BF16), shape((experts, count, hidden), BF16)],
+        scratch_shapes=[
+            pltpu.VMEM((experts, depth, 2 * hidden), BF16),
+            pltpu.VMEM((experts, hidden, depth), BF16),
+            pltpu.SemaphoreType.DMA((sum(pieces),)),
+        ],
         input_output_aliases={len(inputs) + i: 6 + i for i in range(len(compact))},
         compiler_params=pltpu.CompilerParams(vmem_limit_bytes=60 * MIB),
         cost_estimate=pl.CostEstimate(
             flops=4 * steps * CAP * experts * depth * (7 * hidden + 2 * rows),
-            bytes_accessed=40 * MIB,
+            bytes_accessed=60 * MIB,
             transcendentals=2 * steps * CAP * experts * hidden,
         ),
         name="experts",
     )(*inputs, *compact)
+
+
+def product_kernel(me_ref, left_ref, right_ref, out_ref):
+    out_ref[0, 0] = t_matmul(left_ref[0], right_ref[0]).astype(BF16)
+
+
+def products(left, right, part, chosen, count, me, name):
+    experts, rows, _ = left.shape
+    columns = right.shape[2]
+    wide = min(columns, 1024)
+    start, step = chosen[0], chosen[1] - chosen[0] if len(chosen) > 1 else 1
+
+    def place(e, k, j, me):
+        return (e, 0, lax.rem(me[0] ^ (start + step * k), count))
+
+    return pl.pallas_call(
+        product_kernel,
+        grid_spec=pltpu.PrefetchScalarGridSpec(
+            num_scalar_prefetch=1,
+            grid=(experts, len(chosen), columns // wide),
+            in_specs=[
+                pl.BlockSpec((1, rows, part), place),
+                pl.BlockSpec((1, rows, wide), lambda e, k, j, me: (e, 0, j)),
+            ],
+            out_specs=pl.BlockSpec((1, 1, part, wide), lambda e, k, j, me: (k, e, 0, j)),
+        ),
+        out_shape=jax.ShapeDtypeStruct((len(chosen), experts, part, columns), BF16),
+        compiler_params=pltpu.CompilerParams(vmem_limit_bytes=56 * MIB),
+        cost_estimate=pl.CostEstimate(
+            flops=2 * len(chosen) * experts * rows * part * columns,
+            bytes_accessed=2 * experts * rows * (part * len(chosen) + columns),
+            transcendentals=0,
+        ),
+        name=name,
+    )(me, left, right)
 
 
 def rotate(values, cosine, sine, heads):
@@ -596,8 +628,8 @@
             routes[0].astype(BF16).reshape(-1),
         ]
     )
-    small = lax.all_gather(small, ("seq", "fsdp"), axis=0, tiled=False).reshape(S, F, -1)
     tokens_even, tokens_odd = gather_seq(tokens_low, S)
+    small = gather_small(small, S, F, s, f).reshape(S, F, -1)
 
     stacked = jnp.stack([w_query, w_key, w_value], 1).reshape(part, 3, S, C)
     stacked = stacked.transpose(2, 0, 1, 3).reshape(S, part, 3 * C)
@@ -625,30 +657,22 @@
         ranks = jnp.where(chosen, ranks, -1)
         return ranks[: S // 2], ranks[S // 2 :]
 
-    def split_hidden(weight):
-        mine = lax.dynamic_slice_in_dim(weight, (f // half_f) * hidden_half, hidden_half, 2)
-        other = lax.dynamic_slice_in_dim(weight, (1 - f // half_f) * hidden_half, hidden_half, 2)
-        return mine, other
-
-    gate_pieces, up_pieces, down_pieces = {}, {}, {0: w_down}
-    gate_pieces[0], gate_other = split_hidden(w_gate)
-    up_pieces[0], up_other = split_hidden(w_up)
-    gate_pieces[half_f] = swap(after(gate_other, qkv_ring[-2]), "fsdp", F, half_f)
-    up_pieces[half_f] = swap(after(up_other, gate_pieces[half_f]), "fsdp", F, half_f)
+    half_at = f // half_f
+
+    def hidden_part(which):
+        at = which * hidden_half
+        return jnp.concatenate(
+            [lax.dynamic_slice_in_dim(weight, at, hidden_half, 2) for weight in (w_gate, w_up)], 2
+        )
+
+    in_pieces = {0: hidden_part(half_at)}
+    far_part = swap(after(hidden_part(1 - half_at), qkv_ring[-2]), "fsdp", F, half_f)
+    in_pieces[0] = after(in_pieces[0], qkv_ring[-1])
+    near_swaps(in_pieces, 0, F)
+
     upstream_low = cotangent[0]
-    partner_up = swap(after(upstream_low, up_pieces[half_f]), "fsdp", F, half_f)
-    dep = near_swaps(gate_pieces, 0, F, qkv_ring[-1])
-    dep = near_swaps(up_pieces, 0, F, dep)
-    dep = near_swaps(gate_pieces, half_f, F, dep)
-    dep = near_swaps(up_pieces, half_f, F, dep)
-    dep = near_swaps(down_pieces, 0, F, dep)
-    own_gate = place_swapped(gate_pieces, f, experts)
-    own_up = place_swapped(up_pieces, f, experts)
-    own_down = place_swapped(down_pieces, f, experts)
-
-    own_up_even, own_up_odd = gather_seq(after(upstream_low, tokens_even), S)
-    out_even, out_odd = gather_seq(after(own_output, own_up_even), S)
-    other_up_even, other_up_odd = gather_seq(after(partner_up, out_even), S)
+    own_u = gather_seq(after(upstream_low, tokens_even), S)
+    out_even, out_odd = gather_seq(after(own_output, own_u[0]), S)
 
     me = s.reshape(1).astype(jnp.int32)
     normed_all, query_pre, key_pre, value_low, squares = project(
@@ -667,6 +691,8 @@
     seg_col = segments.reshape(L, 1)
     attended, lse = attention_forward(query_low, key_low, value_low, seg_row, seg_col)
     attended_blocks = attended.reshape(S, T, C)
+    in_pieces[half_f] = after(far_part, attended)
+    near_swaps(in_pieces, half_f, F)
     come = lax.all_to_all(attended_blocks, "seq", split_axis=0, concat_axis=0, tiled=True)
     come = relative(come, s).transpose(1, 0, 2).reshape(T, D)
     residual = inputs + matmul(come[:, : D // 2], out_even) + matmul(come[:, D // 2 :], out_odd)
@@ -676,28 +702,36 @@
     second_low = (residual_n * gain_moe).astype(BF16)
     partner_low = swap(second_low, "fsdp", F, half_f)
     own_x = gather_seq(second_low, S)
+    down_pieces = {0: after(w_down, own_x[0])}
+    near_swaps(down_pieces, 0, F)
     other_x = gather_seq(after(partner_low, own_x[0]), S)
+    partner_up = swap(after(upstream_low, partner_low), "fsdp", F, half_f)
+    other_u = gather_seq(after(partner_up, other_x[0]), S)
     logits = matmul(second_low, full_router)
     router_probs = jax.nn.softmax(logits, axis=-1)
-    expert_weights = (own_gate, own_up, own_down)
+    in_pieces = [in_pieces[r] for r in range(F)]
+    down_pieces = [down_pieces[r] for r in range(half_f)]
     wide_router = jnp.pad(full_router, ((0, 0), (0, 128 - E)))
-    first = (s * experts).reshape(1).astype(jnp.int32)
+    expert_places = jnp.stack([s * experts, f]).astype(jnp.int32)
     own_parts = run_experts(
-        own_x, (own_up_even, own_up_odd), ranks_of(f), expert_weights, wide_router, first, 0, ()
+        own_x, own_u, ranks_of(f), in_pieces, down_pieces, wide_router, expert_places, 0, ()
     )
     other_parts = run_experts(
         other_x,
-        (other_up_even, other_up_odd),
+        other_u,
         ranks_of(f ^ half_f),
-        expert_weights,
+        in_pieces,
+        down_pieces,
         wide_router,
-        first,
+        expert_places,
         1,
         own_parts[6:],
     )
-    x_rows, u_rows, gated_low, upward_low, hidden_gate = other_parts[6:]
-    own_rows = scatter_sum(own_parts[2], own_parts[3], S)
-    other_rows = scatter_sum(other_parts[2], other_parts[3], S).astype(BF16)
+    x_rows, u_rows, in_grads, hidden_gate = other_parts[6:]
+    own_got = swap(own_parts[3], "seq", S, 1)
+    other_got = swap(other_parts[3], "seq", S, 1)
+    other_rows = scatter_sum(other_parts[2], other_got, S).astype(BF16)
+    own_rows = scatter_sum(own_parts[2], after(own_got, other_rows), S)
     back_rows = swap(other_rows, "fsdp", F, half_f)
     row_grads = own_rows + back_rows.astype(F32)
 
@@ -713,12 +747,16 @@
     gate_grads = gate_grads[:, 0] + swap(gate_grads[:, 1], "fsdp", F, half_f)
     gate_grads = gate_grads.reshape(S, T, experts).transpose(1, 0, 2).reshape(T, E)
 
-    down_term = jnp.stack([t_matmul(hidden_gate[e], u_rows[e]) for e in range(experts)], 0)
-    gate_term = jnp.stack([t_matmul(x_rows[e], gated_low[e]) for e in range(experts)], 0)
-    up_term = jnp.stack([t_matmul(x_rows[e], upward_low[e]) for e in range(experts)], 0)
-    grad_down, dep = scatter_expert_rows(down_term.astype(BF16), f, F, own_rows)
-    grad_gate, dep = scatter_expert_cols(gate_term.astype(BF16), f, F, back_rows)
-    grad_up, dep = scatter_expert_cols(up_term.astype(BF16), f, F, dep)
+    f_at = f.reshape(1).astype(jnp.int32)
+    down_part = w_down.shape[1]
+    in_part = w_gate.shape[1]
+    hidden_gate = after(hidden_gate, other_got)
+    down_terms = products(
+        hidden_gate, u_rows, down_part, range(half_f), half_f, f_at, "down_products"
+    )
+    in_grads = after(in_grads, other_rows)
+    in_send = products(x_rows, in_grads, in_part, range(1, F, 2), F, f_at, "in_products_sent")
+    in_keep = products(x_rows, in_grads, in_part, range(0, F, 2), F, f_at, "in_products_kept")
 
     upstream = upstream_low.astype(F32)
     logit_grads = router_probs * (
@@ -740,12 +778,25 @@
     ).astype(BF16)
     head_grads = absolute(head_grads.reshape(S, T, C), s).reshape(L, C)
     attended_rel = relative(attended_blocks, s).reshape(2, L // 2, C)
-    output_term = t_matmul(attended_rel[0], branch_even) + t_matmul(attended_rel[1], branch_odd)
     query_back, key_back, value_back = attention_backward(
         query_low, key_low, value_low, head_grads, lse, seg_row, seg_col
     )
-    own_outs = scatter_sum(own_parts[0], after(own_parts[1], branch_even), S)
-    other_outs = scatter_sum(other_parts[0], after(other_parts[1], own_outs), S).astype(BF16)
+    attended_rel = after(attended_rel, query_back)
+    output_term = t_matmul(attended_rel[0], branch_even) + t_matmul(attended_rel[1], branch_odd)
+    own_out_got = after(swap(after(own_parts[1], branch_even), "seq", S, 1), query_back)
+    other_out_got = after(swap(after(other_parts[1], own_out_got), "seq", S, 1), query_back)
+    other_outs = scatter_sum(other_parts[0], other_out_got, S).astype(BF16)
+    own_outs = scatter_sum(own_parts[0], after(own_out_got, other_outs), S)
+    down_sums = scatter_down(down_terms, half_f, F, query_back)
+    in_sums = sum_near(in_send, in_keep, F, query_back)
+    far_sums = swap(in_sums[half_f].astype(BF16), "fsdp", F, half_f).astype(F32)
+    first_half = half_at == 0
+    lower = jnp.where(first_half, in_sums[0], far_sums)
+    upper = jnp.where(first_half, far_sums, in_sums[0])
+    grad_gate, grad_up = (
+        jnp.concatenate([lower[..., at], upper[..., at]], axis=-1)
+        for at in (slice(0, hidden_half), slice(hidden_half, 2 * hidden_half))
+    )
     other_outs = swap(other_outs, "fsdp", F, half_f).astype(F32)
     mixed = (residual + own_outs + other_outs).astype(BF16)[None]
     query_turned = rotate(query_back.astype(F32), cosine, -sine, heads)
@@ -760,9 +811,8 @@
     key_pre_low = (factors[1][:, None] * (key_pulled - key_n * means[1][:, None])).astype(BF16)
     pre_low = jnp.concatenate([query_pre_low, key_pre_low, value_back], 1)
     pre_rel = relative(pre_low.reshape(S, T, 3 * C), s).reshape(2, L // 2, 3 * C)
-    normed_grads = scatter_sum(
-        matmul_t(pre_rel[0], w_qkv).astype(BF16), matmul_t(pre_rel[1], w_qkv).astype(BF16), S
-    )
+    normed_got = swap(matmul_t(pre_rel[1], w_qkv).astype(BF16), "seq", S, 1)
+    normed_grads = scatter_sum(matmul_t(pre_rel[0], w_qkv).astype(BF16), normed_got, S)
 
     def weight_sum(grads):
         term = t_matmul(normed_all, grads).astype(BF16)
@@ -780,13 +830,14 @@
     )
     attn_factor = rms_factor(inputs)
     inputs_n = inputs * attn_factor
-    attn_gain_term = jnp.sum(normed_grads * inputs_n, axis=0)
     attn_pulled = normed_grads * gain_attn
     grad_tokens = residual_grads + attn_factor * (
         attn_pulled - inputs_n * jnp.mean(attn_pulled * inputs_n, axis=-1, keepdims=True)
     )
-    gain_terms = jnp.concatenate([router_term, moe_gain_term[:, None], attn_gain_term[:, None]], 1)
+    gain_terms = jnp.concatenate([router_term, moe_gain_term[:, None]], 1)
     gain_terms = lax.psum_scatter(gain_terms, ("seq", "fsdp"), scatter_dimension=0, tiled=True)
+    own_weights = jnp.stack([w_query, w_key, w_value], 0).astype(F32)
+    grad_attn_gain = jnp.sum(qkv_term * own_weights, axis=(0, 2)) / attn_gain.astype(F32)
     return (
         mixed,
         grad_tokens[None],
@@ -795,13 +846,13 @@
         qkv_term[2],
         grad_output,
         gain_terms[:, :E],
-        gain_terms[:, E + 1],
+        grad_attn_gain,
         gain_terms[:, E],
         head_gains[:, 0],
         head_gains[:, 1],
         grad_gate,
         grad_up,
-        grad_down,
+        down_sums,
     )
 
 

time: 1480 us -> 1510 us (1.020)
  waiting for transfers between devices: 644 us -> 807 us
  blocking collectives: 71.3 us -> 0 us
  Pallas kernels: 179 us -> 233 us
  matrix products: 94.4 us -> 47.5 us
  local copies, waits for them, and re-layouts: 200 us -> 163 us
    ppermute x91 -> x89, waiting for transfers between devices: 492 us -> 595 us  [swap(): return lax.ppermute(values, axis, [(i, i ^ mask) for i in range(size)])]
    all_gather x1 -> x0, blocking collectives: 71.3 us -> none  [per_device(): lax.all_gather(small, ('seq', 'fsdp'), axis=0, tiled=False)]
    pallas_call x2 -> x5, Pallas kernels: 116 us -> 171 us  [the longest x2 120 us: run_experts(): pl.pallas_call(partial(expert_kernel, pieces), grid=(steps,), in_specs=[p...]
    unnamed x4, waiting for transfers between devices: 133 us -> 183 us
    dot_general x10 -> x4, matrix products: 66.1 us -> 16.2 us  [t_matmul(): lax.dot_general(left, right, (((0,), (0,)), ((), ())), preferred_element_...]
    another operation x12 -> x9, local copies, waits for them, and re-layouts: 36 us -> 5.73 us  [the longest x3 5.53 us: per_device(): own_weights = jnp.stack([w_query, w_key, w_value], 0).astype(F32)]
    dot_general x2 -> x0, local copies, waits for them, and re-layouts: 21.3 us -> none  [t_matmul(): lax.dot_general(left, right, (((0,), (0,)), ((), ())), preferred_element_...]
    ppermute x91 -> x89, starting transfers between devices: 90.3 us -> 80.3 us  [swap(): return lax.ppermute(values, axis, [(i, i ^ mask) for i in range(size)])]
  transfers between devices with their start and end apart: 103 -> 101, of which waited for: 44 -> 60; matrix products, arithmetic and copies ran while one was open for 29% -> 21% of each run, Pallas kernels for 12% -> 11%
where the time goes in v3:
time: 1510 us; the launch traced here: 1500 us
  waiting for transfers between devices  807 us (53%)
  Pallas kernels  233 us (15%)
  local copies, waits for them, and re-layouts  163 us (11%)
  other arithmetic  132 us (9%)
  starting transfers between devices  101 us (7%)
  matrix products  47.5 us (3%)
  between operations  18.5 us (1%)
    ppermute x89, waiting for transfers between devices, swap(): return lax.ppermute(values, axis, [(i, i ^ mask) for i in range(size)])  595 us
    unnamed x4, waiting for transfers between devices  183 us
    pallas_call x2, Pallas kernels, run_experts(): pl.pallas_call(partial(expert_kernel, pieces), grid=(steps,), in_specs=[p...  120 us
    ppermute x89, starting transfers between devices, swap(): return lax.ppermute(values, axis, [(i, i ^ mask) for i in range(size)])  80.3 us
    unnamed x306, local copies, waits for them, and re-layouts  66 us
    pallas_call x3, Pallas kernels, products(): pl.pallas_call(product_kernel, grid_spec=pltpu.PrefetchScalarGridSpec(num...  50.9 us
  transfers between devices with their start and end apart: 101, of which 60 were waited for; matrix products, arithmetic and copies ran while one was open for 21% of the time, Pallas kernels for 11%

profile of v3, /device:TPU:0, one launch (start us, length us, event | category | flops | bytes accessed | tf_op | source)
XLA Modules:
  0.0 1502.0 jit_solution(12473560302572940677)
XLA Ops:
  90.5 18.5 %collective-permute-done.19 = bf16[256,2048]{1,0:T(8,128)(2,1)S(1)} collective-permute-done((bf16[256,2048]{1,0:T(8,128)(2,1)S(1)}, bf16[256,2048]{1,0:T(8,128)(2,1)S(1)}, u32[]{:S(2)}, u32[]{:S(2)}) %collective-permute-start.19) | collective-permute-done | bytes 1048608 | tf_op jit(solution)/shard_map/ppermute | solution.py:42
  133.0 15.9 %collective-permute-done.23 = bf16[256,2048]{1,0:T(8,128)(2,1)S(1)} collective-permute-done((bf16[256,2048]{1,0:T(8,128)(2,1)S(1)}, bf16[256,2048]{1,0:T(8,128)(2,1)S(1)}, u32[]{:S(2)}, u32[]{:S(2)}) %collective-permute-start.23) | collective-permute-done | bytes 1048608 | tf_op jit(solution)/shard_map/ppermute | solution.py:42
  153.0 13.1 project.1
  200.0 21.4 %attend.1 = (bf16[2048,256]{1,0:T(8,128)(2,1)S(1)}, f32[2,1,2048]{2,1,0:T(1,128)S(1)}) custom-call(bf16[2048,256]{1,0:T(8,128)(2,1)S(1)} %bitcast.348, bf16[2048,256]{1,0:T(8,128)(2,1)S(1)} %bitcast.346, bf16[2048,256]{1,0:T(8,128)(2,1)S(1)} %copy-done.11, s32[1,2048]{1,0:T(1,128)S(1)} %copy-done.9, s32[2048,1]{1,0:T(8,128)S(1)} %copy.212.seg_col_ref), custom_call_target="tpu_custom_call" | custom-call | flops 2684354560 | bytes 4194304 | tf_op jit(solution)/shard_map/attend/pallas_call | solution.py:294
  308.1 10.1 collective-permute-done.39
  325.4 18.0 %collective-permute-done.40 = bf16[256,2048]{1,0:T(8,128)(2,1)S(1)} collective-permute-done((bf16[256,2048]{1,0:T(8,128)(2,1)}, bf16[256,2048]{1,0:T(8,128)(2,1)S(1)}, u32[]{:S(2)}, u32[]{:S(2)}) %collective-permute-start.40) | collective-permute-done | bytes 1048608 | tf_op jit(solution)/shard_map/ppermute | solution.py:42
  361.2 97.9 %collective-permute-done.45 = bf16[256,2048]{1,0:T(8,128)(2,1)S(1)} collective-permute-done((bf16[256,2048]{1,0:T(8,128)(2,1)S(1)}, bf16[256,2048]{1,0:T(8,128)(2,1)S(1)}, u32[]{:S(2)}, u32[]{:S(2)}) %collective-permute-start.45) | collective-permute-done | bytes 1048608 | tf_op jit(solution)/shard_map/ppermute | solution.py:42
  461.2 22.9 %collective-permute-done.46 = bf16[256,2048]{1,0:T(8,128)(2,1)S(1)} collective-permute-done((bf16[256,2048]{1,0:T(8,128)(2,1)S(1)}, bf16[256,2048]{1,0:T(8,128)(2,1)S(1)}, u32[]{:S(2)}, u32[]{:S(2)}) %collective-permute-start.46) | collective-permute-done | bytes 1048608 | tf_op jit(solution)/shard_map/ppermute | solution.py:42
  511.0 22.0 %collective-permute-done.34.refs_1_ = bf16[2,512,1024]{2,1,0:T(8,128)(2,1)} collective-permute-done((bf16[2,512,1024]{2,1,0:T(8,128)(2,1)}, bf16[2,512,1024]{2,1,0:T(8,128)(2,1)}, u32[]{:S(2)}, u32[]{:S(2)}) %collective-permute-start.34) | collective-permute-done | bytes 2097184 | tf_op jit(solution)/shard_map/ppermute | solution.py:42
  534.8 43.2 %collective-permute-done.36.refs_3_ = bf16[2,512,1024]{2,1,0:T(8,128)(2,1)} collective-permute-done((bf16[2,512,1024]{2,1,0:T(8,128)(2,1)}, bf16[2,512,1024]{2,1,0:T(8,128)(2,1)}, u32[]{:S(2)}, u32[]{:S(2)}) %collective-permute-start.36) | collective-permute-done | bytes 2097184 | tf_op jit(solution)/shard_map/ppermute | solution.py:42
  578.0 43.1 %collective-permute-done.37.refs_5_ = bf16[2,256,2048]{2,1,0:T(8,128)(2,1)} collective-permute-done((bf16[2,256,2048]{2,1,0:T(8,128)(2,1)}, bf16[2,256,2048]{2,1,0:T(8,128)(2,1)}, u32[]{:S(2)}, u32[]{:S(2)}) %collective-permute-start.37) | collective-permute-done | bytes 2097184 | tf_op jit(solution)/shard_map/ppermute | solution.py:42
  621.1 59.6 %experts.2 = (bf16[1024,2048]{1,0:T(8,128)(2,1)}, bf16[1024,2048]{1,0:T(8,128)(2,1)}, bf16[1024,2048]{1,0:T(8,128)(2,1)}, bf16[1024,2048]{1,0:T(8,128)(2,1)}, f3...) custom-call(s32[2]{0:T(128)} %pad_add_fusion.first_ref, ...), custom_call_target="tpu_custom_call" | custom-call | flops 38654705664 | bytes 62914560 | tf_op jit(solution)/shard_map/experts/pallas_call | solution.py:514
  680.7 60.1 %experts.3 = (bf16[1024,2048]{1,0:T(8,128)(2,1)}, bf16[1024,2048]{1,0:T(8,128)(2,1)}, bf16[1024,2048]{1,0:T(8,128)(2,1)}, bf16[1024,2048]{1,0:T(8,128)(2,1)}, f3...) custom-call(s32[2]{0:T(128)} %pad_add_fusion.first_ref, ...), custom_call_target="tpu_custom_call", output_to_operand_aliasing={{6}: (14, {}), {7}: (15, {}), {8}: (16, {}), {9}: (17, {})} | custom-call | flops 38654705664 | bytes 62914560 | tf_op jit(solution)/shard_map/experts/pallas_call | solution.py:514
  753.7 11.8 collective-permute-done.52
  769.8 23.1 %collective-permute-done.53 = bf16[256,2048]{1,0:T(8,128)(2,1)S(1)} collective-permute-done((bf16[256,2048]{1,0:T(8,128)(2,1)S(1)}, bf16[256,2048]{1,0:T(8,128)(2,1)S(1)}, u32[]{:S(2)}, u32[]{:S(2)}) %collective-permute-start.53) | collective-permute-done | bytes 1048608 | tf_op jit(solution)/shard_map/ppermute | solution.py:42
  801.1 9.6 collective-permute-done.56
  825.7 13.4 all-to-all-done.2
  844.0 33.8 %collective-permute-done.61 = f32[8,512]{0,1:T(8,128)S(1)} collective-permute-done((f32[8,512]{0,1:T(8,128)S(1)}, f32[8,512]{0,1:T(8,128)S(1)}, u32[]{:S(2)}, u32[]{:S(2)}) %collective-permute-start.61) | collective-permute-done | bytes 16416 | tf_op jit(solution)/shard_map/ppermute | solution.py:42
  884.2 16.1 %collective-permute-done.60 = bf16[256,2048]{1,0:T(8,128)(2,1)} collective-permute-done((bf16[256,2048]{1,0:T(8,128)(2,1)}, bf16[256,2048]{1,0:T(8,128)(2,1)}, u32[]{:S(2)}, u32[]{:S(2)}) %collective-permute-start.60) | collective-permute-done | bytes 1048608 | tf_op jit(solution)/shard_map/ppermute | solution.py:42
  914.9 16.2 %collective-permute-done.62 = bf16[256,2048]{1,0:T(8,128)(2,1)S(1)} collective-permute-done((bf16[256,2048]{1,0:T(8,128)(2,1)}, bf16[256,2048]{1,0:T(8,128)(2,1)S(1)}, u32[]{:S(2)}, u32[]{:S(2)}) %collective-permute-start.62) | collective-permute-done | bytes 1048608 | tf_op jit(solution)/shard_map/ppermute | solution.py:42
  949.4 15.4 %in_products_sent.1 = bf16[2,2,512,1024]{3,2,1,0:T(8,128)(2,1)} custom-call(s32[1]{0:T(128)} %bitcast.26.me_ref, bf16[2,2304,2048]{2,1,0:T(8,128)(2,1)} %get-tuple-element.108.left_ref, bf16[2,2304,1024]{2,1,0:T(8,128)(2,1)} %get-tuple-element.110.right_ref), custom_call_target="tpu_custom_call" | custom-call | flops 9663676416 | bytes 18874368 | tf_op jit(solution)/shard_map/in_products_sent/pallas_call | solution.py:556
  964.9 20.1 %down_products.1 = bf16[2,2,256,2048]{3,2,1,0:T(8,128)(2,1)} custom-call(s32[1]{0:T(128)} %bitcast.26.me_ref, bf16[2,2304,512]{2,1,0:T(8,128)(2,1)} %get-tuple-element.113.left_ref, bf16[2,2304,2048]{2,1,0:T(8,128)(2,1)} %get-tuple-element.114.right_ref), custom_call_target="tpu_custom_call" | custom-call | flops 9663676416 | bytes 23592960 | tf_op jit(solution)/shard_map/down_products/pallas_call | solution.py:556
  992.1 15.4 %in_products_kept.1 = bf16[2,2,512,1024]{3,2,1,0:T(8,128)(2,1)} custom-call(s32[1]{0:T(128)} %bitcast.26.me_ref, bf16[2,2304,2048]{2,1,0:T(8,128)(2,1)} %get-tuple-element.108.left_ref, bf16[2,2304,1024]{2,1,0:T(8,128)(2,1)} %get-tuple-element.110.right_ref), custom_call_target="tpu_custom_call" | custom-call | flops 9663676416 | bytes 18874368 | tf_op jit(solution)/shard_map/in_products_kept/pallas_call | solution.py:556
  1007.5 126.0 %reduce-scatter.7.cloned.1.call-done = f32[64,17]{1,0:T(8,128)} async-done(((f32[2048,17]{1,0:T(8,128)}), f32[64,17]{1,0:T(8,128)}) %reduce-scatter.7.cloned.1.call-update) | async-done | bytes 4368
  1145.3 27.7 %attend_back.1 = (bf16[2048,256]{1,0:T(8,128)(2,1)S(1)}, bf16[2048,256]{1,0:T(8,128)(2,1)S(1)}, bf16[2048,256]{1,0:T(8,128)(2,1)S(1)}) custom-call(bf16[2048,256]{1,0:T(8,128)(2,1)S(1)} %bitcast.349, bf16[2048,256]{1,0:T(8,128)(2,1)S(1)} %bitcast.347, bf16[2048,256]{1,0:T(8,128)(2,1)} %copy-done.10, bf16[2048,256]{1,0:T(8,128)(2,1)} %bitcast.431, ...), custom_call_target="tpu_custom_call" | custom-call | flops 6710886400 | bytes 7340032 | tf_op jit(solution)/shard_map/attend_back/pallas_call | solution.py:326
  1217.2 56.8 %reduce-scatter.9.cloned.1.call-done = f32[64,2]{1,0:T(8,128)} async-done(((f32[256,2]{1,0:T(8,128)}), f32[64,2]{1,0:T(8,128)}) %reduce-scatter.9.cloned.1.call-update) | async-done | bytes 528
  1305.2 14.8 collective-permute-done.86
  1320.4 12.5 collective-permute-done.89
  1334.0 23.1 %collective-permute-done.87 = bf16[1,8,64,512]{3,2,1,0:T(8,128)(2,1)S(1)} collective-permute-done((bf16[1,8,64,512]{3,2,1,0:T(8,128)(2,1)S(1)}, bf16[1,8,64,512]{3,2,1,0:T(8,128)(2,1)S(1)}, u32[]{:S(2)}, u32[]{:S(2)}) %collective-permute-start.87) | collective-permute-done | bytes 524320 | tf_op jit(solution)/shard_map/ppermute | solution.py:42
  1399.7 15.4 %collective-permute-done.70 = bf16[256,2048]{1,0:T(8,128)(2,1)S(1)} collective-permute-done((bf16[256,2048]{1,0:T(8,128)(2,1)S(1)}, bf16[256,2048]{1,0:T(8,128)(2,1)S(1)}, u32[]{:S(2)}, u32[]{:S(2)}) %collective-permute-start.70) | collective-permute-done | bytes 1048608 | tf_op jit(solution)/shard_map/ppermute | solution.py:42
  1446.6 13.5 collective-permute-done.83
  1464.3 16.3 %collective-permute-done.74 = bf16[256,2048]{1,0:T(8,128)(2,1)S(1)} collective-permute-done((bf16[256,2048]{1,0:T(8,128)(2,1)S(1)}, bf16[256,2048]{1,0:T(8,128)(2,1)S(1)}, u32[]{:S(2)}, u32[]{:S(2)}) %collective-permute-start.74) | collective-permute-done | bytes 1048608 | tf_op jit(solution)/shard_map/ppermute | solution.py:42
  (755 shorter events, 556.7 us)
Async XLA Ops:
  8.0 59.0 %collective-permute-start = (bf16[256,2048]{1,0:T(8,128)(2,1)}, bf16[256,2048]{1,0:T(8,128)(2,1)}, u32[]{:S(2)}, u32[]{:S(2)}) collective-permute-start(bf16[256,2048]{1,0:T(8,128)(2,1)} %bitcast.351), channel_id=1, source_target_pairs={{0,8},{4,12},{8,0},{12,4},{16,24},{20,28},{24,16},{28,20},{1,9},{5... | collective-permute-start | bytes 3145736 | tf_op jit(solution)/shard_map/ppermute | solution.py:42
  11.0 59.8 %collective-permute-start.1 = (bf16[256,2048]{1,0:T(8,128)(2,1)}, bf16[256,2048]{1,0:T(8,128)(2,1)}, u32[]{:S(2)}, u32[]{:S(2)}) collective-permute-start(bf16[256,2048]{1,0:T(8,128)(2,1)} %bitcast.352), channel_id=1, source_target_pairs={{0,16},{4,20},{8,24},{12,28},{16,0},{20,4},{24,8},{28,12},{1,17},{... | collective-permute-start | bytes 3145736 | tf_op jit(solution)/shard_map/ppermute | solution.py:42
  24.8 46.0 %all-to-all-start = ((bf16[8,64,768]{2,1,0:T(8,128)(2,1)}), bf16[8,64,768]{2,1,0:T(8,128)(2,1)}, u32[]{:S(2)}, u32[]{:S(2)}) async-start(bf16[8,64,768]{2,1,0:T(8,128)(2,1)} %reshape.542), calls=%async_computation | async-start | bytes 1572864 | tf_op jit(solution)/shard_map/all_to_all | solution.py:636
  82.9 70.1 %collective-permute-start.4 = (bf16[1024,2048]{1,0:T(8,128)(2,1)}, bf16[1024,2048]{1,0:T(8,128)(2,1)}, u32[]{:S(2)}, u32[]{:S(2)}) collective-permute-start(bf16[1024,2048]{1,0:T(8,128)(2,1)} %constant_dynamic-update-slice_fusion.even_ref), channel_id=1, source_target_pairs={{0,4},{4,0},{8,12},{12,8},{16,20},{20,16},{24,28},{28,24},{1,5},{5... | collective-permute-start | bytes 12582920 | tf_op jit(solution)/shard_map/ppermute | solution.py:42
  173.8 68.4 %collective-permute-start.27 = (bf16[1024,2048]{1,0:T(8,128)(2,1)}, bf16[1024,2048]{1,0:T(8,128)(2,1)}, u32[]{:S(2)}, u32[]{:S(2)}) collective-permute-start(bf16[1024,2048]{1,0:T(8,128)(2,1)} %constant_dynamic-update-slice_fusion.18), channel_id=1, source_target_pairs={{0,4},{4,0},{8,12},{12,8},{16,20},{20,16},{24,28},{28,24},{1,5},{5... | collective-permute-start | bytes 12582920 | tf_op jit(solution)/shard_map/ppermute | solution.py:42
  269.6 48.5 %collective-permute-start.39 = (bf16[256,2048]{1,0:T(8,128)(2,1)}, bf16[256,2048]{1,0:T(8,128)(2,1)}, u32[]{:S(2)}, u32[]{:S(2)}) collective-permute-start(bf16[256,2048]{1,0:T(8,128)(2,1)} %get-tuple-element.127), channel_id=1, source_target_pairs={{0,2},{1,3},{2,0},{3,1},{4,6},{5,7},{6,4},{7,5},{8,10},{9,11},{10,... | collective-permute-start | bytes 3145736 | tf_op jit(solution)/shard_map/ppermute | solution.py:42
  322.5 165.4 %collective-permute-start.35 = (bf16[2,512,1024]{2,1,0:T(8,128)(2,1)S(1)}, bf16[2,512,1024]{2,1,0:T(8,128)(2,1)S(1)}, u32[]{:S(2)}, u32[]{:S(2)}) collective-permute-start(bf16[2,512,1024]{2,1,0:T(8,128)(2,1)S(1)} %copy-done.49), channel_id=1, source_target_pairs={{0,2},{1,3},{2,0},{3,1},{4,6},{5,7},{6,4},{7,5},{8,10},{9,11},{10,... | collective-permute-start | bytes 6291464 | tf_op jit(solution)/shard_map/ppermute | solution.py:42
  322.5 210.6 %collective-permute-start.33 = (bf16[1024,2048]{1,0:T(8,128)(2,1)}, bf16[1024,2048]{1,0:T(8,128)(2,1)}, u32[]{:S(2)}, u32[]{:S(2)}) collective-permute-start(bf16[1024,2048]{1,0:T(8,128)(2,1)} %constant_dynamic-update-slice_fusion.13.ua_ref), channel_id=1, source_target_pairs={{0,4},{4,0},{8,12},{12,8},{16,20},{20,16},{24,28},{28,24},{1,5},{5... | collective-permute-start | bytes 12582920 | tf_op jit(solution)/shard_map/ppermute | solution.py:42
  322.6 136.5 %collective-permute-start.45 = (bf16[256,2048]{1,0:T(8,128)(2,1)S(1)}, bf16[256,2048]{1,0:T(8,128)(2,1)S(1)}, u32[]{:S(2)}, u32[]{:S(2)}) collective-permute-start(bf16[256,2048]{1,0:T(8,128)(2,1)S(1)} %bitcast.362), channel_id=1, source_target_pairs={{0,2},{1,3},{2,0},{3,1},{4,6},{5,7},{6,4},{7,5},{8,10},{9,11},{10,... | collective-permute-start | bytes 3145736 | tf_op jit(solution)/shard_map/ppermute | solution.py:42
  356.5 264.6 %collective-permute-start.32 = (bf16[1024,2048]{1,0:T(8,128)(2,1)}, bf16[1024,2048]{1,0:T(8,128)(2,1)}, u32[]{:S(2)}, u32[]{:S(2)}) collective-permute-start(bf16[1024,2048]{1,0:T(8,128)(2,1)} %constant_dynamic-update-slice_fusion.23.xa_ref), channel_id=1, source_target_pairs={{0,4},{4,0},{8,12},{12,8},{16,20},{20,16},{24,28},{28,24},{1,5},{5... | collective-permute-start | bytes 12582920 | tf_op jit(solution)/shard_map/ppermute | solution.py:42
  484.2 48.9 %collective-permute-start.34 = (bf16[2,512,1024]{2,1,0:T(8,128)(2,1)}, bf16[2,512,1024]{2,1,0:T(8,128)(2,1)}, u32[]{:S(2)}, u32[]{:S(2)}) collective-permute-start(bf16[2,512,1024]{2,1,0:T(8,128)(2,1)} %pad_maximum_fusion.3.refs_0_), channel_id=1, source_target_pairs={{0,1},{1,0},{2,3},{3,2},{4,5},{5,4},{6,7},{7,6},{8,9},{9,8},{10,11... | collective-permute-start | bytes 6291464 | tf_op jit(solution)/shard_map/ppermute | solution.py:42
  499.4 78.6 %collective-permute-start.36 = (bf16[2,512,1024]{2,1,0:T(8,128)(2,1)}, bf16[2,512,1024]{2,1,0:T(8,128)(2,1)}, u32[]{:S(2)}, u32[]{:S(2)}) collective-permute-start(bf16[2,512,1024]{2,1,0:T(8,128)(2,1)} %copy-done.104), channel_id=1, source_target_pairs={{0,1},{1,0},{2,3},{3,2},{4,5},{5,4},{6,7},{7,6},{8,9},{9,8},{10,11... | collective-permute-start | bytes 6291464 | tf_op jit(solution)/shard_map/ppermute | solution.py:42
  501.2 119.8 %collective-permute-start.37 = (bf16[2,256,2048]{2,1,0:T(8,128)(2,1)}, bf16[2,256,2048]{2,1,0:T(8,128)(2,1)}, u32[]{:S(2)}, u32[]{:S(2)}) collective-permute-start(bf16[2,256,2048]{2,1,0:T(8,128)(2,1)} %refs_4_.1), channel_id=1, source_target_pairs={{0,1},{1,0},{2,3},{3,2},{4,5},{5,4},{6,7},{7,6},{8,9},{9,8},{10,11... | collective-permute-start | bytes 6291464 | tf_op jit(solution)/shard_map/ppermute | solution.py:42
  533.1 147.6 %collective-permute-start.44 = (bf16[1024,2048]{1,0:T(8,128)(2,1)}, bf16[1024,2048]{1,0:T(8,128)(2,1)}, u32[]{:S(2)}, u32[]{:S(2)}) collective-permute-start(bf16[1024,2048]{1,0:T(8,128)(2,1)} %constant_dynamic-update-slice_fusion.36.xa_ref), channel_id=1, source_target_pairs={{0,4},{4,0},{8,12},{12,8},{16,20},{20,16},{24,28},{28,24},{1,5},{5... | collective-permute-start | bytes 12582920 | tf_op jit(solution)/shard_map/ppermute | solution.py:42
  533.1 147.6 %collective-permute-start.50 = (bf16[1024,2048]{1,0:T(8,128)(2,1)}, bf16[1024,2048]{1,0:T(8,128)(2,1)}, u32[]{:S(2)}, u32[]{:S(2)}) collective-permute-start(bf16[1024,2048]{1,0:T(8,128)(2,1)} %constant_dynamic-update-slice_fusion.41.ua_ref), channel_id=1, source_target_pairs={{0,4},{4,0},{8,12},{12,8},{16,20},{20,16},{24,28},{28,24},{1,5},{5... | collective-permute-start | bytes 12582920 | tf_op jit(solution)/shard_map/ppermute | solution.py:42
  740.8 55.6 %collective-permute-start.38 = (bf16[1024,2048]{1,0:T(8,128)(2,1)}, bf16[1024,2048]{1,0:T(8,128)(2,1)}, u32[]{:S(2)}, u32[]{:S(2)}) collective-permute-start(bf16[1024,2048]{1,0:T(8,128)(2,1)} %get-tuple-element.80), channel_id=1, source_target_pairs={{0,4},{4,0},{8,12},{12,8},{16,20},{20,16},{24,28},{28,24},{1,5},{5... | collective-permute-start | bytes 12582920 | tf_op jit(solution)/shard_map/ppermute | solution.py:42
  814.1 64.9 %collective-permute-start.57 = (bf16[256,2048]{1,0:T(8,128)(2,1)}, bf16[256,2048]{1,0:T(8,128)(2,1)}, u32[]{:S(2)}, u32[]{:S(2)}) collective-permute-start(bf16[256,2048]{1,0:T(8,128)(2,1)} %pad_maximum_fusion.14), channel_id=1, source_target_pairs={{0,16},{4,20},{8,24},{12,28},{16,0},{20,4},{24,8},{28,12},{1,17},{... | collective-permute-start | bytes 3145736 | tf_op jit(solution)/shard_map/ppermute | solution.py:42
  816.5 64.0 %collective-permute-start.59 = (bf16[256,2048]{1,0:T(8,128)(2,1)}, bf16[256,2048]{1,0:T(8,128)(2,1)}, u32[]{:S(2)}, u32[]{:S(2)}) collective-permute-start(bf16[256,2048]{1,0:T(8,128)(2,1)} %pad_maximum_fusion.15), channel_id=1, source_target_pairs={{0,8},{4,12},{8,0},{12,4},{16,24},{20,28},{24,16},{28,20},{1,9},{5... | collective-permute-start | bytes 3145736 | tf_op jit(solution)/shard_map/ppermute | solution.py:42
  823.8 309.7 %reduce-scatter.7.cloned.1.call-start = ((), (), s32[]{:S(2)}) async-start(), calls=%async_computation.6 | async-start | bytes 1081344
  842.3 58.1 %collective-permute-start.60 = (bf16[256,2048]{1,0:T(8,128)(2,1)}, bf16[256,2048]{1,0:T(8,128)(2,1)}, u32[]{:S(2)}, u32[]{:S(2)}) collective-permute-start(bf16[256,2048]{1,0:T(8,128)(2,1)} %pad_maximum_fusion.13), channel_id=1, source_target_pairs={{0,2},{1,3},{2,0},{3,1},{4,6},{5,7},{6,4},{7,5},{8,10},{9,11},{10,... | collective-permute-start | bytes 3145736 | tf_op jit(solution)/shard_map/ppermute | solution.py:42
  947.2 192.7 %collective-permute-start.67 = (bf16[1024,2048]{1,0:T(8,128)(2,1)}, bf16[1024,2048]{1,0:T(8,128)(2,1)}, u32[]{:S(2)}, u32[]{:S(2)}) collective-permute-start(bf16[1024,2048]{1,0:T(8,128)(2,1)} %constant_dynamic-update-slice_fusion.74), channel_id=1, source_target_pairs={{0,4},{4,0},{8,12},{12,8},{16,20},{20,16},{24,28},{28,24},{1,5},{5... | collective-permute-start | bytes 12582920 | tf_op jit(solution)/shard_map/ppermute | solution.py:42
  964.9 210.1 %collective-permute-start.92 = (bf16[2,2,512,1024]{3,2,1,0:T(8,128)(2,1)}, bf16[2,2,512,1024]{3,2,1,0:T(8,128)(2,1)}, u32[]{:S(2)}, u32[]{:S(2)}) collective-permute-start(bf16[2,2,512,1024]{3,2,1,0:T(8,128)(2,1)} %in_products_sent.1), channel_id=1, source_target_pairs={{0,1},{1,0},{2,3},{3,2},{4,5},{5,4},{6,7},{7,6},{8,9},{9,8},{10,11... | collective-permute-start | bytes 12582920 | tf_op jit(solution)/shard_map/ppermute | solution.py:42
  988.2 186.7 %collective-permute-start.94 = (bf16[1,2,256,2048]{3,2,1,0:T(8,128)(2,1)}, bf16[1,2,256,2048]{3,2,1,0:T(8,128)(2,1)}, u32[]{:S(2)}, u32[]{:S(2)}) collective-permute-start(bf16[1,2,256,2048]{3,2,1,0:T(8,128)(2,1)} %slice.798), channel_id=1, source_target_pairs={{0,1},{1,0},{2,3},{3,2},{4,5},{5,4},{6,7},{7,6},{8,9},{9,8},{10,11... | collective-permute-start | bytes 6291464 | tf_op jit(solution)/shard_map/ppermute | solution.py:42
  991.6 282.4 %reduce-scatter.9.cloned.1.call-start = ((), (), s32[]{:S(2)}) async-start(), calls=%async_computation.7 | async-start | bytes 163840
  1136.4 79.3 %collective-permute-start.66 = (bf16[1024,2048]{1,0:T(8,128)(2,1)}, bf16[1024,2048]{1,0:T(8,128)(2,1)}, u32[]{:S(2)}, u32[]{:S(2)}) collective-permute-start(bf16[1024,2048]{1,0:T(8,128)(2,1)} %get-tuple-element.95), channel_id=1, source_target_pairs={{0,4},{4,0},{8,12},{12,8},{16,20},{20,16},{24,28},{28,24},{1,5},{5... | collective-permute-start | bytes 12582920 | tf_op jit(solution)/shard_map/ppermute | solution.py:42
  1179.5 182.9 %collective-permute-start.93 = (bf16[2,512,1024]{2,1,0:T(8,128)(2,1)}, bf16[2,512,1024]{2,1,0:T(8,128)(2,1)}, u32[]{:S(2)}, u32[]{:S(2)}) collective-permute-start(bf16[2,512,1024]{2,1,0:T(8,128)(2,1)} %fusion.10), channel_id=1, source_target_pairs={{0,2},{1,3},{2,0},{3,1},{4,6},{5,7},{6,4},{7,5},{8,10},{9,11},{10,... | collective-permute-start | bytes 6291464 | tf_op jit(solution)/shard_map/ppermute | solution.py:42
  1203.8 97.7 %collective-permute-start.90 = (bf16[2,64,2048]{2,1,0:T(8,128)(2,1)}, bf16[2,64,2048]{2,1,0:T(8,128)(2,1)}, u32[]{:S(2)}, u32[]{:S(2)}) collective-permute-start(bf16[2,64,2048]{2,1,0:T(8,128)(2,1)} %pad_maximum_fusion.27), channel_id=1, source_target_pairs={{0,1},{1,0},{2,3},{3,2},{4,5},{5,4},{6,7},{7,6},{8,9},{9,8},{10,11... | collective-permute-start | bytes 1572872 | tf_op jit(solution)/shard_map/ppermute | solution.py:42
  1214.9 88.1 %collective-permute-start.88 = (bf16[2,8,64,256]{3,2,1,0:T(8,128)(2,1)}, bf16[2,8,64,256]{3,2,1,0:T(8,128)(2,1)}, u32[]{:S(2)}, u32[]{:S(2)}) collective-permute-start(bf16[2,8,64,256]{3,2,1,0:T(8,128)(2,1)} %pad_maximum_fusion.26), channel_id=1, source_target_pairs={{0,1},{1,0},{2,3},{3,2},{4,5},{5,4},{6,7},{7,6},{8,9},{9,8},{10,11... | collective-permute-start | bytes 1572872 | tf_op jit(solution)/shard_map/ppermute | solution.py:42
  1215.6 151.4 %collective-permute-start.68 = (bf16[1024,2048]{1,0:T(8,128)(2,1)}, bf16[1024,2048]{1,0:T(8,128)(2,1)}, u32[]{:S(2)}, u32[]{:S(2)}) collective-permute-start(bf16[1024,2048]{1,0:T(8,128)(2,1)} %get-tuple-element.101), channel_id=1, source_target_pairs={{0,4},{4,0},{8,12},{12,8},{16,20},{20,16},{24,28},{28,24},{1,5},{5... | collective-permute-start | bytes 12582920 | tf_op jit(solution)/shard_map/ppermute | solution.py:42
  1216.4 59.6 %collective-permute-start.80 = (f32[2,2048]{1,0:T(2,128)S(1)}, f32[2,2048]{1,0:T(2,128)S(1)}, u32[]{:S(2)}, u32[]{:S(2)}) collective-permute-start(f32[2,2048]{1,0:T(2,128)S(1)} %fusion.105), channel_id=1, source_target_pairs={{0,16},{4,20},{8,24},{12,28},{16,0},{20,4},{24,8},{28,12},{1,17},{... | collective-permute-start | bytes 49160 | tf_op jit(solution)/shard_map/ppermute | solution.py:42
  1301.5 93.6 %collective-permute-start.81 = (bf16[1024,2048]{1,0:T(8,128)(2,1)}, bf16[1024,2048]{1,0:T(8,128)(2,1)}, u32[]{:S(2)}, u32[]{:S(2)}) collective-permute-start(bf16[1024,2048]{1,0:T(8,128)(2,1)} %convolution_convert_fusion.1), channel_id=1, source_target_pairs={{0,4},{4,0},{8,12},{12,8},{16,20},{20,16},{24,28},{28,24},{1,5},{5... | collective-permute-start | bytes 12582920 | tf_op jit(solution)/shard_map/ppermute | solution.py:42
  1446.6 43.9 %collective-permute-start.77 = (bf16[256,2048]{1,0:T(8,128)(2,1)S(1)}, bf16[256,2048]{1,0:T(8,128)(2,1)S(1)}, u32[]{:S(2)}, u32[]{:S(2)}) collective-permute-start(bf16[256,2048]{1,0:T(8,128)(2,1)S(1)} %pad_maximum_fusion.19), channel_id=1, source_target_pairs={{0,2},{1,3},{2,0},{3,1},{4,6},{5,7},{6,4},{7,5},{8,10},{9,11},{10,... | collective-permute-start | bytes 3145736 | tf_op jit(solution)/shard_map/ppermute | solution.py:42
  (177 other events, 4945.9 us)
Sparse Core Ops, SparseCore 0:
  991.7 141.7 reduce-scatter.6
Sparse Core Ops, SparseCore 1:
  1197.5 76.4 reduce-scatter.8

commit v4 on v3

--- a/solution.py
+++ b/solution.py
@@ -54,22 +54,32 @@
     return lax.optimization_barrier((values, others))[0]
 
 
-def gather_seq(values, size):
+def tie(*values):
+    return lax.optimization_barrier(values)
+
+
+def gather_first(values, size):
+    return {r: swap(values, "seq", size, r) for r in range(2, size, 2) if r == low_bit(r)}
+
+
+def gather_more(values, first, size):
     rows = values.shape[0] // 2
-    pieces = {0: values}
+    pieces = dict(first)
     for r in range(2, size, 2):
-        if r == low_bit(r):
-            pieces[r] = swap(values, "seq", size, r)
-        else:
+        if r not in pieces:
             up, down = high_bit(r), low_bit(r)
-            pieces[r] = jnp.concatenate(
-                [
-                    swap(pieces[r ^ up][:rows], "seq", size, up),
-                    swap(pieces[r ^ down][rows:], "seq", size, down),
-                ],
-                0,
-            )
-    even = jnp.concatenate([pieces[r] for r in range(0, size, 2)], 0)
+            upper, lower = pieces[r ^ up], pieces[r ^ down]
+            upper = upper[0] if isinstance(upper, tuple) else upper[:rows]
+            lower = lower[1] if isinstance(lower, tuple) else lower[rows:]
+            pieces[r] = (swap(upper, "seq", size, up), swap(lower, "seq", size, down))
+    return {r: piece for r, piece in pieces.items() if r not in first}
+
+
+def gather_end(values, first, more, size):
+    blocks = [values]
+    for r in range(2, size, 2):
+        blocks.extend([first[r]] if r in first else more[r])
+    even = jnp.concatenate(blocks, 0)
     return even, swap(even, "seq", size, 1)
 
 
@@ -85,7 +95,7 @@
     return jnp.concatenate([lax.dynamic_slice_in_dim(blocks, at, 1, 0) for at in places], 0)
 
 
-def scatter_sum(even, got, size):
+def sum_first(even, got, size, dep=()):
     rows = even.shape[0] // (size // 2)
     half = rows // 2
 
@@ -95,15 +105,25 @@
 
     sums = {r: [part(r, 0, half), part(r, half, half)] for r in range(0, size, 2)}
     for r in range(size - 2, 0, -2):
-        if r == low_bit(r):
-            whole = jnp.concatenate([value.astype(BF16) for value in sums[r]], 0)
-            come = swap(whole, "seq", size, r).astype(F32)
-            sums[0] = [sums[0][0] + come[:half], sums[0][1] + come[half:]]
-        else:
+        if r != low_bit(r):
             up, down = high_bit(r), low_bit(r)
-            sums[r ^ up][0] += swap(sums[r][0].astype(BF16), "seq", size, up).astype(F32)
-            sums[r ^ down][1] += swap(sums[r][1].astype(BF16), "seq", size, down).astype(F32)
-    return jnp.concatenate(sums[0], 0)
+            upper = after(swap(sums[r][0].astype(BF16), "seq", size, up), dep)
+            lower = after(swap(sums[r][1].astype(BF16), "seq", size, down), dep)
+            sums[r ^ up][0] += upper.astype(F32)
+            sums[r ^ down][1] += lower.astype(F32)
+            del sums[r]
+    return {
+        r: jnp.concatenate([v.astype(BF16) if r else v for v in value], 0)
+        for r, value in sums.items()
+    }
+
+
+def sum_last(sums, size, dep=()):
+    total = sums[0]
+    for r in sums:
+        if r:
+            total += after(swap(sums[r], "seq", size, r), dep).astype(F32)
+    return total
 
 
 def sum_all(values, axis, size):
@@ -114,27 +134,29 @@
     return values
 
 
-def ring_pieces(values, size):
-    pieces = [values]
-    for _ in range(1, size):
-        pieces.append(lax.ppermute(pieces[-1], "fsdp", [(i, (i + 1) % size) for i in range(size)]))
+def fsdp_pieces(values, size):
+    pieces = {0: values}
+    for r in range(1, size):
+        low = low_bit(r)
+        pieces[r] = swap(pieces[r ^ low], "fsdp", size, low)
     return pieces
 
 
-def place_ring(pieces, me, axis):
+def place_fsdp(pieces, me, axis):
     size = len(pieces)
     shape = pieces[0].shape
     whole = jnp.zeros(shape[:axis] + (size,) + shape[axis:], pieces[0].dtype)
-    for k, piece in enumerate(pieces):
-        at = lax.rem(me + size - k, size)
-        whole = lax.dynamic_update_slice_in_dim(whole, jnp.expand_dims(piece, axis), at, axis)
+    for r, piece in pieces.items():
+        whole = lax.dynamic_update_slice_in_dim(whole, jnp.expand_dims(piece, axis), me ^ r, axis)
     return whole
 
 
-def near_swaps(pieces, base, size):
+def near_pieces(values, size):
+    pieces = {0: values}
     for r in range(1, size // 2):
         up = high_bit(r)
-        pieces[base + r] = swap(pieces[base + (r ^ up)], "fsdp", size, up)
+        pieces[r] = swap(pieces[r ^ up], "fsdp", size, up)
+    return pieces
 
 
 def gather_small(values, seq_size, fsdp_size, s, f):
@@ -151,29 +173,22 @@
     return matmul(pick, whole).astype(values.dtype)
 
 
-def sum_near(send, keep, size, dep):
-    got = after(swap(send, "fsdp", size, 1), dep)
-    sums = {2 * k: keep[k].astype(F32) + got[k].astype(F32) for k in range(size // 2)}
-    mask = 2
-    while mask < size // 2:
-        stay = [r for r in sums if not r & mask]
-        moved = jnp.stack([sums[r | mask].astype(BF16) for r in stay], 0)
-        got = swap(moved, "fsdp", size, mask)
-        sums = {r: sums[r] + got[i].astype(F32) for i, r in enumerate(stay)}
-        mask *= 2
-    return sums
-
-
-def scatter_down(terms, half, size, dep):
-    sums = {r: terms[r].astype(F32) for r in range(half)}
-    mask = 1
-    while mask < half:
-        stay = [r for r in sums if not r & mask]
-        moved = terms[1::2] if mask == 1 else jnp.stack([sums[r | mask].astype(BF16) for r in stay])
-        got = after(swap(moved, "fsdp", size, mask), dep)
-        sums = {r: sums[r] + got[i].astype(F32) for i, r in enumerate(stay)}
-        mask *= 2
-    return sums[0]
+def sum_small(values, axes):
+    count = values.shape[0]
+    index = jnp.arange(count, dtype=jnp.int32)
+    source, stride = jnp.zeros_like(index), 1
+    for _, size, me in reversed(axes):
+        source += ((index // stride % size) ^ me) * stride
+        stride *= size
+    pick = (source[:, None] == index[None, :]).astype(F32)
+    values = jnp.dot(pick, values, precision=HIGHEST)
+    for name, size, _ in axes:
+        mask = size // 2
+        while mask:
+            half = values.shape[0] // 2
+            values = values[:half] + swap(values[half:], name, size, mask)
+            mask //= 2
+    return values[0]
 
 
 def scatter_rows(partial_sum, me, size):
@@ -349,18 +364,28 @@
 
 
 def qkv_kernel(
-    me_ref, even_ref, odd_ref, weight_ref, gain_ref, normed_ref, q_ref, k_ref, v_ref, square_ref
+    me_ref,
+    even_ref,
+    odd_ref,
+    weight_ref,
+    gain_ref,
+    normed_even_ref,
+    normed_odd_ref,
+    q_ref,
+    k_ref,
+    v_ref,
+    square_ref,
 ):
-    turned = me_ref[0] % 2 == 1
+    turned = me_ref[0] % 2
     rows = even_ref.shape[0]
     columns = q_ref.shape[1]
-    first, second = even_ref[...], odd_ref[...]
-    blocks = (jnp.where(turned, second, first), jnp.where(turned, first, second))
-    for k, block in enumerate(blocks):
-        at = pl.ds(k * rows, rows)
-        wide = block.astype(F32)
+    for k, (token_ref, normed_ref) in enumerate(
+        ((even_ref, normed_even_ref), (odd_ref, normed_odd_ref))
+    ):
+        at = pl.ds(pl.multiple_of((turned ^ k) * rows, rows), rows)
+        wide = token_ref[...].astype(F32)
         normed = (wide * rms_factor(wide) * gain_ref[...]).astype(BF16)
-        normed_ref[at, :] = normed
+        normed_ref[...] = normed
         pre = matmul(normed, weight_ref[...])
         q_ref[at, :] = pre[:, :columns]
         k_ref[at, :] = pre[:, columns : 2 * columns]
@@ -394,7 +419,8 @@
                 pl.BlockSpec((1, depth), lambda i, me: (0, 0)),
             ],
             out_specs=[
-                placed((2 * rows, depth)),
+                token,
+                token,
                 placed((2 * rows, columns)),
                 placed((2 * rows, columns)),
                 placed((2 * rows, columns)),
@@ -402,7 +428,8 @@
             ],
         ),
         out_shape=[
-            jax.ShapeDtypeStruct((length, depth), BF16),
+            jax.ShapeDtypeStruct((length // 2, depth), BF16),
+            jax.ShapeDtypeStruct((length // 2, depth), BF16),
             head,
             head,
             jax.ShapeDtypeStruct((length, columns), BF16),
@@ -418,6 +445,170 @@
     )(me, even, odd, weight, gain)
 
 
+def split_kernel(q_ref, k_ref, v_ref, out_ref):
+    columns = q_ref.shape[1]
+    for j, ref in enumerate((q_ref, k_ref, v_ref)):
+        out_ref[0, :, j * columns : (j + 1) * columns] = ref[...]
+
+
+def split_heads(w_query, w_key, w_value, parts):
+    rows, columns = w_query.shape[0], w_query.shape[1] // parts
+    block = pl.BlockSpec((rows, columns), lambda i: (0, i))
+    return pl.pallas_call(
+        split_kernel,
+        grid=(parts,),
+        in_specs=[block] * 3,
+        out_specs=pl.BlockSpec((1, rows, 3 * columns), lambda i: (i, 0, 0)),
+        out_shape=jax.ShapeDtypeStruct((parts, rows, 3 * columns), BF16),
+        name="split_heads",
+    )(w_query, w_key, w_value)
+
+
+def spread(row, columns):
+    return jnp.broadcast_to(row, (columns, row.shape[1])).T
+
+
+def factor_of(square_row):
+    return lax.rsqrt(square_row / D + EPSILON)
+
+
+def turn(values, cosine, sine):
+    return values * cosine + pltpu.roll(values, DH // 2, 1) * sine
+
+
+def rope_kernel(q_ref, k_ref, square_ref, gain_ref, cos_ref, sin_ref, q_out, k_out):
+    cosine, sine = cos_ref[...], sin_ref[...]
+    for j, (pre_ref, out_ref) in enumerate(((q_ref, q_out), (k_ref, k_out))):
+        factor = spread(factor_of(square_ref[j : j + 1, :]), DH)
+        for c in range(0, pre_ref.shape[1], DH):
+            at = slice(c, c + DH)
+            normed = pre_ref[:, at] * factor * gain_ref[j : j + 1, at]
+            out_ref[:, at] = turn(normed, cosine, sine).astype(BF16)
+
+
+def rope(query_pre, key_pre, squares, gains, cosine, sine):
+    length, columns = query_pre.shape
+    rows = min(512, length)
+    block = pl.BlockSpec((rows, columns), lambda i: (i, 0))
+    table = pl.BlockSpec((rows, DH), lambda i: (i, 0))
+    return pl.pallas_call(
+        rope_kernel,
+        grid=(length // rows,),
+        in_specs=[
+            block,
+            block,
+            pl.BlockSpec((2, rows), lambda i: (0, i)),
+            pl.BlockSpec((2, columns), lambda i: (0, 0)),
+            table,
+            table,
+        ],
+        out_specs=[block, block],
+        out_shape=[jax.ShapeDtypeStruct((length, columns), BF16)] * 2,
+        compiler_params=pltpu.CompilerParams(vmem_limit_bytes=32 * MIB),
+        name="rope",
+    )(query_pre, key_pre, squares, gains, cosine, sine)
+
+
+def pulled_of(grad_ref, pre_ref, factor, gain_ref, cosine, sine, j, at):
+    turned = turn(grad_ref[:, at].astype(F32), cosine, -sine)
+    return turned, turned * gain_ref[j : j + 1, at], pre_ref[:, at] * factor
+
+
+def rope_mean_kernel(
+    dq_ref, dk_ref, q_ref, k_ref, square_ref, gain_ref, cos_ref, sin_ref, mean_ref, term_ref
+):
+    @pl.when(pl.program_id(0) == 0)
+    def _():
+        term_ref[...] = jnp.zeros_like(term_ref)
+
+    cosine, sine = cos_ref[...], sin_ref[...]
+    for j, (grad_ref, pre_ref) in enumerate(((dq_ref, q_ref), (dk_ref, k_ref))):
+        factor = spread(factor_of(square_ref[j : j + 1, :]), DH)
+        total = 0.0
+        for c in range(0, pre_ref.shape[1], DH):
+            at = slice(c, c + DH)
+            turned, pulled, normed = pulled_of(
+                grad_ref, pre_ref, factor, gain_ref, cosine, sine, j, at
+            )
+            term_ref[j : j + 1, at] += jnp.sum(turned * normed, axis=0, keepdims=True)
+            total += pulled * normed
+        mean_ref[j : j + 1, :] = jnp.sum(total.T, axis=0, keepdims=True)
+
+
+def rope_means(query_back, key_back, query_pre, key_pre, squares, gains, cosine, sine):
+    length, columns = query_pre.shape
+    rows = min(512, length)
+    block = pl.BlockSpec((rows, columns), lambda i: (i, 0))
+    table = pl.BlockSpec((rows, DH), lambda i: (i, 0))
+    row = pl.BlockSpec((2, rows), lambda i: (0, i))
+    fixed = pl.BlockSpec((2, columns), lambda i: (0, 0))
+    return pl.pallas_call(
+        rope_mean_kernel,
+        grid=(length // rows,),
+        in_specs=[block, block, block, block, row, fixed, table, table],
+        out_specs=[row, fixed],
+        out_shape=[
+            jax.ShapeDtypeStruct((2, length), F32),
+            jax.ShapeDtypeStruct((2, columns), F32),
+        ],
+        compiler_params=pltpu.CompilerParams(vmem_limit_bytes=32 * MIB),
+        name="rope_means",
+    )(query_back, key_back, query_pre, key_pre, squares, gains, cosine, sine)
+
+
+def rope_back_kernel(
+    me_ref,
+    dq_ref,
+    dk_ref,
+    dv_ref,
+    q_ref,
+    k_ref,
+    square_ref,
+    mean_ref,
+    gain_ref,
+    cos_ref,
+    sin_ref,
+    out_ref,
+):
+    cosine, sine = cos_ref[...], sin_ref[...]
+    columns = q_ref.shape[1]
+    for j, (grad_ref, pre_ref) in enumerate(((dq_ref, q_ref), (dk_ref, k_ref))):
+        factor = spread(factor_of(square_ref[j : j + 1, :]), DH)
+        mean = spread(mean_ref[j : j + 1, :] / D, DH)
+        for c in range(0, columns, DH):
+            at = slice(c, c + DH)
+            _, pulled, normed = pulled_of(grad_ref, pre_ref, factor, gain_ref, cosine, sine, j, at)
+            out_ref[:, j * columns + c : j * columns + c + DH] = (
+                factor * (pulled - normed * mean)
+            ).astype(BF16)
+    out_ref[:, 2 * columns :] = dv_ref[...]
+
+
+def rope_back(grads, query_pre, key_pre, squares, means, gains, cosine, sine, me, rows):
+    length, columns = query_pre.shape
+    half = length // rows // 2
+
+    def source(p, me):
+        return me[0] ^ (p % half * 2 + p // half)
+
+    block = pl.BlockSpec((rows, columns), lambda p, me: (source(p, me), 0))
+    table = pl.BlockSpec((rows, DH), lambda p, me: (source(p, me), 0))
+    row = pl.BlockSpec((2, rows), lambda p, me: (0, source(p, me)))
+    return pl.pallas_call(
+        rope_back_kernel,
+        grid_spec=pltpu.PrefetchScalarGridSpec(
+            num_scalar_prefetch=1,
+            grid=(2 * half,),
+            in_specs=[block] * 5
+            + [row, row, pl.BlockSpec((2, columns), lambda p, me: (0, 0)), table, table],
+            out_specs=pl.BlockSpec((rows, 3 * columns), lambda p, me: (p, 0)),
+        ),
+        out_shape=jax.ShapeDtypeStruct((length, 3 * columns), BF16),
+        compiler_params=pltpu.CompilerParams(vmem_limit_bytes=32 * MIB),
+        name="rope_back",
+    )(me, *grads, query_pre, key_pre, squares, means, gains, cosine, sine)
+
+
 def expert_kernel(pieces, first_ref, xa_ref, xb_ref, ua_ref, ub_ref, ra_ref, rb_ref, router_ref, *refs):
     weight_refs = refs[: sum(pieces)]
     (ya_ref, yb_ref, za_ref, zb_ref, ga_ref, gb_ref, xc_ref, uc_ref, dg_ref, hid_ref) = refs[-13:-3]
@@ -428,10 +619,11 @@
     @pl.when(pl.program_id(0) == 0)
     def _():
         copies = []
-        for r, ref in enumerate(weight_refs[: pieces[0]]):
+        for n, ref in enumerate(weight_refs[: pieces[0]]):
             part = ref.shape[1]
-            at = pl.ds(pl.multiple_of((first_ref[1] ^ r) * part, part), part)
-            copies.append(pltpu.make_async_copy(ref, wi_ref.at[:, at, :], sems.at[r]))
+            place = (first_ref[1] ^ (n // 2)) * 2 + n % 2
+            at = pl.ds(pl.multiple_of(place * part, part), part)
+            copies.append(pltpu.make_async_copy(ref, wi_ref.at[:, at, :], sems.at[n]))
         for r, ref in enumerate(weight_refs[pieces[0] :]):
             part = ref.shape[1]
             place = lax.rem(first_ref[1] ^ r, pieces[1])
@@ -493,7 +685,7 @@
 
 def run_experts(x, u, ranks, in_pieces, down_pieces, router, places, which, compact):
     experts, part, hidden = in_pieces[0].shape
-    hidden //= 2
+    hidden = hidden // 2
     depth = part * len(in_pieces)
     rows = ranks[0].shape[2]
     steps = x[0].shape[0] // rows
@@ -541,48 +733,33 @@
 
 
 def product_kernel(me_ref, left_ref, right_ref, out_ref):
-    out_ref[0, 0] = t_matmul(left_ref[0], right_ref[0]).astype(BF16)
-
-
-def products(left, right, part, chosen, count, me, name):
+    out_ref[0] = t_matmul(left_ref[0], right_ref[0]).astype(BF16)
+
+
+def products(left, right, part, r, count, me, name):
     experts, rows, _ = left.shape
     columns = right.shape[2]
     wide = min(columns, 1024)
-    start, step = chosen[0], chosen[1] - chosen[0] if len(chosen) > 1 else 1
-
-    def place(e, k, j, me):
-        return (e, 0, lax.rem(me[0] ^ (start + step * k), count))
-
     return pl.pallas_call(
         product_kernel,
         grid_spec=pltpu.PrefetchScalarGridSpec(
             num_scalar_prefetch=1,
-            grid=(experts, len(chosen), columns // wide),
+            grid=(experts, columns // wide),
             in_specs=[
-                pl.BlockSpec((1, rows, part), place),
-                pl.BlockSpec((1, rows, wide), lambda e, k, j, me: (e, 0, j)),
+                pl.BlockSpec((1, rows, part), lambda e, j, me: (e, 0, lax.rem(me[0] ^ r, count))),
+                pl.BlockSpec((1, rows, wide), lambda e, j, me: (e, 0, j)),
             ],
-            out_specs=pl.BlockSpec((1, 1, part, wide), lambda e, k, j, me: (k, e, 0, j)),
+            out_specs=pl.BlockSpec((1, part, wide), lambda e, j, me: (e, 0, j)),
         ),
-        out_shape=jax.ShapeDtypeStruct((len(chosen), experts, part, columns), BF16),
+        out_shape=jax.ShapeDtypeStruct((experts, part, columns), BF16),
         compiler_params=pltpu.CompilerParams(vmem_limit_bytes=56 * MIB),
         cost_estimate=pl.CostEstimate(
-            flops=2 * len(chosen) * experts * rows * part * columns,
-            bytes_accessed=2 * experts * rows * (part * len(chosen) + columns),
+            flops=2 * experts * rows * part * columns,
+            bytes_accessed=2 * experts * rows * (part + columns),
             transcendentals=0,
         ),
         name=name,
     )(me, left, right)
-
-
-def rotate(values, cosine, sine, heads):
-    half = DH // 2
-    shaped = values.reshape(values.shape[0], heads, DH)
-    first, second = shaped[..., :half], shaped[..., half:]
-    cosine, sine = cosine[:, None, :], sine[:, None, :]
-    return jnp.concatenate(
-        [first * cosine - second * sine, second * cosine + first * sine], axis=-1
-    ).reshape(values.shape)
 
 
 def per_device(
@@ -616,8 +793,33 @@
     half_f = F // 2
     hidden_half = w_gate.shape[2] // 2
 
+    me = s.reshape(1).astype(jnp.int32)
+    f_at = f.reshape(1).astype(jnp.int32)
     tokens_low = tokens[0]
+    upstream_low = cotangent[0]
     inputs = tokens_low.astype(F32)
+    token_first = gather_first(tokens_low, S)
+    crossed = split_heads(w_query, w_key, w_value, S)
+    crossed = lax.all_to_all(crossed, "seq", split_axis=0, concat_axis=0, tiled=True)
+    half_at = f // half_f
+    quarter = w_gate.shape[1] // 4
+
+    def hidden_part(which, first, count):
+        return jnp.concatenate(
+            [
+                lax.dynamic_slice(
+                    weight, (0, first, which * hidden_half), (experts, count, hidden_half)
+                )
+                for weight in (w_gate, w_up)
+            ],
+            2,
+        )
+
+    near = {}
+    near[0, 0] = near_pieces(hidden_part(half_at, 0, 2 * quarter), F)
+    out_pieces = fsdp_pieces(w_output, F)
+    crossed, near[0, 0], out_pieces = tie(crossed, near[0, 0], out_pieces)
+    own_output = place_fsdp(out_pieces, f, 0).reshape(C, D)
     small = jnp.concatenate(
         [
             router.reshape(-1),
@@ -628,24 +830,25 @@
             routes[0].astype(BF16).reshape(-1),
         ]
     )
-    tokens_even, tokens_odd = gather_seq(tokens_low, S)
     small = gather_small(small, S, F, s, f).reshape(S, F, -1)
-
-    stacked = jnp.stack([w_query, w_key, w_value], 1).reshape(part, 3, S, C)
-    stacked = stacked.transpose(2, 0, 1, 3).reshape(S, part, 3 * C)
-    crossed = lax.all_to_all(stacked, "seq", split_axis=0, concat_axis=0, tiled=True)
-    output_ring = ring_pieces(w_output, F)
-    own_output = place_ring(output_ring, f, 0).reshape(C, D)
-    qkv_ring = ring_pieces(after(crossed, output_ring[-1]), F)
-    w_qkv = place_ring(qkv_ring, f, 1).reshape(D, 3 * C)
+    token_more = gather_more(tokens_low, token_first, S)
+    tokens_even, tokens_odd = gather_end(tokens_low, token_first, token_more, S)
+    qkv_pieces = fsdp_pieces(crossed, F)
+
+    def far_part(n, dep):
+        part = hidden_part(1 - half_at, n * quarter, quarter)
+        return swap(after(part, dep), "fsdp", F, half_f)
+
+    far = [far_part(0, qkv_pieces[half_f])]
+    w_qkv = place_fsdp(qkv_pieces, f, 1).reshape(D, 3 * C)
+    w_qkv, far[0] = tie(w_qkv, far[0])
 
     full_router = small[:, :, : part * E].reshape(D, E)
     gains = [
         small[:, :, part * (E + i) : part * (E + i + 1)].reshape(D).astype(F32) for i in range(4)
     ]
     gain_attn, gain_moe = gains[0], gains[1]
-    gain_query = lax.dynamic_slice_in_dim(gains[2], s * C, C, 0)
-    gain_key = lax.dynamic_slice_in_dim(gains[3], s * C, C, 0)
+    head_gain = lax.dynamic_slice(jnp.stack(gains[2:], 0), (0, s * C), (2, C))
     route_part = small[:, :, part * (E + 4) :].reshape(S, F, T, -1)
     expert_ids = s * experts + jnp.arange(experts, dtype=jnp.int32)
 
@@ -657,65 +860,74 @@
         ranks = jnp.where(chosen, ranks, -1)
         return ranks[: S // 2], ranks[S // 2 :]
 
-    half_at = f // half_f
-
-    def hidden_part(which):
-        at = which * hidden_half
-        return jnp.concatenate(
-            [lax.dynamic_slice_in_dim(weight, at, hidden_half, 2) for weight in (w_gate, w_up)], 2
-        )
-
-    in_pieces = {0: hidden_part(half_at)}
-    far_part = swap(after(hidden_part(1 - half_at), qkv_ring[-2]), "fsdp", F, half_f)
-    in_pieces[0] = after(in_pieces[0], qkv_ring[-1])
-    near_swaps(in_pieces, 0, F)
-
-    upstream_low = cotangent[0]
-    own_u = gather_seq(after(upstream_low, tokens_even), S)
-    out_even, out_odd = gather_seq(after(own_output, own_u[0]), S)
-
-    me = s.reshape(1).astype(jnp.int32)
-    normed_all, query_pre, key_pre, value_low, squares = project(
-        tokens_even, tokens_odd, w_qkv, gain_attn[None], me, T
-    )
     places = jnp.arange(L, dtype=jnp.int32).astype(F32)
     freqs = ROPE_BASE ** (-(jnp.arange(DH // 2, dtype=F32) * 2.0 / DH))
     angles = places[:, None] * freqs[None, :]
     cosine, sine = jnp.cos(angles), jnp.sin(angles)
-    factors = lax.rsqrt(sum_all(squares, "seq", S) / D + EPSILON)
-    query_n = query_pre * factors[0][:, None]
-    key_n = key_pre * factors[1][:, None]
-    query_low = rotate(query_n * gain_query, cosine, sine, heads).astype(BF16)
-    key_low = rotate(key_n * gain_key, cosine, sine, heads).astype(BF16)
+    cosine = jnp.concatenate([cosine, cosine], 1)
+    sine = jnp.concatenate([-sine, sine], 1)
+
+    out_first = gather_first(after(own_output, token_more), S)
+    far.append(far_part(1, far[-1]))
+    normed_even, normed_odd, query_pre, key_pre, value_low, squares = project(
+        tokens_even, tokens_odd, w_qkv, gain_attn[None], me, T
+    )
+    squares, out_first, far[1] = tie(squares, out_first, far[1])
+    squares = sum_all(squares, "seq", S)
+    out_more = gather_more(own_output, out_first, S)
+    far.append(far_part(2, far[-1]))
+    query_low, key_low = rope(query_pre, key_pre, squares, head_gain, cosine, sine)
+    query_low, out_more, far[2] = tie(query_low, out_more, far[2])
     seg_row = segments
     seg_col = segments.reshape(L, 1)
+    own_up_first = gather_first(after(upstream_low, out_more), S)
+    far.append(far_part(3, far[-1]))
     attended, lse = attention_forward(query_low, key_low, value_low, seg_row, seg_col)
+    attended, own_up_first, far[3] = tie(attended, own_up_first, far[3])
     attended_blocks = attended.reshape(S, T, C)
-    in_pieces[half_f] = after(far_part, attended)
-    near_swaps(in_pieces, half_f, F)
     come = lax.all_to_all(attended_blocks, "seq", split_axis=0, concat_axis=0, tiled=True)
     come = relative(come, s).transpose(1, 0, 2).reshape(T, D)
+    out_even, out_odd = gather_end(own_output, out_first, out_more, S)
+    own_up_more = gather_more(upstream_low, own_up_first, S)
+    near[0, 1] = near_pieces(after(hidden_part(half_at, 2 * quarter, 2 * quarter), far[3]), F)
     residual = inputs + matmul(come[:, : D // 2], out_even) + matmul(come[:, D // 2 :], out_odd)
-
     moe_factor = rms_factor(residual)
     residual_n = residual * moe_factor
     second_low = (residual_n * gain_moe).astype(BF16)
+    second_low, own_up_more, near[0, 1] = tie(second_low, own_up_more, near[0, 1])
+
+    own_u = gather_end(upstream_low, own_up_first, own_up_more, S)
     partner_low = swap(second_low, "fsdp", F, half_f)
-    own_x = gather_seq(second_low, S)
-    down_pieces = {0: after(w_down, own_x[0])}
-    near_swaps(down_pieces, 0, F)
-    other_x = gather_seq(after(partner_low, own_x[0]), S)
+    own_first = gather_first(second_low, S)
+    near[1, 0] = near_pieces(after(jnp.concatenate(far[:2], 1), second_low), F)
+    own_first, near[1, 0] = tie(own_first, near[1, 0])
+    own_more = gather_more(second_low, own_first, S)
+    near[1, 1] = near_pieces(after(jnp.concatenate(far[2:], 1), near[1, 0]), F)
+    own_x = gather_end(second_low, own_first, own_more, S)
+    partner_first = gather_first(after(partner_low, own_more), S)
+    partner_first, near[1, 1] = tie(partner_first, near[1, 1])
+    down_pieces = near_pieces(after(w_down, near[1, 1]), F)
     partner_up = swap(after(upstream_low, partner_low), "fsdp", F, half_f)
-    other_u = gather_seq(after(partner_up, other_x[0]), S)
-    logits = matmul(second_low, full_router)
-    router_probs = jax.nn.softmax(logits, axis=-1)
-    in_pieces = [in_pieces[r] for r in range(F)]
+    partner_more = gather_more(partner_low, partner_first, S)
+    other_x = gather_end(partner_low, partner_first, partner_more, S)
+    partner_up_first = gather_first(after(partner_up, partner_more), S)
+    partner_up_first, down_pieces, own_x, other_x = tie(
+        partner_up_first, down_pieces, own_x, other_x
+    )
+    partner_up_more = gather_more(partner_up, partner_up_first, S)
+    in_pieces = [
+        near[r // half_f, k][r % half_f] for r in range(F) for k in range(2)
+    ]
     down_pieces = [down_pieces[r] for r in range(half_f)]
     wide_router = jnp.pad(full_router, ((0, 0), (0, 128 - E)))
     expert_places = jnp.stack([s * experts, f]).astype(jnp.int32)
     own_parts = run_experts(
         own_x, own_u, ranks_of(f), in_pieces, down_pieces, wide_router, expert_places, 0, ()
     )
+    own_parts, partner_up_more = tie(own_parts, partner_up_more)
+    other_u = gather_end(partner_up, partner_up_first, partner_up_more, S)
+    own_got = swap(own_parts[3], "seq", S, 1)
+    own_out_got = swap(own_parts[1], "seq", S, 1)
     other_parts = run_experts(
         other_x,
         other_u,
@@ -727,13 +939,32 @@
         1,
         own_parts[6:],
     )
+    other_parts, own_got, own_out_got = tie(other_parts, own_got, own_out_got)
+    logits = matmul(second_low, full_router)
+    router_probs = jax.nn.softmax(logits, axis=-1)
+
     x_rows, u_rows, in_grads, hidden_gate = other_parts[6:]
-    own_got = swap(own_parts[3], "seq", S, 1)
-    other_got = swap(other_parts[3], "seq", S, 1)
-    other_rows = scatter_sum(other_parts[2], other_got, S).astype(BF16)
-    own_rows = scatter_sum(own_parts[2], after(own_got, other_rows), S)
-    back_rows = swap(other_rows, "fsdp", F, half_f)
-    row_grads = own_rows + back_rows.astype(F32)
+    down_part, in_part = w_down.shape[1], w_gate.shape[1]
+    other_got = swap(other_parts[2 + 1], "seq", S, 1)
+    other_sums = sum_first(other_parts[2], other_got, S)
+    hidden_gate = after(hidden_gate, other_got)
+    down_terms = {
+        r: products(hidden_gate, u_rows, down_part, r, half_f, f_at, "down_products")
+        for r in reversed(range(half_f))
+    }
+    other_out_got = swap(after(other_parts[1], other_got), "seq", S, 1)
+    other_rows = sum_last(other_sums, S, (down_terms, other_out_got)).astype(BF16)
+    half_rows = T // 2
+    back_first = swap(other_rows[:half_rows], "fsdp", F, half_f)
+    own_sums = sum_first(own_parts[2], after(own_got, other_rows), S, back_first)
+    back_last = swap(after(other_rows[half_rows:], back_first), "fsdp", F, half_f)
+    in_grads = after(in_grads, other_rows)
+    order = [r for r in reversed(range(F)) if r & 1] + [r for r in reversed(range(F)) if not r & 1]
+    in_terms = {
+        r: products(x_rows, in_grads, in_part, r, F, f_at, "in_products") for r in order
+    }
+    own_rows = sum_last(own_sums, S, [in_terms[r] for r in order])
+    row_grads = own_rows + jnp.concatenate([back_first, back_last], 0).astype(F32)
 
     def to_home(even, odd):
         return absolute(jnp.concatenate([even, odd], 0).transpose(0, 2, 1), s)
@@ -746,17 +977,6 @@
     ).reshape(S, 2, T * experts)
     gate_grads = gate_grads[:, 0] + swap(gate_grads[:, 1], "fsdp", F, half_f)
     gate_grads = gate_grads.reshape(S, T, experts).transpose(1, 0, 2).reshape(T, E)
-
-    f_at = f.reshape(1).astype(jnp.int32)
-    down_part = w_down.shape[1]
-    in_part = w_gate.shape[1]
-    hidden_gate = after(hidden_gate, other_got)
-    down_terms = products(
-        hidden_gate, u_rows, down_part, range(half_f), half_f, f_at, "down_products"
-    )
-    in_grads = after(in_grads, other_rows)
-    in_send = products(x_rows, in_grads, in_part, range(1, F, 2), F, f_at, "in_products_sent")
-    in_keep = products(x_rows, in_grads, in_part, range(0, F, 2), F, f_at, "in_products_kept")
 
     upstream = upstream_low.astype(F32)
     logit_grads = router_probs * (
@@ -772,70 +992,128 @@
     )
     branch_low = residual_grads.astype(BF16)
 
-    branch_even, branch_odd = gather_seq(branch_low, S)
+    def sum_near(terms, count, deps):
+        terms = {r: value.astype(F32) for r, value in terms.items()}
+        mask = 2
+        while mask < half_f:
+            stay = [r for r in terms if not r & mask]
+            terms = {
+                r: terms[r] + swap(terms[r | mask].astype(BF16), "fsdp", F, mask).astype(F32)
+                for r in stay
+            }
+            mask *= 2
+        return terms
+
+    down_got = {r: swap(down_terms[r], "fsdp", F, 1) for r in range(1, half_f, 2)}
+    branch_first = gather_first(branch_low, S)
+    branch_first, down_got = tie(branch_first, down_got)
+    odd = [r for r in range(F) if r & 1]
+    far_odd = [r for r in odd if r & half_f]
+    near_odd = [r for r in odd if not r & half_f]
+    in_got = {r: swap(after(in_terms[r], down_got), "fsdp", F, 1) for r in far_odd}
+    branch_more = gather_more(branch_low, branch_first, S)
+    branch_even, branch_odd = gather_end(branch_low, branch_first, branch_more, S)
+
     head_grads = jnp.concatenate(
         [matmul_t(branch_even, own_output), matmul_t(branch_odd, own_output)], 0
     ).astype(BF16)
     head_grads = absolute(head_grads.reshape(S, T, C), s).reshape(L, C)
-    attended_rel = relative(attended_blocks, s).reshape(2, L // 2, C)
+    head_grads, in_got = tie(head_grads, in_got)
+    far_terms = {
+        r ^ 1: in_terms[r ^ 1].astype(F32) + in_got[r].astype(F32) for r in far_odd
+    }
+    far_term = sum_near(far_terms, F, ())[half_f].astype(BF16)
+    eighth = far_term.shape[1] // 4
+
+    def far_sum(n, dep):
+        return swap(
+            after(far_term[:, n * eighth : (n + 1) * eighth], dep), "fsdp", F, half_f
+        )
+
+    far_sums = [far_sum(0, head_grads)]
+    near_got = {r: swap(after(in_terms[r], in_got), "fsdp", F, 1) for r in near_odd}
+    other_out_sums = sum_first(other_parts[0], after(other_out_got, branch_more), S)
     query_back, key_back, value_back = attention_backward(
         query_low, key_low, value_low, head_grads, lse, seg_row, seg_col
     )
-    attended_rel = after(attended_rel, query_back)
+    query_back, far_sums[0], near_got, other_out_sums = tie(
+        query_back, far_sums[0], near_got, other_out_sums
+    )
+    value_rel = relative(value_back.reshape(S, T, C), s).reshape(2, L // 2, C)
+
+    def weight_sum(even, odd):
+        term = (t_matmul(normed_even, even) + t_matmul(normed_odd, odd)).astype(BF16)
+        term = term.reshape(S, F, part, -1).transpose(1, 0, 2, 3)
+        return scatter_rows(term, f, F).astype(BF16)
+
+    far_sums.append(far_sum(1, far_sums[-1]))
+    means, gain_term = rope_means(
+        query_back, key_back, query_pre, key_pre, squares, head_gain, cosine, sine
+    )
+    other_outs = sum_last(other_out_sums, S).astype(BF16)
+    means, far_sums[1], other_outs = tie(sum_all(means, "seq", S), far_sums[1], other_outs)
+    far_sums.append(far_sum(2, far_sums[-1]))
+    pre_rel = rope_back(
+        (query_back, key_back, value_back),
+        query_pre,
+        key_pre,
+        squares,
+        means,
+        head_gain,
+        cosine,
+        sine,
+        me,
+        T,
+    ).reshape(2, L // 2, 3 * C)
+    normed_got = swap(matmul_t(pre_rel[1], w_qkv).astype(BF16), "seq", S, 1)
+    normed_kept = matmul_t(pre_rel[0], w_qkv).astype(BF16)
+    value_term = weight_sum(value_rel[0], value_rel[1])
+    normed_got, far_sums[2] = tie(normed_got, far_sums[2])
+    normed_sums = sum_first(normed_kept, normed_got, S)
+    far_sums.append(far_sum(3, far_sums[-1]))
+    turned_term = weight_sum(pre_rel[0][:, : 2 * C], pre_rel[1][:, : 2 * C])
+    normed_grads = sum_last(normed_sums, S)
+    outs_back = swap(after(other_outs, far_sums[2]), "fsdp", F, half_f).astype(F32)
+    own_out_sums = sum_first(own_parts[0], after(own_out_got, normed_sums), S)
+    own_outs = sum_last(own_out_sums, S)
+    mixed = (residual + own_outs + outs_back).astype(BF16)[None]
+
+    qkv_term = jnp.concatenate([turned_term, value_term], -1)
+    qkv_term = lax.all_to_all(qkv_term, "seq", split_axis=0, concat_axis=0, tiled=True)
+    qkv_term = qkv_term.reshape(S, part, 3, C).transpose(2, 1, 0, 3).reshape(3, part, D).astype(F32)
+    attended_rel = relative(after(attended_blocks, query_back), s).reshape(2, L // 2, C)
     output_term = t_matmul(attended_rel[0], branch_even) + t_matmul(attended_rel[1], branch_odd)
-    own_out_got = after(swap(after(own_parts[1], branch_even), "seq", S, 1), query_back)
-    other_out_got = after(swap(after(other_parts[1], own_out_got), "seq", S, 1), query_back)
-    other_outs = scatter_sum(other_parts[0], other_out_got, S).astype(BF16)
-    own_outs = scatter_sum(own_parts[0], after(own_out_got, other_outs), S)
-    down_sums = scatter_down(down_terms, half_f, F, query_back)
-    in_sums = sum_near(in_send, in_keep, F, query_back)
-    far_sums = swap(in_sums[half_f].astype(BF16), "fsdp", F, half_f).astype(F32)
+    grad_output = scatter_rows(output_term.astype(BF16).reshape(F, part, D), f, F)
+
+    near_terms = {
+        r ^ 1: in_terms[r ^ 1].astype(F32) + near_got[r].astype(F32) for r in near_odd
+    }
+    own_term = sum_near(near_terms, F, ())[0]
+    far_term = jnp.concatenate(far_sums, 1).astype(F32)
     first_half = half_at == 0
-    lower = jnp.where(first_half, in_sums[0], far_sums)
-    upper = jnp.where(first_half, far_sums, in_sums[0])
+    lower = jnp.where(first_half, own_term, far_term)
+    upper = jnp.where(first_half, far_term, own_term)
     grad_gate, grad_up = (
         jnp.concatenate([lower[..., at], upper[..., at]], axis=-1)
         for at in (slice(0, hidden_half), slice(hidden_half, 2 * hidden_half))
     )
-    other_outs = swap(other_outs, "fsdp", F, half_f).astype(F32)
-    mixed = (residual + own_outs + other_outs).astype(BF16)[None]
-    query_turned = rotate(query_back.astype(F32), cosine, -sine, heads)
-    key_turned = rotate(key_back.astype(F32), cosine, -sine, heads)
-    query_gain_term = jnp.sum(query_turned * query_n, axis=0)
-    key_gain_term = jnp.sum(key_turned * key_n, axis=0)
-    query_pulled = query_turned * gain_query
-    key_pulled = key_turned * gain_key
-    means = jnp.stack([jnp.sum(query_pulled * query_n, -1), jnp.sum(key_pulled * key_n, -1)], 0)
-    means = sum_all(means, "seq", S) / D
-    query_pre_low = (factors[0][:, None] * (query_pulled - query_n * means[0][:, None])).astype(BF16)
-    key_pre_low = (factors[1][:, None] * (key_pulled - key_n * means[1][:, None])).astype(BF16)
-    pre_low = jnp.concatenate([query_pre_low, key_pre_low, value_back], 1)
-    pre_rel = relative(pre_low.reshape(S, T, 3 * C), s).reshape(2, L // 2, 3 * C)
-    normed_got = swap(matmul_t(pre_rel[1], w_qkv).astype(BF16), "seq", S, 1)
-    normed_grads = scatter_sum(matmul_t(pre_rel[0], w_qkv).astype(BF16), normed_got, S)
-
-    def weight_sum(grads):
-        term = t_matmul(normed_all, grads).astype(BF16)
-        term = term.reshape(S, F, part, -1).transpose(1, 0, 2, 3)
-        return scatter_rows(term, f, F).astype(BF16)
-
-    value_term = weight_sum(value_back)
-    turned_term = weight_sum(pre_low[:, : 2 * C])
-    qkv_term = jnp.concatenate([turned_term, value_term], -1)
-    qkv_term = lax.all_to_all(qkv_term, "seq", split_axis=0, concat_axis=0, tiled=True)
-    qkv_term = qkv_term.reshape(S, part, 3, C).transpose(2, 1, 0, 3).reshape(3, part, D).astype(F32)
-    grad_output = scatter_rows(output_term.astype(BF16).reshape(F, part, D), f, F)
-    head_gains = lax.psum_scatter(
-        jnp.stack([query_gain_term, key_gain_term], 1), "fsdp", scatter_dimension=0, tiled=True
-    )
+    down_sums = {
+        r ^ 1: down_terms[r ^ 1].astype(F32) + down_got[r].astype(F32) for r in down_got
+    }
+    grad_down = sum_near(down_sums, half_f, ())[0]
+
     attn_factor = rms_factor(inputs)
     inputs_n = inputs * attn_factor
     attn_pulled = normed_grads * gain_attn
     grad_tokens = residual_grads + attn_factor * (
         attn_pulled - inputs_n * jnp.mean(attn_pulled * inputs_n, axis=-1, keepdims=True)
     )
-    gain_terms = jnp.concatenate([router_term, moe_gain_term[:, None]], 1)
-    gain_terms = lax.psum_scatter(gain_terms, ("seq", "fsdp"), scatter_dimension=0, tiled=True)
+    gain_terms = jnp.concatenate(
+        [router_term.reshape(S * F, part * E), moe_gain_term.reshape(S * F, part)], 1
+    )
+    gain_terms = sum_small(after(gain_terms, query_back), (("seq", S, s), ("fsdp", F, f)))
+    head_terms = gain_term.reshape(2, F, part).transpose(1, 0, 2).reshape(F, 2 * part)
+    head_terms = sum_small(head_terms, (("fsdp", F, f),))
     own_weights = jnp.stack([w_query, w_key, w_value], 0).astype(F32)
     grad_attn_gain = jnp.sum(qkv_term * own_weights, axis=(0, 2)) / attn_gain.astype(F32)
     return (
@@ -845,14 +1123,14 @@
         qkv_term[1],
         qkv_term[2],
         grad_output,
-        gain_terms[:, :E],
+        gain_terms[: part * E].reshape(part, E),
         grad_attn_gain,
-        gain_terms[:, E],
-        head_gains[:, 0],
-        head_gains[:, 1],
+        gain_terms[part * E :],
+        head_terms[:part],
+        head_terms[part:],
         grad_gate,
         grad_up,
-        down_sums,
+        grad_down,
     )
 
 

time: 1510 us -> 1280 us (0.85)
  waiting for transfers between devices: 807 us -> 597 us
  local copies, waits for them, and re-layouts: 163 us -> 132 us
  other arithmetic: 132 us -> 107 us
  starting transfers between devices: 101 us -> 125 us
  Pallas kernels: 233 us -> 255 us
    unnamed x4 -> x0, waiting for transfers between devices: 183 us -> none
    ppermute x89 -> x112, starting transfers between devices: 80.3 us -> 109 us  [swap(): return lax.ppermute(values, axis, [(i, i ^ mask) for i in range(size)])]
    dynamic_slice x18 -> x19, local copies, waits for them, and re-layouts: 23.5 us -> 4.72 us  [relative(): lax.dynamic_slice_in_dim(blocks, me ^ r, 1, 0)]
    pallas_call x3 -> x6, Pallas kernels: 50.9 us -> 59.8 us  [products(): pl.pallas_call(product_kernel, grid_spec=pltpu.PrefetchScalarGridSpec(num...]
    ppermute x89 -> x112, waiting for transfers between devices: 595 us -> 592 us  [swap(): return lax.ppermute(values, axis, [(i, i ^ mask) for i in range(size)])]
    convert_element_type x23 -> x14, other arithmetic: 35.3 us -> 33.9 us  [the longest x8 23.4 us: sum_first(): v.astype(BF16)]
    unnamed x306 -> x293, local copies, waits for them, and re-layouts: 66 us -> 65.9 us
  transfers between devices with their start and end apart: 101 -> 116, of which waited for: 60 -> 56; matrix products, arithmetic and copies ran while one was open for 21% -> 21% of each run, Pallas kernels for 11% -> 20%
where the time goes in v4:
time: 1280 us; the launch traced here: 1270 us
  waiting for transfers between devices  597 us (47%)
  Pallas kernels  255 us (20%)
  local copies, waits for them, and re-layouts  132 us (10%)
  starting transfers between devices  125 us (10%)
  other arithmetic  107 us (8%)
  matrix products  52.2 us (4%)
    ppermute x112, waiting for transfers between devices, swap(): return lax.ppermute(values, axis, [(i, i ^ mask) for i in range(size)])  592 us
    pallas_call x2, Pallas kernels, run_experts(): pl.pallas_call(partial(expert_kernel, pieces), grid=(steps,), in_specs=[p...  119 us
    ppermute x112, starting transfers between devices, swap(): return lax.ppermute(values, axis, [(i, i ^ mask) for i in range(size)])  109 us
    unnamed x293, local copies, waits for them, and re-layouts  65.9 us
    pallas_call x6, Pallas kernels, products(): pl.pallas_call(product_kernel, grid_spec=pltpu.PrefetchScalarGridSpec(num...  59.8 us
    pallas_call x1, Pallas kernels, attention_backward(): pl.pallas_call(partial(backward_kernel, span), grid=(heads, length // row...  27.7 us
  transfers between devices with their start and end apart: 116, of which 56 were waited for; matrix products, arithmetic and copies ran while one was open for 21% of the time, Pallas kernels for 20%

profile of v4, /device:TPU:0, one launch (start us, length us, event | category | flops | bytes accessed | tf_op | source)
XLA Modules:
  0.0 1272.3 jit_solution(13261336910908657906)
XLA Ops:
  89.9 32.6 %collective-permute-done.10 = bf16[8,64,768]{2,1,0:T(8,128)(2,1)S(1)} collective-permute-done((bf16[8,64,768]{2,1,0:T(8,128)(2,1)}, bf16[8,64,768]{2,1,0:T(8,128)(2,1)S(1)}, u32[]{:S(2)}, u32[]{:S(2)}) %collective-permute-start.10) | collective-permute-done | bytes 786464 | tf_op jit(solution)/shard_map/ppermute | solution.py:42
  126.1 25.4 %collective-permute-done.11 = bf16[8,64,768]{2,1,0:T(8,128)(2,1)S(1)} collective-permute-done((bf16[8,64,768]{2,1,0:T(8,128)(2,1)S(1)}, bf16[8,64,768]{2,1,0:T(8,128)(2,1)S(1)}, u32[]{:S(2)}, u32[]{:S(2)}) %collective-permute-start.11) | collective-permute-done | bytes 786464 | tf_op jit(solution)/shard_map/ppermute | solution.py:42
  153.4 12.7 project.1
  179.7 10.4 collective-permute-done.22
  209.4 21.4 %attend.1 = (bf16[2048,256]{1,0:T(8,128)(2,1)S(1)}, f32[2,1,2048]{2,1,0:T(1,128)S(1)}) custom-call(bf16[2048,256]{1,0:T(8,128)(2,1)S(1)} %get-tuple-element.185.q_ref, bf16[2048,256]{1,0:T(8,128)(2,1)S(1)} %copy-done.27, bf16[2048,256]{1,0:T(8,128)(2,1)S(1)} %copy-done.30, s32[1,2048]{1,0:T(1,128)S(1)} %copy-done.25, s32[2048,1]{1,0:T(8,128)S(1)} %copy.210.seg_col_ref), custom_call_target="tpu_custom_call" | custom-call | flops 2684354560 | bytes 4194304 | tf_op jit(solution)/shard_map/attend/pallas_call | solution.py:309
  268.3 12.4 collective-permute-done.33.refs_3_
  292.3 12.2 collective-permute-done.36
  304.9 17.5 %collective-permute-done.38.refs_6_ = bf16[2,256,1024]{2,1,0:T(8,128)(2,1)} collective-permute-done((bf16[2,256,1024]{2,1,0:T(8,128)(2,1)}, bf16[2,256,1024]{2,1,0:T(8,128)(2,1)}, u32[]{:S(2)}, u32[]{:S(2)}) %collective-permute-start.38) | collective-permute-done | bytes 1048608 | tf_op jit(solution)/shard_map/ppermute | solution.py:42
  346.5 9.9 collective-permute-done.43.refs_7_
  382.1 45.7 %collective-permute-done.35 = bf16[256,2048]{1,0:T(8,128)(2,1)} collective-permute-done((bf16[256,2048]{1,0:T(8,128)(2,1)}, bf16[256,2048]{1,0:T(8,128)(2,1)}, u32[]{:S(2)}, u32[]{:S(2)}) %collective-permute-start.35) | collective-permute-done | bytes 1048608 | tf_op jit(solution)/shard_map/ppermute | solution.py:42
  432.3 20.6 %collective-permute-done.46 = bf16[256,2048]{1,0:T(8,128)(2,1)} collective-permute-done((bf16[256,2048]{1,0:T(8,128)(2,1)}, bf16[256,2048]{1,0:T(8,128)(2,1)}, u32[]{:S(2)}, u32[]{:S(2)}) %collective-permute-start.46) | collective-permute-done | bytes 1048608 | tf_op jit(solution)/shard_map/ppermute | solution.py:42
  459.8 17.3 %collective-permute-done.47 = bf16[256,2048]{1,0:T(8,128)(2,1)} collective-permute-done((bf16[256,2048]{1,0:T(8,128)(2,1)}, bf16[256,2048]{1,0:T(8,128)(2,1)}, u32[]{:S(2)}, u32[]{:S(2)}) %collective-permute-start.47) | collective-permute-done | bytes 1048608 | tf_op jit(solution)/shard_map/ppermute | solution.py:42
  483.8 60.0 %experts.2 = (bf16[1024,2048]{1,0:T(8,128)(2,1)}, bf16[1024,2048]{1,0:T(8,128)(2,1)}, bf16[1024,2048]{1,0:T(8,128)(2,1)}, bf16[1024,2048]{1,0:T(8,128)(2,1)}, f3...) custom-call(s32[2]{0:T(128)} %pad_add_fusion.first_ref, ...), custom_call_target="tpu_custom_call" | custom-call | flops 38654705664 | bytes 62914560 | tf_op jit(solution)/shard_map/experts/pallas_call | solution.py:706
  551.3 12.2 collective-permute-done.54.ub_ref
  565.5 59.4 %experts.3 = (bf16[1024,2048]{1,0:T(8,128)(2,1)}, bf16[1024,2048]{1,0:T(8,128)(2,1)}, bf16[1024,2048]{1,0:T(8,128)(2,1)}, bf16[1024,2048]{1,0:T(8,128)(2,1)}, f3...) custom-call(s32[2]{0:T(128)} %pad_add_fusion.first_ref, ...), custom_call_target="tpu_custom_call", output_to_operand_aliasing={{6}: (18, {}), {7}: (19, {}), {8}: (20, {}), {9}: (21, {})} | custom-call | flops 38654705664 | bytes 62914560 | tf_op jit(solution)/shard_map/experts/pallas_call | solution.py:706
  635.3 12.9 %collective-permute-done.58 = bf16[128,2048]{1,0:T(8,128)(2,1)S(1)} collective-permute-done((bf16[128,2048]{1,0:T(8,128)(2,1)S(1)}, bf16[128,2048]{1,0:T(8,128)(2,1)S(1)}, u32[]{:S(2)}, u32[]{:S(2)}) %collective-permute-start.58) | collective-permute-done | bytes 524320 | tf_op jit(solution)/shard_map/ppermute | solution.py:42
  673.4 11.0 down_products.2
  684.4 11.1 down_products.3
  704.7 28.4 %collective-permute-done.69 = f32[8,512]{0,1:T(8,128)S(1)} collective-permute-done((f32[8,512]{0,1:T(8,128)S(1)}, f32[8,512]{0,1:T(8,128)S(1)}, u32[]{:S(2)}, u32[]{:S(2)}) %collective-permute-start.69) | collective-permute-done | bytes 16416 | tf_op jit(solution)/shard_map/ppermute | solution.py:42
  756.5 9.4 in_products.5
  779.2 9.6 in_products.7
  799.8 22.1 %collective-permute-done.70 = bf16[256,2048]{1,0:T(8,128)(2,1)S(1)} collective-permute-done((bf16[256,2048]{1,0:T(8,128)(2,1)S(1)}, bf16[256,2048]{1,0:T(8,128)(2,1)S(1)}, u32[]{:S(2)}, u32[]{:S(2)}) %collective-permute-start.70) | collective-permute-done | bytes 1048608 | tf_op jit(solution)/shard_map/ppermute | solution.py:42
  879.6 16.5 %collective-permute-done.76 = bf16[2,512,1024]{2,1,0:T(8,128)(2,1)S(1)} collective-permute-done((bf16[2,512,1024]{2,1,0:T(8,128)(2,1)}, bf16[2,512,1024]{2,1,0:T(8,128)(2,1)S(1)}, u32[]{:S(2)}, u32[]{:S(2)}) %collective-permute-start.76) | collective-permute-done | bytes 2097184 | tf_op jit(solution)/shard_map/ppermute | solution.py:42
  897.8 27.7 %attend_back.1 = (bf16[2048,256]{1,0:T(8,128)(2,1)S(1)}, bf16[2048,256]{1,0:T(8,128)(2,1)S(1)}, bf16[2048,256]{1,0:T(8,128)(2,1)S(1)}) custom-call(bf16[2048,256]{1,0:T(8,128)(2,1)S(1)} %get-tuple-element.185.q_ref, bf16[2048,256]{1,0:T(8,128)(2,1)S(1)} %copy-done.28, bf16[2048,256]{1,0:T(8,128)(2,1)} %copy-done.29, bf16[2048,256]{1,0:T(8,128)(2,1)} %bitcast.339, ...), custom_call_target="tpu_custom_call" | custom-call | flops 6710886400 | bytes 7340032 | tf_op jit(solution)/shard_map/attend_back/pallas_call | solution.py:341
  935.8 30.2 %collective-permute-done.100 = bf16[2,8,64,256]{3,2,1,0:T(8,128)(2,1)S(1)} collective-permute-done((bf16[2,8,64,256]{3,2,1,0:T(8,128)(2,1)S(1)}, bf16[2,8,64,256]{3,2,1,0:T(8,128)(2,1)S(1)}, u32[]{:S(2)}, u32[]{:S(2)}) %collective-permute-start.100) | collective-permute-done | bytes 524320 | tf_op jit(solution)/shard_map/ppermute | solution.py:42
  968.5 10.6 collective-permute-done.101
  999.0 11.6 collective-permute-done.104
  1052.2 28.1 %collective-permute-done.98 = bf16[2,8,64,512]{3,2,1,0:T(8,128)(2,1)S(1)} collective-permute-done((bf16[2,8,64,512]{3,2,1,0:T(8,128)(2,1)S(1)}, bf16[2,8,64,512]{3,2,1,0:T(8,128)(2,1)S(1)}, u32[]{:S(2)}, u32[]{:S(2)}) %collective-permute-start.98) | collective-permute-done | bytes 1048608 | tf_op jit(solution)/shard_map/ppermute | solution.py:42
  1088.7 31.8 %collective-permute-done.99 = bf16[1,8,64,512]{3,2,1,0:T(8,128)(2,1)} collective-permute-done((bf16[1,8,64,512]{3,2,1,0:T(8,128)(2,1)}, bf16[1,8,64,512]{3,2,1,0:T(8,128)(2,1)}, u32[]{:S(2)}, u32[]{:S(2)}) %collective-permute-start.99) | collective-permute-done | bytes 524320 | tf_op jit(solution)/shard_map/ppermute | solution.py:42
  1173.3 51.9 %collective-permute-done.111 = bf16[2,128,1024]{2,1,0:T(8,128)(2,1)S(1)} collective-permute-done((bf16[2,128,1024]{2,1,0:T(8,128)(2,1)S(1)}, bf16[2,128,1024]{2,1,0:T(8,128)(2,1)S(1)}, u32[]{:S(2)}, u32[]{:S(2)}) %collective-permute-start.111) | collective-permute-done | bytes 524320 | tf_op jit(solution)/shard_map/ppermute | solution.py:42
  1228.8 10.3 collective-permute-done.93
  1249.3 15.9 %collective-permute-done.94 = bf16[256,2048]{1,0:T(8,128)(2,1)S(1)} collective-permute-done((bf16[256,2048]{1,0:T(8,128)(2,1)S(1)}, bf16[256,2048]{1,0:T(8,128)(2,1)S(1)}, u32[]{:S(2)}, u32[]{:S(2)}) %collective-permute-start.94) | collective-permute-done | bytes 1048608 | tf_op jit(solution)/shard_map/ppermute | solution.py:42
  (776 shorter events, 560.0 us)
Async XLA Ops:
  0.7 77.5 %collective-permute-start.6 = (bf16[64,2048]{1,0:T(8,128)(2,1)}, bf16[64,2048]{1,0:T(8,128)(2,1)}, u32[]{:S(2)}, u32[]{:S(2)}) collective-permute-start(bf16[64,2048]{1,0:T(8,128)(2,1)} %param.23), channel_id=1, source_target_pairs={{0,1},{1,0},{2,3},{3,2},{4,5},{5,4},{6,7},{7,6},{8,9},{9,8},{10,11... | collective-permute-start | bytes 786440 | tf_op jit(solution)/shard_map/ppermute | solution.py:42
  3.7 73.2 %collective-permute-start.7 = (bf16[64,2048]{1,0:T(8,128)(2,1)}, bf16[64,2048]{1,0:T(8,128)(2,1)}, u32[]{:S(2)}, u32[]{:S(2)}) collective-permute-start(bf16[64,2048]{1,0:T(8,128)(2,1)} %param.23), channel_id=1, source_target_pairs={{0,2},{1,3},{2,0},{3,1},{4,6},{5,7},{6,4},{7,5},{8,10},{9,11},{10,... | collective-permute-start | bytes 786440 | tf_op jit(solution)/shard_map/ppermute | solution.py:42
  18.7 66.9 %all-to-all-start = ((bf16[8,64,768]{2,1,0:T(8,128)(2,1)}), bf16[8,64,768]{2,1,0:T(8,128)(2,1)}, u32[]{:S(2)}, u32[]{:S(2)}) async-start(bf16[8,64,768]{2,1,0:T(8,128)(2,1)} %split_heads.1), calls=%async_computation | async-start | bytes 1572864 | tf_op jit(solution)/shard_map/all_to_all | solution.py:803
  33.6 51.9 %collective-permute-start.5 = (bf16[2,256,1024]{2,1,0:T(8,128)(2,1)S(1)}, bf16[2,256,1024]{2,1,0:T(8,128)(2,1)}, u32[]{:S(2)}, u32[]{:S(2)}) collective-permute-start(bf16[2,256,1024]{2,1,0:T(8,128)(2,1)S(1)} %pad_maximum_fusion.5.refs_0_), channel_id=1, source_target_pairs={{0,1},{1,0},{2,3},{3,2},{4,5},{5,4},{6,7},{7,6},{8,9},{9,8},{10,11... | collective-permute-start | bytes 3145736 | tf_op jit(solution)/shard_map/ppermute | solution.py:42
  55.2 97.5 %collective-permute-start.4 = (bf16[1024,2048]{1,0:T(8,128)(2,1)}, bf16[1024,2048]{1,0:T(8,128)(2,1)}, u32[]{:S(2)}, u32[]{:S(2)}) collective-permute-start(bf16[1024,2048]{1,0:T(8,128)(2,1)} %constant_dynamic-update-slice_fusion.even_ref), channel_id=1, source_target_pairs={{0,4},{4,0},{8,12},{12,8},{16,20},{20,16},{24,28},{28,24},{1,5},{5... | collective-permute-start | bytes 12582920 | tf_op jit(solution)/shard_map/ppermute | solution.py:42
  124.0 42.0 %collective-permute-start.18 = (bf16[256,2048]{1,0:T(8,128)(2,1)S(1)}, bf16[256,2048]{1,0:T(8,128)(2,1)S(1)}, u32[]{:S(2)}, u32[]{:S(2)}) collective-permute-start(bf16[256,2048]{1,0:T(8,128)(2,1)S(1)} %bitcast.298), channel_id=1, source_target_pairs={{0,8},{4,12},{8,0},{12,4},{16,24},{20,28},{24,16},{28,20},{1,9},{5... | collective-permute-start | bytes 3145736 | tf_op jit(solution)/shard_map/ppermute | solution.py:42
  203.0 58.1 %collective-permute-start.30 = (bf16[1024,2048]{1,0:T(8,128)(2,1)}, bf16[1024,2048]{1,0:T(8,128)(2,1)}, u32[]{:S(2)}, u32[]{:S(2)}) collective-permute-start(bf16[1024,2048]{1,0:T(8,128)(2,1)} %constant_dynamic-update-slice_fusion.13), channel_id=1, source_target_pairs={{0,4},{4,0},{8,12},{12,8},{16,20},{20,16},{24,28},{28,24},{1,5},{5... | collective-permute-start | bytes 12582920 | tf_op jit(solution)/shard_map/ppermute | solution.py:42
  287.4 46.6 %collective-permute-start.34 = (bf16[256,2048]{1,0:T(8,128)(2,1)S(1)}, bf16[256,2048]{1,0:T(8,128)(2,1)S(1)}, u32[]{:S(2)}, u32[]{:S(2)}) collective-permute-start(bf16[256,2048]{1,0:T(8,128)(2,1)S(1)} %multiply_convert_fusion), channel_id=1, source_target_pairs={{0,2},{1,3},{2,0},{3,1},{4,6},{5,7},{6,4},{7,5},{8,10},{9,11},{10,... | collective-permute-start | bytes 3145736 | tf_op jit(solution)/shard_map/ppermute | solution.py:42
  341.2 142.6 %collective-permute-start.51 = (bf16[1024,2048]{1,0:T(8,128)(2,1)}, bf16[1024,2048]{1,0:T(8,128)(2,1)}, u32[]{:S(2)}, u32[]{:S(2)}) collective-permute-start(bf16[1024,2048]{1,0:T(8,128)(2,1)} %constant_dynamic-update-slice_fusion.28.ua_ref), channel_id=1, source_target_pairs={{0,4},{4,0},{8,12},{12,8},{16,20},{20,16},{24,28},{28,24},{1,5},{5... | collective-permute-start | bytes 12582920 | tf_op jit(solution)/shard_map/ppermute | solution.py:42
  360.0 118.3 %collective-permute-start.49 = (bf16[1024,2048]{1,0:T(8,128)(2,1)}, bf16[1024,2048]{1,0:T(8,128)(2,1)}, u32[]{:S(2)}, u32[]{:S(2)}) collective-permute-start(bf16[1024,2048]{1,0:T(8,128)(2,1)} %constant_dynamic-update-slice_fusion.18.xa_ref), channel_id=1, source_target_pairs={{0,4},{4,0},{8,12},{12,8},{16,20},{20,16},{24,28},{28,24},{1,5},{5... | collective-permute-start | bytes 12582920 | tf_op jit(solution)/shard_map/ppermute | solution.py:42
  375.4 102.9 %collective-permute-start.50 = (bf16[1024,2048]{1,0:T(8,128)(2,1)}, bf16[1024,2048]{1,0:T(8,128)(2,1)}, u32[]{:S(2)}, u32[]{:S(2)}) collective-permute-start(bf16[1024,2048]{1,0:T(8,128)(2,1)} %constant_dynamic-update-slice_fusion.23.xa_ref), channel_id=1, source_target_pairs={{0,4},{4,0},{8,12},{12,8},{16,20},{20,16},{24,28},{28,24},{1,5},{5... | collective-permute-start | bytes 12582920 | tf_op jit(solution)/shard_map/ppermute | solution.py:42
  378.5 49.3 %collective-permute-start.35 = (bf16[256,2048]{1,0:T(8,128)(2,1)}, bf16[256,2048]{1,0:T(8,128)(2,1)}, u32[]{:S(2)}, u32[]{:S(2)}) collective-permute-start(bf16[256,2048]{1,0:T(8,128)(2,1)} %bitcast.17), channel_id=1, source_target_pairs={{0,2},{1,3},{2,0},{3,1},{4,6},{5,7},{6,4},{7,5},{8,10},{9,11},{10,... | collective-permute-start | bytes 3145736 | tf_op jit(solution)/shard_map/ppermute | solution.py:42
  430.6 47.7 %collective-permute-start.48 = (bf16[2,256,2048]{2,1,0:T(8,128)(2,1)}, bf16[2,256,2048]{2,1,0:T(8,128)(2,1)}, u32[]{:S(2)}, u32[]{:S(2)}) collective-permute-start(bf16[2,256,2048]{2,1,0:T(8,128)(2,1)} %refs_8_.1), channel_id=1, source_target_pairs={{0,1},{1,0},{2,3},{3,2},{4,5},{5,4},{6,7},{7,6},{8,9},{9,8},{10,11... | collective-permute-start | bytes 6291464 | tf_op jit(solution)/shard_map/ppermute | solution.py:42
  480.2 68.3 %collective-permute-start.52 = (bf16[128,2048]{1,0:T(8,128)(2,1)}, bf16[128,2048]{1,0:T(8,128)(2,1)S(1)}, u32[]{:S(2)}, u32[]{:S(2)}) collective-permute-start(bf16[128,2048]{1,0:T(8,128)(2,1)} %slice.512), channel_id=1, source_target_pairs={{0,16},{4,20},{8,24},{12,28},{16,0},{20,4},{24,8},{28,12},{1,17},{... | collective-permute-start | bytes 1572872 | tf_op jit(solution)/shard_map/ppermute | solution.py:42
  483.2 65.3 %collective-permute-start.53 = (bf16[128,2048]{1,0:T(8,128)(2,1)}, bf16[128,2048]{1,0:T(8,128)(2,1)S(1)}, u32[]{:S(2)}, u32[]{:S(2)}) collective-permute-start(bf16[128,2048]{1,0:T(8,128)(2,1)} %slice.513), channel_id=1, source_target_pairs={{0,8},{4,12},{8,0},{12,4},{16,24},{20,28},{24,16},{28,20},{1,9},{5... | collective-permute-start | bytes 1572872 | tf_op jit(solution)/shard_map/ppermute | solution.py:42
  550.2 74.7 %collective-permute-start.55 = (bf16[1024,2048]{1,0:T(8,128)(2,1)}, bf16[1024,2048]{1,0:T(8,128)(2,1)}, u32[]{:S(2)}, u32[]{:S(2)}) collective-permute-start(bf16[1024,2048]{1,0:T(8,128)(2,1)} %get-tuple-element.255), channel_id=1, source_target_pairs={{0,4},{4,0},{8,12},{12,8},{16,20},{20,16},{24,28},{28,24},{1,5},{5... | collective-permute-start | bytes 12582920 | tf_op jit(solution)/shard_map/ppermute | solution.py:42
  550.7 74.2 %collective-permute-start.56 = (bf16[1024,2048]{1,0:T(8,128)(2,1)}, bf16[1024,2048]{1,0:T(8,128)(2,1)}, u32[]{:S(2)}, u32[]{:S(2)}) collective-permute-start(bf16[1024,2048]{1,0:T(8,128)(2,1)} %get-tuple-element.256), channel_id=1, source_target_pairs={{0,4},{4,0},{8,12},{12,8},{16,20},{20,16},{24,28},{28,24},{1,5},{5... | collective-permute-start | bytes 12582920 | tf_op jit(solution)/shard_map/ppermute | solution.py:42
  632.5 63.1 %collective-permute-start.60 = (bf16[1024,2048]{1,0:T(8,128)(2,1)}, bf16[1024,2048]{1,0:T(8,128)(2,1)}, u32[]{:S(2)}, u32[]{:S(2)}) collective-permute-start(bf16[1024,2048]{1,0:T(8,128)(2,1)} %get-tuple-element.266), channel_id=1, source_target_pairs={{0,4},{4,0},{8,12},{12,8},{16,20},{20,16},{24,28},{28,24},{1,5},{5... | collective-permute-start | bytes 12582920 | tf_op jit(solution)/shard_map/ppermute | solution.py:42
  733.3 66.5 %collective-permute-start.72 = (bf16[2,256,2048]{2,1,0:T(8,128)(2,1)}, bf16[2,256,2048]{2,1,0:T(8,128)(2,1)}, u32[]{:S(2)}, u32[]{:S(2)}) collective-permute-start(bf16[2,256,2048]{2,1,0:T(8,128)(2,1)} %down_products.3), channel_id=1, source_target_pairs={{0,1},{1,0},{2,3},{3,2},{4,5},{5,4},{6,7},{7,6},{8,9},{9,8},{10,11... | collective-permute-start | bytes 6291464 | tf_op jit(solution)/shard_map/ppermute | solution.py:42
  845.8 50.2 %collective-permute-start.76 = (bf16[2,512,1024]{2,1,0:T(8,128)(2,1)}, bf16[2,512,1024]{2,1,0:T(8,128)(2,1)S(1)}, u32[]{:S(2)}, u32[]{:S(2)}) collective-permute-start(bf16[2,512,1024]{2,1,0:T(8,128)(2,1)} %in_products.4), channel_id=1, source_target_pairs={{0,1},{1,0},{2,3},{3,2},{4,5},{5,4},{6,7},{7,6},{8,9},{9,8},{10,11... | collective-permute-start | bytes 6291464 | tf_op jit(solution)/shard_map/ppermute | solution.py:42
  896.1 83.2 %collective-permute-start.78 = (bf16[2,512,1024]{2,1,0:T(8,128)(2,1)S(1)}, bf16[2,512,1024]{2,1,0:T(8,128)(2,1)S(1)}, u32[]{:S(2)}, u32[]{:S(2)}) collective-permute-start(bf16[2,512,1024]{2,1,0:T(8,128)(2,1)S(1)} %copy-done.54), channel_id=1, source_target_pairs={{0,1},{1,0},{2,3},{3,2},{4,5},{5,4},{6,7},{7,6},{8,9},{9,8},{10,11... | collective-permute-start | bytes 6291464 | tf_op jit(solution)/shard_map/ppermute | solution.py:42
  935.5 43.7 %collective-permute-start.77 = (bf16[2,128,1024]{2,1,0:T(8,128)(2,1)S(1)}, bf16[2,128,1024]{2,1,0:T(8,128)(2,1)S(1)}, u32[]{:S(2)}, u32[]{:S(2)}) collective-permute-start(bf16[2,128,1024]{2,1,0:T(8,128)(2,1)S(1)} %get-tuple-element.290), channel_id=1, source_target_pairs={{0,2},{1,3},{2,0},{3,1},{4,6},{5,7},{6,4},{7,5},{8,10},{9,11},{10,... | collective-permute-start | bytes 1572872 | tf_op jit(solution)/shard_map/ppermute | solution.py:42
  983.2 51.9 %collective-permute-start.84 = (bf16[2,128,1024]{2,1,0:T(8,128)(2,1)}, bf16[2,128,1024]{2,1,0:T(8,128)(2,1)}, u32[]{:S(2)}, u32[]{:S(2)}) collective-permute-start(bf16[2,128,1024]{2,1,0:T(8,128)(2,1)} %get-tuple-element.299), channel_id=1, source_target_pairs={{0,2},{1,3},{2,0},{3,1},{4,6},{5,7},{6,4},{7,5},{8,10},{9,11},{10,... | collective-permute-start | bytes 1572872 | tf_op jit(solution)/shard_map/ppermute | solution.py:42
  983.2 48.1 %collective-permute-start.86 = (bf16[256,2048]{1,0:T(8,128)(2,1)}, bf16[256,2048]{1,0:T(8,128)(2,1)}, u32[]{:S(2)}, u32[]{:S(2)}) collective-permute-start(bf16[256,2048]{1,0:T(8,128)(2,1)} %pad_maximum_fusion.17), channel_id=1, source_target_pairs={{0,16},{4,20},{8,24},{12,28},{16,0},{20,4},{24,8},{28,12},{1,17},{... | collective-permute-start | bytes 3145736 | tf_op jit(solution)/shard_map/ppermute | solution.py:42
  984.3 47.1 %collective-permute-start.85 = (bf16[256,2048]{1,0:T(8,128)(2,1)}, bf16[256,2048]{1,0:T(8,128)(2,1)}, u32[]{:S(2)}, u32[]{:S(2)}) collective-permute-start(bf16[256,2048]{1,0:T(8,128)(2,1)} %pad_maximum_fusion.16), channel_id=1, source_target_pairs={{0,8},{4,12},{8,0},{12,4},{16,24},{20,28},{24,16},{28,20},{1,9},{5... | collective-permute-start | bytes 3145736 | tf_op jit(solution)/shard_map/ppermute | solution.py:42
  1046.3 101.8 %collective-permute-start.87 = (bf16[1024,2048]{1,0:T(8,128)(2,1)}, bf16[1024,2048]{1,0:T(8,128)(2,1)}, u32[]{:S(2)}, u32[]{:S(2)}) collective-permute-start(bf16[1024,2048]{1,0:T(8,128)(2,1)} %convolution_convert_fusion.1), channel_id=1, source_target_pairs={{0,4},{4,0},{8,12},{12,8},{16,20},{20,16},{24,28},{28,24},{1,5},{5... | collective-permute-start | bytes 12582920 | tf_op jit(solution)/shard_map/ppermute | solution.py:42
  1085.8 62.2 %collective-permute-start.88 = (bf16[2,128,1024]{2,1,0:T(8,128)(2,1)}, bf16[2,128,1024]{2,1,0:T(8,128)(2,1)}, u32[]{:S(2)}, u32[]{:S(2)}) collective-permute-start(bf16[2,128,1024]{2,1,0:T(8,128)(2,1)} %get-tuple-element.305), channel_id=1, source_target_pairs={{0,2},{1,3},{2,0},{3,1},{4,6},{5,7},{6,4},{7,5},{8,10},{9,11},{10,... | collective-permute-start | bytes 1572872 | tf_op jit(solution)/shard_map/ppermute | solution.py:42
  1155.6 111.2 %collective-permute-start.95 = (bf16[256,2048]{1,0:T(8,128)(2,1)S(1)}, bf16[256,2048]{1,0:T(8,128)(2,1)S(1)}, u32[]{:S(2)}, u32[]{:S(2)}) collective-permute-start(bf16[256,2048]{1,0:T(8,128)(2,1)S(1)} %copy-done.63), channel_id=1, source_target_pairs={{0,2},{1,3},{2,0},{3,1},{4,6},{5,7},{6,4},{7,5},{8,10},{9,11},{10,... | collective-permute-start | bytes 3145736 | tf_op jit(solution)/shard_map/ppermute | solution.py:42
  1155.6 69.6 %collective-permute-start.111 = (bf16[2,128,1024]{2,1,0:T(8,128)(2,1)S(1)}, bf16[2,128,1024]{2,1,0:T(8,128)(2,1)S(1)}, u32[]{:S(2)}, u32[]{:S(2)}) collective-permute-start(bf16[2,128,1024]{2,1,0:T(8,128)(2,1)S(1)} %copy-done.83), channel_id=1, source_target_pairs={{0,2},{1,3},{2,0},{3,1},{4,6},{5,7},{6,4},{7,5},{8,10},{9,11},{10,... | collective-permute-start | bytes 1572872 | tf_op jit(solution)/shard_map/ppermute | solution.py:42
  1167.3 81.2 %collective-permute-start.97 = (bf16[256,2048]{1,0:T(8,128)(2,1)S(1)}, bf16[256,2048]{1,0:T(8,128)(2,1)S(1)}, u32[]{:S(2)}, u32[]{:S(2)}) collective-permute-start(bf16[256,2048]{1,0:T(8,128)(2,1)S(1)} %pad_maximum_fusion.19), channel_id=1, source_target_pairs={{0,16},{4,20},{8,24},{12,28},{16,0},{20,4},{24,8},{28,12},{1,17},{... | collective-permute-start | bytes 3145736 | tf_op jit(solution)/shard_map/ppermute | solution.py:42
  1167.9 80.7 %collective-permute-start.96 = (bf16[256,2048]{1,0:T(8,128)(2,1)S(1)}, bf16[256,2048]{1,0:T(8,128)(2,1)S(1)}, u32[]{:S(2)}, u32[]{:S(2)}) collective-permute-start(bf16[256,2048]{1,0:T(8,128)(2,1)S(1)} %pad_maximum_fusion.18), channel_id=1, source_target_pairs={{0,8},{4,12},{8,0},{12,4},{16,24},{20,28},{24,16},{28,20},{1,9},{5... | collective-permute-start | bytes 3145736 | tf_op jit(solution)/shard_map/ppermute | solution.py:42
  1172.9 55.9 %collective-permute-start.91 = (bf16[128,2048]{1,0:T(8,128)(2,1)S(1)}, bf16[128,2048]{1,0:T(8,128)(2,1)S(1)}, u32[]{:S(2)}, u32[]{:S(2)}) collective-permute-start(bf16[128,2048]{1,0:T(8,128)(2,1)S(1)} %get-tuple-element.418), channel_id=1, source_target_pairs={{0,16},{4,20},{8,24},{12,28},{16,0},{20,4},{24,8},{28,12},{1,17},{... | collective-permute-start | bytes 1572872 | tf_op jit(solution)/shard_map/ppermute | solution.py:42
  (193 other events, 3926.6 us)

commit v5 on v4

--- a/solution.py
+++ b/solution.py
@@ -95,35 +95,56 @@
     return jnp.concatenate([lax.dynamic_slice_in_dim(blocks, at, 1, 0) for at in places], 0)
 
 
-def sum_first(even, got, size, dep=()):
+def sum_cores(even, got, size):
     rows = even.shape[0] // (size // 2)
     half = rows // 2
 
-    def part(r, first, count):
-        at = slice(r // 2 * rows + first, r // 2 * rows + first + count)
+    def part(r, first):
+        at = slice(r // 2 * rows + first, r // 2 * rows + first + half)
         return even[at].astype(F32) + got[at].astype(F32)
 
-    sums = {r: [part(r, 0, half), part(r, half, half)] for r in range(0, size, 2)}
+    return {r: [part(r, 0), part(r, half)] for r in range(0, size, 2)}
+
+
+def sum_first(sums, size):
+    sums = {r: list(value) for r, value in sums.items()}
+    come = {}
     for r in range(size - 2, 0, -2):
         if r != low_bit(r):
             up, down = high_bit(r), low_bit(r)
-            upper = after(swap(sums[r][0].astype(BF16), "seq", size, up), dep)
-            lower = after(swap(sums[r][1].astype(BF16), "seq", size, down), dep)
-            sums[r ^ up][0] += upper.astype(F32)
-            sums[r ^ down][1] += lower.astype(F32)
-            del sums[r]
-    return {
-        r: jnp.concatenate([v.astype(BF16) if r else v for v in value], 0)
-        for r, value in sums.items()
+            for (goal, k, _), piece in come.items():
+                if goal == r:
+                    sums[r][k] += piece.astype(F32)
+            upper, lower = tie(sums[r][0].astype(BF16), sums[r][1].astype(BF16))
+            come[r ^ up, 0, r] = swap(upper, "seq", size, up)
+            come[r ^ down, 1, r] = swap(lower, "seq", size, down)
+    return come
+
+
+def sum_more(sums, come, size):
+    sums = {r: list(value) for r, value in sums.items() if r == 0 or r == low_bit(r)}
+    for (goal, k, _), piece in come.items():
+        if goal in sums:
+            sums[goal][k] += piece.astype(F32)
+    singles = {
+        r: jnp.concatenate([v.astype(BF16) for v in value], 0) for r, value in sums.items() if r
     }
-
-
-def sum_last(sums, size, dep=()):
-    total = sums[0]
-    for r in sums:
-        if r:
-            total += after(swap(sums[r], "seq", size, r), dep).astype(F32)
+    return tie(singles)[0], jnp.concatenate(sums[0], 0)
+
+
+def sum_last(singles, size):
+    return {r: swap(value, "seq", size, r) for r, value in singles.items()}
+
+
+def add_all(total, pieces):
+    for piece in pieces.values():
+        total += piece.astype(F32)
     return total
+
+
+def quarters(values, axis):
+    step = values.shape[axis] // 4
+    return [lax.slice_in_dim(values, k * step, (k + 1) * step, axis=axis) for k in range(4)]
 
 
 def sum_all(values, axis, size):
@@ -191,19 +212,25 @@
     return values[0]
 
 
-def scatter_rows(partial_sum, me, size):
-    sums = {
-        r: lax.dynamic_index_in_dim(partial_sum, me ^ r, 0, keepdims=False).astype(F32)
-        for r in range(size)
-    }
-    mask = 1
+def by_index(partial_sum, me, size):
+    order = [r for r in range(size) if r & 1] + [r for r in range(size) if not r & 1]
+    return jnp.concatenate([lax.dynamic_slice_in_dim(partial_sum, me ^ r, 1, 0) for r in order], 0)
+
+
+def sum_even(stacked, got, size):
+    return (stacked[size // 2 :].astype(F32) + got.astype(F32)).astype(BF16)
+
+
+def sum_rest(stacked, size):
+    mask = 2
+    values = stacked.astype(F32)
     while mask < size:
-        stay = [r for r in sums if not r & mask]
-        moved = jnp.stack([sums[r | mask].astype(BF16) for r in stay], 0)
-        got = swap(moved, "fsdp", size, mask).astype(F32)
-        sums = {r: sums[r] + got[i] for i, r in enumerate(stay)}
+        count = values.shape[0] // 2
+        pairs = values.reshape((count, 2) + values.shape[1:])
+        got = swap(pairs[:, 1].astype(BF16), "fsdp", size, mask)
+        values = pairs[:, 0] + got.astype(F32)
         mask *= 2
-    return sums[0]
+    return values[0]
 
 
 def allowed_keys(seg_row, seg_col, first_query, first_key, rows, span, half_window):
@@ -609,8 +636,10 @@
     )(me, *grads, query_pre, key_pre, squares, means, gains, cosine, sine)
 
 
-def expert_kernel(pieces, first_ref, xa_ref, xb_ref, ua_ref, ub_ref, ra_ref, rb_ref, router_ref, *refs):
-    weight_refs = refs[: sum(pieces)]
+def expert_kernel(
+    in_places, down_places, first_ref, xa_ref, xb_ref, ua_ref, ub_ref, ra_ref, rb_ref, router_ref, *refs
+):
+    weight_refs = refs[: len(in_places) + len(down_places)]
     (ya_ref, yb_ref, za_ref, zb_ref, ga_ref, gb_ref, xc_ref, uc_ref, dg_ref, hid_ref) = refs[-13:-3]
     wi_ref, wd_ref, sems = refs[-3:]
     experts, _, hidden = hid_ref.shape
@@ -619,16 +648,11 @@
     @pl.when(pl.program_id(0) == 0)
     def _():
         copies = []
-        for n, ref in enumerate(weight_refs[: pieces[0]]):
-            part = ref.shape[1]
-            place = (first_ref[1] ^ (n // 2)) * 2 + n % 2
-            at = pl.ds(pl.multiple_of(place * part, part), part)
-            copies.append(pltpu.make_async_copy(ref, wi_ref.at[:, at, :], sems.at[n]))
-        for r, ref in enumerate(weight_refs[pieces[0] :]):
-            part = ref.shape[1]
-            place = lax.rem(first_ref[1] ^ r, pieces[1])
-            at = pl.ds(pl.multiple_of(place * part, part), part)
-            copies.append(pltpu.make_async_copy(ref, wd_ref.at[:, at, :], sems.at[pieces[0] + r]))
+        for n, (ref, (r, first, part)) in enumerate(zip(weight_refs, in_places + down_places)):
+            goal = wi_ref if n < len(in_places) else wd_ref
+            place = lax.rem(first_ref[1] ^ r, goal.shape[1] // part)
+            at = pl.ds(pl.multiple_of(place * part + first, ref.shape[1]), ref.shape[1])
+            copies.append(pltpu.make_async_copy(ref, goal.at[:, at, :], sems.at[n]))
         for copy in copies:
             copy.start()
         for copy in copies:
@@ -683,10 +707,13 @@
             )
 
 
-def run_experts(x, u, ranks, in_pieces, down_pieces, router, places, which, compact):
-    experts, part, hidden = in_pieces[0].shape
+def run_experts(x, u, ranks, in_pieces, down_pieces, router, places, which, compact, parts):
+    experts, _, hidden = in_pieces[0][2].shape
     hidden = hidden // 2
-    depth = part * len(in_pieces)
+    depth = x[0].shape[1]
+    in_places = [(r, at, parts[0]) for r, at, _ in in_pieces]
+    down_places = [(r, at, parts[1]) for r, at, _ in down_pieces]
+    pieces = [array for _, _, array in in_pieces + down_pieces]
     rows = ranks[0].shape[2]
     steps = x[0].shape[0] // rows
     token = pl.BlockSpec((rows, depth), lambda i: (i, 0))
@@ -701,16 +728,15 @@
     gates = shape((steps, experts, rows), F32)
     count = 4 * steps * CAP
     wide = shape((experts, count, depth), BF16)
-    pieces = (len(in_pieces), len(down_pieces))
-    inputs = [places, *x, *u, *ranks, router, *in_pieces, *down_pieces]
+    inputs = [places, *x, *u, *ranks, router, *pieces]
     return pl.pallas_call(
-        partial(expert_kernel, pieces),
+        partial(expert_kernel, in_places, down_places),
         grid=(steps,),
         in_specs=[pl.BlockSpec(memory_space=pltpu.SMEM)]
         + [token] * 4
         + [rank] * 2
         + [pl.BlockSpec(router.shape, lambda i: (0, 0), pipeline_mode=pl.Buffered(1))]
-        + [anywhere] * (sum(pieces) + len(compact)),
+        + [anywhere] * (len(pieces) + len(compact)),
         out_specs=[token] * 4 + [rank] * 2 + [slots(depth)] * 2 + [slots(2 * hidden), slots(hidden)],
         out_shape=[tokens] * 4
         + [gates] * 2
@@ -719,7 +745,7 @@
         scratch_shapes=[
             pltpu.VMEM((experts, depth, 2 * hidden), BF16),
             pltpu.VMEM((experts, hidden, depth), BF16),
-            pltpu.SemaphoreType.DMA((sum(pieces),)),
+            pltpu.SemaphoreType.DMA((len(pieces),)),
         ],
         input_output_aliases={len(inputs) + i: 6 + i for i in range(len(compact))},
         compiler_params=pltpu.CompilerParams(vmem_limit_bytes=60 * MIB),
@@ -795,14 +821,13 @@
 
     me = s.reshape(1).astype(jnp.int32)
     f_at = f.reshape(1).astype(jnp.int32)
+    half_at = f // half_f
     tokens_low = tokens[0]
     upstream_low = cotangent[0]
     inputs = tokens_low.astype(F32)
-    token_first = gather_first(tokens_low, S)
-    crossed = split_heads(w_query, w_key, w_value, S)
-    crossed = lax.all_to_all(crossed, "seq", split_axis=0, concat_axis=0, tiled=True)
-    half_at = f // half_f
-    quarter = w_gate.shape[1] // 4
+    half_rows = T // 2
+    in_part, down_part = w_gate.shape[1], w_down.shape[1]
+    quarter = in_part // 4
 
     def hidden_part(which, first, count):
         return jnp.concatenate(
@@ -815,11 +840,29 @@
             2,
         )
 
-    near = {}
-    near[0, 0] = near_pieces(hidden_part(half_at, 0, 2 * quarter), F)
-    out_pieces = fsdp_pieces(w_output, F)
-    crossed, near[0, 0], out_pieces = tie(crossed, near[0, 0], out_pieces)
-    own_output = place_fsdp(out_pieces, f, 0).reshape(C, D)
+    def far_swap(values, *dep):
+        return swap(after(values, dep), "fsdp", F, half_f)
+
+    def near_swap(values, *dep):
+        return near_pieces(after(values, dep), F)
+
+    token_first = gather_first(tokens_low, S)
+    crossed = split_heads(w_query, w_key, w_value, S)
+    crossed = lax.all_to_all(crossed, "seq", split_axis=0, concat_axis=0, tiled=True)
+    near_own = [near_swap(hidden_part(half_at, 0, 2 * quarter))]
+    crossed, near_own[0] = tie(crossed, near_own[0])
+
+    token_more = gather_more(tokens_low, token_first, S)
+    tokens_even, tokens_odd = gather_end(tokens_low, token_first, token_more, S)
+    qkv_pieces = {0: crossed}
+    for r in range(1, F):
+        low = low_bit(r)
+        qkv_pieces[r] = swap(qkv_pieces[r ^ low], "fsdp", F, low)
+        if r == half_f:
+            own_up_first = gather_first(after(upstream_low, token_more), S)
+            qkv_pieces[r], own_up_first = tie(qkv_pieces[r], own_up_first)
+            own_up_more = gather_more(upstream_low, own_up_first, S)
+            partner_up = [far_swap(upstream_low[:half_rows], qkv_pieces[r])]
     small = jnp.concatenate(
         [
             router.reshape(-1),
@@ -830,18 +873,10 @@
             routes[0].astype(BF16).reshape(-1),
         ]
     )
-    small = gather_small(small, S, F, s, f).reshape(S, F, -1)
-    token_more = gather_more(tokens_low, token_first, S)
-    tokens_even, tokens_odd = gather_end(tokens_low, token_first, token_more, S)
-    qkv_pieces = fsdp_pieces(crossed, F)
-
-    def far_part(n, dep):
-        part = hidden_part(1 - half_at, n * quarter, quarter)
-        return swap(after(part, dep), "fsdp", F, half_f)
-
-    far = [far_part(0, qkv_pieces[half_f])]
+    small = gather_small(after(small, qkv_pieces[half_f]), S, F, s, f).reshape(S, F, -1)
     w_qkv = place_fsdp(qkv_pieces, f, 1).reshape(D, 3 * C)
-    w_qkv, far[0] = tie(w_qkv, far[0])
+    w_qkv, partner_up[0], own_up_more, small = tie(w_qkv, partner_up[0], own_up_more, small)
+    own_u = gather_end(upstream_low, own_up_first, own_up_more, S)
 
     full_router = small[:, :, : part * E].reshape(D, E)
     gains = [
@@ -867,116 +902,180 @@
     cosine = jnp.concatenate([cosine, cosine], 1)
     sine = jnp.concatenate([-sine, sine], 1)
 
-    out_first = gather_first(after(own_output, token_more), S)
-    far.append(far_part(1, far[-1]))
+    def far_part(n, *dep):
+        return far_swap(hidden_part(1 - half_at, n * quarter, quarter), *dep)
+
+    partner_up.append(far_swap(upstream_low[half_rows:], w_qkv))
+    near_own.append(near_swap(hidden_part(half_at, 2 * quarter, quarter), w_qkv))
+    out_pieces = fsdp_pieces(after(w_output, w_qkv), F)
     normed_even, normed_odd, query_pre, key_pre, value_low, squares = project(
         tokens_even, tokens_odd, w_qkv, gain_attn[None], me, T
     )
-    squares, out_first, far[1] = tie(squares, out_first, far[1])
+    squares, partner_up[1], near_own[1], out_pieces = tie(
+        squares, partner_up[1], near_own[1], out_pieces
+    )
+    partner_up = jnp.concatenate(partner_up, 0)
+    own_output = place_fsdp(out_pieces, f, 0).reshape(C, D)
+
+    out_first = gather_first(own_output, S)
+    far = [far_part(0, squares)]
+    near_own.append(near_swap(hidden_part(half_at, 3 * quarter, quarter), squares))
     squares = sum_all(squares, "seq", S)
-    out_more = gather_more(own_output, out_first, S)
-    far.append(far_part(2, far[-1]))
     query_low, key_low = rope(query_pre, key_pre, squares, head_gain, cosine, sine)
-    query_low, out_more, far[2] = tie(query_low, out_more, far[2])
+    query_low, out_first, far[0], near_own[2] = tie(query_low, out_first, far[0], near_own[2])
+
     seg_row = segments
     seg_col = segments.reshape(L, 1)
-    own_up_first = gather_first(after(upstream_low, out_more), S)
-    far.append(far_part(3, far[-1]))
+    out_more = gather_more(own_output, out_first, S)
+    far.append(far_part(1, query_low))
+    down_rows = quarters(w_down, 1)
+    down = [near_swap(down_rows[0], query_low)]
     attended, lse = attention_forward(query_low, key_low, value_low, seg_row, seg_col)
-    attended, own_up_first, far[3] = tie(attended, own_up_first, far[3])
+    attended, out_more, far[1], down[0] = tie(attended, out_more, far[1], down[0])
     attended_blocks = attended.reshape(S, T, C)
     come = lax.all_to_all(attended_blocks, "seq", split_axis=0, concat_axis=0, tiled=True)
+    out_even, out_odd = gather_end(own_output, out_first, out_more, S)
+    far.append(far_part(2, attended))
+    near_far = [near_swap(far[0], attended)]
+    come, far[2], near_far[0] = tie(come, far[2], near_far[0])
+    far.append(far_part(3, come))
+    near_far.append(near_swap(far[1], come))
+    partner_up_first = gather_first(after(partner_up, come), S)
     come = relative(come, s).transpose(1, 0, 2).reshape(T, D)
-    out_even, out_odd = gather_end(own_output, out_first, out_more, S)
-    own_up_more = gather_more(upstream_low, own_up_first, S)
-    near[0, 1] = near_pieces(after(hidden_part(half_at, 2 * quarter, 2 * quarter), far[3]), F)
     residual = inputs + matmul(come[:, : D // 2], out_even) + matmul(come[:, D // 2 :], out_odd)
     moe_factor = rms_factor(residual)
     residual_n = residual * moe_factor
     second_low = (residual_n * gain_moe).astype(BF16)
-    second_low, own_up_more, near[0, 1] = tie(second_low, own_up_more, near[0, 1])
-
-    own_u = gather_end(upstream_low, own_up_first, own_up_more, S)
-    partner_low = swap(second_low, "fsdp", F, half_f)
+    second_low, far[3], near_far[1], partner_up_first = tie(
+        second_low, far[3], near_far[1], partner_up_first
+    )
+
     own_first = gather_first(second_low, S)
-    near[1, 0] = near_pieces(after(jnp.concatenate(far[:2], 1), second_low), F)
-    own_first, near[1, 0] = tie(own_first, near[1, 0])
+    partner_low = [far_swap(second_low[:half_rows])]
+    near_far.append(near_swap(far[2], second_low))
+    own_first, partner_low[0], near_far[2] = tie(own_first, partner_low[0], near_far[2])
     own_more = gather_more(second_low, own_first, S)
-    near[1, 1] = near_pieces(after(jnp.concatenate(far[2:], 1), near[1, 0]), F)
+    partner_low.append(far_swap(second_low[half_rows:], own_first))
+    near_far.append(near_swap(far[3], own_first))
+    own_more, partner_low[1], near_far[3] = tie(own_more, partner_low[1], near_far[3])
+    partner_low = jnp.concatenate(partner_low, 0)
     own_x = gather_end(second_low, own_first, own_more, S)
     partner_first = gather_first(after(partner_low, own_more), S)
-    partner_first, near[1, 1] = tie(partner_first, near[1, 1])
-    down_pieces = near_pieces(after(w_down, near[1, 1]), F)
-    partner_up = swap(after(upstream_low, partner_low), "fsdp", F, half_f)
+    down.append(near_swap(down_rows[1], own_more))
+    down.append(near_swap(down_rows[2], own_more))
+    partner_first, down[1], down[2], own_x = tie(partner_first, down[1], down[2], own_x)
     partner_more = gather_more(partner_low, partner_first, S)
+    down.append(near_swap(down_rows[3], partner_first))
+    partner_more, down[3] = tie(partner_more, down[3])
+    partner_up_more = gather_more(after(partner_up, partner_more), partner_up_first, S)
     other_x = gather_end(partner_low, partner_first, partner_more, S)
-    partner_up_first = gather_first(after(partner_up, partner_more), S)
-    partner_up_first, down_pieces, own_x, other_x = tie(
-        partner_up_first, down_pieces, own_x, other_x
-    )
-    partner_up_more = gather_more(partner_up, partner_up_first, S)
-    in_pieces = [
-        near[r // half_f, k][r % half_f] for r in range(F) for k in range(2)
+    in_pieces = []
+    for r in range(F):
+        for n, rows in enumerate(near_own if r < half_f else near_far):
+            first = (0, 2, 3)[n] if r < half_f else n
+            in_pieces.append((r, first * quarter, rows[r % half_f]))
+    down_pieces = [
+        (r, n * (down_part // 4), down[n][r]) for r in range(half_f) for n in range(4)
     ]
-    down_pieces = [down_pieces[r] for r in range(half_f)]
     wide_router = jnp.pad(full_router, ((0, 0), (0, 128 - E)))
     expert_places = jnp.stack([s * experts, f]).astype(jnp.int32)
+    parts = (in_part, down_part)
+    own_ranks, other_ranks = ranks_of(f), ranks_of(f ^ half_f)
+    own_x, other_x, partner_up_more, own_ranks, other_ranks = tie(
+        own_x, other_x, partner_up_more, own_ranks, other_ranks
+    )
+    other_u = gather_end(partner_up, partner_up_first, partner_up_more, S)
     own_parts = run_experts(
-        own_x, own_u, ranks_of(f), in_pieces, down_pieces, wide_router, expert_places, 0, ()
-    )
-    own_parts, partner_up_more = tie(own_parts, partner_up_more)
-    other_u = gather_end(partner_up, partner_up_first, partner_up_more, S)
+        own_x, own_u, own_ranks, in_pieces, down_pieces, wide_router, expert_places, 0, (), parts
+    )
+    own_parts, other_u = tie(own_parts, other_u)
     own_got = swap(own_parts[3], "seq", S, 1)
     own_out_got = swap(own_parts[1], "seq", S, 1)
     other_parts = run_experts(
         other_x,
         other_u,
-        ranks_of(f ^ half_f),
+        other_ranks,
         in_pieces,
         down_pieces,
         wide_router,
         expert_places,
         1,
         own_parts[6:],
+        parts,
     )
     other_parts, own_got, own_out_got = tie(other_parts, own_got, own_out_got)
     logits = matmul(second_low, full_router)
     router_probs = jax.nn.softmax(logits, axis=-1)
 
     x_rows, u_rows, in_grads, hidden_gate = other_parts[6:]
-    down_part, in_part = w_down.shape[1], w_gate.shape[1]
-    other_got = swap(other_parts[2 + 1], "seq", S, 1)
-    other_sums = sum_first(other_parts[2], other_got, S)
-    hidden_gate = after(hidden_gate, other_got)
-    down_terms = {
-        r: products(hidden_gate, u_rows, down_part, r, half_f, f_at, "down_products")
-        for r in reversed(range(half_f))
-    }
-    other_out_got = swap(after(other_parts[1], other_got), "seq", S, 1)
-    other_rows = sum_last(other_sums, S, (down_terms, other_out_got)).astype(BF16)
-    half_rows = T // 2
-    back_first = swap(other_rows[:half_rows], "fsdp", F, half_f)
-    own_sums = sum_first(own_parts[2], after(own_got, other_rows), S, back_first)
-    back_last = swap(after(other_rows[half_rows:], back_first), "fsdp", F, half_f)
-    in_grads = after(in_grads, other_rows)
-    order = [r for r in reversed(range(F)) if r & 1] + [r for r in reversed(range(F)) if not r & 1]
-    in_terms = {
-        r: products(x_rows, in_grads, in_part, r, F, f_at, "in_products") for r in order
-    }
-    own_rows = sum_last(own_sums, S, [in_terms[r] for r in order])
-    row_grads = own_rows + jnp.concatenate([back_first, back_last], 0).astype(F32)
+    in_terms, down_terms = {}, {}
+
+    def in_products(r, *dep):
+        in_terms[r] = products(
+            x_rows, after(in_grads, dep), in_part, r, F, f_at, "in_products"
+        )
+
+    odd = [r for r in range(F) if r & 1]
+    far_odd = [r for r in odd if r & half_f]
+    near_odd = [r for r in odd if not r & half_f]
 
     def to_home(even, odd):
         return absolute(jnp.concatenate([even, odd], 0).transpose(0, 2, 1), s)
 
     gate_grads = jnp.stack(
         [to_home(own_parts[4], own_parts[5]), to_home(other_parts[4], other_parts[5])], 1
-    )
-    gate_grads = lax.all_to_all(
-        gate_grads.reshape(S, -1), "seq", split_axis=0, concat_axis=0, tiled=True
-    ).reshape(S, 2, T * experts)
-    gate_grads = gate_grads[:, 0] + swap(gate_grads[:, 1], "fsdp", F, half_f)
+    ).reshape(S, -1)
+    other_got = swap(other_parts[3], "seq", S, 1)
+    for r in far_odd:
+        in_products(r)
+    gate_grads = lax.all_to_all(gate_grads, "seq", split_axis=0, concat_axis=0, tiled=True)
+    other_got, in_terms, gate_grads = tie(other_got, in_terms, gate_grads)
+    sent = {r: quarters(in_terms[r], 1) for r in far_odd}
+
+    def send_in(n, *dep):
+        return {r: swap(after(sent[r][n], dep), "fsdp", F, 1) for r in sent}
+
+    other_sums = sum_cores(other_parts[2], other_got, S)
+    come = sum_first(other_sums, S)
+    far_got = [send_in(0, other_got)]
+    other_out_got = swap(after(other_parts[1], other_got), "seq", S, 1)
+    come, far_got[0], other_out_got = tie(come, far_got[0], other_out_got)
+    gate_grads = gate_grads.reshape(S, 2, T * experts)
+    partner_grads = far_swap(gate_grads[:, 1], come)
+    singles, other_total = sum_more(other_sums, come, S)
+    come = sum_last(singles, S)
+    far_got.append(send_in(1, far_got[0]))
+    far_got.append(send_in(2, far_got[0]))
+    for r in range(half_f):
+        down_terms[r] = products(
+            after(hidden_gate, singles), u_rows, down_part, r, half_f, f_at, "down_products"
+        )
+    come, far_got[1], far_got[2], partner_grads, down_terms = tie(
+        come, far_got[1], far_got[2], partner_grads, down_terms
+    )
+    other_rows = add_all(other_total, come).astype(BF16)
+    gate_grads = gate_grads[:, 0] + partner_grads
     gate_grads = gate_grads.reshape(S, T, experts).transpose(1, 0, 2).reshape(T, E)
+    back = [far_swap(other_rows[:half_rows])]
+    own_sums = sum_cores(own_parts[2], after(own_got, other_rows), S)
+    come = sum_first(own_sums, S)
+    far_got.append(send_in(3, other_rows))
+    for r in far_odd:
+        in_products(r ^ 1, other_rows)
+    come, back[0], far_got[3], in_terms = tie(come, back[0], far_got[3], in_terms)
+    back.append(far_swap(other_rows[half_rows:], come))
+    singles, own_total = sum_more(own_sums, come, S)
+    come = sum_last(singles, S)
+    down_sent = {r: quarters(down_terms[r], 1) for r in range(1, half_f, 2)}
+
+    def send_down(n, *dep):
+        return {r: swap(after(down_sent[r][n], dep), "fsdp", F, 1) for r in down_sent}
+
+    down_got = [send_down(0, singles)]
+    for r in near_odd:
+        in_products(r, singles)
+    come, back[1], down_got[0], in_terms = tie(come, back[1], down_got[0], in_terms)
+    row_grads = add_all(own_total, come) + jnp.concatenate(back, 0).astype(F32)
 
     upstream = upstream_low.astype(F32)
     logit_grads = router_probs * (
@@ -984,75 +1083,82 @@
     )
     router_wide = full_router.astype(F32)
     second_grads = row_grads + jnp.dot(logit_grads, router_wide.T, precision=HIGHEST)
-    router_term = jnp.dot(second_low.astype(F32).T, logit_grads, precision=HIGHEST)
-    moe_gain_term = jnp.sum(second_grads * residual_n, axis=0)
     pulled = second_grads * gain_moe
     residual_grads = upstream + moe_factor * (
         pulled - residual_n * jnp.mean(pulled * residual_n, axis=-1, keepdims=True)
     )
     branch_low = residual_grads.astype(BF16)
 
-    def sum_near(terms, count, deps):
-        terms = {r: value.astype(F32) for r, value in terms.items()}
+    def sum_near(terms):
         mask = 2
         while mask < half_f:
-            stay = [r for r in terms if not r & mask]
             terms = {
                 r: terms[r] + swap(terms[r | mask].astype(BF16), "fsdp", F, mask).astype(F32)
-                for r in stay
+                for r in terms
+                if not r & mask
             }
             mask *= 2
-        return terms
-
-    down_got = {r: swap(down_terms[r], "fsdp", F, 1) for r in range(1, half_f, 2)}
+        (total,) = terms.values()
+        return total
+
+    def far_sum(n, *dep):
+        terms = {
+            r ^ 1: quarters(in_terms[r ^ 1], 1)[n].astype(F32) + far_got[n][r].astype(F32)
+            for r in far_odd
+        }
+        return far_swap(sum_near(terms).astype(BF16), *dep)
+
     branch_first = gather_first(branch_low, S)
-    branch_first, down_got = tie(branch_first, down_got)
-    odd = [r for r in range(F) if r & 1]
-    far_odd = [r for r in odd if r & half_f]
-    near_odd = [r for r in odd if not r & half_f]
-    in_got = {r: swap(after(in_terms[r], down_got), "fsdp", F, 1) for r in far_odd}
+    far_sums = [far_sum(0, branch_low)]
+    down_got.append(send_down(1, branch_low))
+    for r in near_odd:
+        in_products(r ^ 1, branch_low)
+    branch_first, far_sums[0], down_got[1], in_terms = tie(
+        branch_first, far_sums[0], down_got[1], in_terms
+    )
     branch_more = gather_more(branch_low, branch_first, S)
+    far_sums.append(far_sum(1, branch_first))
+    down_got.append(send_down(2, branch_first))
     branch_even, branch_odd = gather_end(branch_low, branch_first, branch_more, S)
 
     head_grads = jnp.concatenate(
         [matmul_t(branch_even, own_output), matmul_t(branch_odd, own_output)], 0
     ).astype(BF16)
     head_grads = absolute(head_grads.reshape(S, T, C), s).reshape(L, C)
-    head_grads, in_got = tie(head_grads, in_got)
-    far_terms = {
-        r ^ 1: in_terms[r ^ 1].astype(F32) + in_got[r].astype(F32) for r in far_odd
-    }
-    far_term = sum_near(far_terms, F, ())[half_f].astype(BF16)
-    eighth = far_term.shape[1] // 4
-
-    def far_sum(n, dep):
-        return swap(
-            after(far_term[:, n * eighth : (n + 1) * eighth], dep), "fsdp", F, half_f
-        )
-
-    far_sums = [far_sum(0, head_grads)]
-    near_got = {r: swap(after(in_terms[r], in_got), "fsdp", F, 1) for r in near_odd}
-    other_out_sums = sum_first(other_parts[0], after(other_out_got, branch_more), S)
+    head_grads, far_sums[1], down_got[2] = tie(head_grads, far_sums[1], down_got[2])
+    far_sums.append(far_sum(2, head_grads))
+    down_got.append(send_down(3, head_grads))
+    other_out_sums = sum_cores(other_parts[0], after(other_out_got, head_grads), S)
+    come = sum_first(other_out_sums, S)
     query_back, key_back, value_back = attention_backward(
         query_low, key_low, value_low, head_grads, lse, seg_row, seg_col
     )
-    query_back, far_sums[0], near_got, other_out_sums = tie(
-        query_back, far_sums[0], near_got, other_out_sums
-    )
+    query_back, far_sums[2], down_got[3], come = tie(query_back, far_sums[2], down_got[3], come)
+
+    singles, other_total = sum_more(other_out_sums, come, S)
+    come = sum_last(singles, S)
+    far_sums.append(far_sum(3, query_back))
+    attended_rel = relative(after(attended_blocks, singles), s).reshape(2, L // 2, C)
+    output_term = t_matmul(attended_rel[0], branch_even) + t_matmul(attended_rel[1], branch_odd)
+    output_term = by_index(output_term.astype(BF16).reshape(F, part, D), f, F)
+    output_got = swap(output_term[: F // 2], "fsdp", F, 1)
     value_rel = relative(value_back.reshape(S, T, C), s).reshape(2, L // 2, C)
 
-    def weight_sum(even, odd):
+    def weight_term(even, odd):
         term = (t_matmul(normed_even, even) + t_matmul(normed_odd, odd)).astype(BF16)
-        term = term.reshape(S, F, part, -1).transpose(1, 0, 2, 3)
-        return scatter_rows(term, f, F).astype(BF16)
-
-    far_sums.append(far_sum(1, far_sums[-1]))
+        return by_index(term.reshape(S, F, part, -1).transpose(1, 0, 2, 3), f, F)
+
     means, gain_term = rope_means(
         query_back, key_back, query_pre, key_pre, squares, head_gain, cosine, sine
     )
-    other_outs = sum_last(other_out_sums, S).astype(BF16)
-    means, far_sums[1], other_outs = tie(sum_all(means, "seq", S), far_sums[1], other_outs)
-    far_sums.append(far_sum(2, far_sums[-1]))
+    means = sum_all(means, "seq", S)
+    value_term = weight_term(value_rel[0], value_rel[1])
+    means, come, far_sums[3], output_got, value_term = tie(
+        means, come, far_sums[3], output_got, value_term
+    )
+    other_outs = add_all(other_total, come).astype(BF16)
+    outs_back = [far_swap(other_outs[:half_rows])]
+    value_got = swap(value_term[: F // 2], "fsdp", F, 1)
     pre_rel = rope_back(
         (query_back, key_back, value_back),
         query_pre,
@@ -1067,28 +1173,48 @@
     ).reshape(2, L // 2, 3 * C)
     normed_got = swap(matmul_t(pre_rel[1], w_qkv).astype(BF16), "seq", S, 1)
     normed_kept = matmul_t(pre_rel[0], w_qkv).astype(BF16)
-    value_term = weight_sum(value_rel[0], value_rel[1])
-    normed_got, far_sums[2] = tie(normed_got, far_sums[2])
-    normed_sums = sum_first(normed_kept, normed_got, S)
-    far_sums.append(far_sum(3, far_sums[-1]))
-    turned_term = weight_sum(pre_rel[0][:, : 2 * C], pre_rel[1][:, : 2 * C])
-    normed_grads = sum_last(normed_sums, S)
-    outs_back = swap(after(other_outs, far_sums[2]), "fsdp", F, half_f).astype(F32)
-    own_out_sums = sum_first(own_parts[0], after(own_out_got, normed_sums), S)
-    own_outs = sum_last(own_out_sums, S)
+    normed_got, normed_kept, outs_back[0], value_got = tie(
+        normed_got, normed_kept, outs_back[0], value_got
+    )
+
+    normed_sums = sum_cores(normed_kept, normed_got, S)
+    come = sum_first(normed_sums, S)
+    value_sum = sum_rest(sum_even(value_term, value_got, F), F)
+    turned_term = weight_term(
+        after(pre_rel[0][:, : 2 * C], normed_got), after(pre_rel[1][:, : 2 * C], normed_got)
+    )
+    come, turned_term, value_sum = tie(come, turned_term, value_sum)
+    near_sent = {r: quarters(in_terms[r], 1) for r in near_odd}
+
+    def send_near(n, *dep):
+        return {r: swap(after(near_sent[r][n], dep), "fsdp", F, 1) for r in near_sent}
+
+    turned_got = swap(turned_term[: F // 2], "fsdp", F, 1)
+    singles, normed_total = sum_more(normed_sums, come, S)
+    come = sum_last(singles, S)
+    outs_back.append(far_swap(other_outs[half_rows:], turned_term))
+    come, turned_got, outs_back[1] = tie(come, turned_got, outs_back[1])
+    normed_grads = add_all(normed_total, come)
+    turned_sum = sum_rest(sum_even(turned_term, turned_got, F), F)
+    near_got = [send_near(0, turned_got), send_near(1, turned_got)]
+    own_out_sums = sum_cores(own_parts[0], after(own_out_got, turned_got), S)
+    come = sum_first(own_out_sums, S)
+    turned_sum, come, near_got = tie(turned_sum, come, near_got)
+    near_got.extend([send_near(2, turned_sum), send_near(3, turned_sum)])
+    singles, own_total = sum_more(own_out_sums, come, S)
+    own_outs = add_all(own_total, sum_last(singles, S))
+    outs_back = jnp.concatenate(outs_back, 0).astype(F32)
     mixed = (residual + own_outs + outs_back).astype(BF16)[None]
 
-    qkv_term = jnp.concatenate([turned_term, value_term], -1)
+    qkv_term = jnp.concatenate([turned_sum, value_sum], -1).astype(BF16)
     qkv_term = lax.all_to_all(qkv_term, "seq", split_axis=0, concat_axis=0, tiled=True)
     qkv_term = qkv_term.reshape(S, part, 3, C).transpose(2, 1, 0, 3).reshape(3, part, D).astype(F32)
-    attended_rel = relative(after(attended_blocks, query_back), s).reshape(2, L // 2, C)
-    output_term = t_matmul(attended_rel[0], branch_even) + t_matmul(attended_rel[1], branch_odd)
-    grad_output = scatter_rows(output_term.astype(BF16).reshape(F, part, D), f, F)
-
-    near_terms = {
-        r ^ 1: in_terms[r ^ 1].astype(F32) + near_got[r].astype(F32) for r in near_odd
-    }
-    own_term = sum_near(near_terms, F, ())[0]
+    grad_output = sum_rest(sum_even(output_term, output_got, F), F)
+
+    near_got = {r: jnp.concatenate([got[r] for got in near_got], 1) for r in near_odd}
+    own_term = sum_near(
+        {r ^ 1: in_terms[r ^ 1].astype(F32) + near_got[r].astype(F32) for r in near_odd}
+    )
     far_term = jnp.concatenate(far_sums, 1).astype(F32)
     first_half = half_at == 0
     lower = jnp.where(first_half, own_term, far_term)
@@ -1097,10 +1223,10 @@
         jnp.concatenate([lower[..., at], upper[..., at]], axis=-1)
         for at in (slice(0, hidden_half), slice(hidden_half, 2 * hidden_half))
     )
-    down_sums = {
-        r ^ 1: down_terms[r ^ 1].astype(F32) + down_got[r].astype(F32) for r in down_got
-    }
-    grad_down = sum_near(down_sums, half_f, ())[0]
+    down_got = {r: jnp.concatenate([got[r] for got in down_got], 1) for r in down_sent}
+    grad_down = sum_near(
+        {r ^ 1: down_terms[r ^ 1].astype(F32) + down_got[r].astype(F32) for r in down_sent}
+    )
 
     attn_factor = rms_factor(inputs)
     inputs_n = inputs * attn_factor
@@ -1108,12 +1234,15 @@
     grad_tokens = residual_grads + attn_factor * (
         attn_pulled - inputs_n * jnp.mean(attn_pulled * inputs_n, axis=-1, keepdims=True)
     )
+    late_grads, late_logits = after(second_grads, turned_got), after(logit_grads, turned_got)
+    router_term = jnp.dot(second_low.astype(F32).T, late_logits, precision=HIGHEST)
+    moe_gain_term = jnp.sum(late_grads * residual_n, axis=0)
     gain_terms = jnp.concatenate(
         [router_term.reshape(S * F, part * E), moe_gain_term.reshape(S * F, part)], 1
     )
-    gain_terms = sum_small(after(gain_terms, query_back), (("seq", S, s), ("fsdp", F, f)))
+    gain_terms = sum_small(gain_terms, (("seq", S, s), ("fsdp", F, f)))
     head_terms = gain_term.reshape(2, F, part).transpose(1, 0, 2).reshape(F, 2 * part)
-    head_terms = sum_small(head_terms, (("fsdp", F, f),))
+    head_terms = sum_small(after(head_terms, turned_got), (("fsdp", F, f),))
     own_weights = jnp.stack([w_query, w_key, w_value], 0).astype(F32)
     grad_attn_gain = jnp.sum(qkv_term * own_weights, axis=(0, 2)) / attn_gain.astype(F32)
     return (

time: 1280 us -> 1150 us (0.90)
  waiting for transfers between devices: 597 us -> 390 us
  local copies, waits for them, and re-layouts: 132 us -> 178 us
  starting transfers between devices: 125 us -> 157 us
    ppermute x112 -> x130, waiting for transfers between devices: 592 us -> 389 us  [swap(): return lax.ppermute(values, axis, [(i, i ^ mask) for i in range(size)])]
    ppermute x112 -> x130, starting transfers between devices: 109 us -> 141 us  [swap(): return lax.ppermute(values, axis, [(i, i ^ mask) for i in range(size)])]
    convert_element_type x21 -> x10, other arithmetic: 39.6 us -> 25.3 us  [the longest x5 11.4 us: sum_first(): upper, lower = tie(sums[r][0].astype(BF16), sums[r][1].astype(BF16))]
    unnamed x293 -> x388, local copies, waits for them, and re-layouts: 65.9 us -> 74.1 us
  transfers between devices with their start and end apart: 116 -> 134, of which waited for: 56 -> 60; matrix products, arithmetic and copies ran while one was open for 21% -> 24% of each run, Pallas kernels for 20% -> 22%
where the time goes in v5:
time: 1150 us; the launch traced here: 1140 us
  waiting for transfers between devices  390 us (34%)
  Pallas kernels  255 us (22%)
  local copies, waits for them, and re-layouts  178 us (15%)
  starting transfers between devices  157 us (14%)
  other arithmetic  116 us (10%)
  matrix products  41.7 us (4%)
    ppermute x130, waiting for transfers between devices, swap(): return lax.ppermute(values, axis, [(i, i ^ mask) for i in range(size)])  389 us
    ppermute x130, starting transfers between devices, swap(): return lax.ppermute(values, axis, [(i, i ^ mask) for i in range(size)])  141 us
    pallas_call x2, Pallas kernels, run_experts(): pl.pallas_call(partial(expert_kernel, in_places, down_places), grid=(step...  119 us
    unnamed x388, local copies, waits for them, and re-layouts  74.1 us
    pallas_call x6, Pallas kernels, products(): pl.pallas_call(product_kernel, grid_spec=pltpu.PrefetchScalarGridSpec(num...  60.5 us
    pallas_call x1, Pallas kernels, attention_backward(): pl.pallas_call(partial(backward_kernel, span), grid=(heads, length // row...  28.3 us
  transfers between devices with their start and end apart: 134, of which 60 were waited for; matrix products, arithmetic and copies ran while one was open for 24% of the time, Pallas kernels for 22%

profile of v5, /device:TPU:0, one launch (start us, length us, event | category | flops | bytes accessed | tf_op | source)
XLA Modules:
  0.0 1140.9 jit_solution(8059614126890012283)
XLA Ops:
  17.5 10.4 collective-permute-done
  62.2 10.2 collective-permute-done.7
  87.8 29.2 %collective-permute-done.17 = bf16[8,3328]{1,0:T(8,128)(2,1)S(1)} collective-permute-done((bf16[8,3328]{1,0:T(8,128)(2,1)S(1)}, bf16[8,3328]{1,0:T(8,128)(2,1)S(1)}, u32[]{:S(2)}, u32[]{:S(2)}) %collective-permute-start.17) | collective-permute-done | bytes 53280 | tf_op jit(solution)/shard_map/ppermute | solution.py:42
  133.3 15.1 %collective-permute-done.11 = bf16[128,2048]{1,0:T(8,128)(2,1)S(1)} collective-permute-done((bf16[128,2048]{1,0:T(8,128)(2,1)}, bf16[128,2048]{1,0:T(8,128)(2,1)S(1)}, u32[]{:S(2)}, u32[]{:S(2)}) %collective-permute-start.11) | collective-permute-done | bytes 524320 | tf_op jit(solution)/shard_map/ppermute | solution.py:42
  155.8 8.9 collective-permute-done.22
  164.8 12.7 %project.1 = (bf16[1024,2048]{1,0:T(8,128)(2,1)}, bf16[1024,2048]{1,0:T(8,128)(2,1)}, f32[2048,256]{1,0:T(8,128)S(1)}, f32[2048,256]{1,0:T(8,128)S(1)}, bf16[204...) custom-call(s32[1]{0:T(128)} %bitcast.1.me_ref, bf16[1024,2048]{1,0:T(8,128)(2,1)} %constant_dynamic-update-slice_fusion.even_ref, ...), custom_call_target="tpu_custom_call" | custom-call | flops 6442450944 | bytes 25165824 | tf_op jit(solution)/shard_map/project/pallas_call | solution.py:437
  177.5 11.1 collective-permute-done.20.refs_4_
  243.8 21.6 %attend.1 = (bf16[2048,256]{1,0:T(8,128)(2,1)S(1)}, f32[2,1,2048]{2,1,0:T(1,128)S(1)}) custom-call(bf16[2048,256]{1,0:T(8,128)(2,1)S(1)} %get-tuple-element.307.q_ref, bf16[2048,256]{1,0:T(8,128)(2,1)S(1)} %get-tuple-element.308.k_ref, bf16[2048,256]{1,0:T(8,128)(2,1)S(1)} %copy-done.20, s32[1,2048]{1,0:T(1,128)S(1)} %copy-done.14, s32[2048,1]{1,0:T(8,128)S(1)} %copy-done.9), custom_call_target="tpu_custom_call" | custom-call | flops 2684354560 | bytes 4194304 | tf_op jit(solution)/shard_map/attend/pallas_call | solution.py:336
  282.3 19.1 %collective-permute-done.36.refs_10_ = bf16[2,128,1024]{2,1,0:T(8,128)(2,1)} collective-permute-done((bf16[2,128,1024]{2,1,0:T(8,128)(2,1)}, bf16[2,128,1024]{2,1,0:T(8,128)(2,1)}, u32[]{:S(2)}, u32[]{:S(2)}) %collective-permute-start.36) | collective-permute-done | bytes 524320 | tf_op jit(solution)/shard_map/ppermute | solution.py:42
  335.4 19.0 %collective-permute-done.45.refs_12_ = bf16[2,128,1024]{2,1,0:T(8,128)(2,1)S(1)} collective-permute-done((bf16[2,128,1024]{2,1,0:T(8,128)(2,1)}, bf16[2,128,1024]{2,1,0:T(8,128)(2,1)S(1)}, u32[]{:S(2)}, u32[]{:S(2)}) %collective-permute-start.45) | collective-permute-done | bytes 524320 | tf_op jit(solution)/shard_map/ppermute | solution.py:42
  364.8 12.4 %collective-permute-done.49.refs_13_ = bf16[2,128,1024]{2,1,0:T(8,128)(2,1)S(1)} collective-permute-done((bf16[2,128,1024]{2,1,0:T(8,128)(2,1)S(1)}, bf16[2,128,1024]{2,1,0:T(8,128)(2,1)S(1)}, u32[]{:S(2)}, u32[]{:S(2)}) %collective-permute-start.49) | collective-permute-done | bytes 524320 | tf_op jit(solution)/shard_map/ppermute | solution.py:42
  426.4 10.2 collective-permute-done.52.refs_19_
  469.5 8.2 collective-permute-done.59
  485.4 59.5 %experts.2 = (bf16[1024,2048]{1,0:T(8,128)(2,1)}, bf16[1024,2048]{1,0:T(8,128)(2,1)}, bf16[1024,2048]{1,0:T(8,128)(2,1)}, bf16[1024,2048]{1,0:T(8,128)(2,1)}, f3...) custom-call(s32[2]{0:T(128)} %pad_add_fusion.first_ref, ...), custom_call_target="tpu_custom_call" | custom-call | flops 38654705664 | bytes 62914560 | tf_op jit(solution)/shard_map/experts/pallas_call | solution.py:732
  545.6 59.1 %experts.3 = (bf16[1024,2048]{1,0:T(8,128)(2,1)}, bf16[1024,2048]{1,0:T(8,128)(2,1)}, bf16[1024,2048]{1,0:T(8,128)(2,1)}, bf16[1024,2048]{1,0:T(8,128)(2,1)}, f3...) custom-call(s32[2]{0:T(128)} %pad_add_fusion.first_ref, ...), custom_call_target="tpu_custom_call", output_to_operand_aliasing={{6}: (30, {}), {7}: (31, {}), {8}: (32, {}), {9}: (33, {})} | custom-call | flops 38654705664 | bytes 62914560 | tf_op jit(solution)/shard_map/experts/pallas_call | solution.py:732
  613.3 9.4 in_products.4
  632.6 7.3 collective-permute-done.68
  656.2 11.0 down_products.3
  667.2 11.2 down_products.2
  696.6 9.6 in_products.5
  706.2 8.8 collective-permute-done.77
  729.1 10.0 in_products.6
  739.1 7.6 collective-permute-done.82
  760.6 9.4 in_products.7
  802.9 10.8 collective-permute-done.91
  828.4 28.3 %attend_back.1 = (bf16[2048,256]{1,0:T(8,128)(2,1)S(1)}, bf16[2048,256]{1,0:T(8,128)(2,1)S(1)}, bf16[2048,256]{1,0:T(8,128)(2,1)S(1)}) custom-call(bf16[2048,256]{1,0:T(8,128)(2,1)S(1)} %copy-done.16, bf16[2048,256]{1,0:T(8,128)(2,1)S(1)} %copy-done.18, bf16[2048,256]{1,0:T(8,128)(2,1)} %copy-done.19, bf16[2048,256]{1,0:T(8,128)(2,1)} %bitcast.334, ...), custom_call_target="tpu_custom_call" | custom-call | flops 6710886400 | bytes 7340032 | tf_op jit(solution)/shard_map/attend_back/pallas_call | solution.py:368
  881.1 10.3 collective-permute-done.97
  928.8 17.8 %collective-permute-done.104 = bf16[128,2048]{1,0:T(8,128)(2,1)S(1)} collective-permute-done((bf16[128,2048]{1,0:T(8,128)(2,1)S(1)}, bf16[128,2048]{1,0:T(8,128)(2,1)S(1)}, u32[]{:S(2)}, u32[]{:S(2)}) %collective-permute-start.104) | collective-permute-done | bytes 524320 | tf_op jit(solution)/shard_map/ppermute | solution.py:42
  956.1 12.4 %collective-permute-done.108 = bf16[1,8,64,256]{3,2,1,0:T(8,128)(2,1)S(1)} collective-permute-done((bf16[1,8,64,256]{3,2,1,0:T(8,128)(2,1)S(1)}, bf16[1,8,64,256]{3,2,1,0:T(8,128)(2,1)S(1)}, u32[]{:S(2)}, u32[]{:S(2)}) %collective-permute-start.108) | collective-permute-done | bytes 262176 | tf_op jit(solution)/shard_map/ppermute | solution.py:42
  986.3 9.5 collective-permute-done.112
  1001.4 12.9 %collective-permute-done.111 = bf16[2,8,64,512]{3,2,1,0:T(8,128)(2,1)} collective-permute-done((bf16[2,8,64,512]{3,2,1,0:T(8,128)(2,1)}, bf16[2,8,64,512]{3,2,1,0:T(8,128)(2,1)}, u32[]{:S(2)}, u32[]{:S(2)}) %collective-permute-start.111) | collective-permute-done | bytes 1048608 | tf_op jit(solution)/shard_map/ppermute | solution.py:42
  1065.8 21.2 %collective-permute-done.113 = bf16[1,8,64,512]{3,2,1,0:T(8,128)(2,1)S(1)} collective-permute-done((bf16[1,8,64,512]{3,2,1,0:T(8,128)(2,1)}, bf16[1,8,64,512]{3,2,1,0:T(8,128)(2,1)S(1)}, u32[]{:S(2)}, u32[]{:S(2)}) %collective-permute-start.113) | collective-permute-done | bytes 524320 | tf_op jit(solution)/shard_map/ppermute | solution.py:42
  (916 shorter events, 623.6 us)
Async XLA Ops:
  38.4 34.0 %collective-permute-start.7 = (bf16[8,64,768]{2,1,0:T(8,128)(2,1)S(1)}, bf16[8,64,768]{2,1,0:T(8,128)(2,1)}, u32[]{:S(2)}, u32[]{:S(2)}) collective-permute-start(bf16[8,64,768]{2,1,0:T(8,128)(2,1)S(1)} %all-to-all-done), channel_id=1, source_target_pairs={{0,2},{1,3},{2,0},{3,1},{4,6},{5,7},{6,4},{7,5},{8,10},{9,11},{10,... | collective-permute-start | bytes 2359304 | tf_op jit(solution)/shard_map/ppermute | solution.py:42
  56.4 108.3 %collective-permute-start.4 = (bf16[1024,2048]{1,0:T(8,128)(2,1)}, bf16[1024,2048]{1,0:T(8,128)(2,1)}, u32[]{:S(2)}, u32[]{:S(2)}) collective-permute-start(bf16[1024,2048]{1,0:T(8,128)(2,1)} %constant_dynamic-update-slice_fusion.even_ref), channel_id=1, source_target_pairs={{0,4},{4,0},{8,12},{12,8},{16,20},{20,16},{24,28},{28,24},{1,5},{5... | collective-permute-start | bytes 12582920 | tf_op jit(solution)/shard_map/ppermute | solution.py:42
  79.5 41.3 %collective-permute-start.6 = (bf16[8,64,768]{2,1,0:T(8,128)(2,1)S(1)}, bf16[8,64,768]{2,1,0:T(8,128)(2,1)}, u32[]{:S(2)}, u32[]{:S(2)}) collective-permute-start(bf16[8,64,768]{2,1,0:T(8,128)(2,1)S(1)} %all-to-all-done), channel_id=1, source_target_pairs={{0,1},{1,0},{2,3},{3,2},{4,5},{5,4},{6,7},{7,6},{8,9},{9,8},{10,11... | collective-permute-start | bytes 2359304 | tf_op jit(solution)/shard_map/ppermute | solution.py:42
  82.6 48.5 %collective-permute-start.10 = (bf16[8,64,768]{2,1,0:T(8,128)(2,1)}, bf16[8,64,768]{2,1,0:T(8,128)(2,1)}, u32[]{:S(2)}, u32[]{:S(2)}) collective-permute-start(bf16[8,64,768]{2,1,0:T(8,128)(2,1)} %collective-permute-done.7), channel_id=1, source_target_pairs={{0,1},{1,0},{2,3},{3,2},{4,5},{5,4},{6,7},{7,6},{8,9},{9,8},{10,11... | collective-permute-start | bytes 2359304 | tf_op jit(solution)/shard_map/ppermute | solution.py:42
  85.0 32.0 %collective-permute-start.17 = (bf16[8,3328]{1,0:T(8,128)(2,1)S(1)}, bf16[8,3328]{1,0:T(8,128)(2,1)S(1)}, u32[]{:S(2)}, u32[]{:S(2)}) collective-permute-start(bf16[8,3328]{1,0:T(8,128)(2,1)S(1)} %pad_maximum_fusion.34), channel_id=1, source_target_pairs={{0,1},{1,0},{2,3},{3,2},{4,5},{5,4},{6,7},{7,6},{8,9},{9,8},{10,11... | collective-permute-start | bytes 159752 | tf_op jit(solution)/shard_map/ppermute | solution.py:42
  155.6 33.1 %collective-permute-start.20 = (bf16[2,128,1024]{2,1,0:T(8,128)(2,1)}, bf16[2,128,1024]{2,1,0:T(8,128)(2,1)S(1)}, u32[]{:S(2)}, u32[]{:S(2)}) collective-permute-start(bf16[2,128,1024]{2,1,0:T(8,128)(2,1)} %pad_maximum_fusion.23.refs_1_), channel_id=1, source_target_pairs={{0,1},{1,0},{2,3},{3,2},{4,5},{5,4},{6,7},{7,6},{8,9},{9,8},{10,11... | collective-permute-start | bytes 1572872 | tf_op jit(solution)/shard_map/ppermute | solution.py:42
  155.6 33.1 %collective-permute-start.19 = (bf16[128,2048]{1,0:T(8,128)(2,1)}, bf16[128,2048]{1,0:T(8,128)(2,1)S(1)}, u32[]{:S(2)}, u32[]{:S(2)}) collective-permute-start(bf16[128,2048]{1,0:T(8,128)(2,1)} %get-tuple-element.296), channel_id=1, source_target_pairs={{0,2},{1,3},{2,0},{3,1},{4,6},{5,7},{6,4},{7,5},{8,10},{9,11},{10,... | collective-permute-start | bytes 1572872 | tf_op jit(solution)/shard_map/ppermute | solution.py:42
  197.7 31.5 %collective-permute-start.27 = (bf16[256,2048]{1,0:T(8,128)(2,1)}, bf16[256,2048]{1,0:T(8,128)(2,1)}, u32[]{:S(2)}, u32[]{:S(2)}) collective-permute-start(bf16[256,2048]{1,0:T(8,128)(2,1)} %bitcast.18), channel_id=1, source_target_pairs={{0,8},{4,12},{8,0},{12,4},{16,24},{20,28},{24,16},{28,20},{1,9},{5... | collective-permute-start | bytes 3145736 | tf_op jit(solution)/shard_map/ppermute | solution.py:42
  229.2 37.2 %collective-permute-start.33 = (bf16[2,128,1024]{2,1,0:T(8,128)(2,1)S(1)}, bf16[2,128,1024]{2,1,0:T(8,128)(2,1)S(1)}, u32[]{:S(2)}, u32[]{:S(2)}) collective-permute-start(bf16[2,128,1024]{2,1,0:T(8,128)(2,1)S(1)} %copy-done.111), channel_id=1, source_target_pairs={{0,2},{1,3},{2,0},{3,1},{4,6},{5,7},{6,4},{7,5},{8,10},{9,11},{10,... | collective-permute-start | bytes 1572872 | tf_op jit(solution)/shard_map/ppermute | solution.py:42
  232.8 33.6 %collective-permute-start.34 = (bf16[2,64,2048]{2,1,0:T(8,128)(2,1)S(1)}, bf16[2,64,2048]{2,1,0:T(8,128)(2,1)S(1)}, u32[]{:S(2)}, u32[]{:S(2)}) collective-permute-start(bf16[2,64,2048]{2,1,0:T(8,128)(2,1)S(1)} %copy-done.113), channel_id=1, source_target_pairs={{0,1},{1,0},{2,3},{3,2},{4,5},{5,4},{6,7},{7,6},{8,9},{9,8},{10,11... | collective-permute-start | bytes 1572872 | tf_op jit(solution)/shard_map/ppermute | solution.py:42
  268.2 51.8 %collective-permute-start.37 = (bf16[1024,2048]{1,0:T(8,128)(2,1)}, bf16[1024,2048]{1,0:T(8,128)(2,1)}, u32[]{:S(2)}, u32[]{:S(2)}) collective-permute-start(bf16[1024,2048]{1,0:T(8,128)(2,1)} %constant_dynamic-update-slice_fusion.13), channel_id=1, source_target_pairs={{0,4},{4,0},{8,12},{12,8},{16,20},{20,16},{24,28},{28,24},{1,5},{5... | collective-permute-start | bytes 12582920 | tf_op jit(solution)/shard_map/ppermute | solution.py:42
  270.5 33.1 %all-to-all-start.1 = ((bf16[8,256,256]{1,2,0:T(8,128)(2,1)}), bf16[8,256,256]{1,2,0:T(8,128)(2,1)}, u32[]{:S(2)}, u32[]{:S(2)}) async-start(bf16[8,256,256]{1,2,0:T(8,128)(2,1)} %copy.190), calls=%async_computation.1 | async-start | bytes 2097152 | tf_op jit(solution)/shard_map/all_to_all | solution.py:936
  382.0 54.6 %collective-permute-start.54 = (bf16[1024,2048]{1,0:T(8,128)(2,1)}, bf16[1024,2048]{1,0:T(8,128)(2,1)}, u32[]{:S(2)}, u32[]{:S(2)}) collective-permute-start(bf16[1024,2048]{1,0:T(8,128)(2,1)} %constant_dynamic-update-slice_fusion.18.xa_ref), channel_id=1, source_target_pairs={{0,4},{4,0},{8,12},{12,8},{16,20},{20,16},{24,28},{28,24},{1,5},{5... | collective-permute-start | bytes 12582920 | tf_op jit(solution)/shard_map/ppermute | solution.py:42
  404.6 32.0 %collective-permute-start.50 = (bf16[256,2048]{1,0:T(8,128)(2,1)}, bf16[256,2048]{1,0:T(8,128)(2,1)}, u32[]{:S(2)}, u32[]{:S(2)}) collective-permute-start(bf16[256,2048]{1,0:T(8,128)(2,1)} %pad_maximum_fusion.9), channel_id=1, source_target_pairs={{0,8},{4,12},{8,0},{12,4},{16,24},{20,28},{24,16},{28,20},{1,9},{5... | collective-permute-start | bytes 3145736 | tf_op jit(solution)/shard_map/ppermute | solution.py:42
  426.3 59.1 %collective-permute-start.61 = (bf16[1024,2048]{1,0:T(8,128)(2,1)}, bf16[1024,2048]{1,0:T(8,128)(2,1)}, u32[]{:S(2)}, u32[]{:S(2)}) collective-permute-start(bf16[1024,2048]{1,0:T(8,128)(2,1)} %constant_dynamic-update-slice_fusion.45.ua_ref), channel_id=1, source_target_pairs={{0,4},{4,0},{8,12},{12,8},{16,20},{20,16},{24,28},{28,24},{1,5},{5... | collective-permute-start | bytes 12582920 | tf_op jit(solution)/shard_map/ppermute | solution.py:42
  481.7 63.2 %collective-permute-start.62 = (bf16[1024,2048]{1,0:T(8,128)(2,1)}, bf16[1024,2048]{1,0:T(8,128)(2,1)}, u32[]{:S(2)}, u32[]{:S(2)}) collective-permute-start(bf16[1024,2048]{1,0:T(8,128)(2,1)} %constant_dynamic-update-slice_fusion.50.ua_ref), channel_id=1, source_target_pairs={{0,4},{4,0},{8,12},{12,8},{16,20},{20,16},{24,28},{28,24},{1,5},{5... | collective-permute-start | bytes 12582920 | tf_op jit(solution)/shard_map/ppermute | solution.py:42
  544.9 59.7 %collective-permute-start.63 = (bf16[1024,2048]{1,0:T(8,128)(2,1)}, bf16[1024,2048]{1,0:T(8,128)(2,1)}, u32[]{:S(2)}, u32[]{:S(2)}) collective-permute-start(bf16[1024,2048]{1,0:T(8,128)(2,1)} %get-tuple-element.413), channel_id=1, source_target_pairs={{0,4},{4,0},{8,12},{12,8},{16,20},{20,16},{24,28},{28,24},{1,5},{5... | collective-permute-start | bytes 12582920 | tf_op jit(solution)/shard_map/ppermute | solution.py:42
  545.5 59.2 %collective-permute-start.64 = (bf16[1024,2048]{1,0:T(8,128)(2,1)}, bf16[1024,2048]{1,0:T(8,128)(2,1)}, u32[]{:S(2)}, u32[]{:S(2)}) collective-permute-start(bf16[1024,2048]{1,0:T(8,128)(2,1)} %get-tuple-element.414), channel_id=1, source_target_pairs={{0,4},{4,0},{8,12},{12,8},{16,20},{20,16},{24,28},{28,24},{1,5},{5... | collective-permute-start | bytes 12582920 | tf_op jit(solution)/shard_map/ppermute | solution.py:42
  650.9 32.6 %collective-permute-start.70 = (bf16[256,2048]{1,0:T(8,128)(2,1)}, bf16[256,2048]{1,0:T(8,128)(2,1)}, u32[]{:S(2)}, u32[]{:S(2)}) collective-permute-start(bf16[256,2048]{1,0:T(8,128)(2,1)} %pad_maximum_fusion.10), channel_id=1, source_target_pairs={{0,8},{4,12},{8,0},{12,4},{16,24},{20,28},{24,16},{28,20},{1,9},{5... | collective-permute-start | bytes 3145736 | tf_op jit(solution)/shard_map/ppermute | solution.py:42
  823.0 38.6 %collective-permute-start.94 = (bf16[128,2048]{1,0:T(8,128)(2,1)}, bf16[128,2048]{1,0:T(8,128)(2,1)S(1)}, u32[]{:S(2)}, u32[]{:S(2)}) collective-permute-start(bf16[128,2048]{1,0:T(8,128)(2,1)} %get-tuple-element.486), channel_id=1, source_target_pairs={{0,16},{4,20},{8,24},{12,28},{16,0},{20,4},{24,8},{28,12},{1,17},{... | collective-permute-start | bytes 1572872 | tf_op jit(solution)/shard_map/ppermute | solution.py:42
  823.7 37.8 %collective-permute-start.95 = (bf16[128,2048]{1,0:T(8,128)(2,1)}, bf16[128,2048]{1,0:T(8,128)(2,1)S(1)}, u32[]{:S(2)}, u32[]{:S(2)}) collective-permute-start(bf16[128,2048]{1,0:T(8,128)(2,1)} %get-tuple-element.487), channel_id=1, source_target_pairs={{0,8},{4,12},{8,0},{12,4},{16,24},{20,28},{24,16},{28,20},{1,9},{5... | collective-permute-start | bytes 1572872 | tf_op jit(solution)/shard_map/ppermute | solution.py:42
  825.4 36.1 %collective-permute-start.93 = (bf16[2,64,2048]{2,1,0:T(8,128)(2,1)}, bf16[2,64,2048]{2,1,0:T(8,128)(2,1)S(1)}, u32[]{:S(2)}, u32[]{:S(2)}) collective-permute-start(bf16[2,64,2048]{2,1,0:T(8,128)(2,1)} %get-tuple-element.482), channel_id=1, source_target_pairs={{0,1},{1,0},{2,3},{3,2},{4,5},{5,4},{6,7},{7,6},{8,9},{9,8},{10,11... | collective-permute-start | bytes 1572872 | tf_op jit(solution)/shard_map/ppermute | solution.py:42
  825.4 36.2 %collective-permute-start.92 = (bf16[2,128,1024]{2,1,0:T(8,128)(2,1)}, bf16[2,128,1024]{2,1,0:T(8,128)(2,1)S(1)}, u32[]{:S(2)}, u32[]{:S(2)}) collective-permute-start(bf16[2,128,1024]{2,1,0:T(8,128)(2,1)} %get-tuple-element.481), channel_id=1, source_target_pairs={{0,2},{1,3},{2,0},{3,1},{4,6},{5,7},{6,4},{7,5},{8,10},{9,11},{10,... | collective-permute-start | bytes 1572872 | tf_op jit(solution)/shard_map/ppermute | solution.py:42
  908.4 38.3 %collective-permute-start.103 = (bf16[1024,2048]{1,0:T(8,128)(2,1)}, bf16[1024,2048]{1,0:T(8,128)(2,1)}, u32[]{:S(2)}, u32[]{:S(2)}) collective-permute-start(bf16[1024,2048]{1,0:T(8,128)(2,1)} %convolution_convert_fusion.2), channel_id=1, source_target_pairs={{0,4},{4,0},{8,12},{12,8},{16,20},{20,16},{24,28},{28,24},{1,5},{5... | collective-permute-start | bytes 12582920 | tf_op jit(solution)/shard_map/ppermute | solution.py:42
  923.9 60.7 %collective-permute-start.120 = (bf16[1,64,2048]{2,1,0:T(8,128)(2,1)}, bf16[1,64,2048]{2,1,0:T(8,128)(2,1)}, u32[]{:S(2)}, u32[]{:S(2)}) collective-permute-start(bf16[1,64,2048]{2,1,0:T(8,128)(2,1)} %slice_bitcast_fusion.4), channel_id=1, source_target_pairs={{0,2},{1,3},{2,0},{3,1},{4,6},{5,7},{6,4},{7,5},{8,10},{9,11},{10,... | collective-permute-start | bytes 786440 | tf_op jit(solution)/shard_map/ppermute | solution.py:42
  977.6 36.7 %collective-permute-start.111 = (bf16[2,8,64,512]{3,2,1,0:T(8,128)(2,1)}, bf16[2,8,64,512]{3,2,1,0:T(8,128)(2,1)}, u32[]{:S(2)}, u32[]{:S(2)}) collective-permute-start(bf16[2,8,64,512]{3,2,1,0:T(8,128)(2,1)} %slice.710), channel_id=1, source_target_pairs={{0,1},{1,0},{2,3},{3,2},{4,5},{5,4},{6,7},{7,6},{8,9},{9,8},{10,11... | collective-permute-start | bytes 3145736 | tf_op jit(solution)/shard_map/ppermute | solution.py:42
  1016.9 71.3 %collective-permute-start.117 = (bf16[2,128,1024]{2,1,0:T(8,128)(2,1)}, bf16[2,128,1024]{2,1,0:T(8,128)(2,1)}, u32[]{:S(2)}, u32[]{:S(2)}) collective-permute-start(bf16[2,128,1024]{2,1,0:T(8,128)(2,1)} %get-tuple-element.524), channel_id=1, source_target_pairs={{0,1},{1,0},{2,3},{3,2},{4,5},{5,4},{6,7},{7,6},{8,9},{9,8},{10,11... | collective-permute-start | bytes 1572872 | tf_op jit(solution)/shard_map/ppermute | solution.py:42
  1016.9 71.3 %collective-permute-start.116 = (bf16[2,128,1024]{2,1,0:T(8,128)(2,1)}, bf16[2,128,1024]{2,1,0:T(8,128)(2,1)}, u32[]{:S(2)}, u32[]{:S(2)}) collective-permute-start(bf16[2,128,1024]{2,1,0:T(8,128)(2,1)} %get-tuple-element.523), channel_id=1, source_target_pairs={{0,1},{1,0},{2,3},{3,2},{4,5},{5,4},{6,7},{7,6},{8,9},{9,8},{10,11... | collective-permute-start | bytes 1572872 | tf_op jit(solution)/shard_map/ppermute | solution.py:42
  1021.8 66.4 %collective-permute-start.114 = (bf16[128,2048]{1,0:T(8,128)(2,1)}, bf16[128,2048]{1,0:T(8,128)(2,1)}, u32[]{:S(2)}, u32[]{:S(2)}) collective-permute-start(bf16[128,2048]{1,0:T(8,128)(2,1)} %get-tuple-element.520), channel_id=1, source_target_pairs={{0,16},{4,20},{8,24},{12,28},{16,0},{20,4},{24,8},{28,12},{1,17},{... | collective-permute-start | bytes 1572872 | tf_op jit(solution)/shard_map/ppermute | solution.py:42
  1022.6 65.6 %collective-permute-start.115 = (bf16[128,2048]{1,0:T(8,128)(2,1)}, bf16[128,2048]{1,0:T(8,128)(2,1)}, u32[]{:S(2)}, u32[]{:S(2)}) collective-permute-start(bf16[128,2048]{1,0:T(8,128)(2,1)} %get-tuple-element.521), channel_id=1, source_target_pairs={{0,8},{4,12},{8,0},{12,4},{16,24},{20,28},{24,16},{28,20},{1,9},{5... | collective-permute-start | bytes 1572872 | tf_op jit(solution)/shard_map/ppermute | solution.py:42
  1103.2 34.1 %collective-permute-start.118 = (bf16[256,2048]{1,0:T(8,128)(2,1)}, bf16[256,2048]{1,0:T(8,128)(2,1)}, u32[]{:S(2)}, u32[]{:S(2)}) collective-permute-start(bf16[256,2048]{1,0:T(8,128)(2,1)} %pad_maximum_fusion.20), channel_id=1, source_target_pairs={{0,8},{4,12},{8,0},{12,4},{16,24},{20,28},{24,16},{28,20},{1,9},{5... | collective-permute-start | bytes 3145736 | tf_op jit(solution)/shard_map/ppermute | solution.py:42
  1105.1 32.2 %collective-permute-start.119 = (bf16[256,2048]{1,0:T(8,128)(2,1)}, bf16[256,2048]{1,0:T(8,128)(2,1)}, u32[]{:S(2)}, u32[]{:S(2)}) collective-permute-start(bf16[256,2048]{1,0:T(8,128)(2,1)} %pad_maximum_fusion.21), channel_id=1, source_target_pairs={{0,16},{4,20},{8,24},{12,28},{16,0},{20,4},{24,8},{28,12},{1,17},{... | collective-permute-start | bytes 3145736 | tf_op jit(solution)/shard_map/ppermute | solution.py:42
  (256 other events, 3889.6 us)

commit v6 on v5

--- a/solution.py
+++ b/solution.py
@@ -180,36 +180,37 @@
     return pieces
 
 
-def gather_small(values, seq_size, fsdp_size, s, f):
-    count = seq_size * fsdp_size
-    whole = values[None]
-    for axis, size in (("seq", seq_size), ("fsdp", fsdp_size)):
-        mask = 1
-        while mask < size:
-            whole = jnp.concatenate([whole, swap(whole, axis, size, mask)], 0)
-            mask *= 2
-    index = jnp.arange(count, dtype=jnp.int32)
-    source = ((index % fsdp_size) ^ f) * seq_size + ((index // fsdp_size) ^ s)
-    pick = (source[:, None] == index[None, :]).astype(values.dtype)
-    return matmul(pick, whole).astype(values.dtype)
-
-
-def sum_small(values, axes):
-    count = values.shape[0]
-    index = jnp.arange(count, dtype=jnp.int32)
-    source, stride = jnp.zeros_like(index), 1
-    for _, size, me in reversed(axes):
-        source += ((index // stride % size) ^ me) * stride
-        stride *= size
-    pick = (source[:, None] == index[None, :]).astype(F32)
-    values = jnp.dot(pick, values, precision=HIGHEST)
-    for name, size, _ in axes:
-        mask = size // 2
-        while mask:
-            half = values.shape[0] // 2
-            values = values[:half] + swap(values[half:], name, size, mask)
-            mask //= 2
-    return values[0]
+def double(values, axis, size):
+    mask = 1
+    while mask < size:
+        values = jnp.concatenate([values, swap(values, axis, size, mask)], 0)
+        mask *= 2
+    return values
+
+
+def halve(values, axis, size):
+    mask = size // 2
+    while mask:
+        half = values.shape[0] // 2
+        values = values[:half] + swap(values[half:], axis, size, mask)
+        mask //= 2
+    return values
+
+
+def relative_pick(seq_size, fsdp_size, s, f):
+    index = jnp.arange(seq_size * fsdp_size, dtype=jnp.int32)
+    source = ((index // fsdp_size) ^ s) * fsdp_size + ((index % fsdp_size) ^ f)
+    return source[:, None] == index[None, :]
+
+
+def in_order(values, seq_size, fsdp_size, s, f):
+    pick = relative_pick(seq_size, fsdp_size, s, f).astype(values.dtype)
+    return matmul(pick, values).astype(values.dtype)
+
+
+def in_relative(values, seq_size, fsdp_size, s, f):
+    pick = relative_pick(seq_size, fsdp_size, s, f).astype(F32)
+    return jnp.dot(pick, values, precision=HIGHEST)
 
 
 def by_index(partial_sum, me, size):
@@ -846,23 +847,11 @@
     def near_swap(values, *dep):
         return near_pieces(after(values, dep), F)
 
-    token_first = gather_first(tokens_low, S)
-    crossed = split_heads(w_query, w_key, w_value, S)
-    crossed = lax.all_to_all(crossed, "seq", split_axis=0, concat_axis=0, tiled=True)
-    near_own = [near_swap(hidden_part(half_at, 0, 2 * quarter))]
-    crossed, near_own[0] = tie(crossed, near_own[0])
-
-    token_more = gather_more(tokens_low, token_first, S)
-    tokens_even, tokens_odd = gather_end(tokens_low, token_first, token_more, S)
-    qkv_pieces = {0: crossed}
-    for r in range(1, F):
-        low = low_bit(r)
-        qkv_pieces[r] = swap(qkv_pieces[r ^ low], "fsdp", F, low)
-        if r == half_f:
-            own_up_first = gather_first(after(upstream_low, token_more), S)
-            qkv_pieces[r], own_up_first = tie(qkv_pieces[r], own_up_first)
-            own_up_more = gather_more(upstream_low, own_up_first, S)
-            partner_up = [far_swap(upstream_low[:half_rows], qkv_pieces[r])]
+    named = routes[0].T[None] == jnp.arange(E, dtype=jnp.int32)[:, None, None]
+    chosen = jnp.any(named, axis=1)
+    index = jnp.arange(T, dtype=jnp.int32)
+    before = (index[:, None] <= index[None, :]).astype(BF16)
+    ranks = jnp.where(chosen, matmul(chosen.astype(BF16), before) - 1.0, -1.0)
     small = jnp.concatenate(
         [
             router.reshape(-1),
@@ -870,13 +859,29 @@
             moe_gain,
             query_gain,
             key_gain,
-            routes[0].astype(BF16).reshape(-1),
+            ranks.astype(BF16).reshape(-1),
         ]
-    )
-    small = gather_small(after(small, qkv_pieces[half_f]), S, F, s, f).reshape(S, F, -1)
+    )[None]
+    crossed = split_heads(w_query, w_key, w_value, S)
+    small = double(after(small, crossed), "fsdp", F)
+    crossed = lax.all_to_all(crossed, "seq", split_axis=0, concat_axis=0, tiled=True)
+    near_own = [near_swap(hidden_part(half_at, 0, 2 * quarter), small)]
+    small = double(small, "seq", S)
+    crossed, near_own[0], small = tie(crossed, near_own[0], small)
+
+    small = in_order(small, S, F, s, f).reshape(S, F, -1)
+    token_first = gather_first(after(tokens_low, crossed), S)
+    qkv_pieces = {0: crossed}
+    for r in range(1, F):
+        low = low_bit(r)
+        qkv_pieces[r] = swap(qkv_pieces[r ^ low], "fsdp", F, low)
+        if r == half_f:
+            qkv_pieces, token_first = tie(qkv_pieces, token_first)
+            partner_up = [far_swap(upstream_low[:half_rows], qkv_pieces[r])]
+    token_more = gather_more(tokens_low, token_first, S)
+    qkv_pieces, partner_up[0], token_more = tie(qkv_pieces, partner_up[0], token_more)
+    tokens_even, tokens_odd = gather_end(tokens_low, token_first, token_more, S)
     w_qkv = place_fsdp(qkv_pieces, f, 1).reshape(D, 3 * C)
-    w_qkv, partner_up[0], own_up_more, small = tie(w_qkv, partner_up[0], own_up_more, small)
-    own_u = gather_end(upstream_low, own_up_first, own_up_more, S)
 
     full_router = small[:, :, : part * E].reshape(D, E)
     gains = [
@@ -884,15 +889,11 @@
     ]
     gain_attn, gain_moe = gains[0], gains[1]
     head_gain = lax.dynamic_slice(jnp.stack(gains[2:], 0), (0, s * C), (2, C))
-    route_part = small[:, :, part * (E + 4) :].reshape(S, F, T, -1)
-    expert_ids = s * experts + jnp.arange(experts, dtype=jnp.int32)
+    rank_part = small[:, :, part * (E + 4) :].reshape(S, F, E, T)
 
     def ranks_of(index):
-        named = lax.dynamic_index_in_dim(route_part, index, 1, keepdims=False)
-        named = relative(named, s).astype(jnp.int32)
-        chosen = jnp.any(named[:, None] == expert_ids[None, :, None, None], axis=-1)
-        ranks = jnp.cumsum(chosen.astype(jnp.int32), axis=-1) - 1
-        ranks = jnp.where(chosen, ranks, -1)
+        ranks = lax.dynamic_slice(rank_part, (0, index, s * experts, 0), (S, 1, experts, T))
+        ranks = relative(ranks[:, 0], s).astype(jnp.int32)
         return ranks[: S // 2], ranks[S // 2 :]
 
     places = jnp.arange(L, dtype=jnp.int32).astype(F32)
@@ -908,11 +909,12 @@
     partner_up.append(far_swap(upstream_low[half_rows:], w_qkv))
     near_own.append(near_swap(hidden_part(half_at, 2 * quarter, quarter), w_qkv))
     out_pieces = fsdp_pieces(after(w_output, w_qkv), F)
+    own_up_first = gather_first(after(upstream_low, w_qkv), S)
     normed_even, normed_odd, query_pre, key_pre, value_low, squares = project(
         tokens_even, tokens_odd, w_qkv, gain_attn[None], me, T
     )
-    squares, partner_up[1], near_own[1], out_pieces = tie(
-        squares, partner_up[1], near_own[1], out_pieces
+    squares, partner_up[1], near_own[1], out_pieces, own_up_first = tie(
+        squares, partner_up[1], near_own[1], out_pieces, own_up_first
     )
     partner_up = jnp.concatenate(partner_up, 0)
     own_output = place_fsdp(out_pieces, f, 0).reshape(C, D)
@@ -937,7 +939,9 @@
     out_even, out_odd = gather_end(own_output, out_first, out_more, S)
     far.append(far_part(2, attended))
     near_far = [near_swap(far[0], attended)]
-    come, far[2], near_far[0] = tie(come, far[2], near_far[0])
+    own_up_more = gather_more(after(upstream_low, attended), own_up_first, S)
+    come, far[2], near_far[0], own_up_more = tie(come, far[2], near_far[0], own_up_more)
+    own_u = gather_end(upstream_low, own_up_first, own_up_more, S)
     far.append(far_part(3, come))
     near_far.append(near_swap(far[1], come))
     partner_up_first = gather_first(after(partner_up, come), S)
@@ -957,17 +961,22 @@
     own_more = gather_more(second_low, own_first, S)
     partner_low.append(far_swap(second_low[half_rows:], own_first))
     near_far.append(near_swap(far[3], own_first))
-    own_more, partner_low[1], near_far[3] = tie(own_more, partner_low[1], near_far[3])
+    partner_up_more = gather_more(after(partner_up, own_first), partner_up_first, S)
+    own_more, partner_low[1], near_far[3], partner_up_more = tie(
+        own_more, partner_low[1], near_far[3], partner_up_more
+    )
     partner_low = jnp.concatenate(partner_low, 0)
     own_x = gather_end(second_low, own_first, own_more, S)
     partner_first = gather_first(after(partner_low, own_more), S)
-    down.append(near_swap(down_rows[1], own_more))
-    down.append(near_swap(down_rows[2], own_more))
-    partner_first, down[1], down[2], own_x = tie(partner_first, down[1], down[2], own_x)
+    down.append(near_swap(jnp.concatenate(down_rows[1:3], 1), own_more))
+    own_ranks, other_ranks = ranks_of(f), ranks_of(f ^ half_f)
+    partner_first, down[1], own_x, own_ranks, other_ranks = tie(
+        partner_first, down[1], own_x, own_ranks, other_ranks
+    )
+    other_u = gather_end(partner_up, partner_up_first, partner_up_more, S)
     partner_more = gather_more(partner_low, partner_first, S)
     down.append(near_swap(down_rows[3], partner_first))
-    partner_more, down[3] = tie(partner_more, down[3])
-    partner_up_more = gather_more(after(partner_up, partner_more), partner_up_first, S)
+    partner_more, down[2], other_u = tie(partner_more, down[2], other_u)
     other_x = gather_end(partner_low, partner_first, partner_more, S)
     in_pieces = []
     for r in range(F):
@@ -975,20 +984,15 @@
             first = (0, 2, 3)[n] if r < half_f else n
             in_pieces.append((r, first * quarter, rows[r % half_f]))
     down_pieces = [
-        (r, n * (down_part // 4), down[n][r]) for r in range(half_f) for n in range(4)
+        (r, (0, 1, 3)[n] * (down_part // 4), down[n][r]) for r in range(half_f) for n in range(3)
     ]
     wide_router = jnp.pad(full_router, ((0, 0), (0, 128 - E)))
     expert_places = jnp.stack([s * experts, f]).astype(jnp.int32)
     parts = (in_part, down_part)
-    own_ranks, other_ranks = ranks_of(f), ranks_of(f ^ half_f)
-    own_x, other_x, partner_up_more, own_ranks, other_ranks = tie(
-        own_x, other_x, partner_up_more, own_ranks, other_ranks
-    )
-    other_u = gather_end(partner_up, partner_up_first, partner_up_more, S)
     own_parts = run_experts(
         own_x, own_u, own_ranks, in_pieces, down_pieces, wide_router, expert_places, 0, (), parts
     )
-    own_parts, other_u = tie(own_parts, other_u)
+    own_parts, other_x = tie(own_parts, other_x)
     own_got = swap(own_parts[3], "seq", S, 1)
     own_out_got = swap(own_parts[1], "seq", S, 1)
     other_parts = run_experts(
@@ -1044,15 +1048,23 @@
     partner_grads = far_swap(gate_grads[:, 1], come)
     singles, other_total = sum_more(other_sums, come, S)
     come = sum_last(singles, S)
-    far_got.append(send_in(1, far_got[0]))
-    far_got.append(send_in(2, far_got[0]))
-    for r in range(half_f):
+    middle_sent = {r: jnp.concatenate(sent[r][1:3], 1) for r in sent}
+    middle_got = {
+        r: swap(after(middle_sent[r], far_got[0]), "fsdp", F, 1) for r in middle_sent
+    }
+
+    def down_products(r, dep):
         down_terms[r] = products(
-            after(hidden_gate, singles), u_rows, down_part, r, half_f, f_at, "down_products"
+            after(hidden_gate, dep), u_rows, down_part, r, half_f, f_at, "down_products"
         )
-    come, far_got[1], far_got[2], partner_grads, down_terms = tie(
-        come, far_got[1], far_got[2], partner_grads, down_terms
-    )
+
+    for r in range(1, half_f, 2):
+        down_products(r, singles)
+    come, middle_got, partner_grads, down_terms = tie(
+        come, middle_got, partner_grads, down_terms
+    )
+    for n in range(2):
+        far_got.append({r: got[:, n * quarter : (n + 1) * quarter] for r, got in middle_got.items()})
     other_rows = add_all(other_total, come).astype(BF16)
     gate_grads = gate_grads[:, 0] + partner_grads
     gate_grads = gate_grads.reshape(S, T, experts).transpose(1, 0, 2).reshape(T, E)
@@ -1111,10 +1123,10 @@
     branch_first = gather_first(branch_low, S)
     far_sums = [far_sum(0, branch_low)]
     down_got.append(send_down(1, branch_low))
-    for r in near_odd:
-        in_products(r ^ 1, branch_low)
-    branch_first, far_sums[0], down_got[1], in_terms = tie(
-        branch_first, far_sums[0], down_got[1], in_terms
+    for r in range(0, half_f, 2):
+        down_products(r, branch_low)
+    branch_first, far_sums[0], down_got[1], down_terms = tie(
+        branch_first, far_sums[0], down_got[1], down_terms
     )
     branch_more = gather_more(branch_low, branch_first, S)
     far_sums.append(far_sum(1, branch_first))
@@ -1125,7 +1137,11 @@
         [matmul_t(branch_even, own_output), matmul_t(branch_odd, own_output)], 0
     ).astype(BF16)
     head_grads = absolute(head_grads.reshape(S, T, C), s).reshape(L, C)
-    head_grads, far_sums[1], down_got[2] = tie(head_grads, far_sums[1], down_got[2])
+    for r in near_odd:
+        in_products(r ^ 1, branch_more)
+    head_grads, far_sums[1], down_got[2], in_terms = tie(
+        head_grads, far_sums[1], down_got[2], in_terms
+    )
     far_sums.append(far_sum(2, head_grads))
     down_got.append(send_down(3, head_grads))
     other_out_sums = sum_cores(other_parts[0], after(other_out_got, head_grads), S)
@@ -1157,7 +1173,6 @@
         means, come, far_sums[3], output_got, value_term
     )
     other_outs = add_all(other_total, come).astype(BF16)
-    outs_back = [far_swap(other_outs[:half_rows])]
     value_got = swap(value_term[: F // 2], "fsdp", F, 1)
     pre_rel = rope_back(
         (query_back, key_back, value_back),
@@ -1173,9 +1188,7 @@
     ).reshape(2, L // 2, 3 * C)
     normed_got = swap(matmul_t(pre_rel[1], w_qkv).astype(BF16), "seq", S, 1)
     normed_kept = matmul_t(pre_rel[0], w_qkv).astype(BF16)
-    normed_got, normed_kept, outs_back[0], value_got = tie(
-        normed_got, normed_kept, outs_back[0], value_got
-    )
+    normed_got, normed_kept, value_got = tie(normed_got, normed_kept, value_got)
 
     normed_sums = sum_cores(normed_kept, normed_got, S)
     come = sum_first(normed_sums, S)
@@ -1184,23 +1197,41 @@
         after(pre_rel[0][:, : 2 * C], normed_got), after(pre_rel[1][:, : 2 * C], normed_got)
     )
     come, turned_term, value_sum = tie(come, turned_term, value_sum)
-    near_sent = {r: quarters(in_terms[r], 1) for r in near_odd}
-
-    def send_near(n, *dep):
-        return {r: swap(after(near_sent[r][n], dep), "fsdp", F, 1) for r in near_sent}
-
     turned_got = swap(turned_term[: F // 2], "fsdp", F, 1)
     singles, normed_total = sum_more(normed_sums, come, S)
     come = sum_last(singles, S)
-    outs_back.append(far_swap(other_outs[half_rows:], turned_term))
-    come, turned_got, outs_back[1] = tie(come, turned_got, outs_back[1])
+    outs_back = [far_swap(other_outs[:half_rows], turned_term)]
+    late_grads, late_logits = after(second_grads, turned_term), after(logit_grads, turned_term)
+    router_term = jnp.dot(second_low.astype(F32).T, late_logits, precision=HIGHEST)
+    moe_gain_term = jnp.sum(late_grads * residual_n, axis=0)
+    gain_terms = jnp.concatenate(
+        [router_term.reshape(S * F, part * E), moe_gain_term.reshape(S * F, part)], 1
+    )
+    gain_terms = in_relative(gain_terms, S, F, s, f)
+    head_terms = gain_term.reshape(2, F, part).transpose(1, 0, 2).reshape(F, 2 * part)
+    head_terms = in_relative(head_terms, 1, F, 0, f)
+    come, turned_got, outs_back[0], gain_terms, head_terms = tie(
+        come, turned_got, outs_back[0], gain_terms, head_terms
+    )
     normed_grads = add_all(normed_total, come)
     turned_sum = sum_rest(sum_even(turned_term, turned_got, F), F)
-    near_got = [send_near(0, turned_got), send_near(1, turned_got)]
+    middle = in_part // 2
+
+    def send_near(first, dep):
+        return {
+            r: swap(after(in_terms[r][:, first : first + middle], dep), "fsdp", F, 1)
+            for r in near_odd
+        }
+
+    near_got = [send_near(0, turned_got)]
     own_out_sums = sum_cores(own_parts[0], after(own_out_got, turned_got), S)
     come = sum_first(own_out_sums, S)
-    turned_sum, come, near_got = tie(turned_sum, come, near_got)
-    near_got.extend([send_near(2, turned_sum), send_near(3, turned_sum)])
+    turned_sum, come, near_got[0] = tie(turned_sum, come, near_got[0])
+    near_got.append(send_near(middle, turned_sum))
+    outs_back.append(far_swap(other_outs[half_rows:], turned_sum))
+    gain_terms = halve(after(gain_terms, turned_sum), "seq", S)
+    gain_terms = halve(jnp.concatenate([gain_terms, head_terms], 1), "fsdp", F)[0]
+    head_terms = gain_terms[part * (E + 1) :]
     singles, own_total = sum_more(own_out_sums, come, S)
     own_outs = add_all(own_total, sum_last(singles, S))
     outs_back = jnp.concatenate(outs_back, 0).astype(F32)
@@ -1234,15 +1265,6 @@
     grad_tokens = residual_grads + attn_factor * (
         attn_pulled - inputs_n * jnp.mean(attn_pulled * inputs_n, axis=-1, keepdims=True)
     )
-    late_grads, late_logits = after(second_grads, turned_got), after(logit_grads, turned_got)
-    router_term = jnp.dot(second_low.astype(F32).T, late_logits, precision=HIGHEST)
-    moe_gain_term = jnp.sum(late_grads * residual_n, axis=0)
-    gain_terms = jnp.concatenate(
-        [router_term.reshape(S * F, part * E), moe_gain_term.reshape(S * F, part)], 1
-    )
-    gain_terms = sum_small(gain_terms, (("seq", S, s), ("fsdp", F, f)))
-    head_terms = gain_term.reshape(2, F, part).transpose(1, 0, 2).reshape(F, 2 * part)
-    head_terms = sum_small(after(head_terms, turned_got), (("fsdp", F, f),))
     own_weights = jnp.stack([w_query, w_key, w_value], 0).astype(F32)
     grad_attn_gain = jnp.sum(qkv_term * own_weights, axis=(0, 2)) / attn_gain.astype(F32)
     return (
@@ -1254,7 +1276,7 @@
         grad_output,
         gain_terms[: part * E].reshape(part, E),
         grad_attn_gain,
-        gain_terms[part * E :],
+        gain_terms[part * E : part * (E + 1)],
         head_terms[:part],
         head_terms[part:],
         grad_gate,

time: 1150 us -> 1100 us (0.957)
  local copies, waits for them, and re-layouts: 178 us -> 150 us
  waiting for transfers between devices: 390 us -> 368 us
    ppermute x130 -> x124, waiting for transfers between devices: 389 us -> 368 us  [swap(): return lax.ppermute(values, axis, [(i, i ^ mask) for i in range(size)])]
    dynamic_slice x19 -> x2, local copies, waits for them, and re-layouts: 12.6 us -> 0.16 us  [relative(): lax.dynamic_slice_in_dim(blocks, me ^ r, 1, 0)]
    unnamed x388 -> x346, local copies, waits for them, and re-layouts: 74.1 us -> 65.8 us
    ppermute x130 -> x124, starting transfers between devices: 141 us -> 137 us  [swap(): return lax.ppermute(values, axis, [(i, i ^ mask) for i in range(size)])]
  transfers between devices with their start and end apart: 134 -> 128, of which waited for: 60 -> 56; matrix products, arithmetic and copies ran while one was open for 24% -> 22% of each run, Pallas kernels for 22% -> 23%
where the time goes in v6:
time: 1100 us; the launch traced here: 1090 us
  waiting for transfers between devices  368 us (33%)
  Pallas kernels  255 us (23%)
  starting transfers between devices  153 us (14%)
  local copies, waits for them, and re-layouts  150 us (14%)
  other arithmetic  111 us (10%)
  matrix products  49 us (4%)
    ppermute x124, waiting for transfers between devices, swap(): return lax.ppermute(values, axis, [(i, i ^ mask) for i in range(size)])  368 us
    ppermute x124, starting transfers between devices, swap(): return lax.ppermute(values, axis, [(i, i ^ mask) for i in range(size)])  137 us
    pallas_call x2, Pallas kernels, run_experts(): pl.pallas_call(partial(expert_kernel, in_places, down_places), grid=(step...  119 us
    unnamed x346, local copies, waits for them, and re-layouts  65.8 us
    pallas_call x6, Pallas kernels, products(): pl.pallas_call(product_kernel, grid_spec=pltpu.PrefetchScalarGridSpec(num...  60.5 us
    pallas_call x1, Pallas kernels, attention_backward(): pl.pallas_call(partial(backward_kernel, span), grid=(heads, length // row...  28.1 us
  transfers between devices with their start and end apart: 128, of which 56 were waited for; matrix products, arithmetic and copies ran while one was open for 22% of the time, Pallas kernels for 23%

profile of v6, /device:TPU:0, one launch (start us, length us, event | category | flops | bytes accessed | tf_op | source)
XLA Modules:
  0.0 1088.8 jit_solution(1954837090427084513)
XLA Ops:
  27.7 11.3 %collective-permute-done.4 = bf16[8,5376]{1,0:T(8,128)(2,1)S(1)} collective-permute-done((bf16[8,5376]{1,0:T(8,128)(2,1)S(1)}, bf16[8,5376]{1,0:T(8,128)(2,1)S(1)}, u32[]{:S(2)}, u32[]{:S(2)}) %collective-permute-start.4) | collective-permute-done | bytes 86048 | tf_op jit(solution)/shard_map/ppermute | solution.py:42
  54.4 29.5 %collective-permute-done.6 = bf16[8,64,768]{2,1,0:T(8,128)(2,1)S(1)} collective-permute-done((bf16[8,64,768]{2,1,0:T(8,128)(2,1)S(1)}, bf16[8,64,768]{2,1,0:T(8,128)(2,1)S(1)}, u32[]{:S(2)}, u32[]{:S(2)}) %collective-permute-start.6) | collective-permute-done | bytes 786464 | tf_op jit(solution)/shard_map/ppermute | solution.py:42
  95.7 16.6 %collective-permute-done.11 = bf16[128,2048]{1,0:T(8,128)(2,1)} collective-permute-done((bf16[128,2048]{1,0:T(8,128)(2,1)S(1)}, bf16[128,2048]{1,0:T(8,128)(2,1)}, u32[]{:S(2)}, u32[]{:S(2)}) %collective-permute-start.11) | collective-permute-done | bytes 524320 | tf_op jit(solution)/shard_map/ppermute | solution.py:42
  137.7 11.1 %collective-permute-done.18 = bf16[64,2048]{1,0:T(8,128)(2,1)} collective-permute-done((bf16[64,2048]{1,0:T(8,128)(2,1)S(1)}, bf16[64,2048]{1,0:T(8,128)(2,1)}, u32[]{:S(2)}, u32[]{:S(2)}) %collective-permute-start.18) | collective-permute-done | bytes 262176 | tf_op jit(solution)/shard_map/ppermute | solution.py:42
  152.0 12.7 %project.1 = (bf16[1024,2048]{1,0:T(8,128)(2,1)}, bf16[1024,2048]{1,0:T(8,128)(2,1)}, f32[2048,256]{1,0:T(8,128)S(1)}, f32[2048,256]{1,0:T(8,128)S(1)}, bf16[204...) custom-call(s32[1]{0:T(128)} %bitcast.1.me_ref, bf16[1024,2048]{1,0:T(8,128)(2,1)} %constant_dynamic-update-slice_fusion.even_ref, ...), custom_call_target="tpu_custom_call" | custom-call | flops 6442450944 | bytes 25165824 | tf_op jit(solution)/shard_map/project/pallas_call | solution.py:438
  164.7 10.2 collective-permute-done.16.refs_4_
  198.6 9.4 collective-permute-done.23
  228.4 21.6 %attend.1 = (bf16[2048,256]{1,0:T(8,128)(2,1)S(1)}, f32[2,1,2048]{2,1,0:T(1,128)S(1)}) custom-call(bf16[2048,256]{1,0:T(8,128)(2,1)S(1)} %get-tuple-element.320.q_ref, bf16[2048,256]{1,0:T(8,128)(2,1)S(1)} %get-tuple-element.321.k_ref, bf16[2048,256]{1,0:T(8,128)(2,1)S(1)} %copy-done.20, s32[1,2048]{1,0:T(1,128)S(1)} %copy-done.14, s32[2048,1]{1,0:T(8,128)S(1)} %copy-done.9), custom_call_target="tpu_custom_call" | custom-call | flops 2684354560 | bytes 4194304 | tf_op jit(solution)/shard_map/attend/pallas_call | solution.py:337
  275.1 10.1 collective-permute-done.35
  329.1 12.4 %collective-permute-done.45.refs_12_ = bf16[2,128,1024]{2,1,0:T(8,128)(2,1)} collective-permute-done((bf16[2,128,1024]{2,1,0:T(8,128)(2,1)}, bf16[2,128,1024]{2,1,0:T(8,128)(2,1)}, u32[]{:S(2)}, u32[]{:S(2)}) %collective-permute-start.45) | collective-permute-done | bytes 524320 | tf_op jit(solution)/shard_map/ppermute | solution.py:42
  349.9 7.6 collective-permute-done.50
  392.0 18.6 %collective-permute-done.54.refs_18_ = bf16[2,128,2048]{2,1,0:T(8,128)(2,1)} collective-permute-done((bf16[2,128,2048]{2,1,0:T(8,128)(2,1)}, bf16[2,128,2048]{2,1,0:T(8,128)(2,1)}, u32[]{:S(2)}, u32[]{:S(2)}) %collective-permute-start.54) | collective-permute-done | bytes 1048608 | tf_op jit(solution)/shard_map/ppermute | solution.py:42
  418.4 17.0 %collective-permute-done.53 = bf16[256,2048]{1,0:T(8,128)(2,1)S(1)} collective-permute-done((bf16[256,2048]{1,0:T(8,128)(2,1)S(1)}, bf16[256,2048]{1,0:T(8,128)(2,1)S(1)}, u32[]{:S(2)}, u32[]{:S(2)}) %collective-permute-start.53) | collective-permute-done | bytes 1048608 | tf_op jit(solution)/shard_map/ppermute | solution.py:42
  441.2 7.1 collective-permute-done.59.refs_19_
  457.1 59.4 %experts.2 = (bf16[1024,2048]{1,0:T(8,128)(2,1)}, bf16[1024,2048]{1,0:T(8,128)(2,1)}, bf16[1024,2048]{1,0:T(8,128)(2,1)}, bf16[1024,2048]{1,0:T(8,128)(2,1)}, f3...) custom-call(s32[2]{0:T(128)} %pad_add_fusion.first_ref, ...), custom_call_target="tpu_custom_call" | custom-call | flops 38654705664 | bytes 62914560 | tf_op jit(solution)/shard_map/experts/pallas_call | solution.py:733
  517.2 59.2 %experts.3 = (bf16[1024,2048]{1,0:T(8,128)(2,1)}, bf16[1024,2048]{1,0:T(8,128)(2,1)}, bf16[1024,2048]{1,0:T(8,128)(2,1)}, bf16[1024,2048]{1,0:T(8,128)(2,1)}, f3...) custom-call(s32[2]{0:T(128)} %pad_add_fusion.first_ref, ...), custom_call_target="tpu_custom_call", output_to_operand_aliasing={{6}: (28, {}), {7}: (29, {}), {8}: (30, {}), {9}: (31, {})} | custom-call | flops 38654705664 | bytes 62914560 | tf_op jit(solution)/shard_map/experts/pallas_call | solution.py:733
  585.0 9.4 in_products.4
  627.7 11.0 %down_products.2 = bf16[2,256,2048]{2,1,0:T(8,128)(2,1)} custom-call(s32[1]{0:T(128)} %bitcast.27.me_ref, bf16[2,2304,512]{2,1,0:T(8,128)(2,1)} %get-tuple-element.478.left_ref, bf16[2,2304,2048]{2,1,0:T(8,128)(2,1)} %get-tuple-element.453.right_ref), custom_call_target="tpu_custom_call" | custom-call | flops 4831838208 | bytes 21233664 | tf_op jit(solution)/shard_map/down_products/pallas_call | solution.py:770
  638.6 11.9 %collective-permute-done.72 = f32[8,512]{0,1:T(8,128)S(1)} collective-permute-done((f32[8,512]{0,1:T(8,128)}, f32[8,512]{0,1:T(8,128)S(1)}, u32[]{:S(2)}, u32[]{:S(2)}) %collective-permute-start.72) | collective-permute-done | bytes 16416 | tf_op jit(solution)/shard_map/ppermute | solution.py:42
  664.2 9.5 in_products.5
  674.4 10.6 collective-permute-done.75
  698.0 10.1 in_products.6
  708.1 7.8 collective-permute-done.80
  732.2 11.0 %down_products.3 = bf16[2,256,2048]{2,1,0:T(8,128)(2,1)} custom-call(s32[1]{0:T(128)} %bitcast.27.me_ref, bf16[2,2304,512]{2,1,0:T(8,128)(2,1)} %get-tuple-element.478.left_ref, bf16[2,2304,2048]{2,1,0:T(8,128)(2,1)} %get-tuple-element.453.right_ref), custom_call_target="tpu_custom_call" | custom-call | flops 4831838208 | bytes 21233664 | tf_op jit(solution)/shard_map/down_products/pallas_call | solution.py:770
  776.9 9.6 in_products.7
  806.0 28.1 %attend_back.1 = (bf16[2048,256]{1,0:T(8,128)(2,1)S(1)}, bf16[2048,256]{1,0:T(8,128)(2,1)S(1)}, bf16[2048,256]{1,0:T(8,128)(2,1)S(1)}) custom-call(bf16[2048,256]{1,0:T(8,128)(2,1)S(1)} %copy-done.16, bf16[2048,256]{1,0:T(8,128)(2,1)S(1)} %copy-done.18, bf16[2048,256]{1,0:T(8,128)(2,1)} %copy-done.19, bf16[2048,256]{1,0:T(8,128)(2,1)} %bitcast.365, ...), custom_call_target="tpu_custom_call" | custom-call | flops 6710886400 | bytes 7340032 | tf_op jit(solution)/shard_map/attend_back/pallas_call | solution.py:369
  858.9 8.4 collective-permute-done.95
  880.9 8.1 convolution_convert_fusion.2
  907.3 8.5 collective-permute-done.102
  953.0 23.9 %collective-permute-done.109 = bf16[128,2048]{1,0:T(8,128)(2,1)} collective-permute-done((bf16[128,2048]{1,0:T(8,128)(2,1)}, bf16[128,2048]{1,0:T(8,128)(2,1)}, u32[]{:S(2)}, u32[]{:S(2)}) %collective-permute-start.109) | collective-permute-done | bytes 524320 | tf_op jit(solution)/shard_map/ppermute | solution.py:42
  989.3 23.4 %collective-permute-done.110 = bf16[1,8,64,512]{3,2,1,0:T(8,128)(2,1)S(1)} collective-permute-done((bf16[1,8,64,512]{3,2,1,0:T(8,128)(2,1)S(1)}, bf16[1,8,64,512]{3,2,1,0:T(8,128)(2,1)S(1)}, u32[]{:S(2)}, u32[]{:S(2)}) %collective-permute-start.110) | collective-permute-done | bytes 524320 | tf_op jit(solution)/shard_map/ppermute | solution.py:42
  1038.1 17.1 %collective-permute-done.121 = f32[2,1216]{1,0:T(2,128)S(1)} collective-permute-done((f32[2,1216]{1,0:T(2,128)S(1)}, f32[2,1216]{1,0:T(2,128)S(1)}, u32[]{:S(2)}, u32[]{:S(2)}) %collective-permute-start.121) | collective-permute-done | bytes 9760 | tf_op jit(solution)/shard_map/ppermute | solution.py:42
  (809 shorter events, 563.6 us)
Async XLA Ops:
  47.2 36.7 %collective-permute-start.8 = (bf16[256,2048]{1,0:T(8,128)(2,1)S(1)}, bf16[256,2048]{1,0:T(8,128)(2,1)S(1)}, u32[]{:S(2)}, u32[]{:S(2)}) collective-permute-start(bf16[256,2048]{1,0:T(8,128)(2,1)S(1)} %bitcast.326), channel_id=1, source_target_pairs={{0,8},{4,12},{8,0},{12,4},{16,24},{20,28},{24,16},{28,20},{1,9},{5... | collective-permute-start | bytes 3145736 | tf_op jit(solution)/shard_map/ppermute | solution.py:42
  47.9 36.0 %collective-permute-start.9 = (bf16[256,2048]{1,0:T(8,128)(2,1)S(1)}, bf16[256,2048]{1,0:T(8,128)(2,1)S(1)}, u32[]{:S(2)}, u32[]{:S(2)}) collective-permute-start(bf16[256,2048]{1,0:T(8,128)(2,1)S(1)} %bitcast.327), channel_id=1, source_target_pairs={{0,16},{4,20},{8,24},{12,28},{16,0},{20,4},{24,8},{28,12},{1,17},{... | collective-permute-start | bytes 3145736 | tf_op jit(solution)/shard_map/ppermute | solution.py:42
  49.3 34.6 %collective-permute-start.6 = (bf16[8,64,768]{2,1,0:T(8,128)(2,1)S(1)}, bf16[8,64,768]{2,1,0:T(8,128)(2,1)S(1)}, u32[]{:S(2)}, u32[]{:S(2)}) collective-permute-start(bf16[8,64,768]{2,1,0:T(8,128)(2,1)S(1)} %all-to-all-done), channel_id=1, source_target_pairs={{0,1},{1,0},{2,3},{3,2},{4,5},{5,4},{6,7},{7,6},{8,9},{9,8},{10,11... | collective-permute-start | bytes 2359304 | tf_op jit(solution)/shard_map/ppermute | solution.py:42
  49.7 34.2 %collective-permute-start.7 = (bf16[8,64,768]{2,1,0:T(8,128)(2,1)S(1)}, bf16[8,64,768]{2,1,0:T(8,128)(2,1)S(1)}, u32[]{:S(2)}, u32[]{:S(2)}) collective-permute-start(bf16[8,64,768]{2,1,0:T(8,128)(2,1)S(1)} %all-to-all-done), channel_id=1, source_target_pairs={{0,2},{1,3},{2,0},{3,1},{4,6},{5,7},{6,4},{7,5},{8,10},{9,11},{10,... | collective-permute-start | bytes 2359304 | tf_op jit(solution)/shard_map/ppermute | solution.py:42
  116.1 35.8 %collective-permute-start.14 = (bf16[1024,2048]{1,0:T(8,128)(2,1)}, bf16[1024,2048]{1,0:T(8,128)(2,1)}, u32[]{:S(2)}, u32[]{:S(2)}) collective-permute-start(bf16[1024,2048]{1,0:T(8,128)(2,1)} %constant_dynamic-update-slice_fusion.even_ref), channel_id=1, source_target_pairs={{0,4},{4,0},{8,12},{12,8},{16,20},{20,16},{24,28},{28,24},{1,5},{5... | collective-permute-start | bytes 12582920 | tf_op jit(solution)/shard_map/ppermute | solution.py:42
  131.9 47.0 %collective-permute-start.20 = (bf16[256,2048]{1,0:T(8,128)(2,1)}, bf16[256,2048]{1,0:T(8,128)(2,1)}, u32[]{:S(2)}, u32[]{:S(2)}) collective-permute-start(bf16[256,2048]{1,0:T(8,128)(2,1)} %bitcast.15), channel_id=1, source_target_pairs={{0,8},{4,12},{8,0},{12,4},{16,24},{20,28},{24,16},{28,20},{1,9},{5... | collective-permute-start | bytes 3145736 | tf_op jit(solution)/shard_map/ppermute | solution.py:42
  133.3 45.6 %collective-permute-start.21 = (bf16[256,2048]{1,0:T(8,128)(2,1)}, bf16[256,2048]{1,0:T(8,128)(2,1)}, u32[]{:S(2)}, u32[]{:S(2)}) collective-permute-start(bf16[256,2048]{1,0:T(8,128)(2,1)} %bitcast.15), channel_id=1, source_target_pairs={{0,16},{4,20},{8,24},{12,28},{16,0},{20,4},{24,8},{28,12},{1,17},{... | collective-permute-start | bytes 3145736 | tf_op jit(solution)/shard_map/ppermute | solution.py:42
  215.5 35.4 %collective-permute-start.31 = (bf16[2,128,1024]{2,1,0:T(8,128)(2,1)S(1)}, bf16[2,128,1024]{2,1,0:T(8,128)(2,1)S(1)}, u32[]{:S(2)}, u32[]{:S(2)}) collective-permute-start(bf16[2,128,1024]{2,1,0:T(8,128)(2,1)S(1)} %copy-done.102), channel_id=1, source_target_pairs={{0,2},{1,3},{2,0},{3,1},{4,6},{5,7},{6,4},{7,5},{8,10},{9,11},{10,... | collective-permute-start | bytes 1572872 | tf_op jit(solution)/shard_map/ppermute | solution.py:42
  217.7 33.2 %collective-permute-start.32 = (bf16[2,64,2048]{2,1,0:T(8,128)(2,1)S(1)}, bf16[2,64,2048]{2,1,0:T(8,128)(2,1)S(1)}, u32[]{:S(2)}, u32[]{:S(2)}) collective-permute-start(bf16[2,64,2048]{2,1,0:T(8,128)(2,1)S(1)} %copy-done.104), channel_id=1, source_target_pairs={{0,1},{1,0},{2,3},{3,2},{4,5},{5,4},{6,7},{7,6},{8,9},{9,8},{10,11... | collective-permute-start | bytes 1572872 | tf_op jit(solution)/shard_map/ppermute | solution.py:42
  252.8 55.9 %collective-permute-start.37 = (bf16[1024,2048]{1,0:T(8,128)(2,1)}, bf16[1024,2048]{1,0:T(8,128)(2,1)}, u32[]{:S(2)}, u32[]{:S(2)}) collective-permute-start(bf16[1024,2048]{1,0:T(8,128)(2,1)} %constant_dynamic-update-slice_fusion.13), channel_id=1, source_target_pairs={{0,4},{4,0},{8,12},{12,8},{16,20},{20,16},{24,28},{28,24},{1,5},{5... | collective-permute-start | bytes 12582920 | tf_op jit(solution)/shard_map/ppermute | solution.py:42
  255.0 39.7 %all-to-all-start.1 = ((bf16[8,256,256]{1,2,0:T(8,128)(2,1)}), bf16[8,256,256]{1,2,0:T(8,128)(2,1)}, u32[]{:S(2)}, u32[]{:S(2)}) async-start(bf16[8,256,256]{1,2,0:T(8,128)(2,1)} %copy.99), calls=%async_computation.1 | async-start | bytes 2097152 | tf_op jit(solution)/shard_map/all_to_all | solution.py:938
  325.5 32.0 %collective-permute-start.50 = (bf16[128,2048]{1,0:T(8,128)(2,1)S(1)}, bf16[128,2048]{1,0:T(8,128)(2,1)S(1)}, u32[]{:S(2)}, u32[]{:S(2)}) collective-permute-start(bf16[128,2048]{1,0:T(8,128)(2,1)S(1)} %slice.579), channel_id=1, source_target_pairs={{0,16},{4,20},{8,24},{12,28},{16,0},{20,4},{24,8},{28,12},{1,17},{... | collective-permute-start | bytes 1572872 | tf_op jit(solution)/shard_map/ppermute | solution.py:42
  370.6 64.8 %collective-permute-start.55 = (bf16[1024,2048]{1,0:T(8,128)(2,1)}, bf16[1024,2048]{1,0:T(8,128)(2,1)}, u32[]{:S(2)}, u32[]{:S(2)}) collective-permute-start(bf16[1024,2048]{1,0:T(8,128)(2,1)} %constant_dynamic-update-slice_fusion.18.xa_ref), channel_id=1, source_target_pairs={{0,4},{4,0},{8,12},{12,8},{16,20},{20,16},{24,28},{28,24},{1,5},{5... | collective-permute-start | bytes 12582920 | tf_op jit(solution)/shard_map/ppermute | solution.py:42
  372.3 68.9 %collective-permute-start.60 = (bf16[1024,2048]{1,0:T(8,128)(2,1)}, bf16[1024,2048]{1,0:T(8,128)(2,1)}, u32[]{:S(2)}, u32[]{:S(2)}) collective-permute-start(bf16[1024,2048]{1,0:T(8,128)(2,1)} %constant_dynamic-update-slice_fusion.44.ua_ref), channel_id=1, source_target_pairs={{0,4},{4,0},{8,12},{12,8},{16,20},{20,16},{24,28},{28,24},{1,5},{5... | collective-permute-start | bytes 12582920 | tf_op jit(solution)/shard_map/ppermute | solution.py:42
  383.7 73.4 %collective-permute-start.56 = (bf16[1024,2048]{1,0:T(8,128)(2,1)}, bf16[1024,2048]{1,0:T(8,128)(2,1)}, u32[]{:S(2)}, u32[]{:S(2)}) collective-permute-start(bf16[1024,2048]{1,0:T(8,128)(2,1)} %constant_dynamic-update-slice_fusion.39.ua_ref), channel_id=1, source_target_pairs={{0,4},{4,0},{8,12},{12,8},{16,20},{20,16},{24,28},{28,24},{1,5},{5... | collective-permute-start | bytes 12582920 | tf_op jit(solution)/shard_map/ppermute | solution.py:42
  451.8 64.7 %collective-permute-start.61 = (bf16[1024,2048]{1,0:T(8,128)(2,1)}, bf16[1024,2048]{1,0:T(8,128)(2,1)}, u32[]{:S(2)}, u32[]{:S(2)}) collective-permute-start(bf16[1024,2048]{1,0:T(8,128)(2,1)} %constant_dynamic-update-slice_fusion.50.xa_ref), channel_id=1, source_target_pairs={{0,4},{4,0},{8,12},{12,8},{16,20},{20,16},{24,28},{28,24},{1,5},{5... | collective-permute-start | bytes 12582920 | tf_op jit(solution)/shard_map/ppermute | solution.py:42
  516.5 59.9 %collective-permute-start.62 = (bf16[1024,2048]{1,0:T(8,128)(2,1)}, bf16[1024,2048]{1,0:T(8,128)(2,1)}, u32[]{:S(2)}, u32[]{:S(2)}) collective-permute-start(bf16[1024,2048]{1,0:T(8,128)(2,1)} %get-tuple-element.423), channel_id=1, source_target_pairs={{0,4},{4,0},{8,12},{12,8},{16,20},{20,16},{24,28},{28,24},{1,5},{5... | collective-permute-start | bytes 12582920 | tf_op jit(solution)/shard_map/ppermute | solution.py:42
  517.1 59.3 %collective-permute-start.63 = (bf16[1024,2048]{1,0:T(8,128)(2,1)}, bf16[1024,2048]{1,0:T(8,128)(2,1)}, u32[]{:S(2)}, u32[]{:S(2)}) collective-permute-start(bf16[1024,2048]{1,0:T(8,128)(2,1)} %get-tuple-element.424), channel_id=1, source_target_pairs={{0,4},{4,0},{8,12},{12,8},{16,20},{20,16},{24,28},{28,24},{1,5},{5... | collective-permute-start | bytes 12582920 | tf_op jit(solution)/shard_map/ppermute | solution.py:42
  799.5 38.2 %collective-permute-start.92 = (bf16[128,2048]{1,0:T(8,128)(2,1)}, bf16[128,2048]{1,0:T(8,128)(2,1)S(1)}, u32[]{:S(2)}, u32[]{:S(2)}) collective-permute-start(bf16[128,2048]{1,0:T(8,128)(2,1)} %get-tuple-element.495), channel_id=1, source_target_pairs={{0,16},{4,20},{8,24},{12,28},{16,0},{20,4},{24,8},{28,12},{1,17},{... | collective-permute-start | bytes 1572872 | tf_op jit(solution)/shard_map/ppermute | solution.py:42
  800.2 37.4 %collective-permute-start.93 = (bf16[128,2048]{1,0:T(8,128)(2,1)S(1)}, bf16[128,2048]{1,0:T(8,128)(2,1)S(1)}, u32[]{:S(2)}, u32[]{:S(2)}) collective-permute-start(bf16[128,2048]{1,0:T(8,128)(2,1)S(1)} %get-tuple-element.496), channel_id=1, source_target_pairs={{0,8},{4,12},{8,0},{12,4},{16,24},{20,28},{24,16},{28,20},{1,9},{5... | collective-permute-start | bytes 1572872 | tf_op jit(solution)/shard_map/ppermute | solution.py:42
  800.9 36.8 %collective-permute-start.91 = (bf16[2,64,2048]{2,1,0:T(8,128)(2,1)}, bf16[2,64,2048]{2,1,0:T(8,128)(2,1)S(1)}, u32[]{:S(2)}, u32[]{:S(2)}) collective-permute-start(bf16[2,64,2048]{2,1,0:T(8,128)(2,1)} %get-tuple-element.491), channel_id=1, source_target_pairs={{0,1},{1,0},{2,3},{3,2},{4,5},{5,4},{6,7},{7,6},{8,9},{9,8},{10,11... | collective-permute-start | bytes 1572872 | tf_op jit(solution)/shard_map/ppermute | solution.py:42
  803.3 34.4 %collective-permute-start.90 = (bf16[2,128,1024]{2,1,0:T(8,128)(2,1)}, bf16[2,128,1024]{2,1,0:T(8,128)(2,1)S(1)}, u32[]{:S(2)}, u32[]{:S(2)}) collective-permute-start(bf16[2,128,1024]{2,1,0:T(8,128)(2,1)} %get-tuple-element.490), channel_id=1, source_target_pairs={{0,2},{1,3},{2,0},{3,1},{4,6},{5,7},{6,4},{7,5},{8,10},{9,11},{10,... | collective-permute-start | bytes 1572872 | tf_op jit(solution)/shard_map/ppermute | solution.py:42
  843.2 33.0 %collective-permute-start.97 = (bf16[256,2048]{1,0:T(8,128)(2,1)S(1)}, bf16[256,2048]{1,0:T(8,128)(2,1)S(1)}, u32[]{:S(2)}, u32[]{:S(2)}) collective-permute-start(bf16[256,2048]{1,0:T(8,128)(2,1)S(1)} %pad_maximum_fusion.15), channel_id=1, source_target_pairs={{0,8},{4,12},{8,0},{12,4},{16,24},{20,28},{24,16},{28,20},{1,9},{5... | collective-permute-start | bytes 3145736 | tf_op jit(solution)/shard_map/ppermute | solution.py:42
  844.7 32.5 %collective-permute-start.98 = (bf16[256,2048]{1,0:T(8,128)(2,1)S(1)}, bf16[256,2048]{1,0:T(8,128)(2,1)}, u32[]{:S(2)}, u32[]{:S(2)}) collective-permute-start(bf16[256,2048]{1,0:T(8,128)(2,1)S(1)} %pad_maximum_fusion.16), channel_id=1, source_target_pairs={{0,16},{4,20},{8,24},{12,28},{16,0},{20,4},{24,8},{28,12},{1,17},{... | collective-permute-start | bytes 3145736 | tf_op jit(solution)/shard_map/ppermute | solution.py:42
  896.1 48.9 %collective-permute-start.117 = (bf16[1,64,2048]{2,1,0:T(8,128)(2,1)S(1)}, bf16[1,64,2048]{2,1,0:T(8,128)(2,1)S(1)}, u32[]{:S(2)}, u32[]{:S(2)}) collective-permute-start(bf16[1,64,2048]{2,1,0:T(8,128)(2,1)S(1)} %slice_bitcast_fusion.4), channel_id=1, source_target_pairs={{0,2},{1,3},{2,0},{3,1},{4,6},{5,7},{6,4},{7,5},{8,10},{9,11},{10,... | collective-permute-start | bytes 786440 | tf_op jit(solution)/shard_map/ppermute | solution.py:42
  940.5 36.4 %collective-permute-start.106 = (bf16[256,2048]{1,0:T(8,128)(2,1)}, bf16[256,2048]{1,0:T(8,128)(2,1)}, u32[]{:S(2)}, u32[]{:S(2)}) collective-permute-start(bf16[256,2048]{1,0:T(8,128)(2,1)} %pad_maximum_fusion.18), channel_id=1, source_target_pairs={{0,8},{4,12},{8,0},{12,4},{16,24},{20,28},{24,16},{28,20},{1,9},{5... | collective-permute-start | bytes 3145736 | tf_op jit(solution)/shard_map/ppermute | solution.py:42
  941.3 35.6 %collective-permute-start.107 = (bf16[256,2048]{1,0:T(8,128)(2,1)}, bf16[256,2048]{1,0:T(8,128)(2,1)}, u32[]{:S(2)}, u32[]{:S(2)}) collective-permute-start(bf16[256,2048]{1,0:T(8,128)(2,1)} %pad_maximum_fusion.19), channel_id=1, source_target_pairs={{0,16},{4,20},{8,24},{12,28},{16,0},{20,4},{24,8},{28,12},{1,17},{... | collective-permute-start | bytes 3145736 | tf_op jit(solution)/shard_map/ppermute | solution.py:42
  943.2 34.5 %collective-permute-start.108 = (bf16[2,8,64,512]{3,2,1,0:T(8,128)(2,1)}, bf16[2,8,64,512]{3,2,1,0:T(8,128)(2,1)}, u32[]{:S(2)}, u32[]{:S(2)}) collective-permute-start(bf16[2,8,64,512]{3,2,1,0:T(8,128)(2,1)} %slice.673), channel_id=1, source_target_pairs={{0,1},{1,0},{2,3},{3,2},{4,5},{5,4},{6,7},{7,6},{8,9},{9,8},{10,11... | collective-permute-start | bytes 3145736 | tf_op jit(solution)/shard_map/ppermute | solution.py:42
  979.6 34.0 %collective-permute-start.113 = (bf16[2,256,1024]{2,1,0:T(8,128)(2,1)}, bf16[2,256,1024]{2,1,0:T(8,128)(2,1)}, u32[]{:S(2)}, u32[]{:S(2)}) collective-permute-start(bf16[2,256,1024]{2,1,0:T(8,128)(2,1)} %get-tuple-element.535), channel_id=1, source_target_pairs={{0,1},{1,0},{2,3},{3,2},{4,5},{5,4},{6,7},{7,6},{8,9},{9,8},{10,11... | collective-permute-start | bytes 3145736 | tf_op jit(solution)/shard_map/ppermute | solution.py:42
  1019.7 56.4 %collective-permute-start.123 = (bf16[2,256,1024]{2,1,0:T(8,128)(2,1)}, bf16[2,256,1024]{2,1,0:T(8,128)(2,1)}, u32[]{:S(2)}, u32[]{:S(2)}) collective-permute-start(bf16[2,256,1024]{2,1,0:T(8,128)(2,1)} %get-tuple-element.552), channel_id=1, source_target_pairs={{0,1},{1,0},{2,3},{3,2},{4,5},{5,4},{6,7},{7,6},{8,9},{9,8},{10,11... | collective-permute-start | bytes 3145736 | tf_op jit(solution)/shard_map/ppermute | solution.py:42
  1023.9 37.1 %all-to-all-start.3 = ((bf16[8,64,768]{2,1,0:T(8,128)(2,1)}), bf16[8,64,768]{2,1,0:T(8,128)(2,1)}, u32[]{:S(2)}, u32[]{:S(2)}) async-start(bf16[8,64,768]{2,1,0:T(8,128)(2,1)} %pad_maximum_fusion.22), calls=%async_computation.3 | async-start | bytes 1572864 | tf_op jit(solution)/shard_map/all_to_all | solution.py:1241
  1028.2 56.8 %collective-permute-start.116 = (bf16[128,2048]{1,0:T(8,128)(2,1)}, bf16[128,2048]{1,0:T(8,128)(2,1)}, u32[]{:S(2)}, u32[]{:S(2)}) collective-permute-start(bf16[128,2048]{1,0:T(8,128)(2,1)} %get-tuple-element.542), channel_id=1, source_target_pairs={{0,2},{1,3},{2,0},{3,1},{4,6},{5,7},{6,4},{7,5},{8,10},{9,11},{10,... | collective-permute-start | bytes 1572872 | tf_op jit(solution)/shard_map/ppermute | solution.py:42
  (230 other events, 3442.6 us)

commit v7 on v6

--- a/solution.py
+++ b/solution.py
@@ -188,8 +188,7 @@
     return values
 
 
-def halve(values, axis, size):
-    mask = size // 2
+def halve(values, axis, size, mask):
     while mask:
         half = values.shape[0] // 2
         values = values[:half] + swap(values[half:], axis, size, mask)
@@ -865,21 +864,42 @@
     crossed = split_heads(w_query, w_key, w_value, S)
     small = double(after(small, crossed), "fsdp", F)
     crossed = lax.all_to_all(crossed, "seq", split_axis=0, concat_axis=0, tiled=True)
-    near_own = [near_swap(hidden_part(half_at, 0, 2 * quarter), small)]
+    near_own = {0: near_swap(hidden_part(half_at, 0, quarter), small)}
+    out_pieces = fsdp_pieces(after(w_output, small), F)
     small = double(small, "seq", S)
-    crossed, near_own[0], small = tie(crossed, near_own[0], small)
-
-    small = in_order(small, S, F, s, f).reshape(S, F, -1)
+    crossed, near_own[0], out_pieces, small = tie(crossed, near_own[0], out_pieces, small)
+
+    own_parts = {n: hidden_part(half_at, n * quarter, quarter) for n in range(1, 4)}
+    other_parts = [hidden_part(1 - half_at, n * quarter, quarter) for n in range(4)]
+    down_rows = quarters(w_down, 1)
+    down_rows = [down_rows[0], jnp.concatenate(down_rows[1:3], 1), down_rows[3]]
+    upstream_halves = [upstream_low[:half_rows], upstream_low[half_rows:]]
+    own_output = place_fsdp(out_pieces, f, 0).reshape(C, D)
+    places = jnp.arange(L, dtype=jnp.int32).astype(F32)
+    freqs = ROPE_BASE ** (-(jnp.arange(DH // 2, dtype=F32) * 2.0 / DH))
+    angles = places[:, None] * freqs[None, :]
+    cosine, sine = jnp.cos(angles), jnp.sin(angles)
+    cosine = jnp.concatenate([cosine, cosine], 1)
+    sine = jnp.concatenate([-sine, sine], 1)
+    seg_row, seg_col = segments, segments.reshape(L, 1)
+    prepared = (
+        own_parts, other_parts, down_rows, upstream_halves, own_output, cosine, sine, seg_col
+    )
     token_first = gather_first(after(tokens_low, crossed), S)
     qkv_pieces = {0: crossed}
     for r in range(1, F):
         low = low_bit(r)
         qkv_pieces[r] = swap(qkv_pieces[r ^ low], "fsdp", F, low)
         if r == half_f:
-            qkv_pieces, token_first = tie(qkv_pieces, token_first)
-            partner_up = [far_swap(upstream_low[:half_rows], qkv_pieces[r])]
+            qkv_pieces, token_first, prepared = tie(qkv_pieces, token_first, prepared)
+    own_parts, other_parts, down_rows, upstream_halves, own_output, cosine, sine, seg_col = prepared
+    partner_up = [far_swap(upstream_halves[0])]
     token_more = gather_more(tokens_low, token_first, S)
-    qkv_pieces, partner_up[0], token_more = tie(qkv_pieces, partner_up[0], token_more)
+    out_first = gather_first(own_output, S)
+    small = in_order(small, S, F, s, f).reshape(S, F, -1)
+    qkv_pieces, partner_up[0], token_more, out_first, small = tie(
+        qkv_pieces, partner_up[0], token_more, out_first, small
+    )
     tokens_even, tokens_odd = gather_end(tokens_low, token_first, token_more, S)
     w_qkv = place_fsdp(qkv_pieces, f, 1).reshape(D, 3 * C)
 
@@ -896,51 +916,43 @@
         ranks = relative(ranks[:, 0], s).astype(jnp.int32)
         return ranks[: S // 2], ranks[S // 2 :]
 
-    places = jnp.arange(L, dtype=jnp.int32).astype(F32)
-    freqs = ROPE_BASE ** (-(jnp.arange(DH // 2, dtype=F32) * 2.0 / DH))
-    angles = places[:, None] * freqs[None, :]
-    cosine, sine = jnp.cos(angles), jnp.sin(angles)
-    cosine = jnp.concatenate([cosine, cosine], 1)
-    sine = jnp.concatenate([-sine, sine], 1)
-
     def far_part(n, *dep):
-        return far_swap(hidden_part(1 - half_at, n * quarter, quarter), *dep)
-
-    partner_up.append(far_swap(upstream_low[half_rows:], w_qkv))
-    near_own.append(near_swap(hidden_part(half_at, 2 * quarter, quarter), w_qkv))
-    out_pieces = fsdp_pieces(after(w_output, w_qkv), F)
-    own_up_first = gather_first(after(upstream_low, w_qkv), S)
+        return far_swap(other_parts[n], *dep)
+
+    partner_up.append(far_swap(upstream_halves[1], w_qkv))
+    near_own[2] = near_swap(own_parts[2], w_qkv)
+    out_more = gather_more(after(own_output, w_qkv), out_first, S)
     normed_even, normed_odd, query_pre, key_pre, value_low, squares = project(
         tokens_even, tokens_odd, w_qkv, gain_attn[None], me, T
     )
-    squares, partner_up[1], near_own[1], out_pieces, own_up_first = tie(
-        squares, partner_up[1], near_own[1], out_pieces, own_up_first
-    )
-    partner_up = jnp.concatenate(partner_up, 0)
-    own_output = place_fsdp(out_pieces, f, 0).reshape(C, D)
-
-    out_first = gather_first(own_output, S)
+    squares, partner_up[1], near_own[2], out_more = tie(
+        squares, partner_up[1], near_own[2], out_more
+    )
+
+    out_even, out_odd = gather_end(own_output, out_first, out_more, S)
+    own_up_first = gather_first(after(upstream_low, squares), S)
     far = [far_part(0, squares)]
-    near_own.append(near_swap(hidden_part(half_at, 3 * quarter, quarter), squares))
+    near_own[3] = near_swap(own_parts[3], squares)
     squares = sum_all(squares, "seq", S)
     query_low, key_low = rope(query_pre, key_pre, squares, head_gain, cosine, sine)
-    query_low, out_first, far[0], near_own[2] = tie(query_low, out_first, far[0], near_own[2])
-
-    seg_row = segments
-    seg_col = segments.reshape(L, 1)
-    out_more = gather_more(own_output, out_first, S)
+    query_low, own_up_first, far[0], near_own[3], out_even, out_odd = tie(
+        query_low, own_up_first, far[0], near_own[3], out_even, out_odd
+    )
+
+    own_up_more = gather_more(after(upstream_low, query_low), own_up_first, S)
     far.append(far_part(1, query_low))
-    down_rows = quarters(w_down, 1)
     down = [near_swap(down_rows[0], query_low)]
     attended, lse = attention_forward(query_low, key_low, value_low, seg_row, seg_col)
-    attended, out_more, far[1], down[0] = tie(attended, out_more, far[1], down[0])
+    attended, own_up_more, far[1], down[0] = tie(attended, own_up_more, far[1], down[0])
     attended_blocks = attended.reshape(S, T, C)
     come = lax.all_to_all(attended_blocks, "seq", split_axis=0, concat_axis=0, tiled=True)
-    out_even, out_odd = gather_end(own_output, out_first, out_more, S)
+    partner_up = after(jnp.concatenate(partner_up, 0), attended)
+    near_own[1] = near_swap(own_parts[1], attended)
     far.append(far_part(2, attended))
     near_far = [near_swap(far[0], attended)]
-    own_up_more = gather_more(after(upstream_low, attended), own_up_first, S)
-    come, far[2], near_far[0], own_up_more = tie(come, far[2], near_far[0], own_up_more)
+    come, far[2], near_far[0], near_own[1], partner_up = tie(
+        come, far[2], near_far[0], near_own[1], partner_up
+    )
     own_u = gather_end(upstream_low, own_up_first, own_up_more, S)
     far.append(far_part(3, come))
     near_far.append(near_swap(far[1], come))
@@ -950,14 +962,17 @@
     moe_factor = rms_factor(residual)
     residual_n = residual * moe_factor
     second_low = (residual_n * gain_moe).astype(BF16)
-    second_low, far[3], near_far[1], partner_up_first = tie(
-        second_low, far[3], near_far[1], partner_up_first
+    second_low, far[3], near_far[1], partner_up_first, own_u = tie(
+        second_low, far[3], near_far[1], partner_up_first, own_u
     )
 
     own_first = gather_first(second_low, S)
     partner_low = [far_swap(second_low[:half_rows])]
     near_far.append(near_swap(far[2], second_low))
-    own_first, partner_low[0], near_far[2] = tie(own_first, partner_low[0], near_far[2])
+    own_ranks, other_ranks = ranks_of(f), ranks_of(f ^ half_f)
+    own_first, partner_low[0], near_far[2], own_ranks, other_ranks = tie(
+        own_first, partner_low[0], near_far[2], own_ranks, other_ranks
+    )
     own_more = gather_more(second_low, own_first, S)
     partner_low.append(far_swap(second_low[half_rows:], own_first))
     near_far.append(near_swap(far[3], own_first))
@@ -968,21 +983,18 @@
     partner_low = jnp.concatenate(partner_low, 0)
     own_x = gather_end(second_low, own_first, own_more, S)
     partner_first = gather_first(after(partner_low, own_more), S)
-    down.append(near_swap(jnp.concatenate(down_rows[1:3], 1), own_more))
-    own_ranks, other_ranks = ranks_of(f), ranks_of(f ^ half_f)
-    partner_first, down[1], own_x, own_ranks, other_ranks = tie(
-        partner_first, down[1], own_x, own_ranks, other_ranks
-    )
-    other_u = gather_end(partner_up, partner_up_first, partner_up_more, S)
+    down.append(near_swap(down_rows[1], own_more))
+    partner_first, down[1], own_x = tie(partner_first, down[1], own_x)
+    other_u = gather_end(after(partner_up, partner_first), partner_up_first, partner_up_more, S)
     partner_more = gather_more(partner_low, partner_first, S)
-    down.append(near_swap(down_rows[3], partner_first))
+    down.append(near_swap(down_rows[2], partner_first))
     partner_more, down[2], other_u = tie(partner_more, down[2], other_u)
     other_x = gather_end(partner_low, partner_first, partner_more, S)
     in_pieces = []
     for r in range(F):
-        for n, rows in enumerate(near_own if r < half_f else near_far):
-            first = (0, 2, 3)[n] if r < half_f else n
-            in_pieces.append((r, first * quarter, rows[r % half_f]))
+        for n in range(4):
+            rows = near_own[n] if r < half_f else near_far[n]
+            in_pieces.append((r, n * quarter, rows[r % half_f]))
     down_pieces = [
         (r, (0, 1, 3)[n] * (down_part // 4), down[n][r]) for r in range(half_f) for n in range(3)
     ]
@@ -1137,11 +1149,7 @@
         [matmul_t(branch_even, own_output), matmul_t(branch_odd, own_output)], 0
     ).astype(BF16)
     head_grads = absolute(head_grads.reshape(S, T, C), s).reshape(L, C)
-    for r in near_odd:
-        in_products(r ^ 1, branch_more)
-    head_grads, far_sums[1], down_got[2], in_terms = tie(
-        head_grads, far_sums[1], down_got[2], in_terms
-    )
+    head_grads, far_sums[1], down_got[2] = tie(head_grads, far_sums[1], down_got[2])
     far_sums.append(far_sum(2, head_grads))
     down_got.append(send_down(3, head_grads))
     other_out_sums = sum_cores(other_parts[0], after(other_out_got, head_grads), S)
@@ -1173,6 +1181,7 @@
         means, come, far_sums[3], output_got, value_term
     )
     other_outs = add_all(other_total, come).astype(BF16)
+    outs_back = [far_swap(other_outs[:half_rows])]
     value_got = swap(value_term[: F // 2], "fsdp", F, 1)
     pre_rel = rope_back(
         (query_back, key_back, value_back),
@@ -1188,7 +1197,9 @@
     ).reshape(2, L // 2, 3 * C)
     normed_got = swap(matmul_t(pre_rel[1], w_qkv).astype(BF16), "seq", S, 1)
     normed_kept = matmul_t(pre_rel[0], w_qkv).astype(BF16)
-    normed_got, normed_kept, value_got = tie(normed_got, normed_kept, value_got)
+    normed_got, normed_kept, value_got, outs_back[0] = tie(
+        normed_got, normed_kept, value_got, outs_back[0]
+    )
 
     normed_sums = sum_cores(normed_kept, normed_got, S)
     come = sum_first(normed_sums, S)
@@ -1196,23 +1207,25 @@
     turned_term = weight_term(
         after(pre_rel[0][:, : 2 * C], normed_got), after(pre_rel[1][:, : 2 * C], normed_got)
     )
-    come, turned_term, value_sum = tie(come, turned_term, value_sum)
-    turned_got = swap(turned_term[: F // 2], "fsdp", F, 1)
-    singles, normed_total = sum_more(normed_sums, come, S)
-    come = sum_last(singles, S)
-    outs_back = [far_swap(other_outs[:half_rows], turned_term)]
-    late_grads, late_logits = after(second_grads, turned_term), after(logit_grads, turned_term)
+    late_grads, late_logits = after(second_grads, normed_got), after(logit_grads, normed_got)
     router_term = jnp.dot(second_low.astype(F32).T, late_logits, precision=HIGHEST)
     moe_gain_term = jnp.sum(late_grads * residual_n, axis=0)
     gain_terms = jnp.concatenate(
         [router_term.reshape(S * F, part * E), moe_gain_term.reshape(S * F, part)], 1
     )
-    gain_terms = in_relative(gain_terms, S, F, s, f)
+    gain_terms = in_relative(gain_terms, S, F, s, f).reshape(S, F, -1)
     head_terms = gain_term.reshape(2, F, part).transpose(1, 0, 2).reshape(F, 2 * part)
     head_terms = in_relative(head_terms, 1, F, 0, f)
-    come, turned_got, outs_back[0], gain_terms, head_terms = tie(
-        come, turned_got, outs_back[0], gain_terms, head_terms
-    )
+    gain_terms = jnp.concatenate([gain_terms.transpose(1, 0, 2).reshape(F, -1), head_terms], 1)
+    come, turned_term, value_sum, gain_terms = tie(come, turned_term, value_sum, gain_terms)
+    turned_got = swap(turned_term[: F // 2], "fsdp", F, 1)
+    singles, normed_total = sum_more(normed_sums, come, S)
+    come = sum_last(singles, S)
+    gain_got = swap(gain_terms[F // 2 :], "fsdp", F, half_f)
+    for r in near_odd:
+        in_products(r ^ 1, turned_term)
+    come, turned_got, gain_got, in_terms = tie(come, turned_got, gain_got, in_terms)
+    gain_terms = gain_terms[: F // 2] + gain_got
     normed_grads = add_all(normed_total, come)
     turned_sum = sum_rest(sum_even(turned_term, turned_got, F), F)
     middle = in_part // 2
@@ -1226,12 +1239,13 @@
     near_got = [send_near(0, turned_got)]
     own_out_sums = sum_cores(own_parts[0], after(own_out_got, turned_got), S)
     come = sum_first(own_out_sums, S)
-    turned_sum, come, near_got[0] = tie(turned_sum, come, near_got[0])
+    gain_terms = halve(after(gain_terms, turned_got), "fsdp", F, half_f // 2)
+    turned_sum, come, near_got[0], gain_terms = tie(turned_sum, come, near_got[0], gain_terms)
     near_got.append(send_near(middle, turned_sum))
     outs_back.append(far_swap(other_outs[half_rows:], turned_sum))
-    gain_terms = halve(after(gain_terms, turned_sum), "seq", S)
-    gain_terms = halve(jnp.concatenate([gain_terms, head_terms], 1), "fsdp", F)[0]
-    head_terms = gain_terms[part * (E + 1) :]
+    count = S * part * (E + 1)
+    head_terms = gain_terms[0, count:]
+    gain_terms = halve(gain_terms[0, :count].reshape(S, -1), "seq", S, S // 2)[0]
     singles, own_total = sum_more(own_out_sums, come, S)
     own_outs = add_all(own_total, sum_last(singles, S))
     outs_back = jnp.concatenate(outs_back, 0).astype(F32)
@@ -1239,7 +1253,10 @@
 
     qkv_term = jnp.concatenate([turned_sum, value_sum], -1).astype(BF16)
     qkv_term = lax.all_to_all(qkv_term, "seq", split_axis=0, concat_axis=0, tiled=True)
-    qkv_term = qkv_term.reshape(S, part, 3, C).transpose(2, 1, 0, 3).reshape(3, part, D).astype(F32)
+    qkv_term = [
+        qkv_term[:, :, j * C : (j + 1) * C].transpose(1, 0, 2).reshape(part, D).astype(F32)
+        for j in range(3)
+    ]
     grad_output = sum_rest(sum_even(output_term, output_got, F), F)
 
     near_got = {r: jnp.concatenate([got[r] for got in near_got], 1) for r in near_odd}
@@ -1254,6 +1271,7 @@
         jnp.concatenate([lower[..., at], upper[..., at]], axis=-1)
         for at in (slice(0, hidden_half), slice(hidden_half, 2 * hidden_half))
     )
+    down_got = after(down_got, turned_sum)
     down_got = {r: jnp.concatenate([got[r] for got in down_got], 1) for r in down_sent}
     grad_down = sum_near(
         {r ^ 1: down_terms[r ^ 1].astype(F32) + down_got[r].astype(F32) for r in down_sent}
@@ -1265,8 +1283,10 @@
     grad_tokens = residual_grads + attn_factor * (
         attn_pulled - inputs_n * jnp.mean(attn_pulled * inputs_n, axis=-1, keepdims=True)
     )
-    own_weights = jnp.stack([w_query, w_key, w_value], 0).astype(F32)
-    grad_attn_gain = jnp.sum(qkv_term * own_weights, axis=(0, 2)) / attn_gain.astype(F32)
+    grad_attn_gain = sum(
+        jnp.sum(term * weight.astype(F32), axis=1)
+        for term, weight in zip(qkv_term, (w_query, w_key, w_value))
+    ) / attn_gain.astype(F32)
     return (
         mixed,
         grad_tokens[None],
@@ -1276,7 +1296,7 @@
         grad_output,
         gain_terms[: part * E].reshape(part, E),
         grad_attn_gain,
-        gain_terms[part * E : part * (E + 1)],
+        gain_terms[part * E :],
         head_terms[:part],
         head_terms[part:],
         grad_gate,

time: 1100 us -> 1120 us (1.018)
  waiting for transfers between devices: 368 us -> 421 us
  local copies, waits for them, and re-layouts: 150 us -> 129 us
    ppermute x124 -> x125, waiting for transfers between devices: 368 us -> 421 us  [swap(): return lax.ppermute(values, axis, [(i, i ^ mask) for i in range(size)])]
    ppermute x124 -> x125, starting transfers between devices: 137 us -> 126 us  [swap(): return lax.ppermute(values, axis, [(i, i ^ mask) for i in range(size)])]
    unnamed x346 -> x381, local copies, waits for them, and re-layouts: 65.8 us -> 57.2 us
  transfers between devices with their start and end apart: 128 -> 129, of which waited for: 56 -> 63; matrix products, arithmetic and copies ran while one was open for 22% -> 20% of each run, Pallas kernels for 23% -> 20%
where the time goes in v7:
time: 1120 us; the launch traced here: 1100 us
  waiting for transfers between devices  421 us (38%)
  Pallas kernels  255 us (23%)
  starting transfers between devices  144 us (13%)
  local copies, waits for them, and re-layouts  129 us (12%)
  other arithmetic  108 us (10%)
  matrix products  44.3 us (4%)
    ppermute x125, waiting for transfers between devices, swap(): return lax.ppermute(values, axis, [(i, i ^ mask) for i in range(size)])  421 us
    ppermute x125, starting transfers between devices, swap(): return lax.ppermute(values, axis, [(i, i ^ mask) for i in range(size)])  126 us
    pallas_call x2, Pallas kernels, run_experts(): pl.pallas_call(partial(expert_kernel, in_places, down_places), grid=(step...  118 us
    pallas_call x6, Pallas kernels, products(): pl.pallas_call(product_kernel, grid_spec=pltpu.PrefetchScalarGridSpec(num...  60.4 us
    unnamed x381, local copies, waits for them, and re-layouts  57.2 us
    pallas_call x1, Pallas kernels, attention_backward(): pl.pallas_call(partial(backward_kernel, span), grid=(heads, length // row...  28.4 us
  transfers between devices with their start and end apart: 129, of which 63 were waited for; matrix products, arithmetic and copies ran while one was open for 20% of the time, Pallas kernels for 20%

profile of v7, /device:TPU:0, one launch (start us, length us, event | category | flops | bytes accessed | tf_op | source)
XLA Modules:
  0.0 1104.3 jit_solution(887750199812079175)
XLA Ops:
  41.2 9.0 collective-permute-done.4
  76.6 31.2 %collective-permute-done.10 = bf16[8,64,768]{2,1,0:T(8,128)(2,1)S(1)} collective-permute-done((bf16[8,64,768]{2,1,0:T(8,128)(2,1)}, bf16[8,64,768]{2,1,0:T(8,128)(2,1)S(1)}, u32[]{:S(2)}, u32[]{:S(2)}) %collective-permute-start.10) | collective-permute-done | bytes 786464 | tf_op jit(solution)/shard_map/ppermute | solution.py:42
  115.9 28.6 %collective-permute-done.15 = bf16[128,2048]{1,0:T(8,128)(2,1)} collective-permute-done((bf16[128,2048]{1,0:T(8,128)(2,1)}, bf16[128,2048]{1,0:T(8,128)(2,1)}, u32[]{:S(2)}, u32[]{:S(2)}) %collective-permute-start.15) | collective-permute-done | bytes 524320 | tf_op jit(solution)/shard_map/ppermute | solution.py:42
  149.9 16.3 %collective-permute-done.14 = bf16[128,2048]{1,0:T(8,128)(2,1)} collective-permute-done((bf16[128,2048]{1,0:T(8,128)(2,1)}, bf16[128,2048]{1,0:T(8,128)(2,1)}, u32[]{:S(2)}, u32[]{:S(2)}) %collective-permute-start.14) | collective-permute-done | bytes 524320 | tf_op jit(solution)/shard_map/ppermute | solution.py:42
  187.0 12.9 %project.1 = (bf16[1024,2048]{1,0:T(8,128)(2,1)}, bf16[1024,2048]{1,0:T(8,128)(2,1)}, f32[2048,256]{1,0:T(8,128)S(1)}, f32[2048,256]{1,0:T(8,128)S(1)}, bf16[204...) custom-call(s32[1]{0:T(128)} %bitcast.1.me_ref, bf16[1024,2048]{1,0:T(8,128)(2,1)} %constant_dynamic-update-slice_fusion.even_ref, ...), custom_call_target="tpu_custom_call" | custom-call | flops 6442450944 | bytes 25165824 | tf_op jit(solution)/shard_map/project/pallas_call | solution.py:437
  211.7 17.5 %collective-permute-done.25 = f32[2,2048]{1,0:T(2,128)S(1)} collective-permute-done((f32[2,2048]{1,0:T(2,128)S(1)}, f32[2,2048]{1,0:T(2,128)S(1)}, u32[]{:S(2)}, u32[]{:S(2)}) %collective-permute-start.25) | collective-permute-done | bytes 16416 | tf_op jit(solution)/shard_map/ppermute | solution.py:42
  244.7 8.3 collective-permute-done.30.refs_7_
  270.1 21.6 %attend.1 = (bf16[2048,256]{1,0:T(8,128)(2,1)S(1)}, f32[2,1,2048]{2,1,0:T(1,128)S(1)}) custom-call(bf16[2048,256]{1,0:T(8,128)(2,1)S(1)} %get-tuple-element.361.q_ref, bf16[2048,256]{1,0:T(8,128)(2,1)S(1)} %get-tuple-element.362.k_ref, bf16[2048,256]{1,0:T(8,128)(2,1)S(1)} %copy-done.20, s32[1,2048]{1,0:T(1,128)S(1)} %copy-done.14, s32[2048,1]{1,0:T(8,128)S(1)} %copy-done.9), custom_call_target="tpu_custom_call" | custom-call | flops 2684354560 | bytes 4194304 | tf_op jit(solution)/shard_map/attend/pallas_call | solution.py:336
  313.5 19.5 %collective-permute-done.38.refs_5_ = bf16[2,128,1024]{2,1,0:T(8,128)(2,1)} collective-permute-done((bf16[2,128,1024]{2,1,0:T(8,128)(2,1)}, bf16[2,128,1024]{2,1,0:T(8,128)(2,1)}, u32[]{:S(2)}, u32[]{:S(2)}) %collective-permute-start.38) | collective-permute-done | bytes 524320 | tf_op jit(solution)/shard_map/ppermute | solution.py:42
  333.0 10.7 collective-permute-done.37.refs_12_
  379.9 14.2 %collective-permute-done.47.refs_14_ = bf16[2,128,1024]{2,1,0:T(8,128)(2,1)S(1)} collective-permute-done((bf16[2,128,1024]{2,1,0:T(8,128)(2,1)}, bf16[2,128,1024]{2,1,0:T(8,128)(2,1)S(1)}, u32[]{:S(2)}, u32[]{:S(2)}) %collective-permute-start.47) | collective-permute-done | bytes 524320 | tf_op jit(solution)/shard_map/ppermute | solution.py:42
  422.8 22.7 %collective-permute-done.56.refs_20_ = bf16[2,128,2048]{2,1,0:T(8,128)(2,1)S(1)} collective-permute-done((bf16[2,128,2048]{2,1,0:T(8,128)(2,1)S(1)}, bf16[2,128,2048]{2,1,0:T(8,128)(2,1)S(1)}, u32[]{:S(2)}, u32[]{:S(2)}) %collective-permute-start.56) | collective-permute-done | bytes 1048608 | tf_op jit(solution)/shard_map/ppermute | solution.py:42
  474.4 59.4 %experts.2 = (bf16[1024,2048]{1,0:T(8,128)(2,1)}, bf16[1024,2048]{1,0:T(8,128)(2,1)}, bf16[1024,2048]{1,0:T(8,128)(2,1)}, bf16[1024,2048]{1,0:T(8,128)(2,1)}, f3...) custom-call(s32[2]{0:T(128)} %pad_add_fusion.first_ref, ...), custom_call_target="tpu_custom_call" | custom-call | flops 38654705664 | bytes 62914560 | tf_op jit(solution)/shard_map/experts/pallas_call | solution.py:732
  534.5 59.0 %experts.3 = (bf16[1024,2048]{1,0:T(8,128)(2,1)}, bf16[1024,2048]{1,0:T(8,128)(2,1)}, bf16[1024,2048]{1,0:T(8,128)(2,1)}, bf16[1024,2048]{1,0:T(8,128)(2,1)}, f3...) custom-call(s32[2]{0:T(128)} %pad_add_fusion.first_ref, ...), custom_call_target="tpu_custom_call", output_to_operand_aliasing={{6}: (30, {}), {7}: (31, {}), {8}: (32, {}), {9}: (33, {})} | custom-call | flops 38654705664 | bytes 62914560 | tf_op jit(solution)/shard_map/experts/pallas_call | solution.py:732
  602.1 9.4 in_products.4
  644.7 11.0 down_products.2
  655.7 12.1 %collective-permute-done.73 = f32[8,512]{0,1:T(8,128)S(1)} collective-permute-done((f32[8,512]{0,1:T(8,128)}, f32[8,512]{0,1:T(8,128)S(1)}, u32[]{:S(2)}, u32[]{:S(2)}) %collective-permute-start.73) | collective-permute-done | bytes 16416 | tf_op jit(solution)/shard_map/ppermute | solution.py:42
  681.1 9.5 in_products.5
  690.6 11.7 %collective-permute-done.76 = bf16[128,2048]{1,0:T(8,128)(2,1)} collective-permute-done((bf16[128,2048]{1,0:T(8,128)(2,1)}, bf16[128,2048]{1,0:T(8,128)(2,1)}, u32[]{:S(2)}, u32[]{:S(2)}) %collective-permute-start.76) | collective-permute-done | bytes 524320 | tf_op jit(solution)/shard_map/ppermute | solution.py:42
  715.5 10.0 in_products.6
  725.4 8.2 collective-permute-done.81
  750.8 11.0 down_products.3
  763.1 8.3 collective-permute-done.84
  793.7 14.0 %collective-permute-done.90 = bf16[2,64,2048]{2,1,0:T(8,128)(2,1)S(1)} collective-permute-done((bf16[2,64,2048]{2,1,0:T(8,128)(2,1)S(1)}, bf16[2,64,2048]{2,1,0:T(8,128)(2,1)S(1)}, u32[]{:S(2)}, u32[]{:S(2)}) %collective-permute-start.90) | collective-permute-done | bytes 524320 | tf_op jit(solution)/shard_map/ppermute | solution.py:42
  811.5 28.4 %attend_back.1 = (bf16[2048,256]{1,0:T(8,128)(2,1)S(1)}, bf16[2048,256]{1,0:T(8,128)(2,1)S(1)}, bf16[2048,256]{1,0:T(8,128)(2,1)S(1)}) custom-call(bf16[2048,256]{1,0:T(8,128)(2,1)S(1)} %copy-done.16, bf16[2048,256]{1,0:T(8,128)(2,1)S(1)} %copy-done.18, bf16[2048,256]{1,0:T(8,128)(2,1)} %copy-done.19, bf16[2048,256]{1,0:T(8,128)(2,1)} %bitcast.376, ...), custom_call_target="tpu_custom_call" | custom-call | flops 6710886400 | bytes 7340032 | tf_op jit(solution)/shard_map/attend_back/pallas_call | solution.py:368
  856.2 10.2 collective-permute-done.92
  889.6 8.0 collective-permute-done.96
  930.2 15.0 %collective-permute-done.104 = bf16[128,2048]{1,0:T(8,128)(2,1)S(1)} collective-permute-done((bf16[128,2048]{1,0:T(8,128)(2,1)S(1)}, bf16[128,2048]{1,0:T(8,128)(2,1)S(1)}, u32[]{:S(2)}, u32[]{:S(2)}) %collective-permute-start.104) | collective-permute-done | bytes 524320 | tf_op jit(solution)/shard_map/ppermute | solution.py:42
  991.1 9.6 in_products.7
  1000.6 8.9 collective-permute-done.111
  1028.2 18.8 %collective-permute-done.112 = bf16[1,8,64,512]{3,2,1,0:T(8,128)(2,1)S(1)} collective-permute-done((bf16[1,8,64,512]{3,2,1,0:T(8,128)(2,1)S(1)}, bf16[1,8,64,512]{3,2,1,0:T(8,128)(2,1)S(1)}, u32[]{:S(2)}, u32[]{:S(2)}) %collective-permute-start.112) | collective-permute-done | bytes 524320 | tf_op jit(solution)/shard_map/ppermute | solution.py:42
  1090.8 9.5 collective-permute-done.117
  (850 shorter events, 556.0 us)
Async XLA Ops:
  5.4 62.8 %all-to-all-start = ((bf16[8,64,768]{2,1,0:T(8,128)(2,1)}), bf16[8,64,768]{2,1,0:T(8,128)(2,1)}, u32[]{:S(2)}, u32[]{:S(2)}) async-start(bf16[8,64,768]{2,1,0:T(8,128)(2,1)} %split_heads.1), calls=%async_computation | async-start | bytes 1572864 | tf_op jit(solution)/shard_map/all_to_all | solution.py:866
  68.2 39.7 %collective-permute-start.11 = (bf16[256,2048]{1,0:T(8,128)(2,1)S(1)}, bf16[256,2048]{1,0:T(8,128)(2,1)S(1)}, u32[]{:S(2)}, u32[]{:S(2)}) collective-permute-start(bf16[256,2048]{1,0:T(8,128)(2,1)S(1)} %bitcast.335), channel_id=1, source_target_pairs={{0,8},{4,12},{8,0},{12,4},{16,24},{20,28},{24,16},{28,20},{1,9},{5... | collective-permute-start | bytes 3145736 | tf_op jit(solution)/shard_map/ppermute | solution.py:42
  70.1 37.8 %collective-permute-start.12 = (bf16[256,2048]{1,0:T(8,128)(2,1)S(1)}, bf16[256,2048]{1,0:T(8,128)(2,1)S(1)}, u32[]{:S(2)}, u32[]{:S(2)}) collective-permute-start(bf16[256,2048]{1,0:T(8,128)(2,1)S(1)} %bitcast.336), channel_id=1, source_target_pairs={{0,16},{4,20},{8,24},{12,28},{16,0},{20,4},{24,8},{28,12},{1,17},{... | collective-permute-start | bytes 3145736 | tf_op jit(solution)/shard_map/ppermute | solution.py:42
  71.6 36.2 %collective-permute-start.10 = (bf16[8,64,768]{2,1,0:T(8,128)(2,1)}, bf16[8,64,768]{2,1,0:T(8,128)(2,1)S(1)}, u32[]{:S(2)}, u32[]{:S(2)}) collective-permute-start(bf16[8,64,768]{2,1,0:T(8,128)(2,1)} %all-to-all-done), channel_id=1, source_target_pairs={{0,2},{1,3},{2,0},{3,1},{4,6},{5,7},{6,4},{7,5},{8,10},{9,11},{10,... | collective-permute-start | bytes 2359304 | tf_op jit(solution)/shard_map/ppermute | solution.py:42
  71.6 36.2 %collective-permute-start.9 = (bf16[8,64,768]{2,1,0:T(8,128)(2,1)}, bf16[8,64,768]{2,1,0:T(8,128)(2,1)S(1)}, u32[]{:S(2)}, u32[]{:S(2)}) collective-permute-start(bf16[8,64,768]{2,1,0:T(8,128)(2,1)} %all-to-all-done), channel_id=1, source_target_pairs={{0,1},{1,0},{2,3},{3,2},{4,5},{5,4},{6,7},{7,6},{8,9},{9,8},{10,11... | collective-permute-start | bytes 2359304 | tf_op jit(solution)/shard_map/ppermute | solution.py:42
  107.9 58.4 %collective-permute-start.17 = (bf16[256,2048]{1,0:T(8,128)(2,1)S(1)}, bf16[256,2048]{1,0:T(8,128)(2,1)}, u32[]{:S(2)}, u32[]{:S(2)}) collective-permute-start(bf16[256,2048]{1,0:T(8,128)(2,1)S(1)} %bitcast.345), channel_id=1, source_target_pairs={{0,8},{4,12},{8,0},{12,4},{16,24},{20,28},{24,16},{28,20},{1,9},{5... | collective-permute-start | bytes 3145736 | tf_op jit(solution)/shard_map/ppermute | solution.py:42
  108.5 57.8 %collective-permute-start.18 = (bf16[256,2048]{1,0:T(8,128)(2,1)S(1)}, bf16[256,2048]{1,0:T(8,128)(2,1)}, u32[]{:S(2)}, u32[]{:S(2)}) collective-permute-start(bf16[256,2048]{1,0:T(8,128)(2,1)S(1)} %bitcast.346), channel_id=1, source_target_pairs={{0,16},{4,20},{8,24},{12,28},{16,0},{20,4},{24,8},{28,12},{1,17},{... | collective-permute-start | bytes 3145736 | tf_op jit(solution)/shard_map/ppermute | solution.py:42
  109.9 34.6 %collective-permute-start.15 = (bf16[128,2048]{1,0:T(8,128)(2,1)}, bf16[128,2048]{1,0:T(8,128)(2,1)}, u32[]{:S(2)}, u32[]{:S(2)}) collective-permute-start(bf16[128,2048]{1,0:T(8,128)(2,1)} %slice.569), channel_id=1, source_target_pairs={{0,16},{4,20},{8,24},{12,28},{16,0},{20,4},{24,8},{28,12},{1,17},{... | collective-permute-start | bytes 1572872 | tf_op jit(solution)/shard_map/ppermute | solution.py:42
  112.4 53.8 %collective-permute-start.13 = (bf16[8,64,768]{2,1,0:T(8,128)(2,1)}, bf16[8,64,768]{2,1,0:T(8,128)(2,1)}, u32[]{:S(2)}, u32[]{:S(2)}) collective-permute-start(bf16[8,64,768]{2,1,0:T(8,128)(2,1)} %copy-done.84), channel_id=1, source_target_pairs={{0,1},{1,0},{2,3},{3,2},{4,5},{5,4},{6,7},{7,6},{8,9},{9,8},{10,11... | collective-permute-start | bytes 2359304 | tf_op jit(solution)/shard_map/ppermute | solution.py:42
  114.4 35.5 %collective-permute-start.16 = (bf16[128,2048]{1,0:T(8,128)(2,1)}, bf16[128,2048]{1,0:T(8,128)(2,1)}, u32[]{:S(2)}, u32[]{:S(2)}) collective-permute-start(bf16[128,2048]{1,0:T(8,128)(2,1)} %slice.570), channel_id=1, source_target_pairs={{0,8},{4,12},{8,0},{12,4},{16,24},{20,28},{24,16},{28,20},{1,9},{5... | collective-permute-start | bytes 1572872 | tf_op jit(solution)/shard_map/ppermute | solution.py:42
  203.0 55.0 %collective-permute-start.31 = (bf16[1024,2048]{1,0:T(8,128)(2,1)}, bf16[1024,2048]{1,0:T(8,128)(2,1)}, u32[]{:S(2)}, u32[]{:S(2)}) collective-permute-start(bf16[1024,2048]{1,0:T(8,128)(2,1)} %constant_dynamic-update-slice_fusion.5), channel_id=1, source_target_pairs={{0,4},{4,0},{8,12},{12,8},{16,20},{20,16},{24,28},{28,24},{1,5},{5... | collective-permute-start | bytes 12582920 | tf_op jit(solution)/shard_map/ppermute | solution.py:42
  203.0 55.0 %collective-permute-start.27 = (bf16[256,2048]{1,0:T(8,128)(2,1)}, bf16[256,2048]{1,0:T(8,128)(2,1)}, u32[]{:S(2)}, u32[]{:S(2)}) collective-permute-start(bf16[256,2048]{1,0:T(8,128)(2,1)} %bitcast.21), channel_id=1, source_target_pairs={{0,8},{4,12},{8,0},{12,4},{16,24},{20,28},{24,16},{28,20},{1,9},{5... | collective-permute-start | bytes 3145736 | tf_op jit(solution)/shard_map/ppermute | solution.py:42
  204.4 53.6 %collective-permute-start.28 = (bf16[256,2048]{1,0:T(8,128)(2,1)}, bf16[256,2048]{1,0:T(8,128)(2,1)}, u32[]{:S(2)}, u32[]{:S(2)}) collective-permute-start(bf16[256,2048]{1,0:T(8,128)(2,1)} %bitcast.21), channel_id=1, source_target_pairs={{0,16},{4,20},{8,24},{12,28},{16,0},{20,4},{24,8},{28,12},{1,17},{... | collective-permute-start | bytes 3145736 | tf_op jit(solution)/shard_map/ppermute | solution.py:42
  258.0 34.7 %collective-permute-start.35 = (bf16[2,64,2048]{2,1,0:T(8,128)(2,1)S(1)}, bf16[2,64,2048]{2,1,0:T(8,128)(2,1)S(1)}, u32[]{:S(2)}, u32[]{:S(2)}) collective-permute-start(bf16[2,64,2048]{2,1,0:T(8,128)(2,1)S(1)} %copy-done.116), channel_id=1, source_target_pairs={{0,1},{1,0},{2,3},{3,2},{4,5},{5,4},{6,7},{7,6},{8,9},{9,8},{10,11... | collective-permute-start | bytes 1572872 | tf_op jit(solution)/shard_map/ppermute | solution.py:42
  258.1 34.6 %collective-permute-start.34 = (bf16[2,128,1024]{2,1,0:T(8,128)(2,1)S(1)}, bf16[2,128,1024]{2,1,0:T(8,128)(2,1)S(1)}, u32[]{:S(2)}, u32[]{:S(2)}) collective-permute-start(bf16[2,128,1024]{2,1,0:T(8,128)(2,1)S(1)} %copy-done.114), channel_id=1, source_target_pairs={{0,2},{1,3},{2,0},{3,1},{4,6},{5,7},{6,4},{7,5},{8,10},{9,11},{10,... | collective-permute-start | bytes 1572872 | tf_op jit(solution)/shard_map/ppermute | solution.py:42
  262.1 30.6 %collective-permute-start.32 = (bf16[128,2048]{1,0:T(8,128)(2,1)S(1)}, bf16[128,2048]{1,0:T(8,128)(2,1)S(1)}, u32[]{:S(2)}, u32[]{:S(2)}) collective-permute-start(bf16[128,2048]{1,0:T(8,128)(2,1)S(1)} %slice.576), channel_id=1, source_target_pairs={{0,16},{4,20},{8,24},{12,28},{16,0},{20,4},{24,8},{28,12},{1,17},{... | collective-permute-start | bytes 1572872 | tf_op jit(solution)/shard_map/ppermute | solution.py:42
  294.5 77.6 %collective-permute-start.43 = (bf16[1024,2048]{1,0:T(8,128)(2,1)}, bf16[1024,2048]{1,0:T(8,128)(2,1)}, u32[]{:S(2)}, u32[]{:S(2)}) collective-permute-start(bf16[1024,2048]{1,0:T(8,128)(2,1)} %constant_dynamic-update-slice_fusion.18.ua_ref), channel_id=1, source_target_pairs={{0,4},{4,0},{8,12},{12,8},{16,20},{20,16},{24,28},{28,24},{1,5},{5... | collective-permute-start | bytes 12582920 | tf_op jit(solution)/shard_map/ppermute | solution.py:42
  300.2 43.4 %all-to-all-start.1 = ((bf16[8,256,256]{1,2,0:T(8,128)(2,1)}), bf16[8,256,256]{1,2,0:T(8,128)(2,1)}, u32[]{:S(2)}, u32[]{:S(2)}) async-start(bf16[8,256,256]{1,2,0:T(8,128)(2,1)} %copy.120), calls=%async_computation.1 | async-start | bytes 2097152 | tf_op jit(solution)/shard_map/all_to_all | solution.py:948
  306.8 36.9 %collective-permute-start.37 = (bf16[2,128,1024]{2,1,0:T(8,128)(2,1)}, bf16[2,128,1024]{2,1,0:T(8,128)(2,1)}, u32[]{:S(2)}, u32[]{:S(2)}) collective-permute-start(bf16[2,128,1024]{2,1,0:T(8,128)(2,1)} %collective-permute-done.29.refs_8_), channel_id=1, source_target_pairs={{0,1},{1,0},{2,3},{3,2},{4,5},{5,4},{6,7},{7,6},{8,9},{9,8},{10,11... | collective-permute-start | bytes 1572872 | tf_op jit(solution)/shard_map/ppermute | solution.py:42
  308.7 34.9 %collective-permute-start.36 = (bf16[2,128,1024]{2,1,0:T(8,128)(2,1)}, bf16[2,128,1024]{2,1,0:T(8,128)(2,1)}, u32[]{:S(2)}, u32[]{:S(2)}) collective-permute-start(bf16[2,128,1024]{2,1,0:T(8,128)(2,1)} %pad_maximum_fusion.28), channel_id=1, source_target_pairs={{0,2},{1,3},{2,0},{3,1},{4,6},{5,7},{6,4},{7,5},{8,10},{9,11},{10,... | collective-permute-start | bytes 1572872 | tf_op jit(solution)/shard_map/ppermute | solution.py:42
  376.4 33.7 %collective-permute-start.52 = (bf16[128,2048]{1,0:T(8,128)(2,1)S(1)}, bf16[128,2048]{1,0:T(8,128)(2,1)S(1)}, u32[]{:S(2)}, u32[]{:S(2)}) collective-permute-start(bf16[128,2048]{1,0:T(8,128)(2,1)S(1)} %slice.590), channel_id=1, source_target_pairs={{0,16},{4,20},{8,24},{12,28},{16,0},{20,4},{24,8},{28,12},{1,17},{... | collective-permute-start | bytes 1572872 | tf_op jit(solution)/shard_map/ppermute | solution.py:42
  469.2 64.7 %collective-permute-start.62 = (bf16[1024,2048]{1,0:T(8,128)(2,1)}, bf16[1024,2048]{1,0:T(8,128)(2,1)}, u32[]{:S(2)}, u32[]{:S(2)}) collective-permute-start(bf16[1024,2048]{1,0:T(8,128)(2,1)} %constant_dynamic-update-slice_fusion.49.xa_ref), channel_id=1, source_target_pairs={{0,4},{4,0},{8,12},{12,8},{16,20},{20,16},{24,28},{28,24},{1,5},{5... | collective-permute-start | bytes 12582920 | tf_op jit(solution)/shard_map/ppermute | solution.py:42
  533.9 59.7 %collective-permute-start.63 = (bf16[1024,2048]{1,0:T(8,128)(2,1)}, bf16[1024,2048]{1,0:T(8,128)(2,1)}, u32[]{:S(2)}, u32[]{:S(2)}) collective-permute-start(bf16[1024,2048]{1,0:T(8,128)(2,1)} %get-tuple-element.478), channel_id=1, source_target_pairs={{0,4},{4,0},{8,12},{12,8},{16,20},{20,16},{24,28},{28,24},{1,5},{5... | collective-permute-start | bytes 12582920 | tf_op jit(solution)/shard_map/ppermute | solution.py:42
  534.4 59.1 %collective-permute-start.64 = (bf16[1024,2048]{1,0:T(8,128)(2,1)}, bf16[1024,2048]{1,0:T(8,128)(2,1)}, u32[]{:S(2)}, u32[]{:S(2)}) collective-permute-start(bf16[1024,2048]{1,0:T(8,128)(2,1)} %get-tuple-element.479), channel_id=1, source_target_pairs={{0,4},{4,0},{8,12},{12,8},{16,20},{20,16},{24,28},{28,24},{1,5},{5... | collective-permute-start | bytes 12582920 | tf_op jit(solution)/shard_map/ppermute | solution.py:42
  638.8 29.9 %collective-permute-start.72 = (bf16[2,256,1024]{2,1,0:T(8,128)(2,1)}, bf16[2,256,1024]{2,1,0:T(8,128)(2,1)}, u32[]{:S(2)}, u32[]{:S(2)}) collective-permute-start(bf16[2,256,1024]{2,1,0:T(8,128)(2,1)} %concatenate.252), channel_id=1, source_target_pairs={{0,1},{1,0},{2,3},{3,2},{4,5},{5,4},{6,7},{7,6},{8,9},{9,8},{10,11... | collective-permute-start | bytes 3145736 | tf_op jit(solution)/shard_map/ppermute | solution.py:42
  874.4 30.7 %collective-permute-start.98 = (bf16[256,2048]{1,0:T(8,128)(2,1)S(1)}, bf16[256,2048]{1,0:T(8,128)(2,1)S(1)}, u32[]{:S(2)}, u32[]{:S(2)}) collective-permute-start(bf16[256,2048]{1,0:T(8,128)(2,1)S(1)} %pad_maximum_fusion.14), channel_id=1, source_target_pairs={{0,8},{4,12},{8,0},{12,4},{16,24},{20,28},{24,16},{28,20},{1,9},{5... | collective-permute-start | bytes 3145736 | tf_op jit(solution)/shard_map/ppermute | solution.py:42
  914.8 30.4 %collective-permute-start.102 = (bf16[1024,2048]{1,0:T(8,128)(2,1)}, bf16[1024,2048]{1,0:T(8,128)(2,1)}, u32[]{:S(2)}, u32[]{:S(2)}) collective-permute-start(bf16[1024,2048]{1,0:T(8,128)(2,1)} %convolution_convert_fusion.2), channel_id=1, source_target_pairs={{0,4},{4,0},{8,12},{12,8},{16,20},{20,16},{24,28},{28,24},{1,5},{5... | collective-permute-start | bytes 12582920 | tf_op jit(solution)/shard_map/ppermute | solution.py:42
  923.2 64.1 %collective-permute-start.120 = (bf16[1,64,2048]{2,1,0:T(8,128)(2,1)}, bf16[1,64,2048]{2,1,0:T(8,128)(2,1)}, u32[]{:S(2)}, u32[]{:S(2)}) collective-permute-start(bf16[1,64,2048]{2,1,0:T(8,128)(2,1)} %slice_bitcast_fusion.4), channel_id=1, source_target_pairs={{0,2},{1,3},{2,0},{3,1},{4,6},{5,7},{6,4},{7,5},{8,10},{9,11},{10,... | collective-permute-start | bytes 786440 | tf_op jit(solution)/shard_map/ppermute | solution.py:42
  1016.0 34.0 %collective-permute-start.115 = (bf16[2,256,1024]{2,1,0:T(8,128)(2,1)S(1)}, bf16[2,256,1024]{2,1,0:T(8,128)(2,1)}, u32[]{:S(2)}, u32[]{:S(2)}) collective-permute-start(bf16[2,256,1024]{2,1,0:T(8,128)(2,1)S(1)} %get-tuple-element.589), channel_id=1, source_target_pairs={{0,1},{1,0},{2,3},{3,2},{4,5},{5,4},{6,7},{7,6},{8,9},{9,8},{10,11... | collective-permute-start | bytes 3145736 | tf_op jit(solution)/shard_map/ppermute | solution.py:42
  1050.0 31.9 %collective-permute-start.124 = (bf16[2,256,1024]{2,1,0:T(8,128)(2,1)}, bf16[2,256,1024]{2,1,0:T(8,128)(2,1)}, u32[]{:S(2)}, u32[]{:S(2)}) collective-permute-start(bf16[2,256,1024]{2,1,0:T(8,128)(2,1)} %get-tuple-element.606), channel_id=1, source_target_pairs={{0,1},{1,0},{2,3},{3,2},{4,5},{5,4},{6,7},{7,6},{8,9},{9,8},{10,11... | collective-permute-start | bytes 3145736 | tf_op jit(solution)/shard_map/ppermute | solution.py:42
  1058.7 32.1 %collective-permute-start.119 = (bf16[128,2048]{1,0:T(8,128)(2,1)}, bf16[128,2048]{1,0:T(8,128)(2,1)}, u32[]{:S(2)}, u32[]{:S(2)}) collective-permute-start(bf16[128,2048]{1,0:T(8,128)(2,1)} %get-tuple-element.598), channel_id=1, source_target_pairs={{0,2},{1,3},{2,0},{3,1},{4,6},{5,7},{6,4},{7,5},{8,10},{9,11},{10,... | collective-permute-start | bytes 1572872 | tf_op jit(solution)/shard_map/ppermute | solution.py:42
  1067.5 32.8 %collective-permute-start.118 = (bf16[256,2048]{1,0:T(8,128)(2,1)}, bf16[256,2048]{1,0:T(8,128)(2,1)}, u32[]{:S(2)}, u32[]{:S(2)}) collective-permute-start(bf16[256,2048]{1,0:T(8,128)(2,1)} %pad_maximum_fusion.20), channel_id=1, source_target_pairs={{0,16},{4,20},{8,24},{12,28},{16,0},{20,4},{24,8},{28,12},{1,17},{... | collective-permute-start | bytes 3145736 | tf_op jit(solution)/shard_map/ppermute | solution.py:42
  (252 other events, 3578.2 us)

commit v8 on v7

--- a/solution.py
+++ b/solution.py
@@ -106,7 +106,7 @@
     return {r: [part(r, 0), part(r, half)] for r in range(0, size, 2)}
 
 
-def sum_first(sums, size):
+def sum_first(sums, size, held=None):
     sums = {r: list(value) for r, value in sums.items()}
     come = {}
     for r in range(size - 2, 0, -2):
@@ -115,10 +115,10 @@
             for (goal, k, _), piece in come.items():
                 if goal == r:
                     sums[r][k] += piece.astype(F32)
-            upper, lower = tie(sums[r][0].astype(BF16), sums[r][1].astype(BF16))
+            upper, lower, held = tie(sums[r][0].astype(BF16), sums[r][1].astype(BF16), held)
             come[r ^ up, 0, r] = swap(upper, "seq", size, up)
             come[r ^ down, 1, r] = swap(lower, "seq", size, down)
-    return come
+    return come if held is None else (come, held)
 
 
 def sum_more(sums, come, size):
@@ -864,27 +864,32 @@
     crossed = split_heads(w_query, w_key, w_value, S)
     small = double(after(small, crossed), "fsdp", F)
     crossed = lax.all_to_all(crossed, "seq", split_axis=0, concat_axis=0, tiled=True)
-    near_own = {0: near_swap(hidden_part(half_at, 0, quarter), small)}
-    out_pieces = fsdp_pieces(after(w_output, small), F)
+    near_own = [near_swap(hidden_part(half_at, 0, 2 * quarter), small)]
+    out_dep = small
     small = double(small, "seq", S)
-    crossed, near_own[0], out_pieces, small = tie(crossed, near_own[0], out_pieces, small)
-
-    own_parts = {n: hidden_part(half_at, n * quarter, quarter) for n in range(1, 4)}
-    other_parts = [hidden_part(1 - half_at, n * quarter, quarter) for n in range(4)]
-    down_rows = quarters(w_down, 1)
+    out_far = far_swap(w_output, out_dep)
+    crossed, near_own[0], small, out_far = tie(crossed, near_own[0], small, out_far)
+
+    held = after((w_gate, w_up, w_down, upstream_low), crossed)
+
+    def held_part(which, first, count):
+        return jnp.concatenate(
+            [
+                lax.dynamic_slice(
+                    weight, (0, first, which * hidden_half), (experts, count, hidden_half)
+                )
+                for weight in held[:2]
+            ],
+            2,
+        )
+
+    own_quarters = {n: held_part(half_at, n * quarter, quarter) for n in (2, 3)}
+    far_quarters = [held_part(1 - half_at, n * quarter, quarter) for n in range(4)]
+    down_rows = quarters(held[2], 1)
     down_rows = [down_rows[0], jnp.concatenate(down_rows[1:3], 1), down_rows[3]]
-    upstream_halves = [upstream_low[:half_rows], upstream_low[half_rows:]]
-    own_output = place_fsdp(out_pieces, f, 0).reshape(C, D)
-    places = jnp.arange(L, dtype=jnp.int32).astype(F32)
-    freqs = ROPE_BASE ** (-(jnp.arange(DH // 2, dtype=F32) * 2.0 / DH))
-    angles = places[:, None] * freqs[None, :]
-    cosine, sine = jnp.cos(angles), jnp.sin(angles)
-    cosine = jnp.concatenate([cosine, cosine], 1)
-    sine = jnp.concatenate([-sine, sine], 1)
-    seg_row, seg_col = segments, segments.reshape(L, 1)
-    prepared = (
-        own_parts, other_parts, down_rows, upstream_halves, own_output, cosine, sine, seg_col
-    )
+    upstream_halves = [held[3][:half_rows], held[3][half_rows:]]
+    small = in_order(small, S, F, s, f).reshape(S, F, -1)
+    prepared = (own_quarters, far_quarters, down_rows, upstream_halves, small)
     token_first = gather_first(after(tokens_low, crossed), S)
     qkv_pieces = {0: crossed}
     for r in range(1, F):
@@ -892,14 +897,10 @@
         qkv_pieces[r] = swap(qkv_pieces[r ^ low], "fsdp", F, low)
         if r == half_f:
             qkv_pieces, token_first, prepared = tie(qkv_pieces, token_first, prepared)
-    own_parts, other_parts, down_rows, upstream_halves, own_output, cosine, sine, seg_col = prepared
-    partner_up = [far_swap(upstream_halves[0])]
+            own_quarters, far_quarters, down_rows, upstream_halves, small = prepared
+            partner_up = [far_swap(upstream_halves[0])]
     token_more = gather_more(tokens_low, token_first, S)
-    out_first = gather_first(own_output, S)
-    small = in_order(small, S, F, s, f).reshape(S, F, -1)
-    qkv_pieces, partner_up[0], token_more, out_first, small = tie(
-        qkv_pieces, partner_up[0], token_more, out_first, small
-    )
+    qkv_pieces, partner_up[0], token_more = tie(qkv_pieces, partner_up[0], token_more)
     tokens_even, tokens_odd = gather_end(tokens_low, token_first, token_more, S)
     w_qkv = place_fsdp(qkv_pieces, f, 1).reshape(D, 3 * C)
 
@@ -916,43 +917,56 @@
         ranks = relative(ranks[:, 0], s).astype(jnp.int32)
         return ranks[: S // 2], ranks[S // 2 :]
 
+    places = jnp.arange(L, dtype=jnp.int32).astype(F32)
+    freqs = ROPE_BASE ** (-(jnp.arange(DH // 2, dtype=F32) * 2.0 / DH))
+    angles = places[:, None] * freqs[None, :]
+    cosine, sine = jnp.cos(angles), jnp.sin(angles)
+    cosine = jnp.concatenate([cosine, cosine], 1)
+    sine = jnp.concatenate([-sine, sine], 1)
+
     def far_part(n, *dep):
-        return far_swap(other_parts[n], *dep)
+        return far_swap(far_quarters[n], *dep)
 
     partner_up.append(far_swap(upstream_halves[1], w_qkv))
-    near_own[2] = near_swap(own_parts[2], w_qkv)
-    out_more = gather_more(after(own_output, w_qkv), out_first, S)
+    out_pieces = {0: after(w_output, w_qkv), half_f: after(out_far, w_qkv)}
+    for r in range(1, F):
+        if r != half_f:
+            low = low_bit(r)
+            out_pieces[r] = swap(out_pieces[r ^ low], "fsdp", F, low)
+    own_up_first = gather_first(after(upstream_low, w_qkv), S)
     normed_even, normed_odd, query_pre, key_pre, value_low, squares = project(
         tokens_even, tokens_odd, w_qkv, gain_attn[None], me, T
     )
-    squares, partner_up[1], near_own[2], out_more = tie(
-        squares, partner_up[1], near_own[2], out_more
-    )
-
-    out_even, out_odd = gather_end(own_output, out_first, out_more, S)
-    own_up_first = gather_first(after(upstream_low, squares), S)
+    squares, partner_up[1], out_pieces, own_up_first = tie(
+        squares, partner_up[1], out_pieces, own_up_first
+    )
+    partner_up = jnp.concatenate(partner_up, 0)
+    own_output = place_fsdp(out_pieces, f, 0).reshape(C, D)
+
+    out_first = gather_first(own_output, S)
     far = [far_part(0, squares)]
-    near_own[3] = near_swap(own_parts[3], squares)
+    near_own.append(near_swap(own_quarters[2], squares))
     squares = sum_all(squares, "seq", S)
     query_low, key_low = rope(query_pre, key_pre, squares, head_gain, cosine, sine)
-    query_low, own_up_first, far[0], near_own[3], out_even, out_odd = tie(
-        query_low, own_up_first, far[0], near_own[3], out_even, out_odd
-    )
-
-    own_up_more = gather_more(after(upstream_low, query_low), own_up_first, S)
+    query_low, out_first, far[0], near_own[1] = tie(query_low, out_first, far[0], near_own[1])
+
+    seg_row = segments
+    seg_col = segments.reshape(L, 1)
+    out_more = gather_more(own_output, out_first, S)
     far.append(far_part(1, query_low))
+    near_own.append(near_swap(own_quarters[3], query_low))
     down = [near_swap(down_rows[0], query_low)]
     attended, lse = attention_forward(query_low, key_low, value_low, seg_row, seg_col)
-    attended, own_up_more, far[1], down[0] = tie(attended, own_up_more, far[1], down[0])
+    attended, out_more, far[1], down[0], near_own[2] = tie(
+        attended, out_more, far[1], down[0], near_own[2]
+    )
     attended_blocks = attended.reshape(S, T, C)
     come = lax.all_to_all(attended_blocks, "seq", split_axis=0, concat_axis=0, tiled=True)
-    partner_up = after(jnp.concatenate(partner_up, 0), attended)
-    near_own[1] = near_swap(own_parts[1], attended)
+    out_even, out_odd = gather_end(own_output, out_first, out_more, S)
     far.append(far_part(2, attended))
     near_far = [near_swap(far[0], attended)]
-    come, far[2], near_far[0], near_own[1], partner_up = tie(
-        come, far[2], near_far[0], near_own[1], partner_up
-    )
+    own_up_more = gather_more(after(upstream_low, attended), own_up_first, S)
+    come, far[2], near_far[0], own_up_more = tie(come, far[2], near_far[0], own_up_more)
     own_u = gather_end(upstream_low, own_up_first, own_up_more, S)
     far.append(far_part(3, come))
     near_far.append(near_swap(far[1], come))
@@ -992,9 +1006,9 @@
     other_x = gather_end(partner_low, partner_first, partner_more, S)
     in_pieces = []
     for r in range(F):
-        for n in range(4):
-            rows = near_own[n] if r < half_f else near_far[n]
-            in_pieces.append((r, n * quarter, rows[r % half_f]))
+        for n, rows in enumerate(near_own if r < half_f else near_far):
+            first = (0, 2, 3)[n] if r < half_f else n
+            in_pieces.append((r, first * quarter, rows[r % half_f]))
     down_pieces = [
         (r, (0, 1, 3)[n] * (down_part // 4), down[n][r]) for r in range(half_f) for n in range(3)
     ]
@@ -1153,11 +1167,13 @@
     far_sums.append(far_sum(2, head_grads))
     down_got.append(send_down(3, head_grads))
     other_out_sums = sum_cores(other_parts[0], after(other_out_got, head_grads), S)
-    come = sum_first(other_out_sums, S)
+    come, head_grads = sum_first(other_out_sums, S, head_grads)
     query_back, key_back, value_back = attention_backward(
         query_low, key_low, value_low, head_grads, lse, seg_row, seg_col
     )
-    query_back, far_sums[2], down_got[3], come = tie(query_back, far_sums[2], down_got[3], come)
+    query_back, key_back, value_back, far_sums[2], down_got[3], come = tie(
+        query_back, key_back, value_back, far_sums[2], down_got[3], come
+    )
 
     singles, other_total = sum_more(other_out_sums, come, S)
     come = sum_last(singles, S)
@@ -1217,7 +1233,11 @@
     head_terms = gain_term.reshape(2, F, part).transpose(1, 0, 2).reshape(F, 2 * part)
     head_terms = in_relative(head_terms, 1, F, 0, f)
     gain_terms = jnp.concatenate([gain_terms.transpose(1, 0, 2).reshape(F, -1), head_terms], 1)
-    come, turned_term, value_sum, gain_terms = tie(come, turned_term, value_sum, gain_terms)
+    own_out_sums = sum_cores(own_parts[0], after(own_out_got, normed_got), S)
+    own_come = sum_first(own_out_sums, S)
+    come, turned_term, value_sum, gain_terms, own_come = tie(
+        come, turned_term, value_sum, gain_terms, own_come
+    )
     turned_got = swap(turned_term[: F // 2], "fsdp", F, 1)
     singles, normed_total = sum_more(normed_sums, come, S)
     come = sum_last(singles, S)
@@ -1237,17 +1257,18 @@
         }
 
     near_got = [send_near(0, turned_got)]
-    own_out_sums = sum_cores(own_parts[0], after(own_out_got, turned_got), S)
-    come = sum_first(own_out_sums, S)
     gain_terms = halve(after(gain_terms, turned_got), "fsdp", F, half_f // 2)
-    turned_sum, come, near_got[0], gain_terms = tie(turned_sum, come, near_got[0], gain_terms)
+    singles, own_total = sum_more(after(own_out_sums, turned_got), own_come, S)
+    own_come = sum_last(singles, S)
+    turned_sum, own_come, near_got[0], gain_terms = tie(
+        turned_sum, own_come, near_got[0], gain_terms
+    )
     near_got.append(send_near(middle, turned_sum))
     outs_back.append(far_swap(other_outs[half_rows:], turned_sum))
     count = S * part * (E + 1)
     head_terms = gain_terms[0, count:]
     gain_terms = halve(gain_terms[0, :count].reshape(S, -1), "seq", S, S // 2)[0]
-    singles, own_total = sum_more(own_out_sums, come, S)
-    own_outs = add_all(own_total, sum_last(singles, S))
+    own_outs = add_all(own_total, own_come)
     outs_back = jnp.concatenate(outs_back, 0).astype(F32)
     mixed = (residual + own_outs + outs_back).astype(BF16)[None]
 

time: 1120 us -> 1060 us (0.946)
  waiting for transfers between devices: 421 us -> 350 us
    ppermute x125 -> x124, waiting for transfers between devices: 421 us -> 350 us  [swap(): return lax.ppermute(values, axis, [(i, i ^ mask) for i in range(size)])]
    ppermute x125 -> x124, starting transfers between devices: 126 us -> 131 us  [swap(): return lax.ppermute(values, axis, [(i, i ^ mask) for i in range(size)])]
    unnamed x381 -> x342, local copies, waits for them, and re-layouts: 57.2 us -> 57.9 us
  transfers between devices with their start and end apart: 129 -> 128, of which waited for: 63 -> 58; matrix products, arithmetic and copies ran while one was open for 20% -> 20% of each run, Pallas kernels for 20% -> 24%
where the time goes in v8:
time: 1060 us; the launch traced here: 1040 us
  waiting for transfers between devices  350 us (33%)
  Pallas kernels  255 us (24%)
  starting transfers between devices  147 us (14%)
  local copies, waits for them, and re-layouts  136 us (13%)
  other arithmetic  106 us (10%)
  matrix products  45.7 us (4%)
    ppermute x124, waiting for transfers between devices, swap(): return lax.ppermute(values, axis, [(i, i ^ mask) for i in range(size)])  350 us
    ppermute x124, starting transfers between devices, swap(): return lax.ppermute(values, axis, [(i, i ^ mask) for i in range(size)])  131 us
    pallas_call x2, Pallas kernels, run_experts(): pl.pallas_call(partial(expert_kernel, in_places, down_places), grid=(step...  118 us
    pallas_call x6, Pallas kernels, products(): pl.pallas_call(product_kernel, grid_spec=pltpu.PrefetchScalarGridSpec(num...  60 us
    unnamed x342, local copies, waits for them, and re-layouts  57.9 us
    pallas_call x1, Pallas kernels, attention_backward(): pl.pallas_call(partial(backward_kernel, span), grid=(heads, length // row...  28.4 us
    pallas_call x1, Pallas kernels, attention_forward(): pl.pallas_call(partial(forward_kernel, span), grid=(heads, length // rows...  21.6 us
  transfers between devices with their start and end apart: 128, of which 58 were waited for; matrix products, arithmetic and copies ran while one was open for 20% of the time, Pallas kernels for 24%

profile of v8, /device:TPU:0, one launch (start us, length us, event | category | flops | bytes accessed | tf_op | source)
XLA Modules:
  0.0 1043.5 jit_solution(14569911170543071855)
XLA Ops:
  30.4 8.6 collective-permute-done.4
  72.7 11.2 %collective-permute-done.7 = bf16[8,64,768]{2,1,0:T(8,128)(2,1)} collective-permute-done((bf16[8,64,768]{2,1,0:T(8,128)(2,1)S(1)}, bf16[8,64,768]{2,1,0:T(8,128)(2,1)}, u32[]{:S(2)}, u32[]{:S(2)}) %collective-permute-start.7) | collective-permute-done | bytes 786464 | tf_op jit(solution)/shard_map/ppermute | solution.py:42
  100.0 14.3 %collective-permute-done.12 = bf16[128,2048]{1,0:T(8,128)(2,1)} collective-permute-done((bf16[128,2048]{1,0:T(8,128)(2,1)S(1)}, bf16[128,2048]{1,0:T(8,128)(2,1)}, u32[]{:S(2)}, u32[]{:S(2)}) %collective-permute-start.12) | collective-permute-done | bytes 524320 | tf_op jit(solution)/shard_map/ppermute | solution.py:42
  128.5 12.6 %project.1 = (bf16[1024,2048]{1,0:T(8,128)(2,1)}, bf16[1024,2048]{1,0:T(8,128)(2,1)}, f32[2048,256]{1,0:T(8,128)S(1)}, f32[2048,256]{1,0:T(8,128)S(1)}, bf16[204...) custom-call(s32[1]{0:T(128)} %bitcast.1.me_ref, bf16[1024,2048]{1,0:T(8,128)(2,1)} %constant_dynamic-update-slice_fusion.even_ref, ...), custom_call_target="tpu_custom_call" | custom-call | flops 6442450944 | bytes 25165824 | tf_op jit(solution)/shard_map/project/pallas_call | solution.py:437
  171.7 10.7 %collective-permute-done.22 = f32[2,2048]{1,0:T(2,128)S(1)} collective-permute-done((f32[2,2048]{1,0:T(2,128)S(1)}, f32[2,2048]{1,0:T(2,128)S(1)}, u32[]{:S(2)}, u32[]{:S(2)}) %collective-permute-start.22) | collective-permute-done | bytes 16416 | tf_op jit(solution)/shard_map/ppermute | solution.py:42
  204.1 21.6 %attend.1 = (bf16[2048,256]{1,0:T(8,128)(2,1)S(1)}, f32[2,1,2048]{2,1,0:T(1,128)S(1)}) custom-call(bf16[2048,256]{1,0:T(8,128)(2,1)S(1)} %get-tuple-element.365.q_ref, bf16[2048,256]{1,0:T(8,128)(2,1)S(1)} %get-tuple-element.366.k_ref, bf16[2048,256]{1,0:T(8,128)(2,1)S(1)} %copy-done.20, s32[1,2048]{1,0:T(1,128)S(1)} %copy-done.14, s32[2048,1]{1,0:T(8,128)S(1)} %copy-done.9), custom_call_target="tpu_custom_call" | custom-call | flops 2684354560 | bytes 4194304 | tf_op jit(solution)/shard_map/attend/pallas_call | solution.py:336
  286.0 20.1 %collective-permute-done.38.refs_9_ = bf16[2,128,1024]{2,1,0:T(8,128)(2,1)S(1)} collective-permute-done((bf16[2,128,1024]{2,1,0:T(8,128)(2,1)S(1)}, bf16[2,128,1024]{2,1,0:T(8,128)(2,1)S(1)}, u32[]{:S(2)}, u32[]{:S(2)}) %collective-permute-start.38) | collective-permute-done | bytes 524320 | tf_op jit(solution)/shard_map/ppermute | solution.py:42
  314.7 18.0 %collective-permute-done.46.refs_12_ = bf16[2,128,1024]{2,1,0:T(8,128)(2,1)S(1)} collective-permute-done((bf16[2,128,1024]{2,1,0:T(8,128)(2,1)}, bf16[2,128,1024]{2,1,0:T(8,128)(2,1)S(1)}, u32[]{:S(2)}, u32[]{:S(2)}) %collective-permute-start.46) | collective-permute-done | bytes 524320 | tf_op jit(solution)/shard_map/ppermute | solution.py:42
  338.2 6.3 collective-permute-done.51
  346.5 10.0 collective-permute-done.50.refs_13_
  360.5 24.8 %collective-permute-done.55.refs_18_ = bf16[2,128,2048]{2,1,0:T(8,128)(2,1)S(1)} collective-permute-done((bf16[2,128,2048]{2,1,0:T(8,128)(2,1)S(1)}, bf16[2,128,2048]{2,1,0:T(8,128)(2,1)S(1)}, u32[]{:S(2)}, u32[]{:S(2)}) %collective-permute-start.55) | collective-permute-done | bytes 1048608 | tf_op jit(solution)/shard_map/ppermute | solution.py:42
  395.4 8.0 collective-permute-done.59.refs_19_
  412.3 59.3 %experts.2 = (bf16[1024,2048]{1,0:T(8,128)(2,1)}, bf16[1024,2048]{1,0:T(8,128)(2,1)}, bf16[1024,2048]{1,0:T(8,128)(2,1)}, bf16[1024,2048]{1,0:T(8,128)(2,1)}, f3...) custom-call(s32[2]{0:T(128)} %pad_add_fusion.first_ref, ...), custom_call_target="tpu_custom_call" | custom-call | flops 38654705664 | bytes 62914560 | tf_op jit(solution)/shard_map/experts/pallas_call | solution.py:732
  472.3 59.2 %experts.3 = (bf16[1024,2048]{1,0:T(8,128)(2,1)}, bf16[1024,2048]{1,0:T(8,128)(2,1)}, bf16[1024,2048]{1,0:T(8,128)(2,1)}, bf16[1024,2048]{1,0:T(8,128)(2,1)}, f3...) custom-call(s32[2]{0:T(128)} %pad_add_fusion.first_ref, ...), custom_call_target="tpu_custom_call", output_to_operand_aliasing={{6}: (28, {}), {7}: (29, {}), {8}: (30, {}), {9}: (31, {})} | custom-call | flops 38654705664 | bytes 62914560 | tf_op jit(solution)/shard_map/experts/pallas_call | solution.py:732
  540.9 9.4 in_products.4
  559.8 7.1 collective-permute-done.67
  583.7 11.0 %down_products.2 = bf16[2,256,2048]{2,1,0:T(8,128)(2,1)} custom-call(s32[1]{0:T(128)} %bitcast.25.me_ref, bf16[2,2304,512]{2,1,0:T(8,128)(2,1)} %get-tuple-element.536.left_ref, bf16[2,2304,2048]{2,1,0:T(8,128)(2,1)} %get-tuple-element.511.right_ref), custom_call_target="tpu_custom_call" | custom-call | flops 4831838208 | bytes 21233664 | tf_op jit(solution)/shard_map/down_products/pallas_call | solution.py:769
  594.7 11.8 %collective-permute-done.72 = f32[8,512]{0,1:T(8,128)S(1)} collective-permute-done((f32[8,512]{0,1:T(8,128)}, f32[8,512]{0,1:T(8,128)S(1)}, u32[]{:S(2)}, u32[]{:S(2)}) %collective-permute-start.72) | collective-permute-done | bytes 16416 | tf_op jit(solution)/shard_map/ppermute | solution.py:42
  620.1 9.5 in_products.5
  629.6 11.7 %collective-permute-done.75 = bf16[128,2048]{1,0:T(8,128)(2,1)} collective-permute-done((bf16[128,2048]{1,0:T(8,128)(2,1)}, bf16[128,2048]{1,0:T(8,128)(2,1)}, u32[]{:S(2)}, u32[]{:S(2)}) %collective-permute-start.75) | collective-permute-done | bytes 524320 | tf_op jit(solution)/shard_map/ppermute | solution.py:42
  654.1 9.7 in_products.6
  663.7 8.4 collective-permute-done.80
  689.2 11.0 %down_products.3 = bf16[2,256,2048]{2,1,0:T(8,128)(2,1)} custom-call(s32[1]{0:T(128)} %bitcast.25.me_ref, bf16[2,2304,512]{2,1,0:T(8,128)(2,1)} %get-tuple-element.536.left_ref, bf16[2,2304,2048]{2,1,0:T(8,128)(2,1)} %get-tuple-element.511.right_ref), custom_call_target="tpu_custom_call" | custom-call | flops 4831838208 | bytes 21233664 | tf_op jit(solution)/shard_map/down_products/pallas_call | solution.py:769
  702.1 7.7 collective-permute-done.83
  733.2 13.7 %collective-permute-done.89 = bf16[2,64,2048]{2,1,0:T(8,128)(2,1)S(1)} collective-permute-done((bf16[2,64,2048]{2,1,0:T(8,128)(2,1)S(1)}, bf16[2,64,2048]{2,1,0:T(8,128)(2,1)S(1)}, u32[]{:S(2)}, u32[]{:S(2)}) %collective-permute-start.89) | collective-permute-done | bytes 524320 | tf_op jit(solution)/shard_map/ppermute | solution.py:42
  756.0 28.4 %attend_back.1 = (bf16[2048,256]{1,0:T(8,128)(2,1)S(1)}, bf16[2048,256]{1,0:T(8,128)(2,1)S(1)}, bf16[2048,256]{1,0:T(8,128)(2,1)S(1)}) custom-call(bf16[2048,256]{1,0:T(8,128)(2,1)S(1)} %copy-done.16, bf16[2048,256]{1,0:T(8,128)(2,1)S(1)} %copy-done.18, bf16[2048,256]{1,0:T(8,128)(2,1)} %copy-done.19, bf16[2048,256]{1,0:T(8,128)(2,1)} %bitcast.367, ...), custom_call_target="tpu_custom_call" | custom-call | flops 6710886400 | bytes 7340032 | tf_op jit(solution)/shard_map/attend_back/pallas_call | solution.py:368
  808.1 5.8 collective-permute-done.95
  847.2 15.8 %collective-permute-done.103 = bf16[128,2048]{1,0:T(8,128)(2,1)S(1)} collective-permute-done((bf16[128,2048]{1,0:T(8,128)(2,1)S(1)}, bf16[128,2048]{1,0:T(8,128)(2,1)S(1)}, u32[]{:S(2)}, u32[]{:S(2)}) %collective-permute-start.103) | collective-permute-done | bytes 524320 | tf_op jit(solution)/shard_map/ppermute | solution.py:42
  913.9 9.5 in_products.7
  923.4 7.8 collective-permute-done.112
  951.2 17.2 %collective-permute-done.113 = bf16[1,8,64,512]{3,2,1,0:T(8,128)(2,1)S(1)} collective-permute-done((bf16[1,8,64,512]{3,2,1,0:T(8,128)(2,1)S(1)}, bf16[1,8,64,512]{3,2,1,0:T(8,128)(2,1)S(1)}, u32[]{:S(2)}, u32[]{:S(2)}) %collective-permute-start.113) | collective-permute-done | bytes 524320 | tf_op jit(solution)/shard_map/ppermute | solution.py:42
  995.2 31.7 %collective-permute-done.118 = bf16[128,2048]{1,0:T(8,128)(2,1)} collective-permute-done((bf16[128,2048]{1,0:T(8,128)(2,1)}, bf16[128,2048]{1,0:T(8,128)(2,1)}, u32[]{:S(2)}, u32[]{:S(2)}) %collective-permute-start.118) | collective-permute-done | bytes 524320 | tf_op jit(solution)/shard_map/ppermute | solution.py:42
  (812 shorter events, 528.6 us)
Async XLA Ops:
  20.1 29.5 %collective-permute-start.2 = (bf16[2,256,1024]{2,1,0:T(8,128)(2,1)S(1)}, bf16[2,256,1024]{2,1,0:T(8,128)(2,1)}, u32[]{:S(2)}, u32[]{:S(2)}) collective-permute-start(bf16[2,256,1024]{2,1,0:T(8,128)(2,1)S(1)} %pad_maximum_fusion.5.refs_0_), channel_id=1, source_target_pairs={{0,1},{1,0},{2,3},{3,2},{4,5},{5,4},{6,7},{7,6},{8,9},{9,8},{10,11... | collective-permute-start | bytes 3145736 | tf_op jit(solution)/shard_map/ppermute | solution.py:42
  49.6 39.5 %collective-permute-start.10 = (bf16[256,2048]{1,0:T(8,128)(2,1)S(1)}, bf16[256,2048]{1,0:T(8,128)(2,1)S(1)}, u32[]{:S(2)}, u32[]{:S(2)}) collective-permute-start(bf16[256,2048]{1,0:T(8,128)(2,1)S(1)} %bitcast.331), channel_id=1, source_target_pairs={{0,16},{4,20},{8,24},{12,28},{16,0},{20,4},{24,8},{28,12},{1,17},{... | collective-permute-start | bytes 3145736 | tf_op jit(solution)/shard_map/ppermute | solution.py:42
  51.1 38.0 %collective-permute-start.9 = (bf16[256,2048]{1,0:T(8,128)(2,1)S(1)}, bf16[256,2048]{1,0:T(8,128)(2,1)}, u32[]{:S(2)}, u32[]{:S(2)}) collective-permute-start(bf16[256,2048]{1,0:T(8,128)(2,1)S(1)} %bitcast.332), channel_id=1, source_target_pairs={{0,8},{4,12},{8,0},{12,4},{16,24},{20,28},{24,16},{28,20},{1,9},{5... | collective-permute-start | bytes 3145736 | tf_op jit(solution)/shard_map/ppermute | solution.py:42
  52.6 31.3 %collective-permute-start.7 = (bf16[8,64,768]{2,1,0:T(8,128)(2,1)S(1)}, bf16[8,64,768]{2,1,0:T(8,128)(2,1)}, u32[]{:S(2)}, u32[]{:S(2)}) collective-permute-start(bf16[8,64,768]{2,1,0:T(8,128)(2,1)S(1)} %all-to-all-done), channel_id=1, source_target_pairs={{0,1},{1,0},{2,3},{3,2},{4,5},{5,4},{6,7},{7,6},{8,9},{9,8},{10,11... | collective-permute-start | bytes 2359304 | tf_op jit(solution)/shard_map/ppermute | solution.py:42
  55.0 34.1 %collective-permute-start.8 = (bf16[8,64,768]{2,1,0:T(8,128)(2,1)S(1)}, bf16[8,64,768]{2,1,0:T(8,128)(2,1)}, u32[]{:S(2)}, u32[]{:S(2)}) collective-permute-start(bf16[8,64,768]{2,1,0:T(8,128)(2,1)S(1)} %all-to-all-done), channel_id=1, source_target_pairs={{0,2},{1,3},{2,0},{3,1},{4,6},{5,7},{6,4},{7,5},{8,10},{9,11},{10,... | collective-permute-start | bytes 2359304 | tf_op jit(solution)/shard_map/ppermute | solution.py:42
  157.2 33.9 %collective-permute-start.24 = (bf16[256,2048]{1,0:T(8,128)(2,1)}, bf16[256,2048]{1,0:T(8,128)(2,1)}, u32[]{:S(2)}, u32[]{:S(2)}) collective-permute-start(bf16[256,2048]{1,0:T(8,128)(2,1)} %bitcast.18), channel_id=1, source_target_pairs={{0,8},{4,12},{8,0},{12,4},{16,24},{20,28},{24,16},{28,20},{1,9},{5... | collective-permute-start | bytes 3145736 | tf_op jit(solution)/shard_map/ppermute | solution.py:42
  158.2 32.9 %collective-permute-start.25 = (bf16[256,2048]{1,0:T(8,128)(2,1)}, bf16[256,2048]{1,0:T(8,128)(2,1)}, u32[]{:S(2)}, u32[]{:S(2)}) collective-permute-start(bf16[256,2048]{1,0:T(8,128)(2,1)} %bitcast.18), channel_id=1, source_target_pairs={{0,16},{4,20},{8,24},{12,28},{16,0},{20,4},{24,8},{28,12},{1,17},{... | collective-permute-start | bytes 3145736 | tf_op jit(solution)/shard_map/ppermute | solution.py:42
  191.1 35.6 %collective-permute-start.32 = (bf16[2,128,1024]{2,1,0:T(8,128)(2,1)S(1)}, bf16[2,128,1024]{2,1,0:T(8,128)(2,1)S(1)}, u32[]{:S(2)}, u32[]{:S(2)}) collective-permute-start(bf16[2,128,1024]{2,1,0:T(8,128)(2,1)S(1)} %copy-done.98), channel_id=1, source_target_pairs={{0,1},{1,0},{2,3},{3,2},{4,5},{5,4},{6,7},{7,6},{8,9},{9,8},{10,11... | collective-permute-start | bytes 1572872 | tf_op jit(solution)/shard_map/ppermute | solution.py:42
  191.8 36.4 %collective-permute-start.31 = (bf16[2,64,2048]{2,1,0:T(8,128)(2,1)S(1)}, bf16[2,64,2048]{2,1,0:T(8,128)(2,1)S(1)}, u32[]{:S(2)}, u32[]{:S(2)}) collective-permute-start(bf16[2,64,2048]{2,1,0:T(8,128)(2,1)S(1)} %copy-done.103), channel_id=1, source_target_pairs={{0,1},{1,0},{2,3},{3,2},{4,5},{5,4},{6,7},{7,6},{8,9},{9,8},{10,11... | collective-permute-start | bytes 1572872 | tf_op jit(solution)/shard_map/ppermute | solution.py:42
  193.2 35.5 %collective-permute-start.30 = (bf16[2,128,1024]{2,1,0:T(8,128)(2,1)S(1)}, bf16[2,128,1024]{2,1,0:T(8,128)(2,1)S(1)}, u32[]{:S(2)}, u32[]{:S(2)}) collective-permute-start(bf16[2,128,1024]{2,1,0:T(8,128)(2,1)S(1)} %copy-done.101), channel_id=1, source_target_pairs={{0,2},{1,3},{2,0},{3,1},{4,6},{5,7},{6,4},{7,5},{8,10},{9,11},{10,... | collective-permute-start | bytes 1572872 | tf_op jit(solution)/shard_map/ppermute | solution.py:42
  196.1 32.6 %collective-permute-start.28 = (bf16[128,2048]{1,0:T(8,128)(2,1)S(1)}, bf16[128,2048]{1,0:T(8,128)(2,1)}, u32[]{:S(2)}, u32[]{:S(2)}) collective-permute-start(bf16[128,2048]{1,0:T(8,128)(2,1)S(1)} %slice.566), channel_id=1, source_target_pairs={{0,16},{4,20},{8,24},{12,28},{16,0},{20,4},{24,8},{28,12},{1,17},{... | collective-permute-start | bytes 1572872 | tf_op jit(solution)/shard_map/ppermute | solution.py:42
  198.8 29.9 %collective-permute-start.29 = (bf16[128,2048]{1,0:T(8,128)(2,1)S(1)}, bf16[128,2048]{1,0:T(8,128)(2,1)}, u32[]{:S(2)}, u32[]{:S(2)}) collective-permute-start(bf16[128,2048]{1,0:T(8,128)(2,1)S(1)} %slice.567), channel_id=1, source_target_pairs={{0,8},{4,12},{8,0},{12,4},{16,24},{20,28},{24,16},{28,20},{1,9},{5... | collective-permute-start | bytes 1572872 | tf_op jit(solution)/shard_map/ppermute | solution.py:42
  240.9 39.2 %collective-permute-start.37 = (bf16[1024,2048]{1,0:T(8,128)(2,1)}, bf16[1024,2048]{1,0:T(8,128)(2,1)}, u32[]{:S(2)}, u32[]{:S(2)}) collective-permute-start(bf16[1024,2048]{1,0:T(8,128)(2,1)} %constant_dynamic-update-slice_fusion.13), channel_id=1, source_target_pairs={{0,4},{4,0},{8,12},{12,8},{16,20},{20,16},{24,28},{28,24},{1,5},{5... | collective-permute-start | bytes 12582920 | tf_op jit(solution)/shard_map/ppermute | solution.py:42
  256.7 49.4 %collective-permute-start.42 = (bf16[1024,2048]{1,0:T(8,128)(2,1)}, bf16[1024,2048]{1,0:T(8,128)(2,1)}, u32[]{:S(2)}, u32[]{:S(2)}) collective-permute-start(bf16[1024,2048]{1,0:T(8,128)(2,1)} %constant_dynamic-update-slice_fusion.20.ua_ref), channel_id=1, source_target_pairs={{0,4},{4,0},{8,12},{12,8},{16,20},{20,16},{24,28},{28,24},{1,5},{5... | collective-permute-start | bytes 12582920 | tf_op jit(solution)/shard_map/ppermute | solution.py:42
  266.8 39.3 %collective-permute-start.40 = (bf16[256,2048]{1,0:T(8,128)(2,1)S(1)}, bf16[256,2048]{1,0:T(8,128)(2,1)S(1)}, u32[]{:S(2)}, u32[]{:S(2)}) collective-permute-start(bf16[256,2048]{1,0:T(8,128)(2,1)S(1)} %constant_dynamic-update-slice_fusion.18), channel_id=1, source_target_pairs={{0,8},{4,12},{8,0},{12,4},{16,24},{20,28},{24,16},{28,20},{1,9},{5... | collective-permute-start | bytes 3145736 | tf_op jit(solution)/shard_map/ppermute | solution.py:42
  267.9 38.2 %collective-permute-start.41 = (bf16[256,2048]{1,0:T(8,128)(2,1)S(1)}, bf16[256,2048]{1,0:T(8,128)(2,1)S(1)}, u32[]{:S(2)}, u32[]{:S(2)}) collective-permute-start(bf16[256,2048]{1,0:T(8,128)(2,1)S(1)} %constant_dynamic-update-slice_fusion.18), channel_id=1, source_target_pairs={{0,16},{4,20},{8,24},{12,28},{16,0},{20,4},{24,8},{28,12},{1,17},{... | collective-permute-start | bytes 3145736 | tf_op jit(solution)/shard_map/ppermute | solution.py:42
  312.2 32.3 %collective-permute-start.51 = (bf16[128,2048]{1,0:T(8,128)(2,1)S(1)}, bf16[128,2048]{1,0:T(8,128)(2,1)S(1)}, u32[]{:S(2)}, u32[]{:S(2)}) collective-permute-start(bf16[128,2048]{1,0:T(8,128)(2,1)S(1)} %slice.582), channel_id=1, source_target_pairs={{0,16},{4,20},{8,24},{12,28},{16,0},{20,4},{24,8},{28,12},{1,17},{... | collective-permute-start | bytes 1572872 | tf_op jit(solution)/shard_map/ppermute | solution.py:42
  407.1 64.5 %collective-permute-start.61 = (bf16[1024,2048]{1,0:T(8,128)(2,1)}, bf16[1024,2048]{1,0:T(8,128)(2,1)}, u32[]{:S(2)}, u32[]{:S(2)}) collective-permute-start(bf16[1024,2048]{1,0:T(8,128)(2,1)} %constant_dynamic-update-slice_fusion.51.xa_ref), channel_id=1, source_target_pairs={{0,4},{4,0},{8,12},{12,8},{16,20},{20,16},{24,28},{28,24},{1,5},{5... | collective-permute-start | bytes 12582920 | tf_op jit(solution)/shard_map/ppermute | solution.py:42
  471.7 59.9 %collective-permute-start.62 = (bf16[1024,2048]{1,0:T(8,128)(2,1)}, bf16[1024,2048]{1,0:T(8,128)(2,1)}, u32[]{:S(2)}, u32[]{:S(2)}) collective-permute-start(bf16[1024,2048]{1,0:T(8,128)(2,1)} %get-tuple-element.479), channel_id=1, source_target_pairs={{0,4},{4,0},{8,12},{12,8},{16,20},{20,16},{24,28},{28,24},{1,5},{5... | collective-permute-start | bytes 12582920 | tf_op jit(solution)/shard_map/ppermute | solution.py:42
  472.3 59.3 %collective-permute-start.63 = (bf16[1024,2048]{1,0:T(8,128)(2,1)}, bf16[1024,2048]{1,0:T(8,128)(2,1)}, u32[]{:S(2)}, u32[]{:S(2)}) collective-permute-start(bf16[1024,2048]{1,0:T(8,128)(2,1)} %get-tuple-element.480), channel_id=1, source_target_pairs={{0,4},{4,0},{8,12},{12,8},{16,20},{20,16},{24,28},{28,24},{1,5},{5... | collective-permute-start | bytes 12582920 | tf_op jit(solution)/shard_map/ppermute | solution.py:42
  577.4 30.0 %collective-permute-start.71 = (bf16[2,256,1024]{2,1,0:T(8,128)(2,1)}, bf16[2,256,1024]{2,1,0:T(8,128)(2,1)}, u32[]{:S(2)}, u32[]{:S(2)}) collective-permute-start(bf16[2,256,1024]{2,1,0:T(8,128)(2,1)} %concatenate.248), channel_id=1, source_target_pairs={{0,1},{1,0},{2,3},{3,2},{4,5},{5,4},{6,7},{7,6},{8,9},{9,8},{10,11... | collective-permute-start | bytes 3145736 | tf_op jit(solution)/shard_map/ppermute | solution.py:42
  749.2 35.1 %collective-permute-start.91 = (bf16[2,64,2048]{2,1,0:T(8,128)(2,1)}, bf16[2,64,2048]{2,1,0:T(8,128)(2,1)S(1)}, u32[]{:S(2)}, u32[]{:S(2)}) collective-permute-start(bf16[2,64,2048]{2,1,0:T(8,128)(2,1)} %get-tuple-element.550), channel_id=1, source_target_pairs={{0,1},{1,0},{2,3},{3,2},{4,5},{5,4},{6,7},{7,6},{8,9},{9,8},{10,11... | collective-permute-start | bytes 1572872 | tf_op jit(solution)/shard_map/ppermute | solution.py:42
  749.6 34.8 %collective-permute-start.90 = (bf16[2,128,1024]{2,1,0:T(8,128)(2,1)S(1)}, bf16[2,128,1024]{2,1,0:T(8,128)(2,1)S(1)}, u32[]{:S(2)}, u32[]{:S(2)}) collective-permute-start(bf16[2,128,1024]{2,1,0:T(8,128)(2,1)S(1)} %copy-done.93), channel_id=1, source_target_pairs={{0,2},{1,3},{2,0},{3,1},{4,6},{5,7},{6,4},{7,5},{8,10},{9,11},{10,... | collective-permute-start | bytes 1572872 | tf_op jit(solution)/shard_map/ppermute | solution.py:42
  754.6 29.7 %collective-permute-start.92 = (bf16[128,2048]{1,0:T(8,128)(2,1)}, bf16[128,2048]{1,0:T(8,128)(2,1)S(1)}, u32[]{:S(2)}, u32[]{:S(2)}) collective-permute-start(bf16[128,2048]{1,0:T(8,128)(2,1)} %get-tuple-element.551), channel_id=1, source_target_pairs={{0,16},{4,20},{8,24},{12,28},{16,0},{20,4},{24,8},{28,12},{1,17},{... | collective-permute-start | bytes 1572872 | tf_op jit(solution)/shard_map/ppermute | solution.py:42
  789.8 33.5 %collective-permute-start.97 = (bf16[256,2048]{1,0:T(8,128)(2,1)S(1)}, bf16[256,2048]{1,0:T(8,128)(2,1)S(1)}, u32[]{:S(2)}, u32[]{:S(2)}) collective-permute-start(bf16[256,2048]{1,0:T(8,128)(2,1)S(1)} %pad_maximum_fusion.14), channel_id=1, source_target_pairs={{0,8},{4,12},{8,0},{12,4},{16,24},{20,28},{24,16},{28,20},{1,9},{5... | collective-permute-start | bytes 3145736 | tf_op jit(solution)/shard_map/ppermute | solution.py:42
  791.6 32.8 %collective-permute-start.98 = (bf16[256,2048]{1,0:T(8,128)(2,1)S(1)}, bf16[256,2048]{1,0:T(8,128)(2,1)}, u32[]{:S(2)}, u32[]{:S(2)}) collective-permute-start(bf16[256,2048]{1,0:T(8,128)(2,1)S(1)} %pad_maximum_fusion.15), channel_id=1, source_target_pairs={{0,16},{4,20},{8,24},{12,28},{16,0},{20,4},{24,8},{28,12},{1,17},{... | collective-permute-start | bytes 3145736 | tf_op jit(solution)/shard_map/ppermute | solution.py:42
  833.6 29.7 %collective-permute-start.101 = (bf16[1024,2048]{1,0:T(8,128)(2,1)}, bf16[1024,2048]{1,0:T(8,128)(2,1)}, u32[]{:S(2)}, u32[]{:S(2)}) collective-permute-start(bf16[1024,2048]{1,0:T(8,128)(2,1)} %convolution_convert_fusion.2), channel_id=1, source_target_pairs={{0,4},{4,0},{8,12},{12,8},{16,20},{20,16},{24,28},{28,24},{1,5},{5... | collective-permute-start | bytes 12582920 | tf_op jit(solution)/shard_map/ppermute | solution.py:42
  937.6 32.6 %collective-permute-start.116 = (bf16[2,256,1024]{2,1,0:T(8,128)(2,1)S(1)}, bf16[2,256,1024]{2,1,0:T(8,128)(2,1)}, u32[]{:S(2)}, u32[]{:S(2)}) collective-permute-start(bf16[2,256,1024]{2,1,0:T(8,128)(2,1)S(1)} %get-tuple-element.603), channel_id=1, source_target_pairs={{0,1},{1,0},{2,3},{3,2},{4,5},{5,4},{6,7},{7,6},{8,9},{9,8},{10,11... | collective-permute-start | bytes 3145736 | tf_op jit(solution)/shard_map/ppermute | solution.py:42
  940.6 29.7 %collective-permute-start.114 = (bf16[256,2048]{1,0:T(8,128)(2,1)S(1)}, bf16[256,2048]{1,0:T(8,128)(2,1)S(1)}, u32[]{:S(2)}, u32[]{:S(2)}) collective-permute-start(bf16[256,2048]{1,0:T(8,128)(2,1)S(1)} %pad_maximum_fusion.19), channel_id=1, source_target_pairs={{0,8},{4,12},{8,0},{12,4},{16,24},{20,28},{24,16},{28,20},{1,9},{5... | collective-permute-start | bytes 3145736 | tf_op jit(solution)/shard_map/ppermute | solution.py:42
  974.3 56.4 %all-to-all-start.3 = ((bf16[8,64,768]{2,1,0:T(8,128)(2,1)}), bf16[8,64,768]{2,1,0:T(8,128)(2,1)}, u32[]{:S(2)}, u32[]{:S(2)}) async-start(bf16[8,64,768]{2,1,0:T(8,128)(2,1)} %pad_maximum_fusion.21), calls=%async_computation.3 | async-start | bytes 1572864 | tf_op jit(solution)/shard_map/all_to_all | solution.py:1276
  991.0 42.4 %collective-permute-start.123 = (bf16[2,256,1024]{2,1,0:T(8,128)(2,1)}, bf16[2,256,1024]{2,1,0:T(8,128)(2,1)}, u32[]{:S(2)}, u32[]{:S(2)}) collective-permute-start(bf16[2,256,1024]{2,1,0:T(8,128)(2,1)} %get-tuple-element.618), channel_id=1, source_target_pairs={{0,1},{1,0},{2,3},{3,2},{4,5},{5,4},{6,7},{7,6},{8,9},{9,8},{10,11... | collective-permute-start | bytes 3145736 | tf_op jit(solution)/shard_map/ppermute | solution.py:42
  992.2 34.6 %collective-permute-start.118 = (bf16[128,2048]{1,0:T(8,128)(2,1)}, bf16[128,2048]{1,0:T(8,128)(2,1)}, u32[]{:S(2)}, u32[]{:S(2)}) collective-permute-start(bf16[128,2048]{1,0:T(8,128)(2,1)} %get-tuple-element.610), channel_id=1, source_target_pairs={{0,2},{1,3},{2,0},{3,1},{4,6},{5,7},{6,4},{7,5},{8,10},{9,11},{10,... | collective-permute-start | bytes 1572872 | tf_op jit(solution)/shard_map/ppermute | solution.py:42
  (231 other events, 3277.9 us)

commit v9 on v8

--- a/solution.py
+++ b/solution.py
@@ -707,26 +707,26 @@
             )
 
 
-def run_experts(x, u, ranks, in_pieces, down_pieces, router, places, which, compact, parts):
+def run_experts(x, u, ranks, in_pieces, down_pieces, router, places, which, filled, parts, at, steps):
     experts, _, hidden = in_pieces[0][2].shape
     hidden = hidden // 2
     depth = x[0].shape[1]
-    in_places = [(r, at, parts[0]) for r, at, _ in in_pieces]
-    down_places = [(r, at, parts[1]) for r, at, _ in down_pieces]
+    in_places = [(r, row, parts[0]) for r, row, _ in in_pieces]
+    down_places = [(r, row, parts[1]) for r, row, _ in down_pieces]
     pieces = [array for _, _, array in in_pieces + down_pieces]
     rows = ranks[0].shape[2]
-    steps = x[0].shape[0] // rows
-    token = pl.BlockSpec((rows, depth), lambda i: (i, 0))
-    rank = pl.BlockSpec((1, experts, rows), lambda i: (i, 0, 0))
+    pairs = x[0].shape[0] // rows
+    token = pl.BlockSpec((rows, depth), lambda i: (i + at, 0))
+    rank = pl.BlockSpec((1, experts, rows), lambda i: (i + at, 0, 0))
     anywhere = pl.BlockSpec(memory_space=pl.ANY)
 
     def slots(columns):
-        return pl.BlockSpec((experts, 2 * CAP, columns), lambda i: (0, i + which * steps, 0))
+        return pl.BlockSpec((experts, 2 * CAP, columns), lambda i: (0, i + at + which * pairs, 0))
 
     shape = jax.ShapeDtypeStruct
     tokens = shape(x[0].shape, BF16)
-    gates = shape((steps, experts, rows), F32)
-    count = 4 * steps * CAP
+    gates = shape((pairs, experts, rows), F32)
+    count = 4 * pairs * CAP
     wide = shape((experts, count, depth), BF16)
     inputs = [places, *x, *u, *ranks, router, *pieces]
     return pl.pallas_call(
@@ -736,7 +736,7 @@
         + [token] * 4
         + [rank] * 2
         + [pl.BlockSpec(router.shape, lambda i: (0, 0), pipeline_mode=pl.Buffered(1))]
-        + [anywhere] * (len(pieces) + len(compact)),
+        + [anywhere] * (len(pieces) + len(filled)),
         out_specs=[token] * 4 + [rank] * 2 + [slots(depth)] * 2 + [slots(2 * hidden), slots(hidden)],
         out_shape=[tokens] * 4
         + [gates] * 2
@@ -747,7 +747,7 @@
             pltpu.VMEM((experts, hidden, depth), BF16),
             pltpu.SemaphoreType.DMA((len(pieces),)),
         ],
-        input_output_aliases={len(inputs) + i: 6 + i for i in range(len(compact))},
+        input_output_aliases={len(inputs) + i: k for i, k in enumerate(filled)},
         compiler_params=pltpu.CompilerParams(vmem_limit_bytes=60 * MIB),
         cost_estimate=pl.CostEstimate(
             flops=4 * steps * CAP * experts * depth * (7 * hidden + 2 * rows),
@@ -755,7 +755,7 @@
             transcendentals=2 * steps * CAP * experts * hidden,
         ),
         name="experts",
-    )(*inputs, *compact)
+    )(*inputs, *filled.values())
 
 
 def product_kernel(me_ref, left_ref, right_ref, out_ref):
@@ -886,7 +886,6 @@
     own_quarters = {n: held_part(half_at, n * quarter, quarter) for n in (2, 3)}
     far_quarters = [held_part(1 - half_at, n * quarter, quarter) for n in range(4)]
     down_rows = quarters(held[2], 1)
-    down_rows = [down_rows[0], jnp.concatenate(down_rows[1:3], 1), down_rows[3]]
     upstream_halves = [held[3][:half_rows], held[3][half_rows:]]
     small = in_order(small, S, F, s, f).reshape(S, F, -1)
     prepared = (own_quarters, far_quarters, down_rows, upstream_halves, small)
@@ -955,11 +954,8 @@
     out_more = gather_more(own_output, out_first, S)
     far.append(far_part(1, query_low))
     near_own.append(near_swap(own_quarters[3], query_low))
-    down = [near_swap(down_rows[0], query_low)]
     attended, lse = attention_forward(query_low, key_low, value_low, seg_row, seg_col)
-    attended, out_more, far[1], down[0], near_own[2] = tie(
-        attended, out_more, far[1], down[0], near_own[2]
-    )
+    attended, out_more, far[1], near_own[2] = tie(attended, out_more, far[1], near_own[2])
     attended_blocks = attended.reshape(S, T, C)
     come = lax.all_to_all(attended_blocks, "seq", split_axis=0, concat_axis=0, tiled=True)
     out_even, out_odd = gather_end(own_output, out_first, out_more, S)
@@ -968,16 +964,16 @@
     own_up_more = gather_more(after(upstream_low, attended), own_up_first, S)
     come, far[2], near_far[0], own_up_more = tie(come, far[2], near_far[0], own_up_more)
     own_u = gather_end(upstream_low, own_up_first, own_up_more, S)
-    far.append(far_part(3, come))
     near_far.append(near_swap(far[1], come))
+    down = [near_swap(down_rows[0], come)]
     partner_up_first = gather_first(after(partner_up, come), S)
     come = relative(come, s).transpose(1, 0, 2).reshape(T, D)
     residual = inputs + matmul(come[:, : D // 2], out_even) + matmul(come[:, D // 2 :], out_odd)
     moe_factor = rms_factor(residual)
     residual_n = residual * moe_factor
     second_low = (residual_n * gain_moe).astype(BF16)
-    second_low, far[3], near_far[1], partner_up_first, own_u = tie(
-        second_low, far[3], near_far[1], partner_up_first, own_u
+    second_low, down[0], near_far[1], partner_up_first, own_u = tie(
+        second_low, down[0], near_far[1], partner_up_first, own_u
     )
 
     own_first = gather_first(second_low, S)
@@ -989,20 +985,22 @@
     )
     own_more = gather_more(second_low, own_first, S)
     partner_low.append(far_swap(second_low[half_rows:], own_first))
-    near_far.append(near_swap(far[3], own_first))
+    down.append(near_swap(down_rows[1], own_first))
     partner_up_more = gather_more(after(partner_up, own_first), partner_up_first, S)
-    own_more, partner_low[1], near_far[3], partner_up_more = tie(
-        own_more, partner_low[1], near_far[3], partner_up_more
+    own_more, partner_low[1], down[1], partner_up_more = tie(
+        own_more, partner_low[1], down[1], partner_up_more
     )
     partner_low = jnp.concatenate(partner_low, 0)
     own_x = gather_end(second_low, own_first, own_more, S)
     partner_first = gather_first(after(partner_low, own_more), S)
-    down.append(near_swap(down_rows[1], own_more))
-    partner_first, down[1], own_x = tie(partner_first, down[1], own_x)
+    down.append(near_swap(down_rows[2], own_more))
+    far.append(far_part(3, own_more))
+    partner_first, down[2], own_x, far[3] = tie(partner_first, down[2], own_x, far[3])
     other_u = gather_end(after(partner_up, partner_first), partner_up_first, partner_up_more, S)
     partner_more = gather_more(partner_low, partner_first, S)
-    down.append(near_swap(down_rows[2], partner_first))
-    partner_more, down[2], other_u = tie(partner_more, down[2], other_u)
+    down.append(near_swap(down_rows[3], partner_first))
+    near_far.append(near_swap(far[3], partner_first))
+    partner_more, down[3], other_u, near_far[3] = tie(partner_more, down[3], other_u, near_far[3])
     other_x = gather_end(partner_low, partner_first, partner_more, S)
     in_pieces = []
     for r in range(F):
@@ -1010,34 +1008,50 @@
             first = (0, 2, 3)[n] if r < half_f else n
             in_pieces.append((r, first * quarter, rows[r % half_f]))
     down_pieces = [
-        (r, (0, 1, 3)[n] * (down_part // 4), down[n][r]) for r in range(half_f) for n in range(3)
+        (r, n * (down_part // 4), down[n][r]) for r in range(half_f) for n in range(4)
     ]
     wide_router = jnp.pad(full_router, ((0, 0), (0, 128 - E)))
     expert_places = jnp.stack([s * experts, f]).astype(jnp.int32)
     parts = (in_part, down_part)
-    own_parts = run_experts(
-        own_x, own_u, own_ranks, in_pieces, down_pieces, wide_router, expert_places, 0, (), parts
-    )
+    pairs = S // 2
+    short = max(1, pairs // 4)
+
+    def call(x, u, ranks, which, filled, at, steps):
+        filled = {k: filled[k] for k in sorted(filled)}
+        return run_experts(
+            x,
+            u,
+            ranks,
+            in_pieces,
+            down_pieces,
+            wide_router,
+            expert_places,
+            which,
+            filled,
+            parts,
+            at,
+            steps,
+        )
+
+    own_parts = call(own_x, own_u, own_ranks, 0, {}, 0, short)
     own_parts, other_x = tie(own_parts, other_x)
-    own_got = swap(own_parts[3], "seq", S, 1)
-    own_out_got = swap(own_parts[1], "seq", S, 1)
-    other_parts = run_experts(
-        other_x,
-        other_u,
-        other_ranks,
-        in_pieces,
-        down_pieces,
-        wide_router,
-        expert_places,
-        1,
-        own_parts[6:],
-        parts,
-    )
-    other_parts, own_got, own_out_got = tie(other_parts, own_got, own_out_got)
+    compact = {k: own_parts[k] for k in range(6, 10)}
+    other_parts = call(other_x, other_u, other_ranks, 1, compact, 0, pairs)
+    other_got = swap(other_parts[3], "seq", S, 1)
+    filled = {k: (own_parts if k < 6 else other_parts)[k] for k in range(10)}
+    own_parts = call(own_x, own_u, own_ranks, 0, filled, short, short)
+    own_parts, other_got = tie(own_parts, other_got)
+    other_sums = sum_cores(other_parts[2], other_got, S)
+    come, own_x = sum_first(other_sums, S, own_x)
+    other_out_got = swap(after(other_parts[1], other_got), "seq", S, 1)
+    own_parts = call(
+        own_x, own_u, own_ranks, 0, dict(enumerate(own_parts)), 2 * short, pairs - 2 * short
+    )
+    own_parts, come, other_out_got = tie(own_parts, come, other_out_got)
     logits = matmul(second_low, full_router)
     router_probs = jax.nn.softmax(logits, axis=-1)
 
-    x_rows, u_rows, in_grads, hidden_gate = other_parts[6:]
+    x_rows, u_rows, in_grads, hidden_gate = own_parts[6:]
     in_terms, down_terms = {}, {}
 
     def in_products(r, *dep):
@@ -1055,64 +1069,57 @@
     gate_grads = jnp.stack(
         [to_home(own_parts[4], own_parts[5]), to_home(other_parts[4], other_parts[5])], 1
     ).reshape(S, -1)
-    other_got = swap(other_parts[3], "seq", S, 1)
+    singles, other_total = sum_more(other_sums, come, S)
+    come = sum_last(singles, S)
+    own_got = swap(own_parts[3], "seq", S, 1)
     for r in far_odd:
         in_products(r)
     gate_grads = lax.all_to_all(gate_grads, "seq", split_axis=0, concat_axis=0, tiled=True)
-    other_got, in_terms, gate_grads = tie(other_got, in_terms, gate_grads)
+    come, own_got, in_terms, gate_grads = tie(come, own_got, in_terms, gate_grads)
     sent = {r: quarters(in_terms[r], 1) for r in far_odd}
 
     def send_in(n, *dep):
         return {r: swap(after(sent[r][n], dep), "fsdp", F, 1) for r in sent}
-
-    other_sums = sum_cores(other_parts[2], other_got, S)
-    come = sum_first(other_sums, S)
-    far_got = [send_in(0, other_got)]
-    other_out_got = swap(after(other_parts[1], other_got), "seq", S, 1)
-    come, far_got[0], other_out_got = tie(come, far_got[0], other_out_got)
-    gate_grads = gate_grads.reshape(S, 2, T * experts)
-    partner_grads = far_swap(gate_grads[:, 1], come)
-    singles, other_total = sum_more(other_sums, come, S)
-    come = sum_last(singles, S)
-    middle_sent = {r: jnp.concatenate(sent[r][1:3], 1) for r in sent}
-    middle_got = {
-        r: swap(after(middle_sent[r], far_got[0]), "fsdp", F, 1) for r in middle_sent
-    }
 
     def down_products(r, dep):
         down_terms[r] = products(
             after(hidden_gate, dep), u_rows, down_part, r, half_f, f_at, "down_products"
         )
 
-    for r in range(1, half_f, 2):
-        down_products(r, singles)
-    come, middle_got, partner_grads, down_terms = tie(
-        come, middle_got, partner_grads, down_terms
-    )
-    for n in range(2):
-        far_got.append({r: got[:, n * quarter : (n + 1) * quarter] for r, got in middle_got.items()})
+    gate_grads = gate_grads.reshape(S, 2, T * experts)
     other_rows = add_all(other_total, come).astype(BF16)
-    gate_grads = gate_grads[:, 0] + partner_grads
-    gate_grads = gate_grads.reshape(S, T, experts).transpose(1, 0, 2).reshape(T, E)
+    own_sums = sum_cores(own_parts[2], after(own_got, other_rows), S)
+    come, other_rows = sum_first(own_sums, S, other_rows)
     back = [far_swap(other_rows[:half_rows])]
-    own_sums = sum_cores(own_parts[2], after(own_got, other_rows), S)
-    come = sum_first(own_sums, S)
-    far_got.append(send_in(3, other_rows))
+    far_got = [send_in(0, other_rows)]
+    own_out_got = swap(after(own_parts[1], own_got), "seq", S, 1)
     for r in far_odd:
         in_products(r ^ 1, other_rows)
-    come, back[0], far_got[3], in_terms = tie(come, back[0], far_got[3], in_terms)
+    for r in range(1, half_f, 2):
+        down_products(r, other_rows)
+    come, back[0], far_got[0], in_terms, down_terms, own_out_got = tie(
+        come, back[0], far_got[0], in_terms, down_terms, own_out_got
+    )
+    partner_grads = far_swap(gate_grads[:, 1], come)
     back.append(far_swap(other_rows[half_rows:], come))
     singles, own_total = sum_more(own_sums, come, S)
     come = sum_last(singles, S)
-    down_sent = {r: quarters(down_terms[r], 1) for r in range(1, half_f, 2)}
+    far_got.append(send_in(1, singles))
+    down_sent = {
+        r: [down_terms[r][:, : down_part // 2], down_terms[r][:, down_part // 2 :]]
+        for r in range(1, half_f, 2)
+    }
 
     def send_down(n, *dep):
         return {r: swap(after(down_sent[r][n], dep), "fsdp", F, 1) for r in down_sent}
 
-    down_got = [send_down(0, singles)]
     for r in near_odd:
         in_products(r, singles)
-    come, back[1], down_got[0], in_terms = tie(come, back[1], down_got[0], in_terms)
+    come, back[1], far_got[1], in_terms, partner_grads = tie(
+        come, back[1], far_got[1], in_terms, partner_grads
+    )
+    gate_grads = gate_grads[:, 0] + partner_grads
+    gate_grads = gate_grads.reshape(S, T, experts).transpose(1, 0, 2).reshape(T, E)
     row_grads = add_all(own_total, come) + jnp.concatenate(back, 0).astype(F32)
 
     upstream = upstream_low.astype(F32)
@@ -1148,31 +1155,31 @@
 
     branch_first = gather_first(branch_low, S)
     far_sums = [far_sum(0, branch_low)]
-    down_got.append(send_down(1, branch_low))
+    far_got.append(send_in(2, branch_low))
     for r in range(0, half_f, 2):
         down_products(r, branch_low)
-    branch_first, far_sums[0], down_got[1], down_terms = tie(
-        branch_first, far_sums[0], down_got[1], down_terms
+    branch_first, far_sums[0], far_got[2], down_terms = tie(
+        branch_first, far_sums[0], far_got[2], down_terms
     )
     branch_more = gather_more(branch_low, branch_first, S)
     far_sums.append(far_sum(1, branch_first))
-    down_got.append(send_down(2, branch_first))
+    far_got.append(send_in(3, branch_first))
     branch_even, branch_odd = gather_end(branch_low, branch_first, branch_more, S)
 
     head_grads = jnp.concatenate(
         [matmul_t(branch_even, own_output), matmul_t(branch_odd, own_output)], 0
     ).astype(BF16)
     head_grads = absolute(head_grads.reshape(S, T, C), s).reshape(L, C)
-    head_grads, far_sums[1], down_got[2] = tie(head_grads, far_sums[1], down_got[2])
+    head_grads, far_sums[1], far_got[3] = tie(head_grads, far_sums[1], far_got[3])
     far_sums.append(far_sum(2, head_grads))
-    down_got.append(send_down(3, head_grads))
+    down_got = [send_down(0, head_grads)]
     other_out_sums = sum_cores(other_parts[0], after(other_out_got, head_grads), S)
     come, head_grads = sum_first(other_out_sums, S, head_grads)
     query_back, key_back, value_back = attention_backward(
         query_low, key_low, value_low, head_grads, lse, seg_row, seg_col
     )
-    query_back, key_back, value_back, far_sums[2], down_got[3], come = tie(
-        query_back, key_back, value_back, far_sums[2], down_got[3], come
+    query_back, key_back, value_back, far_sums[2], down_got[0], come = tie(
+        query_back, key_back, value_back, far_sums[2], down_got[0], come
     )
 
     singles, other_total = sum_more(other_out_sums, come, S)
@@ -1199,6 +1206,7 @@
     other_outs = add_all(other_total, come).astype(BF16)
     outs_back = [far_swap(other_outs[:half_rows])]
     value_got = swap(value_term[: F // 2], "fsdp", F, 1)
+    down_got.append(send_down(1, means))
     pre_rel = rope_back(
         (query_back, key_back, value_back),
         query_pre,
@@ -1213,8 +1221,8 @@
     ).reshape(2, L // 2, 3 * C)
     normed_got = swap(matmul_t(pre_rel[1], w_qkv).astype(BF16), "seq", S, 1)
     normed_kept = matmul_t(pre_rel[0], w_qkv).astype(BF16)
-    normed_got, normed_kept, value_got, outs_back[0] = tie(
-        normed_got, normed_kept, value_got, outs_back[0]
+    normed_got, normed_kept, value_got, outs_back[0], down_got[1] = tie(
+        normed_got, normed_kept, value_got, outs_back[0], down_got[1]
     )
 
     normed_sums = sum_cores(normed_kept, normed_got, S)
@@ -1244,7 +1252,10 @@
     gain_got = swap(gain_terms[F // 2 :], "fsdp", F, half_f)
     for r in near_odd:
         in_products(r ^ 1, turned_term)
-    come, turned_got, gain_got, in_terms = tie(come, turned_got, gain_got, in_terms)
+    outs_back.append(far_swap(other_outs[half_rows:], turned_term))
+    come, turned_got, gain_got, in_terms, outs_back[1] = tie(
+        come, turned_got, gain_got, in_terms, outs_back[1]
+    )
     gain_terms = gain_terms[: F // 2] + gain_got
     normed_grads = add_all(normed_total, come)
     turned_sum = sum_rest(sum_even(turned_term, turned_got, F), F)
@@ -1264,7 +1275,6 @@
         turned_sum, own_come, near_got[0], gain_terms
     )
     near_got.append(send_near(middle, turned_sum))
-    outs_back.append(far_swap(other_outs[half_rows:], turned_sum))
     count = S * part * (E + 1)
     head_terms = gain_terms[0, count:]
     gain_terms = halve(gain_terms[0, :count].reshape(S, -1), "seq", S, S // 2)[0]

time: 1060 us -> 1070 us (level)
  Pallas kernels: 255 us -> 287 us
  waiting for transfers between devices: 350 us -> 332 us
    ppermute x124, waiting for transfers between devices: 350 us -> 312 us  [swap(): return lax.ppermute(values, axis, [(i, i ^ mask) for i in range(size)])]
    pallas_call x2 -> x4, Pallas kernels: 118 us -> 151 us  [run_experts(): pl.pallas_call(partial(expert_kernel, in_places, down_places), grid=(step...]
    all_to_all x1, waiting for transfers between devices: 0.01 us -> 11.2 us  [per_device(): lax.all_to_all(qkv_term, 'seq', split_axis=0, concat_axis=0, tiled=True)]
    add x5 -> x6, other arithmetic: 20 us -> 27.3 us  [part(): return even[at].astype(F32) + got[at].astype(F32)]
    unnamed x342 -> x366, local copies, waits for them, and re-layouts: 57.9 us -> 59.2 us
  transfers between devices with their start and end apart: 128 -> 128, of which waited for: 58 -> 50; matrix products, arithmetic and copies ran while one was open for 20% -> 20% of each run, Pallas kernels for 24% -> 21%
where the time goes in v9:
time: 1070 us; the launch traced here: 1060 us
  waiting for transfers between devices  332 us (31%)
  Pallas kernels  287 us (27%)
  starting transfers between devices  143 us (13%)
  local copies, waits for them, and re-layouts  135 us (13%)
  other arithmetic  113 us (11%)
  matrix products  45.5 us (4%)
    ppermute x124, waiting for transfers between devices, swap(): return lax.ppermute(values, axis, [(i, i ^ mask) for i in range(size)])  312 us
    pallas_call x4, Pallas kernels, run_experts(): pl.pallas_call(partial(expert_kernel, in_places, down_places), grid=(step...  151 us
    ppermute x124, starting transfers between devices, swap(): return lax.ppermute(values, axis, [(i, i ^ mask) for i in range(size)])  128 us
    pallas_call x6, Pallas kernels, products(): pl.pallas_call(product_kernel, grid_spec=pltpu.PrefetchScalarGridSpec(num...  60 us
    unnamed x366, local copies, waits for them, and re-layouts  59.2 us
    pallas_call x1, Pallas kernels, attention_backward(): pl.pallas_call(partial(backward_kernel, span), grid=(heads, length // row...  28.4 us
    add x6, other arithmetic, part(): return even[at].astype(F32) + got[at].astype(F32)  27.3 us
    pallas_call x1, Pallas kernels, attention_forward(): pl.pallas_call(partial(forward_kernel, span), grid=(heads, length // rows...  21.6 us
  transfers between devices with their start and end apart: 128, of which 50 were waited for; matrix products, arithmetic and copies ran while one was open for 20% of the time, Pallas kernels for 21%

profile of v9, /device:TPU:0, one launch (start us, length us, event | category | flops | bytes accessed | tf_op | source)
XLA Modules:
  0.0 1060.6 jit_solution(7275135166737667622)
XLA Ops:
  30.7 8.6 collective-permute-done.4
  70.9 14.2 %collective-permute-done.7 = bf16[8,64,768]{2,1,0:T(8,128)(2,1)} collective-permute-done((bf16[8,64,768]{2,1,0:T(8,128)(2,1)}, bf16[8,64,768]{2,1,0:T(8,128)(2,1)}, u32[]{:S(2)}, u32[]{:S(2)}) %collective-permute-start.7) | collective-permute-done | bytes 786464 | tf_op jit(solution)/shard_map/ppermute | solution.py:42
  101.2 16.6 %collective-permute-done.12 = bf16[128,2048]{1,0:T(8,128)(2,1)S(1)} collective-permute-done((bf16[128,2048]{1,0:T(8,128)(2,1)S(1)}, bf16[128,2048]{1,0:T(8,128)(2,1)S(1)}, u32[]{:S(2)}, u32[]{:S(2)}) %collective-permute-start.12) | collective-permute-done | bytes 524320 | tf_op jit(solution)/shard_map/ppermute | solution.py:42
  131.4 12.6 %project.1 = (bf16[1024,2048]{1,0:T(8,128)(2,1)}, bf16[1024,2048]{1,0:T(8,128)(2,1)}, f32[2048,256]{1,0:T(8,128)S(1)}, f32[2048,256]{1,0:T(8,128)S(1)}, bf16[204...) custom-call(s32[1]{0:T(128)} %bitcast.1.me_ref, bf16[1024,2048]{1,0:T(8,128)(2,1)} %constant_dynamic-update-slice_fusion.even_ref, ...), custom_call_target="tpu_custom_call" | custom-call | flops 6442450944 | bytes 25165824 | tf_op jit(solution)/shard_map/project/pallas_call | solution.py:437
  172.4 11.6 %collective-permute-done.22 = f32[2,2048]{1,0:T(2,128)S(1)} collective-permute-done((f32[2,2048]{1,0:T(2,128)S(1)}, f32[2,2048]{1,0:T(2,128)S(1)}, u32[]{:S(2)}, u32[]{:S(2)}) %collective-permute-start.22) | collective-permute-done | bytes 16416 | tf_op jit(solution)/shard_map/ppermute | solution.py:42
  204.7 21.6 %attend.1 = (bf16[2048,256]{1,0:T(8,128)(2,1)S(1)}, f32[2,1,2048]{2,1,0:T(1,128)S(1)}) custom-call(bf16[2048,256]{1,0:T(8,128)(2,1)S(1)} %get-tuple-element.400.q_ref, bf16[2048,256]{1,0:T(8,128)(2,1)S(1)} %get-tuple-element.401.k_ref, bf16[2048,256]{1,0:T(8,128)(2,1)S(1)} %copy-done.20, s32[1,2048]{1,0:T(1,128)S(1)} %copy-done.14, s32[2048,1]{1,0:T(8,128)S(1)} %copy-done.9), custom_call_target="tpu_custom_call" | custom-call | flops 2684354560 | bytes 4194304 | tf_op jit(solution)/shard_map/attend/pallas_call | solution.py:336
  286.1 9.3 collective-permute-done.37.refs_18_
  302.8 17.7 %collective-permute-done.45.refs_12_ = bf16[2,128,1024]{2,1,0:T(8,128)(2,1)S(1)} collective-permute-done((bf16[2,128,1024]{2,1,0:T(8,128)(2,1)}, bf16[2,128,1024]{2,1,0:T(8,128)(2,1)S(1)}, u32[]{:S(2)}, u32[]{:S(2)}) %collective-permute-start.45) | collective-permute-done | bytes 524320 | tf_op jit(solution)/shard_map/ppermute | solution.py:42
  326.3 8.0 collective-permute-done.50
  335.2 11.0 %collective-permute-done.49.refs_19_ = bf16[2,64,2048]{2,1,0:T(8,128)(2,1)S(1)} collective-permute-done((bf16[2,64,2048]{2,1,0:T(8,128)(2,1)S(1)}, bf16[2,64,2048]{2,1,0:T(8,128)(2,1)S(1)}, u32[]{:S(2)}, u32[]{:S(2)}) %collective-permute-start.49) | collective-permute-done | bytes 524320 | tf_op jit(solution)/shard_map/ppermute | solution.py:42
  351.4 22.8 %collective-permute-done.56.refs_9_ = bf16[2,128,1024]{2,1,0:T(8,128)(2,1)S(1)} collective-permute-done((bf16[2,128,1024]{2,1,0:T(8,128)(2,1)S(1)}, bf16[2,128,1024]{2,1,0:T(8,128)(2,1)S(1)}, u32[]{:S(2)}, u32[]{:S(2)}) %collective-permute-start.56) | collective-permute-done | bytes 524320 | tf_op jit(solution)/shard_map/ppermute | solution.py:42
  384.2 7.3 collective-permute-done.61.refs_13_
  391.5 10.8 %collective-permute-done.59.refs_21_ = bf16[2,64,2048]{2,1,0:T(8,128)(2,1)S(1)} collective-permute-done((bf16[2,64,2048]{2,1,0:T(8,128)(2,1)S(1)}, bf16[2,64,2048]{2,1,0:T(8,128)(2,1)S(1)}, u32[]{:S(2)}, u32[]{:S(2)}) %collective-permute-start.59) | collective-permute-done | bytes 524320 | tf_op jit(solution)/shard_map/ppermute | solution.py:42
  410.0 34.1 %experts.4 = (bf16[1024,2048]{1,0:T(8,128)(2,1)}, bf16[1024,2048]{1,0:T(8,128)(2,1)}, bf16[1024,2048]{1,0:T(8,128)(2,1)}, bf16[1024,2048]{1,0:T(8,128)(2,1)}, f3...) custom-call(s32[2]{0:T(128)} %pad_add_fusion.first_ref, ...), custom_call_target="tpu_custom_call" | custom-call | flops 9663676416 | bytes 62914560 | tf_op jit(solution)/shard_map/experts/pallas_call | solution.py:732
  444.1 59.5 %experts.5 = (bf16[1024,2048]{1,0:T(8,128)(2,1)}, bf16[1024,2048]{1,0:T(8,128)(2,1)}, bf16[1024,2048]{1,0:T(8,128)(2,1)}, bf16[1024,2048]{1,0:T(8,128)(2,1)}, f3...) custom-call(s32[2]{0:T(128)} %pad_add_fusion.first_ref, ...), custom_call_target="tpu_custom_call", output_to_operand_aliasing={{6}: (30, {}), {7}: (31, {}), {8}: (32, {}), {9}: (33, {})} | custom-call | flops 38654705664 | bytes 62914560 | tf_op jit(solution)/shard_map/experts/pallas_call | solution.py:732
  504.1 22.2 %experts.6 = (bf16[1024,2048]{1,0:T(8,128)(2,1)}, bf16[1024,2048]{1,0:T(8,128)(2,1)}, bf16[1024,2048]{1,0:T(8,128)(2,1)}, bf16[1024,2048]{1,0:T(8,128)(2,1)}, f3...) custom-call(s32[2]{0:T(128)} %pad_add_fusion.first_ref, ...), custom_call_target="tpu_custom_call", output_to_operand_aliasing={{0}: (30, {}), {1}: (31, {}), {2}: (32, {}), {3}: (33, {}),... | custom-call | flops 9663676416 | bytes 62914560 | tf_op jit(solution)/shard_map/experts/pallas_call | solution.py:732
  531.6 35.3 %experts.7 = (bf16[1024,2048]{1,0:T(8,128)(2,1)}, bf16[1024,2048]{1,0:T(8,128)(2,1)}, bf16[1024,2048]{1,0:T(8,128)(2,1)}, bf16[1024,2048]{1,0:T(8,128)(2,1)}, f3...) custom-call(s32[2]{0:T(128)} %pad_add_fusion.first_ref, ...), custom_call_target="tpu_custom_call", output_to_operand_aliasing={{0}: (30, {}), {1}: (31, {}), {2}: (32, {}), {3}: (33, {}),... | custom-call | flops 19327352832 | bytes 62914560 | tf_op jit(solution)/shard_map/experts/pallas_call | solution.py:732
  583.7 9.3 in_products.4
  593.0 8.9 all-to-all-done.2
  614.8 9.4 in_products.5
  624.2 11.0 %down_products.2 = bf16[2,256,2048]{2,1,0:T(8,128)(2,1)} custom-call(s32[1]{0:T(128)} %bitcast.25.me_ref, bf16[2,2304,512]{2,1,0:T(8,128)(2,1)} %get-tuple-element.606.left_ref, bf16[2,2304,2048]{2,1,0:T(8,128)(2,1)} %get-tuple-element.581.right_ref), custom_call_target="tpu_custom_call" | custom-call | flops 4831838208 | bytes 21233664 | tf_op jit(solution)/shard_map/down_products/pallas_call | solution.py:769
  651.1 9.7 in_products.6
  660.8 22.3 %collective-permute-done.79 = f32[8,512]{0,1:T(8,128)S(1)} collective-permute-done((f32[8,512]{0,1:T(8,128)}, f32[8,512]{0,1:T(8,128)S(1)}, u32[]{:S(2)}, u32[]{:S(2)}) %collective-permute-start.79) | collective-permute-done | bytes 16416 | tf_op jit(solution)/shard_map/ppermute | solution.py:42
  700.8 11.0 %down_products.3 = bf16[2,256,2048]{2,1,0:T(8,128)(2,1)} custom-call(s32[1]{0:T(128)} %bitcast.25.me_ref, bf16[2,2304,512]{2,1,0:T(8,128)(2,1)} %get-tuple-element.606.left_ref, bf16[2,2304,2048]{2,1,0:T(8,128)(2,1)} %get-tuple-element.581.right_ref), custom_call_target="tpu_custom_call" | custom-call | flops 4831838208 | bytes 21233664 | tf_op jit(solution)/shard_map/down_products/pallas_call | solution.py:769
  744.3 15.0 %collective-permute-done.88 = bf16[2,128,1024]{2,1,0:T(8,128)(2,1)S(1)} collective-permute-done((bf16[2,128,1024]{2,1,0:T(8,128)(2,1)S(1)}, bf16[2,128,1024]{2,1,0:T(8,128)(2,1)S(1)}, u32[]{:S(2)}, u32[]{:S(2)}) %collective-permute-start.88) | collective-permute-done | bytes 524320 | tf_op jit(solution)/shard_map/ppermute | solution.py:42
  770.9 28.4 %attend_back.1 = (bf16[2048,256]{1,0:T(8,128)(2,1)S(1)}, bf16[2048,256]{1,0:T(8,128)(2,1)S(1)}, bf16[2048,256]{1,0:T(8,128)(2,1)S(1)}) custom-call(bf16[2048,256]{1,0:T(8,128)(2,1)S(1)} %copy-done.16, bf16[2048,256]{1,0:T(8,128)(2,1)S(1)} %copy-done.18, bf16[2048,256]{1,0:T(8,128)(2,1)} %copy-done.19, bf16[2048,256]{1,0:T(8,128)(2,1)} %bitcast.367, ...), custom_call_target="tpu_custom_call" | custom-call | flops 6710886400 | bytes 7340032 | tf_op jit(solution)/shard_map/attend_back/pallas_call | solution.py:368
  863.2 20.9 %collective-permute-done.102 = bf16[128,2048]{1,0:T(8,128)(2,1)S(1)} collective-permute-done((bf16[128,2048]{1,0:T(8,128)(2,1)S(1)}, bf16[128,2048]{1,0:T(8,128)(2,1)S(1)}, u32[]{:S(2)}, u32[]{:S(2)}) %collective-permute-start.102) | collective-permute-done | bytes 524320 | tf_op jit(solution)/shard_map/ppermute | solution.py:42
  884.2 13.2 %collective-permute-done.101 = bf16[2,8,64,256]{3,2,1,0:T(8,128)(2,1)S(1)} collective-permute-done((bf16[2,8,64,256]{3,2,1,0:T(8,128)(2,1)S(1)}, bf16[2,8,64,256]{3,2,1,0:T(8,128)(2,1)S(1)}, u32[]{:S(2)}, u32[]{:S(2)}) %collective-permute-start.101) | collective-permute-done | bytes 524320 | tf_op jit(solution)/shard_map/ppermute | solution.py:42
  950.4 9.6 in_products.7
  960.0 16.0 %collective-permute-done.112 = f32[2,8832]{1,0:T(2,128)S(1)} collective-permute-done((f32[2,8832]{1,0:T(2,128)}, f32[2,8832]{1,0:T(2,128)S(1)}, u32[]{:S(2)}, u32[]{:S(2)}) %collective-permute-start.112) | collective-permute-done | bytes 70688 | tf_op jit(solution)/shard_map/ppermute | solution.py:42
  996.8 17.0 %collective-permute-done.114 = bf16[1,8,64,512]{3,2,1,0:T(8,128)(2,1)S(1)} collective-permute-done((bf16[1,8,64,512]{3,2,1,0:T(8,128)(2,1)S(1)}, bf16[1,8,64,512]{3,2,1,0:T(8,128)(2,1)S(1)}, u32[]{:S(2)}, u32[]{:S(2)}) %collective-permute-start.114) | collective-permute-done | bytes 524320 | tf_op jit(solution)/shard_map/ppermute | solution.py:42
  1037.5 11.2 %all-to-all-done.3 = bf16[8,64,768]{2,1,0:T(8,128)(2,1)S(1)} async-done(((bf16[8,64,768]{2,1,0:T(8,128)(2,1)}), bf16[8,64,768]{2,1,0:T(8,128)(2,1)S(1)}, u32[]{:S(2)}, u32[]{:S(2)}) %all-to-all-start.3) | async-done | bytes 786464 | tf_op jit(solution)/shard_map/all_to_all | solution.py:1286
  (837 shorter events, 520.1 us)
Async XLA Ops:
  49.5 39.8 %collective-permute-start.10 = (bf16[256,2048]{1,0:T(8,128)(2,1)S(1)}, bf16[256,2048]{1,0:T(8,128)(2,1)}, u32[]{:S(2)}, u32[]{:S(2)}) collective-permute-start(bf16[256,2048]{1,0:T(8,128)(2,1)S(1)} %bitcast.331), channel_id=1, source_target_pairs={{0,16},{4,20},{8,24},{12,28},{16,0},{20,4},{24,8},{28,12},{1,17},{... | collective-permute-start | bytes 3145736 | tf_op jit(solution)/shard_map/ppermute | solution.py:42
  51.0 38.2 %collective-permute-start.9 = (bf16[256,2048]{1,0:T(8,128)(2,1)S(1)}, bf16[256,2048]{1,0:T(8,128)(2,1)}, u32[]{:S(2)}, u32[]{:S(2)}) collective-permute-start(bf16[256,2048]{1,0:T(8,128)(2,1)S(1)} %bitcast.332), channel_id=1, source_target_pairs={{0,8},{4,12},{8,0},{12,4},{16,24},{20,28},{24,16},{28,20},{1,9},{5... | collective-permute-start | bytes 3145736 | tf_op jit(solution)/shard_map/ppermute | solution.py:42
  55.0 34.2 %collective-permute-start.8 = (bf16[8,64,768]{2,1,0:T(8,128)(2,1)}, bf16[8,64,768]{2,1,0:T(8,128)(2,1)}, u32[]{:S(2)}, u32[]{:S(2)}) collective-permute-start(bf16[8,64,768]{2,1,0:T(8,128)(2,1)} %all-to-all-done), channel_id=1, source_target_pairs={{0,2},{1,3},{2,0},{3,1},{4,6},{5,7},{6,4},{7,5},{8,10},{9,11},{10,... | collective-permute-start | bytes 2359304 | tf_op jit(solution)/shard_map/ppermute | solution.py:42
  158.8 35.0 %collective-permute-start.24 = (bf16[256,2048]{1,0:T(8,128)(2,1)}, bf16[256,2048]{1,0:T(8,128)(2,1)}, u32[]{:S(2)}, u32[]{:S(2)}) collective-permute-start(bf16[256,2048]{1,0:T(8,128)(2,1)} %bitcast.18), channel_id=1, source_target_pairs={{0,8},{4,12},{8,0},{12,4},{16,24},{20,28},{24,16},{28,20},{1,9},{5... | collective-permute-start | bytes 3145736 | tf_op jit(solution)/shard_map/ppermute | solution.py:42
  190.1 59.8 %collective-permute-start.34 = (bf16[128,2048]{1,0:T(8,128)(2,1)}, bf16[128,2048]{1,0:T(8,128)(2,1)}, u32[]{:S(2)}, u32[]{:S(2)}) collective-permute-start(bf16[128,2048]{1,0:T(8,128)(2,1)} %slice.564), channel_id=1, source_target_pairs={{0,16},{4,20},{8,24},{12,28},{16,0},{20,4},{24,8},{28,12},{1,17},{... | collective-permute-start | bytes 1572872 | tf_op jit(solution)/shard_map/ppermute | solution.py:42
  193.8 33.5 %collective-permute-start.31 = (bf16[2,128,1024]{2,1,0:T(8,128)(2,1)S(1)}, bf16[2,128,1024]{2,1,0:T(8,128)(2,1)S(1)}, u32[]{:S(2)}, u32[]{:S(2)}) collective-permute-start(bf16[2,128,1024]{2,1,0:T(8,128)(2,1)S(1)} %copy-done.45), channel_id=1, source_target_pairs={{0,1},{1,0},{2,3},{3,2},{4,5},{5,4},{6,7},{7,6},{8,9},{9,8},{10,11... | collective-permute-start | bytes 1572872 | tf_op jit(solution)/shard_map/ppermute | solution.py:42
  195.2 34.0 %collective-permute-start.30 = (bf16[2,128,1024]{2,1,0:T(8,128)(2,1)S(1)}, bf16[2,128,1024]{2,1,0:T(8,128)(2,1)}, u32[]{:S(2)}, u32[]{:S(2)}) collective-permute-start(bf16[2,128,1024]{2,1,0:T(8,128)(2,1)S(1)} %copy-done.113), channel_id=1, source_target_pairs={{0,2},{1,3},{2,0},{3,1},{4,6},{5,7},{6,4},{7,5},{8,10},{9,11},{10,... | collective-permute-start | bytes 1572872 | tf_op jit(solution)/shard_map/ppermute | solution.py:42
  242.6 39.3 %collective-permute-start.36 = (bf16[1024,2048]{1,0:T(8,128)(2,1)}, bf16[1024,2048]{1,0:T(8,128)(2,1)}, u32[]{:S(2)}, u32[]{:S(2)}) collective-permute-start(bf16[1024,2048]{1,0:T(8,128)(2,1)} %constant_dynamic-update-slice_fusion.13), channel_id=1, source_target_pairs={{0,4},{4,0},{8,12},{12,8},{16,20},{20,16},{24,28},{28,24},{1,5},{5... | collective-permute-start | bytes 12582920 | tf_op jit(solution)/shard_map/ppermute | solution.py:42
  258.0 37.4 %collective-permute-start.41 = (bf16[1024,2048]{1,0:T(8,128)(2,1)}, bf16[1024,2048]{1,0:T(8,128)(2,1)}, u32[]{:S(2)}, u32[]{:S(2)}) collective-permute-start(bf16[1024,2048]{1,0:T(8,128)(2,1)} %constant_dynamic-update-slice_fusion.20.ua_ref), channel_id=1, source_target_pairs={{0,4},{4,0},{8,12},{12,8},{16,20},{20,16},{24,28},{28,24},{1,5},{5... | collective-permute-start | bytes 12582920 | tf_op jit(solution)/shard_map/ppermute | solution.py:42
  300.2 34.1 %collective-permute-start.50 = (bf16[128,2048]{1,0:T(8,128)(2,1)S(1)}, bf16[128,2048]{1,0:T(8,128)(2,1)S(1)}, u32[]{:S(2)}, u32[]{:S(2)}) collective-permute-start(bf16[128,2048]{1,0:T(8,128)(2,1)S(1)} %slice.578), channel_id=1, source_target_pairs={{0,16},{4,20},{8,24},{12,28},{16,0},{20,4},{24,8},{28,12},{1,17},{... | collective-permute-start | bytes 1572872 | tf_op jit(solution)/shard_map/ppermute | solution.py:42
  404.7 39.5 %collective-permute-start.62 = (bf16[1024,2048]{1,0:T(8,128)(2,1)}, bf16[1024,2048]{1,0:T(8,128)(2,1)}, u32[]{:S(2)}, u32[]{:S(2)}) collective-permute-start(bf16[1024,2048]{1,0:T(8,128)(2,1)} %constant_dynamic-update-slice_fusion.51.xa_ref), channel_id=1, source_target_pairs={{0,4},{4,0},{8,12},{12,8},{16,20},{20,16},{24,28},{28,24},{1,5},{5... | collective-permute-start | bytes 12582920 | tf_op jit(solution)/shard_map/ppermute | solution.py:42
  526.3 40.6 %collective-permute-start.66 = (bf16[1024,2048]{1,0:T(8,128)(2,1)}, bf16[1024,2048]{1,0:T(8,128)(2,1)}, u32[]{:S(2)}, u32[]{:S(2)}) collective-permute-start(bf16[1024,2048]{1,0:T(8,128)(2,1)} %get-tuple-element.555), channel_id=1, source_target_pairs={{0,4},{4,0},{8,12},{12,8},{16,20},{20,16},{24,28},{28,24},{1,5},{5... | collective-permute-start | bytes 12582920 | tf_op jit(solution)/shard_map/ppermute | solution.py:42
  529.2 37.7 %collective-permute-start.64 = (bf16[128,2048]{1,0:T(8,128)(2,1)}, bf16[128,2048]{1,0:T(8,128)(2,1)}, u32[]{:S(2)}, u32[]{:S(2)}) collective-permute-start(bf16[128,2048]{1,0:T(8,128)(2,1)} %get-tuple-element.552), channel_id=1, source_target_pairs={{0,16},{4,20},{8,24},{12,28},{16,0},{20,4},{24,8},{28,12},{1,17},{... | collective-permute-start | bytes 1572872 | tf_op jit(solution)/shard_map/ppermute | solution.py:42
  530.2 36.8 %collective-permute-start.65 = (bf16[128,2048]{1,0:T(8,128)(2,1)S(1)}, bf16[128,2048]{1,0:T(8,128)(2,1)}, u32[]{:S(2)}, u32[]{:S(2)}) collective-permute-start(bf16[128,2048]{1,0:T(8,128)(2,1)S(1)} %get-tuple-element.553), channel_id=1, source_target_pairs={{0,8},{4,12},{8,0},{12,4},{16,24},{20,28},{24,16},{28,20},{1,9},{5... | collective-permute-start | bytes 1572872 | tf_op jit(solution)/shard_map/ppermute | solution.py:42
  567.0 35.0 %collective-permute-start.69 = (bf16[1024,2048]{1,0:T(8,128)(2,1)}, bf16[1024,2048]{1,0:T(8,128)(2,1)}, u32[]{:S(2)}, u32[]{:S(2)}) collective-permute-start(bf16[1024,2048]{1,0:T(8,128)(2,1)} %get-tuple-element.562), channel_id=1, source_target_pairs={{0,4},{4,0},{8,12},{12,8},{16,20},{20,16},{24,28},{28,24},{1,5},{5... | collective-permute-start | bytes 12582920 | tf_op jit(solution)/shard_map/ppermute | solution.py:42
  602.0 34.9 %collective-permute-start.74 = (bf16[1024,2048]{1,0:T(8,128)(2,1)}, bf16[1024,2048]{1,0:T(8,128)(2,1)}, u32[]{:S(2)}, u32[]{:S(2)}) collective-permute-start(bf16[1024,2048]{1,0:T(8,128)(2,1)} %get-tuple-element.583), channel_id=1, source_target_pairs={{0,4},{4,0},{8,12},{12,8},{16,20},{20,16},{24,28},{28,24},{1,5},{5... | collective-permute-start | bytes 12582920 | tf_op jit(solution)/shard_map/ppermute | solution.py:42
  644.3 38.8 %collective-permute-start.75 = (bf16[256,2048]{1,0:T(8,128)(2,1)}, bf16[256,2048]{1,0:T(8,128)(2,1)}, u32[]{:S(2)}, u32[]{:S(2)}) collective-permute-start(bf16[256,2048]{1,0:T(8,128)(2,1)} %pad_maximum_fusion.11), channel_id=1, source_target_pairs={{0,8},{4,12},{8,0},{12,4},{16,24},{20,28},{24,16},{28,20},{1,9},{5... | collective-permute-start | bytes 3145736 | tf_op jit(solution)/shard_map/ppermute | solution.py:42
  645.6 37.5 %collective-permute-start.76 = (bf16[256,2048]{1,0:T(8,128)(2,1)}, bf16[256,2048]{1,0:T(8,128)(2,1)}, u32[]{:S(2)}, u32[]{:S(2)}) collective-permute-start(bf16[256,2048]{1,0:T(8,128)(2,1)} %pad_maximum_fusion.12), channel_id=1, source_target_pairs={{0,16},{4,20},{8,24},{12,28},{16,0},{20,4},{24,8},{28,12},{1,17},{... | collective-permute-start | bytes 3145736 | tf_op jit(solution)/shard_map/ppermute | solution.py:42
  647.0 36.1 %collective-permute-start.78 = (bf16[2,128,1024]{2,1,0:T(8,128)(2,1)}, bf16[2,128,1024]{2,1,0:T(8,128)(2,1)}, u32[]{:S(2)}, u32[]{:S(2)}) collective-permute-start(bf16[2,128,1024]{2,1,0:T(8,128)(2,1)} %get-tuple-element.592), channel_id=1, source_target_pairs={{0,1},{1,0},{2,3},{3,2},{4,5},{5,4},{6,7},{7,6},{8,9},{9,8},{10,11... | collective-permute-start | bytes 1572872 | tf_op jit(solution)/shard_map/ppermute | solution.py:42
  647.1 36.0 %collective-permute-start.77 = (bf16[128,2048]{1,0:T(8,128)(2,1)}, bf16[128,2048]{1,0:T(8,128)(2,1)}, u32[]{:S(2)}, u32[]{:S(2)}) collective-permute-start(bf16[128,2048]{1,0:T(8,128)(2,1)} %get-tuple-element.591), channel_id=1, source_target_pairs={{0,2},{1,3},{2,0},{3,1},{4,6},{5,7},{6,4},{7,5},{8,10},{9,11},{10,... | collective-permute-start | bytes 1572872 | tf_op jit(solution)/shard_map/ppermute | solution.py:42
  650.2 32.9 %collective-permute-start.79 = (f32[8,512]{0,1:T(8,128)}, f32[8,512]{0,1:T(8,128)S(1)}, u32[]{:S(2)}, u32[]{:S(2)}) collective-permute-start(f32[8,512]{0,1:T(8,128)} %bitcast.362), channel_id=1, source_target_pairs={{0,2},{1,3},{2,0},{3,1},{4,6},{5,7},{6,4},{7,5},{8,10},{9,11},{10,... | collective-permute-start | bytes 49160 | tf_op jit(solution)/shard_map/ppermute | solution.py:42
  761.1 38.3 %collective-permute-start.90 = (bf16[2,128,2048]{2,1,0:T(8,128)(2,1)S(1)}, bf16[2,128,2048]{2,1,0:T(8,128)(2,1)S(1)}, u32[]{:S(2)}, u32[]{:S(2)}) collective-permute-start(bf16[2,128,2048]{2,1,0:T(8,128)(2,1)S(1)} %get-tuple-element.622), channel_id=1, source_target_pairs={{0,1},{1,0},{2,3},{3,2},{4,5},{5,4},{6,7},{7,6},{8,9},{9,8},{10,11... | collective-permute-start | bytes 3145736 | tf_op jit(solution)/shard_map/ppermute | solution.py:42
  763.8 35.6 %collective-permute-start.89 = (bf16[2,128,1024]{2,1,0:T(8,128)(2,1)}, bf16[2,128,1024]{2,1,0:T(8,128)(2,1)S(1)}, u32[]{:S(2)}, u32[]{:S(2)}) collective-permute-start(bf16[2,128,1024]{2,1,0:T(8,128)(2,1)} %get-tuple-element.621), channel_id=1, source_target_pairs={{0,2},{1,3},{2,0},{3,1},{4,6},{5,7},{6,4},{7,5},{8,10},{9,11},{10,... | collective-permute-start | bytes 1572872 | tf_op jit(solution)/shard_map/ppermute | solution.py:42
  805.0 33.0 %collective-permute-start.96 = (bf16[256,2048]{1,0:T(8,128)(2,1)S(1)}, bf16[256,2048]{1,0:T(8,128)(2,1)S(1)}, u32[]{:S(2)}, u32[]{:S(2)}) collective-permute-start(bf16[256,2048]{1,0:T(8,128)(2,1)S(1)} %pad_maximum_fusion.14), channel_id=1, source_target_pairs={{0,8},{4,12},{8,0},{12,4},{16,24},{20,28},{24,16},{28,20},{1,9},{5... | collective-permute-start | bytes 3145736 | tf_op jit(solution)/shard_map/ppermute | solution.py:42
  805.8 33.2 %collective-permute-start.97 = (bf16[256,2048]{1,0:T(8,128)(2,1)S(1)}, bf16[256,2048]{1,0:T(8,128)(2,1)}, u32[]{:S(2)}, u32[]{:S(2)}) collective-permute-start(bf16[256,2048]{1,0:T(8,128)(2,1)S(1)} %pad_maximum_fusion.15), channel_id=1, source_target_pairs={{0,16},{4,20},{8,24},{12,28},{16,0},{20,4},{24,8},{28,12},{1,17},{... | collective-permute-start | bytes 3145736 | tf_op jit(solution)/shard_map/ppermute | solution.py:42
  847.8 49.7 %collective-permute-start.100 = (bf16[1024,2048]{1,0:T(8,128)(2,1)}, bf16[1024,2048]{1,0:T(8,128)(2,1)}, u32[]{:S(2)}, u32[]{:S(2)}) collective-permute-start(bf16[1024,2048]{1,0:T(8,128)(2,1)} %convolution_convert_fusion.2), channel_id=1, source_target_pairs={{0,4},{4,0},{8,12},{12,8},{16,20},{20,16},{24,28},{28,24},{1,5},{5... | collective-permute-start | bytes 12582920 | tf_op jit(solution)/shard_map/ppermute | solution.py:42
  849.2 48.2 %collective-permute-start.103 = (bf16[2,128,2048]{2,1,0:T(8,128)(2,1)}, bf16[2,128,2048]{2,1,0:T(8,128)(2,1)S(1)}, u32[]{:S(2)}, u32[]{:S(2)}) collective-permute-start(bf16[2,128,2048]{2,1,0:T(8,128)(2,1)} %get-tuple-element.642), channel_id=1, source_target_pairs={{0,1},{1,0},{2,3},{3,2},{4,5},{5,4},{6,7},{7,6},{8,9},{9,8},{10,11... | collective-permute-start | bytes 3145736 | tf_op jit(solution)/shard_map/ppermute | solution.py:42
  855.5 41.9 %collective-permute-start.101 = (bf16[2,8,64,256]{3,2,1,0:T(8,128)(2,1)S(1)}, bf16[2,8,64,256]{3,2,1,0:T(8,128)(2,1)S(1)}, u32[]{:S(2)}, u32[]{:S(2)}) collective-permute-start(bf16[2,8,64,256]{3,2,1,0:T(8,128)(2,1)S(1)} %slice.645), channel_id=1, source_target_pairs={{0,1},{1,0},{2,3},{3,2},{4,5},{5,4},{6,7},{7,6},{8,9},{9,8},{10,11... | collective-permute-start | bytes 1572872 | tf_op jit(solution)/shard_map/ppermute | solution.py:42
  938.6 37.3 %collective-permute-start.109 = (bf16[256,2048]{1,0:T(8,128)(2,1)}, bf16[256,2048]{1,0:T(8,128)(2,1)S(1)}, u32[]{:S(2)}, u32[]{:S(2)}) collective-permute-start(bf16[256,2048]{1,0:T(8,128)(2,1)} %pad_maximum_fusion.17), channel_id=1, source_target_pairs={{0,8},{4,12},{8,0},{12,4},{16,24},{20,28},{24,16},{28,20},{1,9},{5... | collective-permute-start | bytes 3145736 | tf_op jit(solution)/shard_map/ppermute | solution.py:42
  939.6 36.4 %collective-permute-start.110 = (bf16[256,2048]{1,0:T(8,128)(2,1)}, bf16[256,2048]{1,0:T(8,128)(2,1)}, u32[]{:S(2)}, u32[]{:S(2)}) collective-permute-start(bf16[256,2048]{1,0:T(8,128)(2,1)} %pad_maximum_fusion.18), channel_id=1, source_target_pairs={{0,16},{4,20},{8,24},{12,28},{16,0},{20,4},{24,8},{28,12},{1,17},{... | collective-permute-start | bytes 3145736 | tf_op jit(solution)/shard_map/ppermute | solution.py:42
  941.7 35.4 %collective-permute-start.111 = (bf16[2,8,64,512]{3,2,1,0:T(8,128)(2,1)}, bf16[2,8,64,512]{3,2,1,0:T(8,128)(2,1)}, u32[]{:S(2)}, u32[]{:S(2)}) collective-permute-start(bf16[2,8,64,512]{3,2,1,0:T(8,128)(2,1)} %slice.684), channel_id=1, source_target_pairs={{0,1},{1,0},{2,3},{3,2},{4,5},{5,4},{6,7},{7,6},{8,9},{9,8},{10,11... | collective-permute-start | bytes 3145736 | tf_op jit(solution)/shard_map/ppermute | solution.py:42
  982.6 32.8 %collective-permute-start.117 = (bf16[2,256,1024]{2,1,0:T(8,128)(2,1)S(1)}, bf16[2,256,1024]{2,1,0:T(8,128)(2,1)}, u32[]{:S(2)}, u32[]{:S(2)}) collective-permute-start(bf16[2,256,1024]{2,1,0:T(8,128)(2,1)S(1)} %get-tuple-element.677), channel_id=1, source_target_pairs={{0,1},{1,0},{2,3},{3,2},{4,5},{5,4},{6,7},{7,6},{8,9},{9,8},{10,11... | collective-permute-start | bytes 3145736 | tf_op jit(solution)/shard_map/ppermute | solution.py:42
  (243 other events, 3485.5 us)

commit v10 on v8

--- a/solution.py
+++ b/solution.py
@@ -886,7 +886,6 @@
     own_quarters = {n: held_part(half_at, n * quarter, quarter) for n in (2, 3)}
     far_quarters = [held_part(1 - half_at, n * quarter, quarter) for n in range(4)]
     down_rows = quarters(held[2], 1)
-    down_rows = [down_rows[0], jnp.concatenate(down_rows[1:3], 1), down_rows[3]]
     upstream_halves = [held[3][:half_rows], held[3][half_rows:]]
     small = in_order(small, S, F, s, f).reshape(S, F, -1)
     prepared = (own_quarters, far_quarters, down_rows, upstream_halves, small)
@@ -955,11 +954,8 @@
     out_more = gather_more(own_output, out_first, S)
     far.append(far_part(1, query_low))
     near_own.append(near_swap(own_quarters[3], query_low))
-    down = [near_swap(down_rows[0], query_low)]
     attended, lse = attention_forward(query_low, key_low, value_low, seg_row, seg_col)
-    attended, out_more, far[1], down[0], near_own[2] = tie(
-        attended, out_more, far[1], down[0], near_own[2]
-    )
+    attended, out_more, far[1], near_own[2] = tie(attended, out_more, far[1], near_own[2])
     attended_blocks = attended.reshape(S, T, C)
     come = lax.all_to_all(attended_blocks, "seq", split_axis=0, concat_axis=0, tiled=True)
     out_even, out_odd = gather_end(own_output, out_first, out_more, S)
@@ -968,16 +964,16 @@
     own_up_more = gather_more(after(upstream_low, attended), own_up_first, S)
     come, far[2], near_far[0], own_up_more = tie(come, far[2], near_far[0], own_up_more)
     own_u = gather_end(upstream_low, own_up_first, own_up_more, S)
-    far.append(far_part(3, come))
     near_far.append(near_swap(far[1], come))
+    down = [near_swap(down_rows[0], come)]
     partner_up_first = gather_first(after(partner_up, come), S)
     come = relative(come, s).transpose(1, 0, 2).reshape(T, D)
     residual = inputs + matmul(come[:, : D // 2], out_even) + matmul(come[:, D // 2 :], out_odd)
     moe_factor = rms_factor(residual)
     residual_n = residual * moe_factor
     second_low = (residual_n * gain_moe).astype(BF16)
-    second_low, far[3], near_far[1], partner_up_first, own_u = tie(
-        second_low, far[3], near_far[1], partner_up_first, own_u
+    second_low, down[0], near_far[1], partner_up_first, own_u = tie(
+        second_low, down[0], near_far[1], partner_up_first, own_u
     )
 
     own_first = gather_first(second_low, S)
@@ -989,20 +985,22 @@
     )
     own_more = gather_more(second_low, own_first, S)
     partner_low.append(far_swap(second_low[half_rows:], own_first))
-    near_far.append(near_swap(far[3], own_first))
+    down.append(near_swap(down_rows[1], own_first))
     partner_up_more = gather_more(after(partner_up, own_first), partner_up_first, S)
-    own_more, partner_low[1], near_far[3], partner_up_more = tie(
-        own_more, partner_low[1], near_far[3], partner_up_more
+    own_more, partner_low[1], down[1], partner_up_more = tie(
+        own_more, partner_low[1], down[1], partner_up_more
     )
     partner_low = jnp.concatenate(partner_low, 0)
     own_x = gather_end(second_low, own_first, own_more, S)
     partner_first = gather_first(after(partner_low, own_more), S)
-    down.append(near_swap(down_rows[1], own_more))
-    partner_first, down[1], own_x = tie(partner_first, down[1], own_x)
+    down.append(near_swap(down_rows[2], own_more))
+    far.append(far_part(3, own_more))
+    partner_first, down[2], own_x, far[3] = tie(partner_first, down[2], own_x, far[3])
     other_u = gather_end(after(partner_up, partner_first), partner_up_first, partner_up_more, S)
     partner_more = gather_more(partner_low, partner_first, S)
-    down.append(near_swap(down_rows[2], partner_first))
-    partner_more, down[2], other_u = tie(partner_more, down[2], other_u)
+    down.append(near_swap(down_rows[3], partner_first))
+    near_far.append(near_swap(far[3], partner_first))
+    partner_more, down[3], other_u, near_far[3] = tie(partner_more, down[3], other_u, near_far[3])
     other_x = gather_end(partner_low, partner_first, partner_more, S)
     in_pieces = []
     for r in range(F):
@@ -1010,7 +1008,7 @@
             first = (0, 2, 3)[n] if r < half_f else n
             in_pieces.append((r, first * quarter, rows[r % half_f]))
     down_pieces = [
-        (r, (0, 1, 3)[n] * (down_part // 4), down[n][r]) for r in range(half_f) for n in range(3)
+        (r, n * (down_part // 4), down[n][r]) for r in range(half_f) for n in range(4)
     ]
     wide_router = jnp.pad(full_router, ((0, 0), (0, 128 - E)))
     expert_places = jnp.stack([s * experts, f]).astype(jnp.int32)
@@ -1069,9 +1067,11 @@
     come = sum_first(other_sums, S)
     far_got = [send_in(0, other_got)]
     other_out_got = swap(after(other_parts[1], other_got), "seq", S, 1)
-    come, far_got[0], other_out_got = tie(come, far_got[0], other_out_got)
     gate_grads = gate_grads.reshape(S, 2, T * experts)
-    partner_grads = far_swap(gate_grads[:, 1], come)
+    partner_grads = far_swap(gate_grads[:, 1])
+    come, far_got[0], other_out_got, partner_grads = tie(
+        come, far_got[0], other_out_got, partner_grads
+    )
     singles, other_total = sum_more(other_sums, come, S)
     come = sum_last(singles, S)
     middle_sent = {r: jnp.concatenate(sent[r][1:3], 1) for r in sent}
@@ -1086,9 +1086,7 @@
 
     for r in range(1, half_f, 2):
         down_products(r, singles)
-    come, middle_got, partner_grads, down_terms = tie(
-        come, middle_got, partner_grads, down_terms
-    )
+    come, middle_got, down_terms = tie(come, middle_got, down_terms)
     for n in range(2):
         far_got.append({r: got[:, n * quarter : (n + 1) * quarter] for r, got in middle_got.items()})
     other_rows = add_all(other_total, come).astype(BF16)
@@ -1269,11 +1267,13 @@
     head_terms = gain_terms[0, count:]
     gain_terms = halve(gain_terms[0, :count].reshape(S, -1), "seq", S, S // 2)[0]
     own_outs = add_all(own_total, own_come)
+    qkv_term = jnp.concatenate([turned_sum, value_sum], -1).astype(BF16)
+    qkv_term = lax.all_to_all(qkv_term, "seq", split_axis=0, concat_axis=0, tiled=True)
+    qkv_term, outs_back[1], near_got[1], gain_terms = tie(
+        qkv_term, outs_back[1], near_got[1], gain_terms
+    )
     outs_back = jnp.concatenate(outs_back, 0).astype(F32)
     mixed = (residual + own_outs + outs_back).astype(BF16)[None]
-
-    qkv_term = jnp.concatenate([turned_sum, value_sum], -1).astype(BF16)
-    qkv_term = lax.all_to_all(qkv_term, "seq", split_axis=0, concat_axis=0, tiled=True)
     qkv_term = [
         qkv_term[:, :, j * C : (j + 1) * C].transpose(1, 0, 2).reshape(part, D).astype(F32)
         for j in range(3)

time: 1060 us -> 1040 us (0.981)
  waiting for transfers between devices: 350 us -> 319 us
    ppermute x124 -> x125, waiting for transfers between devices: 350 us -> 318 us  [swap(): return lax.ppermute(values, axis, [(i, i ^ mask) for i in range(size)])]
    ppermute x124 -> x125, starting transfers between devices: 131 us -> 135 us  [swap(): return lax.ppermute(values, axis, [(i, i ^ mask) for i in range(size)])]
    unnamed x342 -> x346, local copies, waits for them, and re-layouts: 57.9 us -> 59.4 us
  transfers between devices with their start and end apart: 128 -> 129, of which waited for: 58 -> 60; matrix products, arithmetic and copies ran while one was open for 20% -> 19% of each run, Pallas kernels for 24% -> 24%
where the time goes in v10:
time: 1040 us; the launch traced here: 1020 us
  waiting for transfers between devices  319 us (31%)
  Pallas kernels  254 us (24%)
  starting transfers between devices  150 us (14%)
  local copies, waits for them, and re-layouts  141 us (14%)
  other arithmetic  111 us (11%)
  matrix products  45.6 us (4%)
    ppermute x125, waiting for transfers between devices, swap(): return lax.ppermute(values, axis, [(i, i ^ mask) for i in range(size)])  318 us
    ppermute x125, starting transfers between devices, swap(): return lax.ppermute(values, axis, [(i, i ^ mask) for i in range(size)])  135 us
    pallas_call x2, Pallas kernels, run_experts(): pl.pallas_call(partial(expert_kernel, in_places, down_places), grid=(step...  118 us
    pallas_call x6, Pallas kernels, products(): pl.pallas_call(product_kernel, grid_spec=pltpu.PrefetchScalarGridSpec(num...  59.9 us
    unnamed x346, local copies, waits for them, and re-layouts  59.4 us
    pallas_call x1, Pallas kernels, attention_backward(): pl.pallas_call(partial(backward_kernel, span), grid=(heads, length // row...  28.3 us
    pallas_call x1, Pallas kernels, attention_forward(): pl.pallas_call(partial(forward_kernel, span), grid=(heads, length // rows...  21.6 us
  transfers between devices with their start and end apart: 129, of which 60 were waited for; matrix products, arithmetic and copies ran while one was open for 19% of the time, Pallas kernels for 24%

profile of v10, /device:TPU:0, one launch (start us, length us, event | category | flops | bytes accessed | tf_op | source)
XLA Modules:
  0.0 1024.9 jit_solution(3167523592888567073)
XLA Ops:
  30.4 8.6 collective-permute-done.4
  71.2 12.7 %collective-permute-done.7 = bf16[8,64,768]{2,1,0:T(8,128)(2,1)} collective-permute-done((bf16[8,64,768]{2,1,0:T(8,128)(2,1)S(1)}, bf16[8,64,768]{2,1,0:T(8,128)(2,1)}, u32[]{:S(2)}, u32[]{:S(2)}) %collective-permute-start.7) | collective-permute-done | bytes 786464 | tf_op jit(solution)/shard_map/ppermute | solution.py:42
  100.0 14.3 %collective-permute-done.12 = bf16[128,2048]{1,0:T(8,128)(2,1)} collective-permute-done((bf16[128,2048]{1,0:T(8,128)(2,1)S(1)}, bf16[128,2048]{1,0:T(8,128)(2,1)}, u32[]{:S(2)}, u32[]{:S(2)}) %collective-permute-start.12) | collective-permute-done | bytes 524320 | tf_op jit(solution)/shard_map/ppermute | solution.py:42
  128.5 12.6 %project.1 = (bf16[1024,2048]{1,0:T(8,128)(2,1)}, bf16[1024,2048]{1,0:T(8,128)(2,1)}, f32[2048,256]{1,0:T(8,128)S(1)}, f32[2048,256]{1,0:T(8,128)S(1)}, bf16[204...) custom-call(s32[1]{0:T(128)} %bitcast.1.me_ref, bf16[1024,2048]{1,0:T(8,128)(2,1)} %constant_dynamic-update-slice_fusion.even_ref, ...), custom_call_target="tpu_custom_call" | custom-call | flops 6442450944 | bytes 25165824 | tf_op jit(solution)/shard_map/project/pallas_call | solution.py:437
  171.7 10.7 %collective-permute-done.22 = f32[2,2048]{1,0:T(2,128)S(1)} collective-permute-done((f32[2,2048]{1,0:T(2,128)S(1)}, f32[2,2048]{1,0:T(2,128)S(1)}, u32[]{:S(2)}, u32[]{:S(2)}) %collective-permute-start.22) | collective-permute-done | bytes 16416 | tf_op jit(solution)/shard_map/ppermute | solution.py:42
  204.9 21.6 %attend.1 = (bf16[2048,256]{1,0:T(8,128)(2,1)S(1)}, f32[2,1,2048]{2,1,0:T(1,128)S(1)}) custom-call(bf16[2048,256]{1,0:T(8,128)(2,1)S(1)} %get-tuple-element.372.q_ref, bf16[2048,256]{1,0:T(8,128)(2,1)S(1)} %get-tuple-element.373.k_ref, bf16[2048,256]{1,0:T(8,128)(2,1)S(1)} %copy-done.20, s32[1,2048]{1,0:T(1,128)S(1)} %copy-done.14, s32[2048,1]{1,0:T(8,128)S(1)} %copy-done.9), custom_call_target="tpu_custom_call" | custom-call | flops 2684354560 | bytes 4194304 | tf_op jit(solution)/shard_map/attend/pallas_call | solution.py:336
  285.0 8.4 collective-permute-done.37.refs_18_
  301.9 17.8 %collective-permute-done.45.refs_12_ = bf16[2,128,1024]{2,1,0:T(8,128)(2,1)S(1)} collective-permute-done((bf16[2,128,1024]{2,1,0:T(8,128)(2,1)}, bf16[2,128,1024]{2,1,0:T(8,128)(2,1)S(1)}, u32[]{:S(2)}, u32[]{:S(2)}) %collective-permute-start.45) | collective-permute-done | bytes 524320 | tf_op jit(solution)/shard_map/ppermute | solution.py:42
  325.5 6.4 collective-permute-done.50
  334.1 8.8 collective-permute-done.49.refs_19_
  349.2 22.8 %collective-permute-done.56.refs_9_ = bf16[2,128,1024]{2,1,0:T(8,128)(2,1)S(1)} collective-permute-done((bf16[2,128,1024]{2,1,0:T(8,128)(2,1)S(1)}, bf16[2,128,1024]{2,1,0:T(8,128)(2,1)S(1)}, u32[]{:S(2)}, u32[]{:S(2)}) %collective-permute-start.56) | collective-permute-done | bytes 524320 | tf_op jit(solution)/shard_map/ppermute | solution.py:42
  383.5 7.0 collective-permute-done.61.refs_13_
  390.6 11.1 %collective-permute-done.59.refs_21_ = bf16[2,64,2048]{2,1,0:T(8,128)(2,1)S(1)} collective-permute-done((bf16[2,64,2048]{2,1,0:T(8,128)(2,1)S(1)}, bf16[2,64,2048]{2,1,0:T(8,128)(2,1)S(1)}, u32[]{:S(2)}, u32[]{:S(2)}) %collective-permute-start.59) | collective-permute-done | bytes 524320 | tf_op jit(solution)/shard_map/ppermute | solution.py:42
  409.3 59.1 %experts.2 = (bf16[1024,2048]{1,0:T(8,128)(2,1)}, bf16[1024,2048]{1,0:T(8,128)(2,1)}, bf16[1024,2048]{1,0:T(8,128)(2,1)}, bf16[1024,2048]{1,0:T(8,128)(2,1)}, f3...) custom-call(s32[2]{0:T(128)} %pad_add_fusion.first_ref, ...), custom_call_target="tpu_custom_call" | custom-call | flops 38654705664 | bytes 62914560 | tf_op jit(solution)/shard_map/experts/pallas_call | solution.py:732
  469.1 59.1 %experts.3 = (bf16[1024,2048]{1,0:T(8,128)(2,1)}, bf16[1024,2048]{1,0:T(8,128)(2,1)}, bf16[1024,2048]{1,0:T(8,128)(2,1)}, bf16[1024,2048]{1,0:T(8,128)(2,1)}, f3...) custom-call(s32[2]{0:T(128)} %pad_add_fusion.first_ref, ...), custom_call_target="tpu_custom_call", output_to_operand_aliasing={{6}: (30, {}), {7}: (31, {}), {8}: (32, {}), {9}: (33, {})} | custom-call | flops 38654705664 | bytes 62914560 | tf_op jit(solution)/shard_map/experts/pallas_call | solution.py:732
  537.3 9.4 in_products.4
  560.4 9.8 collective-permute-done.70
  571.0 6.0 add_convert_fusion.29
  585.5 11.0 %down_products.2 = bf16[2,256,2048]{2,1,0:T(8,128)(2,1)} custom-call(s32[1]{0:T(128)} %bitcast.25.me_ref, bf16[2,2304,512]{2,1,0:T(8,128)(2,1)} %get-tuple-element.546.left_ref, bf16[2,2304,2048]{2,1,0:T(8,128)(2,1)} %get-tuple-element.521.right_ref), custom_call_target="tpu_custom_call" | custom-call | flops 4831838208 | bytes 21233664 | tf_op jit(solution)/shard_map/down_products/pallas_call | solution.py:769
  616.1 9.3 in_products.5
  627.7 10.2 collective-permute-done.76
  650.9 9.7 in_products.6
  660.6 8.4 collective-permute-done.81
  685.8 11.0 %down_products.3 = bf16[2,256,2048]{2,1,0:T(8,128)(2,1)} custom-call(s32[1]{0:T(128)} %bitcast.25.me_ref, bf16[2,2304,512]{2,1,0:T(8,128)(2,1)} %get-tuple-element.546.left_ref, bf16[2,2304,2048]{2,1,0:T(8,128)(2,1)} %get-tuple-element.521.right_ref), custom_call_target="tpu_custom_call" | custom-call | flops 4831838208 | bytes 21233664 | tf_op jit(solution)/shard_map/down_products/pallas_call | solution.py:769
  698.4 8.0 collective-permute-done.84
  729.1 14.3 %collective-permute-done.90 = bf16[2,64,2048]{2,1,0:T(8,128)(2,1)S(1)} collective-permute-done((bf16[2,64,2048]{2,1,0:T(8,128)(2,1)S(1)}, bf16[2,64,2048]{2,1,0:T(8,128)(2,1)S(1)}, u32[]{:S(2)}, u32[]{:S(2)}) %collective-permute-start.90) | collective-permute-done | bytes 524320 | tf_op jit(solution)/shard_map/ppermute | solution.py:42
  752.9 28.3 %attend_back.1 = (bf16[2048,256]{1,0:T(8,128)(2,1)S(1)}, bf16[2048,256]{1,0:T(8,128)(2,1)S(1)}, bf16[2048,256]{1,0:T(8,128)(2,1)S(1)}) custom-call(bf16[2048,256]{1,0:T(8,128)(2,1)S(1)} %copy-done.16, bf16[2048,256]{1,0:T(8,128)(2,1)S(1)} %copy-done.18, bf16[2048,256]{1,0:T(8,128)(2,1)} %copy-done.19, bf16[2048,256]{1,0:T(8,128)(2,1)} %bitcast.365, ...), custom_call_target="tpu_custom_call" | custom-call | flops 6710886400 | bytes 7340032 | tf_op jit(solution)/shard_map/attend_back/pallas_call | solution.py:368
  842.8 15.9 %collective-permute-done.104 = bf16[128,2048]{1,0:T(8,128)(2,1)S(1)} collective-permute-done((bf16[128,2048]{1,0:T(8,128)(2,1)S(1)}, bf16[128,2048]{1,0:T(8,128)(2,1)S(1)}, u32[]{:S(2)}, u32[]{:S(2)}) %collective-permute-start.104) | collective-permute-done | bytes 524320 | tf_op jit(solution)/shard_map/ppermute | solution.py:42
  909.5 9.5 in_products.7
  918.9 7.7 collective-permute-done.113
  948.0 16.0 %collective-permute-done.114 = bf16[1,8,64,512]{3,2,1,0:T(8,128)(2,1)S(1)} collective-permute-done((bf16[1,8,64,512]{3,2,1,0:T(8,128)(2,1)S(1)}, bf16[1,8,64,512]{3,2,1,0:T(8,128)(2,1)S(1)}, u32[]{:S(2)}, u32[]{:S(2)}) %collective-permute-start.114) | collective-permute-done | bytes 524320 | tf_op jit(solution)/shard_map/ppermute | solution.py:42
  989.6 10.2 collective-permute-done.119
  (818 shorter events, 545.7 us)
Async XLA Ops:
  20.1 29.5 %collective-permute-start.2 = (bf16[2,256,1024]{2,1,0:T(8,128)(2,1)S(1)}, bf16[2,256,1024]{2,1,0:T(8,128)(2,1)}, u32[]{:S(2)}, u32[]{:S(2)}) collective-permute-start(bf16[2,256,1024]{2,1,0:T(8,128)(2,1)S(1)} %pad_maximum_fusion.5.refs_0_), channel_id=1, source_target_pairs={{0,1},{1,0},{2,3},{3,2},{4,5},{5,4},{6,7},{7,6},{8,9},{9,8},{10,11... | collective-permute-start | bytes 3145736 | tf_op jit(solution)/shard_map/ppermute | solution.py:42
  49.6 39.5 %collective-permute-start.10 = (bf16[256,2048]{1,0:T(8,128)(2,1)S(1)}, bf16[256,2048]{1,0:T(8,128)(2,1)S(1)}, u32[]{:S(2)}, u32[]{:S(2)}) collective-permute-start(bf16[256,2048]{1,0:T(8,128)(2,1)S(1)} %bitcast.329), channel_id=1, source_target_pairs={{0,16},{4,20},{8,24},{12,28},{16,0},{20,4},{24,8},{28,12},{1,17},{... | collective-permute-start | bytes 3145736 | tf_op jit(solution)/shard_map/ppermute | solution.py:42
  51.1 38.0 %collective-permute-start.9 = (bf16[256,2048]{1,0:T(8,128)(2,1)S(1)}, bf16[256,2048]{1,0:T(8,128)(2,1)}, u32[]{:S(2)}, u32[]{:S(2)}) collective-permute-start(bf16[256,2048]{1,0:T(8,128)(2,1)S(1)} %bitcast.330), channel_id=1, source_target_pairs={{0,8},{4,12},{8,0},{12,4},{16,24},{20,28},{24,16},{28,20},{1,9},{5... | collective-permute-start | bytes 3145736 | tf_op jit(solution)/shard_map/ppermute | solution.py:42
  52.6 31.3 %collective-permute-start.7 = (bf16[8,64,768]{2,1,0:T(8,128)(2,1)S(1)}, bf16[8,64,768]{2,1,0:T(8,128)(2,1)}, u32[]{:S(2)}, u32[]{:S(2)}) collective-permute-start(bf16[8,64,768]{2,1,0:T(8,128)(2,1)S(1)} %all-to-all-done), channel_id=1, source_target_pairs={{0,1},{1,0},{2,3},{3,2},{4,5},{5,4},{6,7},{7,6},{8,9},{9,8},{10,11... | collective-permute-start | bytes 2359304 | tf_op jit(solution)/shard_map/ppermute | solution.py:42
  55.0 34.1 %collective-permute-start.8 = (bf16[8,64,768]{2,1,0:T(8,128)(2,1)S(1)}, bf16[8,64,768]{2,1,0:T(8,128)(2,1)}, u32[]{:S(2)}, u32[]{:S(2)}) collective-permute-start(bf16[8,64,768]{2,1,0:T(8,128)(2,1)S(1)} %all-to-all-done), channel_id=1, source_target_pairs={{0,2},{1,3},{2,0},{3,1},{4,6},{5,7},{6,4},{7,5},{8,10},{9,11},{10,... | collective-permute-start | bytes 2359304 | tf_op jit(solution)/shard_map/ppermute | solution.py:42
  122.8 28.4 %collective-permute-start.19 = (bf16[256,2048]{1,0:T(8,128)(2,1)}, bf16[256,2048]{1,0:T(8,128)(2,1)}, u32[]{:S(2)}, u32[]{:S(2)}) collective-permute-start(bf16[256,2048]{1,0:T(8,128)(2,1)} %bitcast.4), channel_id=1, source_target_pairs={{0,8},{4,12},{8,0},{12,4},{16,24},{20,28},{24,16},{28,20},{1,9},{5... | collective-permute-start | bytes 3145736 | tf_op jit(solution)/shard_map/ppermute | solution.py:42
  157.2 35.3 %collective-permute-start.24 = (bf16[256,2048]{1,0:T(8,128)(2,1)}, bf16[256,2048]{1,0:T(8,128)(2,1)}, u32[]{:S(2)}, u32[]{:S(2)}) collective-permute-start(bf16[256,2048]{1,0:T(8,128)(2,1)} %bitcast.18), channel_id=1, source_target_pairs={{0,8},{4,12},{8,0},{12,4},{16,24},{20,28},{24,16},{28,20},{1,9},{5... | collective-permute-start | bytes 3145736 | tf_op jit(solution)/shard_map/ppermute | solution.py:42
  158.2 34.3 %collective-permute-start.25 = (bf16[256,2048]{1,0:T(8,128)(2,1)}, bf16[256,2048]{1,0:T(8,128)(2,1)}, u32[]{:S(2)}, u32[]{:S(2)}) collective-permute-start(bf16[256,2048]{1,0:T(8,128)(2,1)} %bitcast.18), channel_id=1, source_target_pairs={{0,16},{4,20},{8,24},{12,28},{16,0},{20,4},{24,8},{28,12},{1,17},{... | collective-permute-start | bytes 3145736 | tf_op jit(solution)/shard_map/ppermute | solution.py:42
  163.5 28.9 %collective-permute-start.27 = (bf16[2,128,1024]{2,1,0:T(8,128)(2,1)}, bf16[2,128,1024]{2,1,0:T(8,128)(2,1)}, u32[]{:S(2)}, u32[]{:S(2)}) collective-permute-start(bf16[2,128,1024]{2,1,0:T(8,128)(2,1)} %pad_maximum_fusion.22.refs_1_), channel_id=1, source_target_pairs={{0,1},{1,0},{2,3},{3,2},{4,5},{5,4},{6,7},{7,6},{8,9},{9,8},{10,11... | collective-permute-start | bytes 1572872 | tf_op jit(solution)/shard_map/ppermute | solution.py:42
  163.6 28.9 %collective-permute-start.26 = (bf16[2,128,1024]{2,1,0:T(8,128)(2,1)}, bf16[2,128,1024]{2,1,0:T(8,128)(2,1)}, u32[]{:S(2)}, u32[]{:S(2)}) collective-permute-start(bf16[2,128,1024]{2,1,0:T(8,128)(2,1)} %pad_maximum_fusion.24), channel_id=1, source_target_pairs={{0,2},{1,3},{2,0},{3,1},{4,6},{5,7},{6,4},{7,5},{8,10},{9,11},{10,... | collective-permute-start | bytes 1572872 | tf_op jit(solution)/shard_map/ppermute | solution.py:42
  188.2 60.1 %collective-permute-start.34 = (bf16[128,2048]{1,0:T(8,128)(2,1)}, bf16[128,2048]{1,0:T(8,128)(2,1)}, u32[]{:S(2)}, u32[]{:S(2)}) collective-permute-start(bf16[128,2048]{1,0:T(8,128)(2,1)} %slice.577), channel_id=1, source_target_pairs={{0,16},{4,20},{8,24},{12,28},{16,0},{20,4},{24,8},{28,12},{1,17},{... | collective-permute-start | bytes 1572872 | tf_op jit(solution)/shard_map/ppermute | solution.py:42
  192.5 34.9 %collective-permute-start.31 = (bf16[2,128,1024]{2,1,0:T(8,128)(2,1)S(1)}, bf16[2,128,1024]{2,1,0:T(8,128)(2,1)S(1)}, u32[]{:S(2)}, u32[]{:S(2)}) collective-permute-start(bf16[2,128,1024]{2,1,0:T(8,128)(2,1)S(1)} %copy-done.94), channel_id=1, source_target_pairs={{0,1},{1,0},{2,3},{3,2},{4,5},{5,4},{6,7},{7,6},{8,9},{9,8},{10,11... | collective-permute-start | bytes 1572872 | tf_op jit(solution)/shard_map/ppermute | solution.py:42
  192.6 35.6 %collective-permute-start.30 = (bf16[2,128,1024]{2,1,0:T(8,128)(2,1)S(1)}, bf16[2,128,1024]{2,1,0:T(8,128)(2,1)S(1)}, u32[]{:S(2)}, u32[]{:S(2)}) collective-permute-start(bf16[2,128,1024]{2,1,0:T(8,128)(2,1)S(1)} %copy-done.97), channel_id=1, source_target_pairs={{0,2},{1,3},{2,0},{3,1},{4,6},{5,7},{6,4},{7,5},{8,10},{9,11},{10,... | collective-permute-start | bytes 1572872 | tf_op jit(solution)/shard_map/ppermute | solution.py:42
  196.8 31.4 %collective-permute-start.28 = (bf16[128,2048]{1,0:T(8,128)(2,1)S(1)}, bf16[128,2048]{1,0:T(8,128)(2,1)}, u32[]{:S(2)}, u32[]{:S(2)}) collective-permute-start(bf16[128,2048]{1,0:T(8,128)(2,1)S(1)} %slice.575), channel_id=1, source_target_pairs={{0,16},{4,20},{8,24},{12,28},{16,0},{20,4},{24,8},{28,12},{1,17},{... | collective-permute-start | bytes 1572872 | tf_op jit(solution)/shard_map/ppermute | solution.py:42
  198.8 29.4 %collective-permute-start.29 = (bf16[128,2048]{1,0:T(8,128)(2,1)S(1)}, bf16[128,2048]{1,0:T(8,128)(2,1)}, u32[]{:S(2)}, u32[]{:S(2)}) collective-permute-start(bf16[128,2048]{1,0:T(8,128)(2,1)S(1)} %slice.576), channel_id=1, source_target_pairs={{0,8},{4,12},{8,0},{12,4},{16,24},{20,28},{24,16},{28,20},{1,9},{5... | collective-permute-start | bytes 1572872 | tf_op jit(solution)/shard_map/ppermute | solution.py:42
  240.9 38.3 %collective-permute-start.36 = (bf16[1024,2048]{1,0:T(8,128)(2,1)}, bf16[1024,2048]{1,0:T(8,128)(2,1)}, u32[]{:S(2)}, u32[]{:S(2)}) collective-permute-start(bf16[1024,2048]{1,0:T(8,128)(2,1)} %constant_dynamic-update-slice_fusion.13), channel_id=1, source_target_pairs={{0,4},{4,0},{8,12},{12,8},{16,20},{20,16},{24,28},{28,24},{1,5},{5... | collective-permute-start | bytes 12582920 | tf_op jit(solution)/shard_map/ppermute | solution.py:42
  256.3 37.1 %collective-permute-start.41 = (bf16[1024,2048]{1,0:T(8,128)(2,1)}, bf16[1024,2048]{1,0:T(8,128)(2,1)}, u32[]{:S(2)}, u32[]{:S(2)}) collective-permute-start(bf16[1024,2048]{1,0:T(8,128)(2,1)} %constant_dynamic-update-slice_fusion.20.ua_ref), channel_id=1, source_target_pairs={{0,4},{4,0},{8,12},{12,8},{16,20},{20,16},{24,28},{28,24},{1,5},{5... | collective-permute-start | bytes 12582920 | tf_op jit(solution)/shard_map/ppermute | solution.py:42
  299.4 32.5 %collective-permute-start.50 = (bf16[128,2048]{1,0:T(8,128)(2,1)S(1)}, bf16[128,2048]{1,0:T(8,128)(2,1)S(1)}, u32[]{:S(2)}, u32[]{:S(2)}) collective-permute-start(bf16[128,2048]{1,0:T(8,128)(2,1)S(1)} %slice.591), channel_id=1, source_target_pairs={{0,16},{4,20},{8,24},{12,28},{16,0},{20,4},{24,8},{28,12},{1,17},{... | collective-permute-start | bytes 1572872 | tf_op jit(solution)/shard_map/ppermute | solution.py:42
  404.0 64.4 %collective-permute-start.62 = (bf16[1024,2048]{1,0:T(8,128)(2,1)}, bf16[1024,2048]{1,0:T(8,128)(2,1)}, u32[]{:S(2)}, u32[]{:S(2)}) collective-permute-start(bf16[1024,2048]{1,0:T(8,128)(2,1)} %constant_dynamic-update-slice_fusion.51.xa_ref), channel_id=1, source_target_pairs={{0,4},{4,0},{8,12},{12,8},{16,20},{20,16},{24,28},{28,24},{1,5},{5... | collective-permute-start | bytes 12582920 | tf_op jit(solution)/shard_map/ppermute | solution.py:42
  468.5 59.7 %collective-permute-start.63 = (bf16[1024,2048]{1,0:T(8,128)(2,1)}, bf16[1024,2048]{1,0:T(8,128)(2,1)}, u32[]{:S(2)}, u32[]{:S(2)}) collective-permute-start(bf16[1024,2048]{1,0:T(8,128)(2,1)} %get-tuple-element.490), channel_id=1, source_target_pairs={{0,4},{4,0},{8,12},{12,8},{16,20},{20,16},{24,28},{28,24},{1,5},{5... | collective-permute-start | bytes 12582920 | tf_op jit(solution)/shard_map/ppermute | solution.py:42
  469.0 59.3 %collective-permute-start.64 = (bf16[1024,2048]{1,0:T(8,128)(2,1)}, bf16[1024,2048]{1,0:T(8,128)(2,1)}, u32[]{:S(2)}, u32[]{:S(2)}) collective-permute-start(bf16[1024,2048]{1,0:T(8,128)(2,1)} %get-tuple-element.491), channel_id=1, source_target_pairs={{0,4},{4,0},{8,12},{12,8},{16,20},{20,16},{24,28},{28,24},{1,5},{5... | collective-permute-start | bytes 12582920 | tf_op jit(solution)/shard_map/ppermute | solution.py:42
  744.7 36.5 %collective-permute-start.92 = (bf16[2,64,2048]{2,1,0:T(8,128)(2,1)}, bf16[2,64,2048]{2,1,0:T(8,128)(2,1)S(1)}, u32[]{:S(2)}, u32[]{:S(2)}) collective-permute-start(bf16[2,64,2048]{2,1,0:T(8,128)(2,1)} %get-tuple-element.560), channel_id=1, source_target_pairs={{0,1},{1,0},{2,3},{3,2},{4,5},{5,4},{6,7},{7,6},{8,9},{9,8},{10,11... | collective-permute-start | bytes 1572872 | tf_op jit(solution)/shard_map/ppermute | solution.py:42
  745.1 36.2 %collective-permute-start.91 = (bf16[2,128,1024]{2,1,0:T(8,128)(2,1)S(1)}, bf16[2,128,1024]{2,1,0:T(8,128)(2,1)S(1)}, u32[]{:S(2)}, u32[]{:S(2)}) collective-permute-start(bf16[2,128,1024]{2,1,0:T(8,128)(2,1)S(1)} %copy-done.87), channel_id=1, source_target_pairs={{0,2},{1,3},{2,0},{3,1},{4,6},{5,7},{6,4},{7,5},{8,10},{9,11},{10,... | collective-permute-start | bytes 1572872 | tf_op jit(solution)/shard_map/ppermute | solution.py:42
  750.1 31.1 %collective-permute-start.93 = (bf16[128,2048]{1,0:T(8,128)(2,1)}, bf16[128,2048]{1,0:T(8,128)(2,1)S(1)}, u32[]{:S(2)}, u32[]{:S(2)}) collective-permute-start(bf16[128,2048]{1,0:T(8,128)(2,1)} %get-tuple-element.561), channel_id=1, source_target_pairs={{0,16},{4,20},{8,24},{12,28},{16,0},{20,4},{24,8},{28,12},{1,17},{... | collective-permute-start | bytes 1572872 | tf_op jit(solution)/shard_map/ppermute | solution.py:42
  751.1 30.2 %collective-permute-start.94 = (bf16[128,2048]{1,0:T(8,128)(2,1)S(1)}, bf16[128,2048]{1,0:T(8,128)(2,1)S(1)}, u32[]{:S(2)}, u32[]{:S(2)}) collective-permute-start(bf16[128,2048]{1,0:T(8,128)(2,1)S(1)} %get-tuple-element.562), channel_id=1, source_target_pairs={{0,8},{4,12},{8,0},{12,4},{16,24},{20,28},{24,16},{28,20},{1,9},{5... | collective-permute-start | bytes 1572872 | tf_op jit(solution)/shard_map/ppermute | solution.py:42
  786.7 32.2 %collective-permute-start.98 = (bf16[256,2048]{1,0:T(8,128)(2,1)S(1)}, bf16[256,2048]{1,0:T(8,128)(2,1)S(1)}, u32[]{:S(2)}, u32[]{:S(2)}) collective-permute-start(bf16[256,2048]{1,0:T(8,128)(2,1)S(1)} %pad_maximum_fusion.14), channel_id=1, source_target_pairs={{0,8},{4,12},{8,0},{12,4},{16,24},{20,28},{24,16},{28,20},{1,9},{5... | collective-permute-start | bytes 3145736 | tf_op jit(solution)/shard_map/ppermute | solution.py:42
  787.0 32.9 %collective-permute-start.99 = (bf16[256,2048]{1,0:T(8,128)(2,1)S(1)}, bf16[256,2048]{1,0:T(8,128)(2,1)}, u32[]{:S(2)}, u32[]{:S(2)}) collective-permute-start(bf16[256,2048]{1,0:T(8,128)(2,1)S(1)} %pad_maximum_fusion.15), channel_id=1, source_target_pairs={{0,16},{4,20},{8,24},{12,28},{16,0},{20,4},{24,8},{28,12},{1,17},{... | collective-permute-start | bytes 3145736 | tf_op jit(solution)/shard_map/ppermute | solution.py:42
  829.1 29.7 %collective-permute-start.102 = (bf16[1024,2048]{1,0:T(8,128)(2,1)}, bf16[1024,2048]{1,0:T(8,128)(2,1)}, u32[]{:S(2)}, u32[]{:S(2)}) collective-permute-start(bf16[1024,2048]{1,0:T(8,128)(2,1)} %convolution_convert_fusion.2), channel_id=1, source_target_pairs={{0,4},{4,0},{8,12},{12,8},{16,20},{20,16},{24,28},{28,24},{1,5},{5... | collective-permute-start | bytes 12582920 | tf_op jit(solution)/shard_map/ppermute | solution.py:42
  933.2 32.6 %collective-permute-start.117 = (bf16[2,256,1024]{2,1,0:T(8,128)(2,1)S(1)}, bf16[2,256,1024]{2,1,0:T(8,128)(2,1)}, u32[]{:S(2)}, u32[]{:S(2)}) collective-permute-start(bf16[2,256,1024]{2,1,0:T(8,128)(2,1)S(1)} %get-tuple-element.613), channel_id=1, source_target_pairs={{0,1},{1,0},{2,3},{3,2},{4,5},{5,4},{6,7},{7,6},{8,9},{9,8},{10,11... | collective-permute-start | bytes 3145736 | tf_op jit(solution)/shard_map/ppermute | solution.py:42
  936.1 29.7 %collective-permute-start.115 = (bf16[256,2048]{1,0:T(8,128)(2,1)S(1)}, bf16[256,2048]{1,0:T(8,128)(2,1)S(1)}, u32[]{:S(2)}, u32[]{:S(2)}) collective-permute-start(bf16[256,2048]{1,0:T(8,128)(2,1)S(1)} %pad_maximum_fusion.19), channel_id=1, source_target_pairs={{0,8},{4,12},{8,0},{12,4},{16,24},{20,28},{24,16},{28,20},{1,9},{5... | collective-permute-start | bytes 3145736 | tf_op jit(solution)/shard_map/ppermute | solution.py:42
  969.0 31.7 %collective-permute-start.120 = (bf16[2,256,1024]{2,1,0:T(8,128)(2,1)}, bf16[2,256,1024]{2,1,0:T(8,128)(2,1)}, u32[]{:S(2)}, u32[]{:S(2)}) collective-permute-start(bf16[2,256,1024]{2,1,0:T(8,128)(2,1)} %get-tuple-element.622), channel_id=1, source_target_pairs={{0,1},{1,0},{2,3},{3,2},{4,5},{5,4},{6,7},{7,6},{8,9},{9,8},{10,11... | collective-permute-start | bytes 3145736 | tf_op jit(solution)/shard_map/ppermute | solution.py:42
  970.3 29.4 %collective-permute-start.119 = (bf16[128,2048]{1,0:T(8,128)(2,1)}, bf16[128,2048]{1,0:T(8,128)(2,1)}, u32[]{:S(2)}, u32[]{:S(2)}) collective-permute-start(bf16[128,2048]{1,0:T(8,128)(2,1)} %get-tuple-element.621), channel_id=1, source_target_pairs={{0,2},{1,3},{2,0},{3,1},{4,6},{5,7},{6,4},{7,5},{8,10},{9,11},{10,... | collective-permute-start | bytes 1572872 | tf_op jit(solution)/shard_map/ppermute | solution.py:42
  (235 other events, 3241.9 us)

commit v11 on v10

--- a/solution.py
+++ b/solution.py
@@ -634,6 +634,61 @@
         compiler_params=pltpu.CompilerParams(vmem_limit_bytes=32 * MIB),
         name="rope_back",
     )(me, *grads, query_pre, key_pre, squares, means, gains, cosine, sine)
+
+
+def output_kernel(
+    me_ref, come_ref, even_ref, odd_ref, token_ref, gain_ref, residual_ref, second_ref, total_ref
+):
+    step, half = pl.program_id(0), pl.num_programs(0) // 2
+
+    @pl.when(step == 0)
+    def _():
+        total_ref[...] = token_ref[...].astype(F32)
+
+    @pl.when(step < half)
+    def _():
+        total_ref[...] += matmul(come_ref[0], even_ref[...])
+
+    @pl.when(step >= half)
+    def _():
+        total_ref[...] += matmul(come_ref[0], odd_ref[...])
+
+    @pl.when(step == 2 * half - 1)
+    def _():
+        total = total_ref[...]
+        residual_ref[...] = total
+        second_ref[...] = (total * rms_factor(total) * gain_ref[...]).astype(BF16)
+
+
+def project_out(come, even, odd, tokens, gain, me):
+    size, rows, columns = come.shape
+    depth = even.shape[1]
+    half = size // 2
+    whole = pl.BlockSpec((rows, depth), lambda p, me: (0, 0))
+    return pl.pallas_call(
+        output_kernel,
+        grid_spec=pltpu.PrefetchScalarGridSpec(
+            num_scalar_prefetch=1,
+            grid=(size,),
+            in_specs=[
+                pl.BlockSpec(
+                    (1, rows, columns), lambda p, me: (me[0] ^ (p % half * 2 + p // half), 0, 0)
+                ),
+                pl.BlockSpec((columns, depth), lambda p, me: (jnp.minimum(p, half - 1), 0)),
+                pl.BlockSpec((columns, depth), lambda p, me: (jnp.maximum(p - half, 0), 0)),
+                whole,
+                pl.BlockSpec((1, depth), lambda p, me: (0, 0)),
+            ],
+            out_specs=[whole, whole],
+            scratch_shapes=[pltpu.VMEM((rows, depth), F32)],
+        ),
+        out_shape=[
+            jax.ShapeDtypeStruct((rows, depth), F32),
+            jax.ShapeDtypeStruct((rows, depth), BF16),
+        ],
+        compiler_params=pltpu.CompilerParams(vmem_limit_bytes=32 * MIB),
+        name="project_out",
+    )(me, come, even, odd, tokens, gain)
 
 
 def expert_kernel(
@@ -899,7 +954,17 @@
             own_quarters, far_quarters, down_rows, upstream_halves, small = prepared
             partner_up = [far_swap(upstream_halves[0])]
     token_more = gather_more(tokens_low, token_first, S)
-    qkv_pieces, partner_up[0], token_more = tie(qkv_pieces, partner_up[0], token_more)
+    rank_part = small[:, :, part * (E + 4) :].reshape(S, F, E, T)
+
+    def ranks_of(index):
+        ranks = lax.dynamic_slice(rank_part, (0, index, s * experts, 0), (S, 1, experts, T))
+        ranks = relative(ranks[:, 0], s).astype(jnp.int32)
+        return ranks[: S // 2], ranks[S // 2 :]
+
+    own_ranks, other_ranks = ranks_of(f), ranks_of(f ^ half_f)
+    qkv_pieces, partner_up[0], token_more, own_ranks, other_ranks = tie(
+        qkv_pieces, partner_up[0], token_more, own_ranks, other_ranks
+    )
     tokens_even, tokens_odd = gather_end(tokens_low, token_first, token_more, S)
     w_qkv = place_fsdp(qkv_pieces, f, 1).reshape(D, 3 * C)
 
@@ -909,13 +974,6 @@
     ]
     gain_attn, gain_moe = gains[0], gains[1]
     head_gain = lax.dynamic_slice(jnp.stack(gains[2:], 0), (0, s * C), (2, C))
-    rank_part = small[:, :, part * (E + 4) :].reshape(S, F, E, T)
-
-    def ranks_of(index):
-        ranks = lax.dynamic_slice(rank_part, (0, index, s * experts, 0), (S, 1, experts, T))
-        ranks = relative(ranks[:, 0], s).astype(jnp.int32)
-        return ranks[: S // 2], ranks[S // 2 :]
-
     places = jnp.arange(L, dtype=jnp.int32).astype(F32)
     freqs = ROPE_BASE ** (-(jnp.arange(DH // 2, dtype=F32) * 2.0 / DH))
     angles = places[:, None] * freqs[None, :]
@@ -967,11 +1025,7 @@
     near_far.append(near_swap(far[1], come))
     down = [near_swap(down_rows[0], come)]
     partner_up_first = gather_first(after(partner_up, come), S)
-    come = relative(come, s).transpose(1, 0, 2).reshape(T, D)
-    residual = inputs + matmul(come[:, : D // 2], out_even) + matmul(come[:, D // 2 :], out_odd)
-    moe_factor = rms_factor(residual)
-    residual_n = residual * moe_factor
-    second_low = (residual_n * gain_moe).astype(BF16)
+    residual, second_low = project_out(come, out_even, out_odd, tokens_low, gain_moe[None], me)
     second_low, down[0], near_far[1], partner_up_first, own_u = tie(
         second_low, down[0], near_far[1], partner_up_first, own_u
     )
@@ -979,10 +1033,7 @@
     own_first = gather_first(second_low, S)
     partner_low = [far_swap(second_low[:half_rows])]
     near_far.append(near_swap(far[2], second_low))
-    own_ranks, other_ranks = ranks_of(f), ranks_of(f ^ half_f)
-    own_first, partner_low[0], near_far[2], own_ranks, other_ranks = tie(
-        own_first, partner_low[0], near_far[2], own_ranks, other_ranks
-    )
+    own_first, partner_low[0], near_far[2] = tie(own_first, partner_low[0], near_far[2])
     own_more = gather_more(second_low, own_first, S)
     partner_low.append(far_swap(second_low[half_rows:], own_first))
     down.append(near_swap(down_rows[1], own_first))
@@ -1032,6 +1083,8 @@
         parts,
     )
     other_parts, own_got, own_out_got = tie(other_parts, own_got, own_out_got)
+    moe_factor = rms_factor(residual)
+    residual_n = residual * moe_factor
     logits = matmul(second_low, full_router)
     router_probs = jax.nn.softmax(logits, axis=-1)
 
@@ -1054,30 +1107,26 @@
         [to_home(own_parts[4], own_parts[5]), to_home(other_parts[4], other_parts[5])], 1
     ).reshape(S, -1)
     other_got = swap(other_parts[3], "seq", S, 1)
+    gate_grads = lax.all_to_all(gate_grads, "seq", split_axis=0, concat_axis=0, tiled=True)
+    other_got, gate_grads = tie(other_got, gate_grads)
     for r in far_odd:
-        in_products(r)
-    gate_grads = lax.all_to_all(gate_grads, "seq", split_axis=0, concat_axis=0, tiled=True)
-    other_got, in_terms, gate_grads = tie(other_got, in_terms, gate_grads)
-    sent = {r: quarters(in_terms[r], 1) for r in far_odd}
+        in_products(r, other_got)
 
     def send_in(n, *dep):
         return {r: swap(after(sent[r][n], dep), "fsdp", F, 1) for r in sent}
 
     other_sums = sum_cores(other_parts[2], other_got, S)
     come = sum_first(other_sums, S)
-    far_got = [send_in(0, other_got)]
     other_out_got = swap(after(other_parts[1], other_got), "seq", S, 1)
     gate_grads = gate_grads.reshape(S, 2, T * experts)
     partner_grads = far_swap(gate_grads[:, 1])
-    come, far_got[0], other_out_got, partner_grads = tie(
-        come, far_got[0], other_out_got, partner_grads
-    )
+    come, in_terms, other_out_got, partner_grads = tie(
+        come, in_terms, other_out_got, partner_grads
+    )
+    sent = {r: quarters(in_terms[r], 1) for r in far_odd}
     singles, other_total = sum_more(other_sums, come, S)
     come = sum_last(singles, S)
-    middle_sent = {r: jnp.concatenate(sent[r][1:3], 1) for r in sent}
-    middle_got = {
-        r: swap(after(middle_sent[r], far_got[0]), "fsdp", F, 1) for r in middle_sent
-    }
+    start_got = {r: swap(in_terms[r][:, : 2 * quarter], "fsdp", F, 1) for r in far_odd}
 
     def down_products(r, dep):
         down_terms[r] = products(
@@ -1086,31 +1135,35 @@
 
     for r in range(1, half_f, 2):
         down_products(r, singles)
-    come, middle_got, down_terms = tie(come, middle_got, down_terms)
-    for n in range(2):
-        far_got.append({r: got[:, n * quarter : (n + 1) * quarter] for r, got in middle_got.items()})
+    come, start_got, down_terms = tie(come, start_got, down_terms)
+    far_got = [
+        {r: got[:, n * quarter : (n + 1) * quarter] for r, got in start_got.items()}
+        for n in range(2)
+    ]
     other_rows = add_all(other_total, come).astype(BF16)
     gate_grads = gate_grads[:, 0] + partner_grads
     gate_grads = gate_grads.reshape(S, T, experts).transpose(1, 0, 2).reshape(T, E)
     back = [far_swap(other_rows[:half_rows])]
     own_sums = sum_cores(own_parts[2], after(own_got, other_rows), S)
     come = sum_first(own_sums, S)
-    far_got.append(send_in(3, other_rows))
+    far_got.append(send_in(2, other_rows))
     for r in far_odd:
         in_products(r ^ 1, other_rows)
-    come, back[0], far_got[3], in_terms = tie(come, back[0], far_got[3], in_terms)
+    come, back[0], far_got[2], in_terms = tie(come, back[0], far_got[2], in_terms)
     back.append(far_swap(other_rows[half_rows:], come))
     singles, own_total = sum_more(own_sums, come, S)
     come = sum_last(singles, S)
     down_sent = {r: quarters(down_terms[r], 1) for r in range(1, half_f, 2)}
+    for r in down_sent:
+        down_sent[r] = down_sent[r][:2] + [jnp.concatenate(down_sent[r][2:], 1)]
 
     def send_down(n, *dep):
         return {r: swap(after(down_sent[r][n], dep), "fsdp", F, 1) for r in down_sent}
 
-    down_got = [send_down(0, singles)]
+    far_got.append(send_in(3, singles))
     for r in near_odd:
         in_products(r, singles)
-    come, back[1], down_got[0], in_terms = tie(come, back[1], down_got[0], in_terms)
+    come, back[1], far_got[3], in_terms = tie(come, back[1], far_got[3], in_terms)
     row_grads = add_all(own_total, come) + jnp.concatenate(back, 0).astype(F32)
 
     upstream = upstream_low.astype(F32)
@@ -1146,31 +1199,31 @@
 
     branch_first = gather_first(branch_low, S)
     far_sums = [far_sum(0, branch_low)]
-    down_got.append(send_down(1, branch_low))
+    down_got = [send_down(0, branch_low)]
     for r in range(0, half_f, 2):
         down_products(r, branch_low)
-    branch_first, far_sums[0], down_got[1], down_terms = tie(
-        branch_first, far_sums[0], down_got[1], down_terms
+    branch_first, far_sums[0], down_got[0], down_terms = tie(
+        branch_first, far_sums[0], down_got[0], down_terms
     )
     branch_more = gather_more(branch_low, branch_first, S)
     far_sums.append(far_sum(1, branch_first))
-    down_got.append(send_down(2, branch_first))
+    down_got.append(send_down(1, branch_first))
     branch_even, branch_odd = gather_end(branch_low, branch_first, branch_more, S)
 
     head_grads = jnp.concatenate(
         [matmul_t(branch_even, own_output), matmul_t(branch_odd, own_output)], 0
     ).astype(BF16)
     head_grads = absolute(head_grads.reshape(S, T, C), s).reshape(L, C)
-    head_grads, far_sums[1], down_got[2] = tie(head_grads, far_sums[1], down_got[2])
+    head_grads, far_sums[1], down_got[1] = tie(head_grads, far_sums[1], down_got[1])
     far_sums.append(far_sum(2, head_grads))
-    down_got.append(send_down(3, head_grads))
+    down_got.append(send_down(2, head_grads))
     other_out_sums = sum_cores(other_parts[0], after(other_out_got, head_grads), S)
     come, head_grads = sum_first(other_out_sums, S, head_grads)
     query_back, key_back, value_back = attention_backward(
         query_low, key_low, value_low, head_grads, lse, seg_row, seg_col
     )
-    query_back, key_back, value_back, far_sums[2], down_got[3], come = tie(
-        query_back, key_back, value_back, far_sums[2], down_got[3], come
+    query_back, key_back, value_back, far_sums[2], down_got[2], come = tie(
+        query_back, key_back, value_back, far_sums[2], down_got[2], come
     )
 
     singles, other_total = sum_more(other_out_sums, come, S)
@@ -1195,7 +1248,6 @@
         means, come, far_sums[3], output_got, value_term
     )
     other_outs = add_all(other_total, come).astype(BF16)
-    outs_back = [far_swap(other_outs[:half_rows])]
     value_got = swap(value_term[: F // 2], "fsdp", F, 1)
     pre_rel = rope_back(
         (query_back, key_back, value_back),
@@ -1211,9 +1263,7 @@
     ).reshape(2, L // 2, 3 * C)
     normed_got = swap(matmul_t(pre_rel[1], w_qkv).astype(BF16), "seq", S, 1)
     normed_kept = matmul_t(pre_rel[0], w_qkv).astype(BF16)
-    normed_got, normed_kept, value_got, outs_back[0] = tie(
-        normed_got, normed_kept, value_got, outs_back[0]
-    )
+    normed_got, normed_kept, value_got = tie(normed_got, normed_kept, value_got)
 
     normed_sums = sum_cores(normed_kept, normed_got, S)
     come = sum_first(normed_sums, S)
@@ -1242,7 +1292,10 @@
     gain_got = swap(gain_terms[F // 2 :], "fsdp", F, half_f)
     for r in near_odd:
         in_products(r ^ 1, turned_term)
-    come, turned_got, gain_got, in_terms = tie(come, turned_got, gain_got, in_terms)
+    outs_back = [far_swap(other_outs[:half_rows], turned_term)]
+    come, turned_got, gain_got, in_terms, outs_back[0] = tie(
+        come, turned_got, gain_got, in_terms, outs_back[0]
+    )
     gain_terms = gain_terms[: F // 2] + gain_got
     normed_grads = add_all(normed_total, come)
     turned_sum = sum_rest(sum_even(turned_term, turned_got, F), F)

time: 1040 us -> 1060 us (1.019)
  waiting for transfers between devices: 319 us -> 338 us
    ppermute x125 -> x124, waiting for transfers between devices: 318 us -> 338 us  [swap(): return lax.ppermute(values, axis, [(i, i ^ mask) for i in range(size)])]
    unnamed x346 -> x339, local copies, waits for them, and re-layouts: 59.4 us -> 63.6 us
    ppermute x125 -> x124, starting transfers between devices: 135 us -> 133 us  [swap(): return lax.ppermute(values, axis, [(i, i ^ mask) for i in range(size)])]
  transfers between devices with their start and end apart: 129 -> 127, of which waited for: 60 -> 61; matrix products, arithmetic and copies ran while one was open for 19% -> 18% of each run, Pallas kernels for 24% -> 24%
where the time goes in v11:
time: 1060 us; the launch traced here: 1050 us
  waiting for transfers between devices  338 us (32%)
  Pallas kernels  263 us (25%)
  starting transfers between devices  144 us (14%)
  local copies, waits for them, and re-layouts  142 us (13%)
  other arithmetic  113 us (11%)
  matrix products  38.4 us (4%)
    ppermute x124, waiting for transfers between devices, swap(): return lax.ppermute(values, axis, [(i, i ^ mask) for i in range(size)])  338 us
    ppermute x124, starting transfers between devices, swap(): return lax.ppermute(values, axis, [(i, i ^ mask) for i in range(size)])  133 us
    pallas_call x2, Pallas kernels, run_experts(): pl.pallas_call(partial(expert_kernel, in_places, down_places), grid=(step...  118 us
    unnamed x339, local copies, waits for them, and re-layouts  63.6 us
    pallas_call x6, Pallas kernels, products(): pl.pallas_call(product_kernel, grid_spec=pltpu.PrefetchScalarGridSpec(num...  60.5 us
    pallas_call x1, Pallas kernels, attention_backward(): pl.pallas_call(partial(backward_kernel, span), grid=(heads, length // row...  28.3 us
    pallas_call x1, Pallas kernels, attention_forward(): pl.pallas_call(partial(forward_kernel, span), grid=(heads, length // rows...  22.1 us
  transfers between devices with their start and end apart: 127, of which 61 were waited for; matrix products, arithmetic and copies ran while one was open for 18% of the time, Pallas kernels for 24%

profile of v11, /device:TPU:0, one launch (start us, length us, event | category | flops | bytes accessed | tf_op | source)
XLA Modules:
  0.0 1050.3 jit_solution(11500727782187798882)
XLA Ops:
  33.0 9.3 collective-permute-done.5
  74.3 15.5 %collective-permute-done.7 = bf16[8,64,768]{2,1,0:T(8,128)(2,1)} collective-permute-done((bf16[8,64,768]{2,1,0:T(8,128)(2,1)S(1)}, bf16[8,64,768]{2,1,0:T(8,128)(2,1)}, u32[]{:S(2)}, u32[]{:S(2)}) %collective-permute-start.7) | collective-permute-done | bytes 786464 | tf_op jit(solution)/shard_map/ppermute | solution.py:42
  113.4 13.0 %collective-permute-done.12 = bf16[128,2048]{1,0:T(8,128)(2,1)} collective-permute-done((bf16[128,2048]{1,0:T(8,128)(2,1)}, bf16[128,2048]{1,0:T(8,128)(2,1)}, u32[]{:S(2)}, u32[]{:S(2)}) %collective-permute-start.12) | collective-permute-done | bytes 524320 | tf_op jit(solution)/shard_map/ppermute | solution.py:42
  144.5 12.6 %project.1 = (bf16[1024,2048]{1,0:T(8,128)(2,1)}, bf16[1024,2048]{1,0:T(8,128)(2,1)}, f32[2048,256]{1,0:T(8,128)S(1)}, f32[2048,256]{1,0:T(8,128)S(1)}, bf16[204...) custom-call(s32[1]{0:T(128)} %bitcast.me_ref, bf16[1024,2048]{1,0:T(8,128)(2,1)} %constant_dynamic-update-slice_fusion.16.even_ref, ...), custom_call_target="tpu_custom_call" | custom-call | flops 6442450944 | bytes 25165824 | tf_op jit(solution)/shard_map/project/pallas_call | solution.py:437
  186.8 10.0 collective-permute-done.22
  224.8 22.1 %attend.1 = (bf16[2048,256]{1,0:T(8,128)(2,1)}, f32[2,1,2048]{2,1,0:T(1,128)S(1)}) custom-call(bf16[2048,256]{1,0:T(8,128)(2,1)S(1)} %get-tuple-element.372.q_ref, bf16[2048,256]{1,0:T(8,128)(2,1)S(1)} %get-tuple-element.373.k_ref, bf16[2048,256]{1,0:T(8,128)(2,1)S(1)} %copy-done.28, s32[1,2048]{1,0:T(1,128)S(1)} %copy-done.22, s32[2048,1]{1,0:T(8,128)S(1)} %copy-done.17), custom_call_target="tpu_custom_call" | custom-call | flops 2684354560 | bytes 4194304 | tf_op jit(solution)/shard_map/attend/pallas_call | solution.py:336
  261.4 17.8 %collective-permute-done.33.refs_10_ = bf16[2,128,1024]{2,1,0:T(8,128)(2,1)S(1)} collective-permute-done((bf16[2,128,1024]{2,1,0:T(8,128)(2,1)}, bf16[2,128,1024]{2,1,0:T(8,128)(2,1)S(1)}, u32[]{:S(2)}, u32[]{:S(2)}) %collective-permute-start.33) | collective-permute-done | bytes 524320 | tf_op jit(solution)/shard_map/ppermute | solution.py:42
  294.6 8.3 project_out.1
  306.3 10.2 collective-permute-done.37.refs_18_
  323.6 17.1 %collective-permute-done.45.refs_12_ = bf16[2,128,1024]{2,1,0:T(8,128)(2,1)S(1)} collective-permute-done((bf16[2,128,1024]{2,1,0:T(8,128)(2,1)}, bf16[2,128,1024]{2,1,0:T(8,128)(2,1)S(1)}, u32[]{:S(2)}, u32[]{:S(2)}) %collective-permute-start.45) | collective-permute-done | bytes 524320 | tf_op jit(solution)/shard_map/ppermute | solution.py:42
  346.6 7.9 collective-permute-done.50
  356.3 9.3 collective-permute-done.49.refs_19_
  372.7 22.8 %collective-permute-done.56.refs_9_ = bf16[2,128,1024]{2,1,0:T(8,128)(2,1)S(1)} collective-permute-done((bf16[2,128,1024]{2,1,0:T(8,128)(2,1)S(1)}, bf16[2,128,1024]{2,1,0:T(8,128)(2,1)S(1)}, u32[]{:S(2)}, u32[]{:S(2)}) %collective-permute-start.56) | collective-permute-done | bytes 524320 | tf_op jit(solution)/shard_map/ppermute | solution.py:42
  408.9 8.2 collective-permute-done.61.refs_13_
  417.1 10.9 %collective-permute-done.59.refs_21_ = bf16[2,64,2048]{2,1,0:T(8,128)(2,1)S(1)} collective-permute-done((bf16[2,64,2048]{2,1,0:T(8,128)(2,1)S(1)}, bf16[2,64,2048]{2,1,0:T(8,128)(2,1)S(1)}, u32[]{:S(2)}, u32[]{:S(2)}) %collective-permute-start.59) | collective-permute-done | bytes 524320 | tf_op jit(solution)/shard_map/ppermute | solution.py:42
  435.8 59.0 %experts.2 = (bf16[1024,2048]{1,0:T(8,128)(2,1)}, bf16[1024,2048]{1,0:T(8,128)(2,1)}, bf16[1024,2048]{1,0:T(8,128)(2,1)}, bf16[1024,2048]{1,0:T(8,128)(2,1)}, f3...) custom-call(s32[2]{0:T(128)} %pad_add_fusion.first_ref, ...), custom_call_target="tpu_custom_call" | custom-call | flops 38654705664 | bytes 62914560 | tf_op jit(solution)/shard_map/experts/pallas_call | solution.py:787
  495.4 59.1 %experts.3 = (bf16[1024,2048]{1,0:T(8,128)(2,1)}, bf16[1024,2048]{1,0:T(8,128)(2,1)}, bf16[1024,2048]{1,0:T(8,128)(2,1)}, bf16[1024,2048]{1,0:T(8,128)(2,1)}, f3...) custom-call(s32[2]{0:T(128)} %pad_add_fusion.first_ref, ...), custom_call_target="tpu_custom_call", output_to_operand_aliasing={{6}: (30, {}), {7}: (31, {}), {8}: (32, {}), {9}: (33, {})} | custom-call | flops 38654705664 | bytes 62914560 | tf_op jit(solution)/shard_map/experts/pallas_call | solution.py:787
  571.4 9.7 in_products.4
  596.3 11.0 %down_products.2 = bf16[2,256,2048]{2,1,0:T(8,128)(2,1)} custom-call(s32[1]{0:T(128)} %bitcast.38.me_ref, bf16[2,2304,512]{2,1,0:T(8,128)(2,1)} %get-tuple-element.547.left_ref, bf16[2,2304,2048]{2,1,0:T(8,128)(2,1)} %get-tuple-element.521.right_ref), custom_call_target="tpu_custom_call" | custom-call | flops 4831838208 | bytes 21233664 | tf_op jit(solution)/shard_map/down_products/pallas_call | solution.py:824
  607.3 8.7 collective-permute-done.70
  631.2 9.3 in_products.5
  643.2 10.4 collective-permute-done.75
  667.9 9.9 in_products.6
  677.7 8.7 collective-permute-done.80
  706.8 11.0 %down_products.3 = bf16[2,256,2048]{2,1,0:T(8,128)(2,1)} custom-call(s32[1]{0:T(128)} %bitcast.38.me_ref, bf16[2,2304,512]{2,1,0:T(8,128)(2,1)} %get-tuple-element.547.left_ref, bf16[2,2304,2048]{2,1,0:T(8,128)(2,1)} %get-tuple-element.521.right_ref), custom_call_target="tpu_custom_call" | custom-call | flops 4831838208 | bytes 21233664 | tf_op jit(solution)/shard_map/down_products/pallas_call | solution.py:824
  719.3 8.0 collective-permute-done.83
  750.5 14.8 %collective-permute-done.89 = bf16[2,64,2048]{2,1,0:T(8,128)(2,1)S(1)} collective-permute-done((bf16[2,64,2048]{2,1,0:T(8,128)(2,1)S(1)}, bf16[2,64,2048]{2,1,0:T(8,128)(2,1)S(1)}, u32[]{:S(2)}, u32[]{:S(2)}) %collective-permute-start.89) | collective-permute-done | bytes 524320 | tf_op jit(solution)/shard_map/ppermute | solution.py:42
  773.5 28.3 %attend_back.1 = (bf16[2048,256]{1,0:T(8,128)(2,1)S(1)}, bf16[2048,256]{1,0:T(8,128)(2,1)S(1)}, bf16[2048,256]{1,0:T(8,128)(2,1)S(1)}) custom-call(bf16[2048,256]{1,0:T(8,128)(2,1)S(1)} %copy-done.24, bf16[2048,256]{1,0:T(8,128)(2,1)S(1)} %copy-done.26, bf16[2048,256]{1,0:T(8,128)(2,1)} %copy-done.27, bf16[2048,256]{1,0:T(8,128)(2,1)} %bitcast.356, ...), custom_call_target="tpu_custom_call" | custom-call | flops 6710886400 | bytes 7340032 | tf_op jit(solution)/shard_map/attend_back/pallas_call | solution.py:368
  921.4 9.6 in_products.7
  931.0 16.1 %collective-permute-done.111 = f32[2,8832]{1,0:T(2,128)S(1)} collective-permute-done((f32[2,8832]{1,0:T(2,128)}, f32[2,8832]{1,0:T(2,128)S(1)}, u32[]{:S(2)}, u32[]{:S(2)}) %collective-permute-start.111) | collective-permute-done | bytes 70688 | tf_op jit(solution)/shard_map/ppermute | solution.py:42
  968.8 18.6 %collective-permute-done.113 = bf16[1,8,64,512]{3,2,1,0:T(8,128)(2,1)S(1)} collective-permute-done((bf16[1,8,64,512]{3,2,1,0:T(8,128)(2,1)S(1)}, bf16[1,8,64,512]{3,2,1,0:T(8,128)(2,1)S(1)}, u32[]{:S(2)}, u32[]{:S(2)}) %collective-permute-start.113) | collective-permute-done | bytes 524320 | tf_op jit(solution)/shard_map/ppermute | solution.py:42
  1011.8 13.2 %collective-permute-done.118 = bf16[128,2048]{1,0:T(8,128)(2,1)} collective-permute-done((bf16[128,2048]{1,0:T(8,128)(2,1)}, bf16[128,2048]{1,0:T(8,128)(2,1)}, u32[]{:S(2)}, u32[]{:S(2)}) %collective-permute-start.118) | collective-permute-done | bytes 524320 | tf_op jit(solution)/shard_map/ppermute | solution.py:42
  (807 shorter events, 546.5 us)
Async XLA Ops:
  19.9 31.5 %collective-permute-start.2 = (bf16[2,256,1024]{2,1,0:T(8,128)(2,1)S(1)}, bf16[2,256,1024]{2,1,0:T(8,128)(2,1)}, u32[]{:S(2)}, u32[]{:S(2)}) collective-permute-start(bf16[2,256,1024]{2,1,0:T(8,128)(2,1)S(1)} %pad_maximum_fusion.5.refs_0_), channel_id=1, source_target_pairs={{0,1},{1,0},{2,3},{3,2},{4,5},{5,4},{6,7},{7,6},{8,9},{9,8},{10,11... | collective-permute-start | bytes 3145736 | tf_op jit(solution)/shard_map/ppermute | solution.py:42
  51.4 42.1 %collective-permute-start.10 = (bf16[256,2048]{1,0:T(8,128)(2,1)S(1)}, bf16[256,2048]{1,0:T(8,128)(2,1)S(1)}, u32[]{:S(2)}, u32[]{:S(2)}) collective-permute-start(bf16[256,2048]{1,0:T(8,128)(2,1)S(1)} %bitcast.319), channel_id=1, source_target_pairs={{0,16},{4,20},{8,24},{12,28},{16,0},{20,4},{24,8},{28,12},{1,17},{... | collective-permute-start | bytes 3145736 | tf_op jit(solution)/shard_map/ppermute | solution.py:42
  53.1 40.4 %collective-permute-start.9 = (bf16[256,2048]{1,0:T(8,128)(2,1)S(1)}, bf16[256,2048]{1,0:T(8,128)(2,1)}, u32[]{:S(2)}, u32[]{:S(2)}) collective-permute-start(bf16[256,2048]{1,0:T(8,128)(2,1)S(1)} %bitcast.320), channel_id=1, source_target_pairs={{0,8},{4,12},{8,0},{12,4},{16,24},{20,28},{24,16},{28,20},{1,9},{5... | collective-permute-start | bytes 3145736 | tf_op jit(solution)/shard_map/ppermute | solution.py:42
  54.6 35.2 %collective-permute-start.7 = (bf16[8,64,768]{2,1,0:T(8,128)(2,1)S(1)}, bf16[8,64,768]{2,1,0:T(8,128)(2,1)}, u32[]{:S(2)}, u32[]{:S(2)}) collective-permute-start(bf16[8,64,768]{2,1,0:T(8,128)(2,1)S(1)} %all-to-all-done), channel_id=1, source_target_pairs={{0,1},{1,0},{2,3},{3,2},{4,5},{5,4},{6,7},{7,6},{8,9},{9,8},{10,11... | collective-permute-start | bytes 2359304 | tf_op jit(solution)/shard_map/ppermute | solution.py:42
  57.3 36.2 %collective-permute-start.8 = (bf16[8,64,768]{2,1,0:T(8,128)(2,1)S(1)}, bf16[8,64,768]{2,1,0:T(8,128)(2,1)}, u32[]{:S(2)}, u32[]{:S(2)}) collective-permute-start(bf16[8,64,768]{2,1,0:T(8,128)(2,1)S(1)} %all-to-all-done), channel_id=1, source_target_pairs={{0,2},{1,3},{2,0},{3,1},{4,6},{5,7},{6,4},{7,5},{8,10},{9,11},{10,... | collective-permute-start | bytes 2359304 | tf_op jit(solution)/shard_map/ppermute | solution.py:42
  132.8 33.1 %collective-permute-start.19 = (bf16[256,2048]{1,0:T(8,128)(2,1)}, bf16[256,2048]{1,0:T(8,128)(2,1)}, u32[]{:S(2)}, u32[]{:S(2)}) collective-permute-start(bf16[256,2048]{1,0:T(8,128)(2,1)} %bitcast.4), channel_id=1, source_target_pairs={{0,8},{4,12},{8,0},{12,4},{16,24},{20,28},{24,16},{28,20},{1,9},{5... | collective-permute-start | bytes 3145736 | tf_op jit(solution)/shard_map/ppermute | solution.py:42
  133.4 32.5 %collective-permute-start.20 = (bf16[256,2048]{1,0:T(8,128)(2,1)}, bf16[256,2048]{1,0:T(8,128)(2,1)}, u32[]{:S(2)}, u32[]{:S(2)}) collective-permute-start(bf16[256,2048]{1,0:T(8,128)(2,1)} %bitcast.4), channel_id=1, source_target_pairs={{0,16},{4,20},{8,24},{12,28},{16,0},{20,4},{24,8},{28,12},{1,17},{... | collective-permute-start | bytes 3145736 | tf_op jit(solution)/shard_map/ppermute | solution.py:42
  171.9 33.7 %collective-permute-start.24 = (bf16[256,2048]{1,0:T(8,128)(2,1)}, bf16[256,2048]{1,0:T(8,128)(2,1)}, u32[]{:S(2)}, u32[]{:S(2)}) collective-permute-start(bf16[256,2048]{1,0:T(8,128)(2,1)} %bitcast.34), channel_id=1, source_target_pairs={{0,8},{4,12},{8,0},{12,4},{16,24},{20,28},{24,16},{28,20},{1,9},{5... | collective-permute-start | bytes 3145736 | tf_op jit(solution)/shard_map/ppermute | solution.py:42
  173.3 32.3 %collective-permute-start.25 = (bf16[256,2048]{1,0:T(8,128)(2,1)}, bf16[256,2048]{1,0:T(8,128)(2,1)}, u32[]{:S(2)}, u32[]{:S(2)}) collective-permute-start(bf16[256,2048]{1,0:T(8,128)(2,1)} %bitcast.34), channel_id=1, source_target_pairs={{0,16},{4,20},{8,24},{12,28},{16,0},{20,4},{24,8},{28,12},{1,17},{... | collective-permute-start | bytes 3145736 | tf_op jit(solution)/shard_map/ppermute | solution.py:42
  205.6 41.3 %collective-permute-start.31 = (bf16[2,128,1024]{2,1,0:T(8,128)(2,1)S(1)}, bf16[2,128,1024]{2,1,0:T(8,128)(2,1)S(1)}, u32[]{:S(2)}, u32[]{:S(2)}) collective-permute-start(bf16[2,128,1024]{2,1,0:T(8,128)(2,1)S(1)} %copy-done.95), channel_id=1, source_target_pairs={{0,1},{1,0},{2,3},{3,2},{4,5},{5,4},{6,7},{7,6},{8,9},{9,8},{10,11... | collective-permute-start | bytes 1572872 | tf_op jit(solution)/shard_map/ppermute | solution.py:42
  207.3 40.3 %collective-permute-start.30 = (bf16[2,128,1024]{2,1,0:T(8,128)(2,1)S(1)}, bf16[2,128,1024]{2,1,0:T(8,128)(2,1)S(1)}, u32[]{:S(2)}, u32[]{:S(2)}) collective-permute-start(bf16[2,128,1024]{2,1,0:T(8,128)(2,1)S(1)} %copy-done.98), channel_id=1, source_target_pairs={{0,2},{1,3},{2,0},{3,1},{4,6},{5,7},{6,4},{7,5},{8,10},{9,11},{10,... | collective-permute-start | bytes 1572872 | tf_op jit(solution)/shard_map/ppermute | solution.py:42
  211.7 35.9 %collective-permute-start.28 = (bf16[128,2048]{1,0:T(8,128)(2,1)S(1)}, bf16[128,2048]{1,0:T(8,128)(2,1)}, u32[]{:S(2)}, u32[]{:S(2)}) collective-permute-start(bf16[128,2048]{1,0:T(8,128)(2,1)S(1)} %slice.571), channel_id=1, source_target_pairs={{0,16},{4,20},{8,24},{12,28},{16,0},{20,4},{24,8},{28,12},{1,17},{... | collective-permute-start | bytes 1572872 | tf_op jit(solution)/shard_map/ppermute | solution.py:42
  214.3 33.3 %collective-permute-start.29 = (bf16[128,2048]{1,0:T(8,128)(2,1)S(1)}, bf16[128,2048]{1,0:T(8,128)(2,1)}, u32[]{:S(2)}, u32[]{:S(2)}) collective-permute-start(bf16[128,2048]{1,0:T(8,128)(2,1)S(1)} %slice.572), channel_id=1, source_target_pairs={{0,8},{4,12},{8,0},{12,4},{16,24},{20,28},{24,16},{28,20},{1,9},{5... | collective-permute-start | bytes 1572872 | tf_op jit(solution)/shard_map/ppermute | solution.py:42
  220.0 41.3 %collective-permute-start.34 = (bf16[128,2048]{1,0:T(8,128)(2,1)}, bf16[128,2048]{1,0:T(8,128)(2,1)}, u32[]{:S(2)}, u32[]{:S(2)}) collective-permute-start(bf16[128,2048]{1,0:T(8,128)(2,1)} %slice.573), channel_id=1, source_target_pairs={{0,16},{4,20},{8,24},{12,28},{16,0},{20,4},{24,8},{28,12},{1,17},{... | collective-permute-start | bytes 1572872 | tf_op jit(solution)/shard_map/ppermute | solution.py:42
  248.3 32.9 %all-to-all-start.1 = ((bf16[8,256,256]{2,1,0:T(8,128)(2,1)}), bf16[8,256,256]{2,1,0:T(8,128)(2,1)S(1)}, u32[]{:S(2)}, u32[]{:S(2)}) async-start(bf16[8,256,256]{2,1,0:T(8,128)(2,1)} %bitcast.36), calls=%async_computation.1 | async-start | bytes 2097152 | tf_op jit(solution)/shard_map/all_to_all | solution.py:1018
  259.0 32.3 %collective-permute-start.36 = (bf16[1024,2048]{1,0:T(8,128)(2,1)}, bf16[1024,2048]{1,0:T(8,128)(2,1)}, u32[]{:S(2)}, u32[]{:S(2)}) collective-permute-start(bf16[1024,2048]{1,0:T(8,128)(2,1)} %constant_dynamic-update-slice_fusion.21.even_ref), channel_id=1, source_target_pairs={{0,4},{4,0},{8,12},{12,8},{16,20},{20,16},{24,28},{28,24},{1,5},{5... | collective-permute-start | bytes 12582920 | tf_op jit(solution)/shard_map/ppermute | solution.py:42
  285.4 31.2 %collective-permute-start.41 = (bf16[1024,2048]{1,0:T(8,128)(2,1)}, bf16[1024,2048]{1,0:T(8,128)(2,1)}, u32[]{:S(2)}, u32[]{:S(2)}) collective-permute-start(bf16[1024,2048]{1,0:T(8,128)(2,1)} %constant_dynamic-update-slice_fusion.28.ua_ref), channel_id=1, source_target_pairs={{0,4},{4,0},{8,12},{12,8},{16,20},{20,16},{24,28},{28,24},{1,5},{5... | collective-permute-start | bytes 12582920 | tf_op jit(solution)/shard_map/ppermute | solution.py:42
  320.8 33.7 %collective-permute-start.50 = (bf16[128,2048]{1,0:T(8,128)(2,1)S(1)}, bf16[128,2048]{1,0:T(8,128)(2,1)S(1)}, u32[]{:S(2)}, u32[]{:S(2)}) collective-permute-start(bf16[128,2048]{1,0:T(8,128)(2,1)S(1)} %slice.580), channel_id=1, source_target_pairs={{0,16},{4,20},{8,24},{12,28},{16,0},{20,4},{24,8},{28,12},{1,17},{... | collective-permute-start | bytes 1572872 | tf_op jit(solution)/shard_map/ppermute | solution.py:42
  430.4 64.4 %collective-permute-start.62 = (bf16[1024,2048]{1,0:T(8,128)(2,1)}, bf16[1024,2048]{1,0:T(8,128)(2,1)}, u32[]{:S(2)}, u32[]{:S(2)}) collective-permute-start(bf16[1024,2048]{1,0:T(8,128)(2,1)} %constant_dynamic-update-slice_fusion.43.xa_ref), channel_id=1, source_target_pairs={{0,4},{4,0},{8,12},{12,8},{16,20},{20,16},{24,28},{28,24},{1,5},{5... | collective-permute-start | bytes 12582920 | tf_op jit(solution)/shard_map/ppermute | solution.py:42
  494.9 59.7 %collective-permute-start.63 = (bf16[1024,2048]{1,0:T(8,128)(2,1)}, bf16[1024,2048]{1,0:T(8,128)(2,1)}, u32[]{:S(2)}, u32[]{:S(2)}) collective-permute-start(bf16[1024,2048]{1,0:T(8,128)(2,1)} %get-tuple-element.492), channel_id=1, source_target_pairs={{0,4},{4,0},{8,12},{12,8},{16,20},{20,16},{24,28},{28,24},{1,5},{5... | collective-permute-start | bytes 12582920 | tf_op jit(solution)/shard_map/ppermute | solution.py:42
  495.3 59.2 %collective-permute-start.64 = (bf16[1024,2048]{1,0:T(8,128)(2,1)}, bf16[1024,2048]{1,0:T(8,128)(2,1)}, u32[]{:S(2)}, u32[]{:S(2)}) collective-permute-start(bf16[1024,2048]{1,0:T(8,128)(2,1)} %get-tuple-element.493), channel_id=1, source_target_pairs={{0,4},{4,0},{8,12},{12,8},{16,20},{20,16},{24,28},{28,24},{1,5},{5... | collective-permute-start | bytes 12582920 | tf_op jit(solution)/shard_map/ppermute | solution.py:42
  767.0 36.2 %collective-permute-start.91 = (bf16[2,128,2048]{2,1,0:T(8,128)(2,1)}, bf16[2,128,2048]{2,1,0:T(8,128)(2,1)S(1)}, u32[]{:S(2)}, u32[]{:S(2)}) collective-permute-start(bf16[2,128,2048]{2,1,0:T(8,128)(2,1)} %concatenate.247), channel_id=1, source_target_pairs={{0,1},{1,0},{2,3},{3,2},{4,5},{5,4},{6,7},{7,6},{8,9},{9,8},{10,11... | collective-permute-start | bytes 3145736 | tf_op jit(solution)/shard_map/ppermute | solution.py:42
  767.0 34.7 %collective-permute-start.90 = (bf16[2,128,1024]{2,1,0:T(8,128)(2,1)S(1)}, bf16[2,128,1024]{2,1,0:T(8,128)(2,1)S(1)}, u32[]{:S(2)}, u32[]{:S(2)}) collective-permute-start(bf16[2,128,1024]{2,1,0:T(8,128)(2,1)S(1)} %copy-done.86), channel_id=1, source_target_pairs={{0,2},{1,3},{2,0},{3,1},{4,6},{5,7},{6,4},{7,5},{8,10},{9,11},{10,... | collective-permute-start | bytes 1572872 | tf_op jit(solution)/shard_map/ppermute | solution.py:42
  808.9 33.9 %collective-permute-start.97 = (bf16[256,2048]{1,0:T(8,128)(2,1)S(1)}, bf16[256,2048]{1,0:T(8,128)(2,1)S(1)}, u32[]{:S(2)}, u32[]{:S(2)}) collective-permute-start(bf16[256,2048]{1,0:T(8,128)(2,1)S(1)} %pad_maximum_fusion.14), channel_id=1, source_target_pairs={{0,8},{4,12},{8,0},{12,4},{16,24},{20,28},{24,16},{28,20},{1,9},{5... | collective-permute-start | bytes 3145736 | tf_op jit(solution)/shard_map/ppermute | solution.py:42
  809.4 34.3 %collective-permute-start.98 = (bf16[256,2048]{1,0:T(8,128)(2,1)S(1)}, bf16[256,2048]{1,0:T(8,128)(2,1)}, u32[]{:S(2)}, u32[]{:S(2)}) collective-permute-start(bf16[256,2048]{1,0:T(8,128)(2,1)S(1)} %pad_maximum_fusion.15), channel_id=1, source_target_pairs={{0,16},{4,20},{8,24},{12,28},{16,0},{20,4},{24,8},{28,12},{1,17},{... | collective-permute-start | bytes 3145736 | tf_op jit(solution)/shard_map/ppermute | solution.py:42
  911.1 36.0 %collective-permute-start.108 = (bf16[256,2048]{1,0:T(8,128)(2,1)}, bf16[256,2048]{1,0:T(8,128)(2,1)}, u32[]{:S(2)}, u32[]{:S(2)}) collective-permute-start(bf16[256,2048]{1,0:T(8,128)(2,1)} %pad_maximum_fusion.17), channel_id=1, source_target_pairs={{0,8},{4,12},{8,0},{12,4},{16,24},{20,28},{24,16},{28,20},{1,9},{5... | collective-permute-start | bytes 3145736 | tf_op jit(solution)/shard_map/ppermute | solution.py:42
  911.5 35.7 %collective-permute-start.109 = (bf16[256,2048]{1,0:T(8,128)(2,1)}, bf16[256,2048]{1,0:T(8,128)(2,1)}, u32[]{:S(2)}, u32[]{:S(2)}) collective-permute-start(bf16[256,2048]{1,0:T(8,128)(2,1)} %pad_maximum_fusion.18), channel_id=1, source_target_pairs={{0,16},{4,20},{8,24},{12,28},{16,0},{20,4},{24,8},{28,12},{1,17},{... | collective-permute-start | bytes 3145736 | tf_op jit(solution)/shard_map/ppermute | solution.py:42
  913.6 35.7 %collective-permute-start.110 = (bf16[2,8,64,512]{3,2,1,0:T(8,128)(2,1)}, bf16[2,8,64,512]{3,2,1,0:T(8,128)(2,1)}, u32[]{:S(2)}, u32[]{:S(2)}) collective-permute-start(bf16[2,8,64,512]{3,2,1,0:T(8,128)(2,1)} %slice.682), channel_id=1, source_target_pairs={{0,1},{1,0},{2,3},{3,2},{4,5},{5,4},{6,7},{7,6},{8,9},{9,8},{10,11... | collective-permute-start | bytes 3145736 | tf_op jit(solution)/shard_map/ppermute | solution.py:42
  915.1 32.0 %collective-permute-start.112 = (bf16[128,2048]{1,0:T(8,128)(2,1)}, bf16[128,2048]{1,0:T(8,128)(2,1)}, u32[]{:S(2)}, u32[]{:S(2)}) collective-permute-start(bf16[128,2048]{1,0:T(8,128)(2,1)} %get-tuple-element.602), channel_id=1, source_target_pairs={{0,2},{1,3},{2,0},{3,1},{4,6},{5,7},{6,4},{7,5},{8,10},{9,11},{10,... | collective-permute-start | bytes 1572872 | tf_op jit(solution)/shard_map/ppermute | solution.py:42
  953.9 34.3 %collective-permute-start.116 = (bf16[2,256,1024]{2,1,0:T(8,128)(2,1)S(1)}, bf16[2,256,1024]{2,1,0:T(8,128)(2,1)}, u32[]{:S(2)}, u32[]{:S(2)}) collective-permute-start(bf16[2,256,1024]{2,1,0:T(8,128)(2,1)S(1)} %get-tuple-element.615), channel_id=1, source_target_pairs={{0,1},{1,0},{2,3},{3,2},{4,5},{5,4},{6,7},{7,6},{8,9},{9,8},{10,11... | collective-permute-start | bytes 3145736 | tf_op jit(solution)/shard_map/ppermute | solution.py:42
  991.4 34.4 %collective-permute-start.119 = (bf16[2,256,1024]{2,1,0:T(8,128)(2,1)}, bf16[2,256,1024]{2,1,0:T(8,128)(2,1)}, u32[]{:S(2)}, u32[]{:S(2)}) collective-permute-start(bf16[2,256,1024]{2,1,0:T(8,128)(2,1)} %get-tuple-element.624), channel_id=1, source_target_pairs={{0,1},{1,0},{2,3},{3,2},{4,5},{5,4},{6,7},{7,6},{8,9},{9,8},{10,11... | collective-permute-start | bytes 3145736 | tf_op jit(solution)/shard_map/ppermute | solution.py:42
  993.8 31.2 %collective-permute-start.118 = (bf16[128,2048]{1,0:T(8,128)(2,1)}, bf16[128,2048]{1,0:T(8,128)(2,1)}, u32[]{:S(2)}, u32[]{:S(2)}) collective-permute-start(bf16[128,2048]{1,0:T(8,128)(2,1)} %get-tuple-element.623), channel_id=1, source_target_pairs={{0,2},{1,3},{2,0},{3,1},{4,6},{5,7},{6,4},{7,5},{8,10},{9,11},{10,... | collective-permute-start | bytes 1572872 | tf_op jit(solution)/shard_map/ppermute | solution.py:42
  (233 other events, 3243.4 us)

commit v12 on v11

--- a/solution.py
+++ b/solution.py
@@ -954,17 +954,7 @@
             own_quarters, far_quarters, down_rows, upstream_halves, small = prepared
             partner_up = [far_swap(upstream_halves[0])]
     token_more = gather_more(tokens_low, token_first, S)
-    rank_part = small[:, :, part * (E + 4) :].reshape(S, F, E, T)
-
-    def ranks_of(index):
-        ranks = lax.dynamic_slice(rank_part, (0, index, s * experts, 0), (S, 1, experts, T))
-        ranks = relative(ranks[:, 0], s).astype(jnp.int32)
-        return ranks[: S // 2], ranks[S // 2 :]
-
-    own_ranks, other_ranks = ranks_of(f), ranks_of(f ^ half_f)
-    qkv_pieces, partner_up[0], token_more, own_ranks, other_ranks = tie(
-        qkv_pieces, partner_up[0], token_more, own_ranks, other_ranks
-    )
+    qkv_pieces, partner_up[0], token_more = tie(qkv_pieces, partner_up[0], token_more)
     tokens_even, tokens_odd = gather_end(tokens_low, token_first, token_more, S)
     w_qkv = place_fsdp(qkv_pieces, f, 1).reshape(D, 3 * C)
 
@@ -1012,8 +1002,11 @@
     out_more = gather_more(own_output, out_first, S)
     far.append(far_part(1, query_low))
     near_own.append(near_swap(own_quarters[3], query_low))
+    down = [near_swap(down_rows[0], query_low)]
     attended, lse = attention_forward(query_low, key_low, value_low, seg_row, seg_col)
-    attended, out_more, far[1], near_own[2] = tie(attended, out_more, far[1], near_own[2])
+    attended, out_more, far[1], near_own[2], down[0] = tie(
+        attended, out_more, far[1], near_own[2], down[0]
+    )
     attended_blocks = attended.reshape(S, T, C)
     come = lax.all_to_all(attended_blocks, "seq", split_axis=0, concat_axis=0, tiled=True)
     out_even, out_odd = gather_end(own_output, out_first, out_more, S)
@@ -1023,17 +1016,26 @@
     come, far[2], near_far[0], own_up_more = tie(come, far[2], near_far[0], own_up_more)
     own_u = gather_end(upstream_low, own_up_first, own_up_more, S)
     near_far.append(near_swap(far[1], come))
-    down = [near_swap(down_rows[0], come)]
     partner_up_first = gather_first(after(partner_up, come), S)
     residual, second_low = project_out(come, out_even, out_odd, tokens_low, gain_moe[None], me)
-    second_low, down[0], near_far[1], partner_up_first, own_u = tie(
-        second_low, down[0], near_far[1], partner_up_first, own_u
+    second_low, near_far[1], partner_up_first, own_u = tie(
+        second_low, near_far[1], partner_up_first, own_u
     )
 
     own_first = gather_first(second_low, S)
     partner_low = [far_swap(second_low[:half_rows])]
     near_far.append(near_swap(far[2], second_low))
-    own_first, partner_low[0], near_far[2] = tie(own_first, partner_low[0], near_far[2])
+    rank_part = after(small, second_low)[:, :, part * (E + 4) :].reshape(S, F, E, T)
+
+    def ranks_of(index):
+        ranks = lax.dynamic_slice(rank_part, (0, index, s * experts, 0), (S, 1, experts, T))
+        ranks = relative(ranks[:, 0], s).astype(jnp.int32)
+        return ranks[: S // 2], ranks[S // 2 :]
+
+    own_ranks, other_ranks = ranks_of(f), ranks_of(f ^ half_f)
+    own_first, partner_low[0], near_far[2], own_ranks, other_ranks = tie(
+        own_first, partner_low[0], near_far[2], own_ranks, other_ranks
+    )
     own_more = gather_more(second_low, own_first, S)
     partner_low.append(far_swap(second_low[half_rows:], own_first))
     down.append(near_swap(down_rows[1], own_first))
@@ -1248,6 +1250,7 @@
         means, come, far_sums[3], output_got, value_term
     )
     other_outs = add_all(other_total, come).astype(BF16)
+    outs_back = [far_swap(other_outs[:half_rows])]
     value_got = swap(value_term[: F // 2], "fsdp", F, 1)
     pre_rel = rope_back(
         (query_back, key_back, value_back),
@@ -1263,7 +1266,9 @@
     ).reshape(2, L // 2, 3 * C)
     normed_got = swap(matmul_t(pre_rel[1], w_qkv).astype(BF16), "seq", S, 1)
     normed_kept = matmul_t(pre_rel[0], w_qkv).astype(BF16)
-    normed_got, normed_kept, value_got = tie(normed_got, normed_kept, value_got)
+    normed_got, normed_kept, value_got, outs_back[0] = tie(
+        normed_got, normed_kept, value_got, outs_back[0]
+    )
 
     normed_sums = sum_cores(normed_kept, normed_got, S)
     come = sum_first(normed_sums, S)
@@ -1292,10 +1297,7 @@
     gain_got = swap(gain_terms[F // 2 :], "fsdp", F, half_f)
     for r in near_odd:
         in_products(r ^ 1, turned_term)
-    outs_back = [far_swap(other_outs[:half_rows], turned_term)]
-    come, turned_got, gain_got, in_terms, outs_back[0] = tie(
-        come, turned_got, gain_got, in_terms, outs_back[0]
-    )
+    come, turned_got, gain_got, in_terms = tie(come, turned_got, gain_got, in_terms)
     gain_terms = gain_terms[: F // 2] + gain_got
     normed_grads = add_all(normed_total, come)
     turned_sum = sum_rest(sum_even(turned_term, turned_got, F), F)

time: 1060 us -> 1060 us (level)
    unnamed x339 -> x355, local copies, waits for them, and re-layouts: 63.6 us -> 69.3 us
  transfers between devices with their start and end apart: 127 -> 127, of which waited for: 61 -> 61; matrix products, arithmetic and copies ran while one was open for 18% -> 19% of each run, Pallas kernels for 24% -> 24%
where the time goes in v12:
time: 1060 us; the launch traced here: 1050 us
  waiting for transfers between devices  330 us (31%)
  Pallas kernels  263 us (25%)
  local copies, waits for them, and re-layouts  151 us (14%)
  starting transfers between devices  137 us (13%)
  other arithmetic  113 us (11%)
  matrix products  40.7 us (4%)
    ppermute x124, waiting for transfers between devices, swap(): return lax.ppermute(values, axis, [(i, i ^ mask) for i in range(size)])  330 us
    ppermute x124, starting transfers between devices, swap(): return lax.ppermute(values, axis, [(i, i ^ mask) for i in range(size)])  125 us
    pallas_call x2, Pallas kernels, run_experts(): pl.pallas_call(partial(expert_kernel, in_places, down_places), grid=(step...  118 us
    unnamed x355, local copies, waits for them, and re-layouts  69.3 us
    pallas_call x6, Pallas kernels, products(): pl.pallas_call(product_kernel, grid_spec=pltpu.PrefetchScalarGridSpec(num...  60.6 us
    pallas_call x1, Pallas kernels, attention_backward(): pl.pallas_call(partial(backward_kernel, span), grid=(heads, length // row...  28.3 us
    pallas_call x1, Pallas kernels, attention_forward(): pl.pallas_call(partial(forward_kernel, span), grid=(heads, length // rows...  21.7 us
  transfers between devices with their start and end apart: 127, of which 61 were waited for; matrix products, arithmetic and copies ran while one was open for 19% of the time, Pallas kernels for 24%

profile of v12, /device:TPU:0, one launch (start us, length us, event | category | flops | bytes accessed | tf_op | source)
XLA Modules:
  0.0 1045.9 jit_solution(12917770811894392739)
XLA Ops:
  30.5 8.6 collective-permute-done.4
  71.1 12.8 %collective-permute-done.7 = bf16[8,64,768]{2,1,0:T(8,128)(2,1)} collective-permute-done((bf16[8,64,768]{2,1,0:T(8,128)(2,1)S(1)}, bf16[8,64,768]{2,1,0:T(8,128)(2,1)}, u32[]{:S(2)}, u32[]{:S(2)}) %collective-permute-start.7) | collective-permute-done | bytes 786464 | tf_op jit(solution)/shard_map/ppermute | solution.py:42
  100.0 14.3 %collective-permute-done.12 = bf16[128,2048]{1,0:T(8,128)(2,1)} collective-permute-done((bf16[128,2048]{1,0:T(8,128)(2,1)S(1)}, bf16[128,2048]{1,0:T(8,128)(2,1)}, u32[]{:S(2)}, u32[]{:S(2)}) %collective-permute-start.12) | collective-permute-done | bytes 524320 | tf_op jit(solution)/shard_map/ppermute | solution.py:42
  133.6 12.6 %project.1 = (bf16[1024,2048]{1,0:T(8,128)(2,1)}, bf16[1024,2048]{1,0:T(8,128)(2,1)}, f32[2048,256]{1,0:T(8,128)S(1)}, f32[2048,256]{1,0:T(8,128)S(1)}, bf16[204...) custom-call(s32[1]{0:T(128)} %bitcast.me_ref, bf16[1024,2048]{1,0:T(8,128)(2,1)} %constant_dynamic-update-slice_fusion.even_ref, ...), custom_call_target="tpu_custom_call" | custom-call | flops 6442450944 | bytes 25165824 | tf_op jit(solution)/shard_map/project/pallas_call | solution.py:437
  175.7 10.8 %collective-permute-done.22 = f32[2,2048]{1,0:T(2,128)S(1)} collective-permute-done((f32[2,2048]{1,0:T(2,128)S(1)}, f32[2,2048]{1,0:T(2,128)S(1)}, u32[]{:S(2)}, u32[]{:S(2)}) %collective-permute-start.22) | collective-permute-done | bytes 16416 | tf_op jit(solution)/shard_map/ppermute | solution.py:42
  212.2 21.7 %attend.1 = (bf16[2048,256]{1,0:T(8,128)(2,1)S(1)}, f32[2,1,2048]{2,1,0:T(1,128)S(1)}) custom-call(bf16[2048,256]{1,0:T(8,128)(2,1)S(1)} %get-tuple-element.372.q_ref, bf16[2048,256]{1,0:T(8,128)(2,1)S(1)} %get-tuple-element.373.k_ref, bf16[2048,256]{1,0:T(8,128)(2,1)S(1)} %copy-done.28, s32[1,2048]{1,0:T(1,128)S(1)} %copy-done.22, s32[2048,1]{1,0:T(8,128)S(1)} %copy-done.17), custom_call_target="tpu_custom_call" | custom-call | flops 2684354560 | bytes 4194304 | tf_op jit(solution)/shard_map/attend/pallas_call | solution.py:336
  252.2 16.8 %collective-permute-done.34.refs_10_ = bf16[2,128,1024]{2,1,0:T(8,128)(2,1)S(1)} collective-permute-done((bf16[2,128,1024]{2,1,0:T(8,128)(2,1)}, bf16[2,128,1024]{2,1,0:T(8,128)(2,1)S(1)}, u32[]{:S(2)}, u32[]{:S(2)}) %collective-permute-start.34) | collective-permute-done | bytes 524320 | tf_op jit(solution)/shard_map/ppermute | solution.py:42
  285.7 8.2 project_out.1
  296.3 8.6 collective-permute-done.39
  323.4 13.0 %collective-permute-done.45.refs_12_ = bf16[2,128,1024]{2,1,0:T(8,128)(2,1)S(1)} collective-permute-done((bf16[2,128,1024]{2,1,0:T(8,128)(2,1)}, bf16[2,128,1024]{2,1,0:T(8,128)(2,1)S(1)}, u32[]{:S(2)}, u32[]{:S(2)}) %collective-permute-start.45) | collective-permute-done | bytes 524320 | tf_op jit(solution)/shard_map/ppermute | solution.py:42
  352.2 10.5 %collective-permute-done.49.refs_19_ = bf16[2,64,2048]{2,1,0:T(8,128)(2,1)S(1)} collective-permute-done((bf16[2,64,2048]{2,1,0:T(8,128)(2,1)S(1)}, bf16[2,64,2048]{2,1,0:T(8,128)(2,1)S(1)}, u32[]{:S(2)}, u32[]{:S(2)}) %collective-permute-start.49) | collective-permute-done | bytes 524320 | tf_op jit(solution)/shard_map/ppermute | solution.py:42
  369.2 22.8 %collective-permute-done.56.refs_9_ = bf16[2,128,1024]{2,1,0:T(8,128)(2,1)S(1)} collective-permute-done((bf16[2,128,1024]{2,1,0:T(8,128)(2,1)S(1)}, bf16[2,128,1024]{2,1,0:T(8,128)(2,1)S(1)}, u32[]{:S(2)}, u32[]{:S(2)}) %collective-permute-start.56) | collective-permute-done | bytes 524320 | tf_op jit(solution)/shard_map/ppermute | solution.py:42
  405.5 7.4 collective-permute-done.61.refs_13_
  412.9 10.9 %collective-permute-done.59.refs_21_ = bf16[2,64,2048]{2,1,0:T(8,128)(2,1)S(1)} collective-permute-done((bf16[2,64,2048]{2,1,0:T(8,128)(2,1)S(1)}, bf16[2,64,2048]{2,1,0:T(8,128)(2,1)S(1)}, u32[]{:S(2)}, u32[]{:S(2)}) %collective-permute-start.59) | collective-permute-done | bytes 524320 | tf_op jit(solution)/shard_map/ppermute | solution.py:42
  431.6 59.4 %experts.2 = (bf16[1024,2048]{1,0:T(8,128)(2,1)}, bf16[1024,2048]{1,0:T(8,128)(2,1)}, bf16[1024,2048]{1,0:T(8,128)(2,1)}, bf16[1024,2048]{1,0:T(8,128)(2,1)}, f3...) custom-call(s32[2]{0:T(128)} %pad_add_fusion.first_ref, ...), custom_call_target="tpu_custom_call" | custom-call | flops 38654705664 | bytes 62914560 | tf_op jit(solution)/shard_map/experts/pallas_call | solution.py:787
  491.6 59.1 %experts.3 = (bf16[1024,2048]{1,0:T(8,128)(2,1)}, bf16[1024,2048]{1,0:T(8,128)(2,1)}, bf16[1024,2048]{1,0:T(8,128)(2,1)}, bf16[1024,2048]{1,0:T(8,128)(2,1)}, f3...) custom-call(s32[2]{0:T(128)} %pad_add_fusion.first_ref, ...), custom_call_target="tpu_custom_call", output_to_operand_aliasing={{6}: (30, {}), {7}: (31, {}), {8}: (32, {}), {9}: (33, {})} | custom-call | flops 38654705664 | bytes 62914560 | tf_op jit(solution)/shard_map/experts/pallas_call | solution.py:787
  555.1 8.2 all_to_all.27
  568.4 9.7 in_products.4
  592.7 11.0 %down_products.2 = bf16[2,256,2048]{2,1,0:T(8,128)(2,1)} custom-call(s32[1]{0:T(128)} %bitcast.22.me_ref, bf16[2,2304,512]{2,1,0:T(8,128)(2,1)} %get-tuple-element.548.left_ref, bf16[2,2304,2048]{2,1,0:T(8,128)(2,1)} %get-tuple-element.522.right_ref), custom_call_target="tpu_custom_call" | custom-call | flops 4831838208 | bytes 21233664 | tf_op jit(solution)/shard_map/down_products/pallas_call | solution.py:824
  603.8 8.7 collective-permute-done.70
  628.9 9.3 in_products.5
  638.8 11.2 %collective-permute-done.75 = bf16[128,2048]{1,0:T(8,128)(2,1)} collective-permute-done((bf16[128,2048]{1,0:T(8,128)(2,1)}, bf16[128,2048]{1,0:T(8,128)(2,1)}, u32[]{:S(2)}, u32[]{:S(2)}) %collective-permute-start.75) | collective-permute-done | bytes 524320 | tf_op jit(solution)/shard_map/ppermute | solution.py:42
  664.2 9.9 in_products.6
  674.1 8.7 collective-permute-done.80
  702.3 11.0 %down_products.3 = bf16[2,256,2048]{2,1,0:T(8,128)(2,1)} custom-call(s32[1]{0:T(128)} %bitcast.22.me_ref, bf16[2,2304,512]{2,1,0:T(8,128)(2,1)} %get-tuple-element.548.left_ref, bf16[2,2304,2048]{2,1,0:T(8,128)(2,1)} %get-tuple-element.522.right_ref), custom_call_target="tpu_custom_call" | custom-call | flops 4831838208 | bytes 21233664 | tf_op jit(solution)/shard_map/down_products/pallas_call | solution.py:824
  714.6 8.1 collective-permute-done.83
  745.8 13.8 %collective-permute-done.89 = bf16[2,64,2048]{2,1,0:T(8,128)(2,1)S(1)} collective-permute-done((bf16[2,64,2048]{2,1,0:T(8,128)(2,1)S(1)}, bf16[2,64,2048]{2,1,0:T(8,128)(2,1)S(1)}, u32[]{:S(2)}, u32[]{:S(2)}) %collective-permute-start.89) | collective-permute-done | bytes 524320 | tf_op jit(solution)/shard_map/ppermute | solution.py:42
  768.6 28.3 %attend_back.1 = (bf16[2048,256]{1,0:T(8,128)(2,1)S(1)}, bf16[2048,256]{1,0:T(8,128)(2,1)S(1)}, bf16[2048,256]{1,0:T(8,128)(2,1)S(1)}) custom-call(bf16[2048,256]{1,0:T(8,128)(2,1)S(1)} %copy-done.24, bf16[2048,256]{1,0:T(8,128)(2,1)S(1)} %copy-done.26, bf16[2048,256]{1,0:T(8,128)(2,1)} %copy-done.27, bf16[2048,256]{1,0:T(8,128)(2,1)} %bitcast.358, ...), custom_call_target="tpu_custom_call" | custom-call | flops 6710886400 | bytes 7340032 | tf_op jit(solution)/shard_map/attend_back/pallas_call | solution.py:368
  862.7 15.5 %collective-permute-done.103 = bf16[128,2048]{1,0:T(8,128)(2,1)S(1)} collective-permute-done((bf16[128,2048]{1,0:T(8,128)(2,1)S(1)}, bf16[128,2048]{1,0:T(8,128)(2,1)S(1)}, u32[]{:S(2)}, u32[]{:S(2)}) %collective-permute-start.103) | collective-permute-done | bytes 524320 | tf_op jit(solution)/shard_map/ppermute | solution.py:42
  930.0 9.6 in_products.7
  968.6 15.6 %collective-permute-done.113 = bf16[1,8,64,512]{3,2,1,0:T(8,128)(2,1)S(1)} collective-permute-done((bf16[1,8,64,512]{3,2,1,0:T(8,128)(2,1)S(1)}, bf16[1,8,64,512]{3,2,1,0:T(8,128)(2,1)S(1)}, u32[]{:S(2)}, u32[]{:S(2)}) %collective-permute-start.113) | collective-permute-done | bytes 524320 | tf_op jit(solution)/shard_map/ppermute | solution.py:42
  1009.7 10.8 %collective-permute-done.118 = bf16[128,2048]{1,0:T(8,128)(2,1)} collective-permute-done((bf16[128,2048]{1,0:T(8,128)(2,1)}, bf16[128,2048]{1,0:T(8,128)(2,1)}, u32[]{:S(2)}, u32[]{:S(2)}) %collective-permute-start.118) | collective-permute-done | bytes 524320 | tf_op jit(solution)/shard_map/ppermute | solution.py:42
  (823 shorter events, 555.7 us)
Async XLA Ops:
  49.6 39.5 %collective-permute-start.10 = (bf16[256,2048]{1,0:T(8,128)(2,1)S(1)}, bf16[256,2048]{1,0:T(8,128)(2,1)S(1)}, u32[]{:S(2)}, u32[]{:S(2)}) collective-permute-start(bf16[256,2048]{1,0:T(8,128)(2,1)S(1)} %bitcast.319), channel_id=1, source_target_pairs={{0,16},{4,20},{8,24},{12,28},{16,0},{20,4},{24,8},{28,12},{1,17},{... | collective-permute-start | bytes 3145736 | tf_op jit(solution)/shard_map/ppermute | solution.py:42
  51.1 38.0 %collective-permute-start.9 = (bf16[256,2048]{1,0:T(8,128)(2,1)S(1)}, bf16[256,2048]{1,0:T(8,128)(2,1)}, u32[]{:S(2)}, u32[]{:S(2)}) collective-permute-start(bf16[256,2048]{1,0:T(8,128)(2,1)S(1)} %bitcast.320), channel_id=1, source_target_pairs={{0,8},{4,12},{8,0},{12,4},{16,24},{20,28},{24,16},{28,20},{1,9},{5... | collective-permute-start | bytes 3145736 | tf_op jit(solution)/shard_map/ppermute | solution.py:42
  52.6 31.3 %collective-permute-start.7 = (bf16[8,64,768]{2,1,0:T(8,128)(2,1)S(1)}, bf16[8,64,768]{2,1,0:T(8,128)(2,1)}, u32[]{:S(2)}, u32[]{:S(2)}) collective-permute-start(bf16[8,64,768]{2,1,0:T(8,128)(2,1)S(1)} %all-to-all-done), channel_id=1, source_target_pairs={{0,1},{1,0},{2,3},{3,2},{4,5},{5,4},{6,7},{7,6},{8,9},{9,8},{10,11... | collective-permute-start | bytes 2359304 | tf_op jit(solution)/shard_map/ppermute | solution.py:42
  55.0 34.1 %collective-permute-start.8 = (bf16[8,64,768]{2,1,0:T(8,128)(2,1)S(1)}, bf16[8,64,768]{2,1,0:T(8,128)(2,1)}, u32[]{:S(2)}, u32[]{:S(2)}) collective-permute-start(bf16[8,64,768]{2,1,0:T(8,128)(2,1)S(1)} %all-to-all-done), channel_id=1, source_target_pairs={{0,2},{1,3},{2,0},{3,1},{4,6},{5,7},{6,4},{7,5},{8,10},{9,11},{10,... | collective-permute-start | bytes 2359304 | tf_op jit(solution)/shard_map/ppermute | solution.py:42
  122.8 33.1 %collective-permute-start.19 = (bf16[256,2048]{1,0:T(8,128)(2,1)}, bf16[256,2048]{1,0:T(8,128)(2,1)}, u32[]{:S(2)}, u32[]{:S(2)}) collective-permute-start(bf16[256,2048]{1,0:T(8,128)(2,1)} %bitcast.4), channel_id=1, source_target_pairs={{0,8},{4,12},{8,0},{12,4},{16,24},{20,28},{24,16},{28,20},{1,9},{5... | collective-permute-start | bytes 3145736 | tf_op jit(solution)/shard_map/ppermute | solution.py:42
  123.4 32.5 %collective-permute-start.20 = (bf16[256,2048]{1,0:T(8,128)(2,1)}, bf16[256,2048]{1,0:T(8,128)(2,1)}, u32[]{:S(2)}, u32[]{:S(2)}) collective-permute-start(bf16[256,2048]{1,0:T(8,128)(2,1)} %bitcast.4), channel_id=1, source_target_pairs={{0,16},{4,20},{8,24},{12,28},{16,0},{20,4},{24,8},{28,12},{1,17},{... | collective-permute-start | bytes 3145736 | tf_op jit(solution)/shard_map/ppermute | solution.py:42
  161.8 33.8 %collective-permute-start.24 = (bf16[256,2048]{1,0:T(8,128)(2,1)}, bf16[256,2048]{1,0:T(8,128)(2,1)}, u32[]{:S(2)}, u32[]{:S(2)}) collective-permute-start(bf16[256,2048]{1,0:T(8,128)(2,1)} %bitcast.18), channel_id=1, source_target_pairs={{0,8},{4,12},{8,0},{12,4},{16,24},{20,28},{24,16},{28,20},{1,9},{5... | collective-permute-start | bytes 3145736 | tf_op jit(solution)/shard_map/ppermute | solution.py:42
  163.3 32.3 %collective-permute-start.25 = (bf16[256,2048]{1,0:T(8,128)(2,1)}, bf16[256,2048]{1,0:T(8,128)(2,1)}, u32[]{:S(2)}, u32[]{:S(2)}) collective-permute-start(bf16[256,2048]{1,0:T(8,128)(2,1)} %bitcast.18), channel_id=1, source_target_pairs={{0,16},{4,20},{8,24},{12,28},{16,0},{20,4},{24,8},{28,12},{1,17},{... | collective-permute-start | bytes 3145736 | tf_op jit(solution)/shard_map/ppermute | solution.py:42
  195.6 39.3 %collective-permute-start.32 = (bf16[2,64,2048]{2,1,0:T(8,128)(2,1)S(1)}, bf16[2,64,2048]{2,1,0:T(8,128)(2,1)S(1)}, u32[]{:S(2)}, u32[]{:S(2)}) collective-permute-start(bf16[2,64,2048]{2,1,0:T(8,128)(2,1)S(1)} %copy-done.107), channel_id=1, source_target_pairs={{0,1},{1,0},{2,3},{3,2},{4,5},{5,4},{6,7},{7,6},{8,9},{9,8},{10,11... | collective-permute-start | bytes 1572872 | tf_op jit(solution)/shard_map/ppermute | solution.py:42
  195.8 40.4 %collective-permute-start.31 = (bf16[2,128,1024]{2,1,0:T(8,128)(2,1)S(1)}, bf16[2,128,1024]{2,1,0:T(8,128)(2,1)S(1)}, u32[]{:S(2)}, u32[]{:S(2)}) collective-permute-start(bf16[2,128,1024]{2,1,0:T(8,128)(2,1)S(1)} %copy-done.95), channel_id=1, source_target_pairs={{0,1},{1,0},{2,3},{3,2},{4,5},{5,4},{6,7},{7,6},{8,9},{9,8},{10,11... | collective-permute-start | bytes 1572872 | tf_op jit(solution)/shard_map/ppermute | solution.py:42
  197.7 40.0 %collective-permute-start.30 = (bf16[2,128,1024]{2,1,0:T(8,128)(2,1)S(1)}, bf16[2,128,1024]{2,1,0:T(8,128)(2,1)S(1)}, u32[]{:S(2)}, u32[]{:S(2)}) collective-permute-start(bf16[2,128,1024]{2,1,0:T(8,128)(2,1)S(1)} %copy-done.98), channel_id=1, source_target_pairs={{0,2},{1,3},{2,0},{3,1},{4,6},{5,7},{6,4},{7,5},{8,10},{9,11},{10,... | collective-permute-start | bytes 1572872 | tf_op jit(solution)/shard_map/ppermute | solution.py:42
  201.3 36.5 %collective-permute-start.28 = (bf16[128,2048]{1,0:T(8,128)(2,1)S(1)}, bf16[128,2048]{1,0:T(8,128)(2,1)}, u32[]{:S(2)}, u32[]{:S(2)}) collective-permute-start(bf16[128,2048]{1,0:T(8,128)(2,1)S(1)} %slice.566), channel_id=1, source_target_pairs={{0,16},{4,20},{8,24},{12,28},{16,0},{20,4},{24,8},{28,12},{1,17},{... | collective-permute-start | bytes 1572872 | tf_op jit(solution)/shard_map/ppermute | solution.py:42
  203.0 34.7 %collective-permute-start.29 = (bf16[128,2048]{1,0:T(8,128)(2,1)S(1)}, bf16[128,2048]{1,0:T(8,128)(2,1)}, u32[]{:S(2)}, u32[]{:S(2)}) collective-permute-start(bf16[128,2048]{1,0:T(8,128)(2,1)S(1)} %slice.567), channel_id=1, source_target_pairs={{0,8},{4,12},{8,0},{12,4},{16,24},{20,28},{24,16},{28,20},{1,9},{5... | collective-permute-start | bytes 1572872 | tf_op jit(solution)/shard_map/ppermute | solution.py:42
  238.5 33.7 %all-to-all-start.1 = ((bf16[8,256,256]{2,1,0:T(8,128)(2,1)}), bf16[8,256,256]{2,1,0:T(8,128)(2,1)S(1)}, u32[]{:S(2)}, u32[]{:S(2)}) async-start(bf16[8,256,256]{2,1,0:T(8,128)(2,1)} %bitcast.322), calls=%async_computation.1 | async-start | bytes 2097152 | tf_op jit(solution)/shard_map/all_to_all | solution.py:1011
  252.1 30.2 %collective-permute-start.37 = (bf16[1024,2048]{1,0:T(8,128)(2,1)}, bf16[1024,2048]{1,0:T(8,128)(2,1)}, u32[]{:S(2)}, u32[]{:S(2)}) collective-permute-start(bf16[1024,2048]{1,0:T(8,128)(2,1)} %constant_dynamic-update-slice_fusion.5.even_ref), channel_id=1, source_target_pairs={{0,4},{4,0},{8,12},{12,8},{16,20},{20,16},{24,28},{28,24},{1,5},{5... | collective-permute-start | bytes 12582920 | tf_op jit(solution)/shard_map/ppermute | solution.py:42
  276.3 30.0 %collective-permute-start.41 = (bf16[1024,2048]{1,0:T(8,128)(2,1)}, bf16[1024,2048]{1,0:T(8,128)(2,1)}, u32[]{:S(2)}, u32[]{:S(2)}) collective-permute-start(bf16[1024,2048]{1,0:T(8,128)(2,1)} %constant_dynamic-update-slice_fusion.12.ua_ref), channel_id=1, source_target_pairs={{0,4},{4,0},{8,12},{12,8},{16,20},{20,16},{24,28},{28,24},{1,5},{5... | collective-permute-start | bytes 12582920 | tf_op jit(solution)/shard_map/ppermute | solution.py:42
  308.6 29.8 %collective-permute-start.42 = (bf16[256,2048]{1,0:T(8,128)(2,1)}, bf16[256,2048]{1,0:T(8,128)(2,1)}, u32[]{:S(2)}, u32[]{:S(2)}) collective-permute-start(bf16[256,2048]{1,0:T(8,128)(2,1)} %get-tuple-element.403), channel_id=1, source_target_pairs={{0,8},{4,12},{8,0},{12,4},{16,24},{20,28},{24,16},{28,20},{1,9},{5... | collective-permute-start | bytes 3145736 | tf_op jit(solution)/shard_map/ppermute | solution.py:42
  314.9 31.7 %collective-permute-start.50 = (bf16[128,2048]{1,0:T(8,128)(2,1)S(1)}, bf16[128,2048]{1,0:T(8,128)(2,1)S(1)}, u32[]{:S(2)}, u32[]{:S(2)}) collective-permute-start(bf16[128,2048]{1,0:T(8,128)(2,1)S(1)} %slice.580), channel_id=1, source_target_pairs={{0,16},{4,20},{8,24},{12,28},{16,0},{20,4},{24,8},{28,12},{1,17},{... | collective-permute-start | bytes 1572872 | tf_op jit(solution)/shard_map/ppermute | solution.py:42
  426.3 64.7 %collective-permute-start.62 = (bf16[1024,2048]{1,0:T(8,128)(2,1)}, bf16[1024,2048]{1,0:T(8,128)(2,1)}, u32[]{:S(2)}, u32[]{:S(2)}) collective-permute-start(bf16[1024,2048]{1,0:T(8,128)(2,1)} %constant_dynamic-update-slice_fusion.43.xa_ref), channel_id=1, source_target_pairs={{0,4},{4,0},{8,12},{12,8},{16,20},{20,16},{24,28},{28,24},{1,5},{5... | collective-permute-start | bytes 12582920 | tf_op jit(solution)/shard_map/ppermute | solution.py:42
  491.0 59.7 %collective-permute-start.63 = (bf16[1024,2048]{1,0:T(8,128)(2,1)}, bf16[1024,2048]{1,0:T(8,128)(2,1)}, u32[]{:S(2)}, u32[]{:S(2)}) collective-permute-start(bf16[1024,2048]{1,0:T(8,128)(2,1)} %get-tuple-element.493), channel_id=1, source_target_pairs={{0,4},{4,0},{8,12},{12,8},{16,20},{20,16},{24,28},{28,24},{1,5},{5... | collective-permute-start | bytes 12582920 | tf_op jit(solution)/shard_map/ppermute | solution.py:42
  491.5 59.2 %collective-permute-start.64 = (bf16[1024,2048]{1,0:T(8,128)(2,1)}, bf16[1024,2048]{1,0:T(8,128)(2,1)}, u32[]{:S(2)}, u32[]{:S(2)}) collective-permute-start(bf16[1024,2048]{1,0:T(8,128)(2,1)} %get-tuple-element.494), channel_id=1, source_target_pairs={{0,4},{4,0},{8,12},{12,8},{16,20},{20,16},{24,28},{28,24},{1,5},{5... | collective-permute-start | bytes 12582920 | tf_op jit(solution)/shard_map/ppermute | solution.py:42
  692.2 30.5 %collective-permute-start.81 = (bf16[256,2048]{1,0:T(8,128)(2,1)}, bf16[256,2048]{1,0:T(8,128)(2,1)S(1)}, u32[]{:S(2)}, u32[]{:S(2)}) collective-permute-start(bf16[256,2048]{1,0:T(8,128)(2,1)} %get-tuple-element.705), channel_id=1, source_target_pairs={{0,8},{4,12},{8,0},{12,4},{16,24},{20,28},{24,16},{28,20},{1,9},{5... | collective-permute-start | bytes 3145736 | tf_op jit(solution)/shard_map/ppermute | solution.py:42
  762.3 36.0 %collective-permute-start.91 = (bf16[2,128,2048]{2,1,0:T(8,128)(2,1)S(1)}, bf16[2,128,2048]{2,1,0:T(8,128)(2,1)S(1)}, u32[]{:S(2)}, u32[]{:S(2)}) collective-permute-start(bf16[2,128,2048]{2,1,0:T(8,128)(2,1)S(1)} %concatenate.247), channel_id=1, source_target_pairs={{0,1},{1,0},{2,3},{3,2},{4,5},{5,4},{6,7},{7,6},{8,9},{9,8},{10,11... | collective-permute-start | bytes 3145736 | tf_op jit(solution)/shard_map/ppermute | solution.py:42
  762.3 34.6 %collective-permute-start.90 = (bf16[2,128,1024]{2,1,0:T(8,128)(2,1)S(1)}, bf16[2,128,1024]{2,1,0:T(8,128)(2,1)S(1)}, u32[]{:S(2)}, u32[]{:S(2)}) collective-permute-start(bf16[2,128,1024]{2,1,0:T(8,128)(2,1)S(1)} %copy-done.88), channel_id=1, source_target_pairs={{0,2},{1,3},{2,0},{3,1},{4,6},{5,7},{6,4},{7,5},{8,10},{9,11},{10,... | collective-permute-start | bytes 1572872 | tf_op jit(solution)/shard_map/ppermute | solution.py:42
  767.2 29.7 %collective-permute-start.92 = (bf16[128,2048]{1,0:T(8,128)(2,1)}, bf16[128,2048]{1,0:T(8,128)(2,1)S(1)}, u32[]{:S(2)}, u32[]{:S(2)}) collective-permute-start(bf16[128,2048]{1,0:T(8,128)(2,1)} %get-tuple-element.563), channel_id=1, source_target_pairs={{0,16},{4,20},{8,24},{12,28},{16,0},{20,4},{24,8},{28,12},{1,17},{... | collective-permute-start | bytes 1572872 | tf_op jit(solution)/shard_map/ppermute | solution.py:42
  804.0 33.3 %collective-permute-start.97 = (bf16[256,2048]{1,0:T(8,128)(2,1)S(1)}, bf16[256,2048]{1,0:T(8,128)(2,1)S(1)}, u32[]{:S(2)}, u32[]{:S(2)}) collective-permute-start(bf16[256,2048]{1,0:T(8,128)(2,1)S(1)} %pad_maximum_fusion.14), channel_id=1, source_target_pairs={{0,8},{4,12},{8,0},{12,4},{16,24},{20,28},{24,16},{28,20},{1,9},{5... | collective-permute-start | bytes 3145736 | tf_op jit(solution)/shard_map/ppermute | solution.py:42
  804.5 33.8 %collective-permute-start.98 = (bf16[256,2048]{1,0:T(8,128)(2,1)S(1)}, bf16[256,2048]{1,0:T(8,128)(2,1)}, u32[]{:S(2)}, u32[]{:S(2)}) collective-permute-start(bf16[256,2048]{1,0:T(8,128)(2,1)S(1)} %pad_maximum_fusion.15), channel_id=1, source_target_pairs={{0,16},{4,20},{8,24},{12,28},{16,0},{20,4},{24,8},{28,12},{1,17},{... | collective-permute-start | bytes 3145736 | tf_op jit(solution)/shard_map/ppermute | solution.py:42
  847.0 31.4 %collective-permute-start.101 = (bf16[1024,2048]{1,0:T(8,128)(2,1)}, bf16[1024,2048]{1,0:T(8,128)(2,1)}, u32[]{:S(2)}, u32[]{:S(2)}) collective-permute-start(bf16[1024,2048]{1,0:T(8,128)(2,1)} %convolution_convert_fusion.2), channel_id=1, source_target_pairs={{0,4},{4,0},{8,12},{12,8},{16,20},{20,16},{24,28},{28,24},{1,5},{5... | collective-permute-start | bytes 12582920 | tf_op jit(solution)/shard_map/ppermute | solution.py:42
  953.8 32.6 %collective-permute-start.116 = (bf16[2,256,1024]{2,1,0:T(8,128)(2,1)S(1)}, bf16[2,256,1024]{2,1,0:T(8,128)(2,1)}, u32[]{:S(2)}, u32[]{:S(2)}) collective-permute-start(bf16[2,256,1024]{2,1,0:T(8,128)(2,1)S(1)} %get-tuple-element.615), channel_id=1, source_target_pairs={{0,1},{1,0},{2,3},{3,2},{4,5},{5,4},{6,7},{7,6},{8,9},{9,8},{10,11... | collective-permute-start | bytes 3145736 | tf_op jit(solution)/shard_map/ppermute | solution.py:42
  956.5 30.0 %collective-permute-start.114 = (bf16[256,2048]{1,0:T(8,128)(2,1)S(1)}, bf16[256,2048]{1,0:T(8,128)(2,1)S(1)}, u32[]{:S(2)}, u32[]{:S(2)}) collective-permute-start(bf16[256,2048]{1,0:T(8,128)(2,1)S(1)} %pad_maximum_fusion.19), channel_id=1, source_target_pairs={{0,8},{4,12},{8,0},{12,4},{16,24},{20,28},{24,16},{28,20},{1,9},{5... | collective-permute-start | bytes 3145736 | tf_op jit(solution)/shard_map/ppermute | solution.py:42
  989.7 31.7 %collective-permute-start.119 = (bf16[2,256,1024]{2,1,0:T(8,128)(2,1)}, bf16[2,256,1024]{2,1,0:T(8,128)(2,1)}, u32[]{:S(2)}, u32[]{:S(2)}) collective-permute-start(bf16[2,256,1024]{2,1,0:T(8,128)(2,1)} %get-tuple-element.624), channel_id=1, source_target_pairs={{0,1},{1,0},{2,3},{3,2},{4,5},{5,4},{6,7},{7,6},{8,9},{9,8},{10,11... | collective-permute-start | bytes 3145736 | tf_op jit(solution)/shard_map/ppermute | solution.py:42
  990.8 29.8 %collective-permute-start.118 = (bf16[128,2048]{1,0:T(8,128)(2,1)}, bf16[128,2048]{1,0:T(8,128)(2,1)}, u32[]{:S(2)}, u32[]{:S(2)}) collective-permute-start(bf16[128,2048]{1,0:T(8,128)(2,1)} %get-tuple-element.623), channel_id=1, source_target_pairs={{0,2},{1,3},{2,0},{3,1},{4,6},{5,7},{6,4},{7,5},{8,10},{9,11},{10,... | collective-permute-start | bytes 1572872 | tf_op jit(solution)/shard_map/ppermute | solution.py:42
  (241 other events, 3530.0 us)

commit v13 on v10

--- a/solution.py
+++ b/solution.py
@@ -909,13 +909,6 @@
     ]
     gain_attn, gain_moe = gains[0], gains[1]
     head_gain = lax.dynamic_slice(jnp.stack(gains[2:], 0), (0, s * C), (2, C))
-    rank_part = small[:, :, part * (E + 4) :].reshape(S, F, E, T)
-
-    def ranks_of(index):
-        ranks = lax.dynamic_slice(rank_part, (0, index, s * experts, 0), (S, 1, experts, T))
-        ranks = relative(ranks[:, 0], s).astype(jnp.int32)
-        return ranks[: S // 2], ranks[S // 2 :]
-
     places = jnp.arange(L, dtype=jnp.int32).astype(F32)
     freqs = ROPE_BASE ** (-(jnp.arange(DH // 2, dtype=F32) * 2.0 / DH))
     angles = places[:, None] * freqs[None, :]
@@ -979,6 +972,13 @@
     own_first = gather_first(second_low, S)
     partner_low = [far_swap(second_low[:half_rows])]
     near_far.append(near_swap(far[2], second_low))
+    rank_part = after(small, second_low)[:, :, part * (E + 4) :].reshape(S, F, E, T)
+
+    def ranks_of(index):
+        ranks = lax.dynamic_slice(rank_part, (0, index, s * experts, 0), (S, 1, experts, T))
+        ranks = relative(ranks[:, 0], s).astype(jnp.int32)
+        return ranks[: S // 2], ranks[S // 2 :]
+
     own_ranks, other_ranks = ranks_of(f), ranks_of(f ^ half_f)
     own_first, partner_low[0], near_far[2], own_ranks, other_ranks = tie(
         own_first, partner_low[0], near_far[2], own_ranks, other_ranks
@@ -1054,30 +1054,26 @@
         [to_home(own_parts[4], own_parts[5]), to_home(other_parts[4], other_parts[5])], 1
     ).reshape(S, -1)
     other_got = swap(other_parts[3], "seq", S, 1)
+    gate_grads = lax.all_to_all(gate_grads, "seq", split_axis=0, concat_axis=0, tiled=True)
+    other_got, gate_grads = tie(other_got, gate_grads)
     for r in far_odd:
-        in_products(r)
-    gate_grads = lax.all_to_all(gate_grads, "seq", split_axis=0, concat_axis=0, tiled=True)
-    other_got, in_terms, gate_grads = tie(other_got, in_terms, gate_grads)
-    sent = {r: quarters(in_terms[r], 1) for r in far_odd}
+        in_products(r, other_got)
 
     def send_in(n, *dep):
         return {r: swap(after(sent[r][n], dep), "fsdp", F, 1) for r in sent}
 
     other_sums = sum_cores(other_parts[2], other_got, S)
     come = sum_first(other_sums, S)
-    far_got = [send_in(0, other_got)]
     other_out_got = swap(after(other_parts[1], other_got), "seq", S, 1)
     gate_grads = gate_grads.reshape(S, 2, T * experts)
     partner_grads = far_swap(gate_grads[:, 1])
-    come, far_got[0], other_out_got, partner_grads = tie(
-        come, far_got[0], other_out_got, partner_grads
-    )
+    come, in_terms, other_out_got, partner_grads = tie(
+        come, in_terms, other_out_got, partner_grads
+    )
+    sent = {r: quarters(in_terms[r], 1) for r in far_odd}
     singles, other_total = sum_more(other_sums, come, S)
     come = sum_last(singles, S)
-    middle_sent = {r: jnp.concatenate(sent[r][1:3], 1) for r in sent}
-    middle_got = {
-        r: swap(after(middle_sent[r], far_got[0]), "fsdp", F, 1) for r in middle_sent
-    }
+    start_got = {r: swap(in_terms[r][:, : 2 * quarter], "fsdp", F, 1) for r in far_odd}
 
     def down_products(r, dep):
         down_terms[r] = products(
@@ -1086,31 +1082,35 @@
 
     for r in range(1, half_f, 2):
         down_products(r, singles)
-    come, middle_got, down_terms = tie(come, middle_got, down_terms)
-    for n in range(2):
-        far_got.append({r: got[:, n * quarter : (n + 1) * quarter] for r, got in middle_got.items()})
+    come, start_got, down_terms = tie(come, start_got, down_terms)
+    far_got = [
+        {r: got[:, n * quarter : (n + 1) * quarter] for r, got in start_got.items()}
+        for n in range(2)
+    ]
     other_rows = add_all(other_total, come).astype(BF16)
     gate_grads = gate_grads[:, 0] + partner_grads
     gate_grads = gate_grads.reshape(S, T, experts).transpose(1, 0, 2).reshape(T, E)
     back = [far_swap(other_rows[:half_rows])]
     own_sums = sum_cores(own_parts[2], after(own_got, other_rows), S)
     come = sum_first(own_sums, S)
-    far_got.append(send_in(3, other_rows))
+    far_got.append(send_in(2, other_rows))
     for r in far_odd:
         in_products(r ^ 1, other_rows)
-    come, back[0], far_got[3], in_terms = tie(come, back[0], far_got[3], in_terms)
+    come, back[0], far_got[2], in_terms = tie(come, back[0], far_got[2], in_terms)
     back.append(far_swap(other_rows[half_rows:], come))
     singles, own_total = sum_more(own_sums, come, S)
     come = sum_last(singles, S)
     down_sent = {r: quarters(down_terms[r], 1) for r in range(1, half_f, 2)}
+    for r in down_sent:
+        down_sent[r] = down_sent[r][:2] + [jnp.concatenate(down_sent[r][2:], 1)]
 
     def send_down(n, *dep):
         return {r: swap(after(down_sent[r][n], dep), "fsdp", F, 1) for r in down_sent}
 
-    down_got = [send_down(0, singles)]
+    far_got.append(send_in(3, singles))
     for r in near_odd:
         in_products(r, singles)
-    come, back[1], down_got[0], in_terms = tie(come, back[1], down_got[0], in_terms)
+    come, back[1], far_got[3], in_terms = tie(come, back[1], far_got[3], in_terms)
     row_grads = add_all(own_total, come) + jnp.concatenate(back, 0).astype(F32)
 
     upstream = upstream_low.astype(F32)
@@ -1146,31 +1146,31 @@
 
     branch_first = gather_first(branch_low, S)
     far_sums = [far_sum(0, branch_low)]
-    down_got.append(send_down(1, branch_low))
+    down_got = [send_down(0, branch_low)]
     for r in range(0, half_f, 2):
         down_products(r, branch_low)
-    branch_first, far_sums[0], down_got[1], down_terms = tie(
-        branch_first, far_sums[0], down_got[1], down_terms
+    branch_first, far_sums[0], down_got[0], down_terms = tie(
+        branch_first, far_sums[0], down_got[0], down_terms
     )
     branch_more = gather_more(branch_low, branch_first, S)
     far_sums.append(far_sum(1, branch_first))
-    down_got.append(send_down(2, branch_first))
+    down_got.append(send_down(1, branch_first))
     branch_even, branch_odd = gather_end(branch_low, branch_first, branch_more, S)
 
     head_grads = jnp.concatenate(
         [matmul_t(branch_even, own_output), matmul_t(branch_odd, own_output)], 0
     ).astype(BF16)
     head_grads = absolute(head_grads.reshape(S, T, C), s).reshape(L, C)
-    head_grads, far_sums[1], down_got[2] = tie(head_grads, far_sums[1], down_got[2])
+    head_grads, far_sums[1], down_got[1] = tie(head_grads, far_sums[1], down_got[1])
     far_sums.append(far_sum(2, head_grads))
-    down_got.append(send_down(3, head_grads))
+    down_got.append(send_down(2, head_grads))
     other_out_sums = sum_cores(other_parts[0], after(other_out_got, head_grads), S)
     come, head_grads = sum_first(other_out_sums, S, head_grads)
     query_back, key_back, value_back = attention_backward(
         query_low, key_low, value_low, head_grads, lse, seg_row, seg_col
     )
-    query_back, key_back, value_back, far_sums[2], down_got[3], come = tie(
-        query_back, key_back, value_back, far_sums[2], down_got[3], come
+    query_back, key_back, value_back, far_sums[2], down_got[2], come = tie(
+        query_back, key_back, value_back, far_sums[2], down_got[2], come
     )
 
     singles, other_total = sum_more(other_out_sums, come, S)

time: 1040 us -> 1040 us (level)
  local copies, waits for them, and re-layouts: 141 us -> 152 us
  starting transfers between devices: 150 us -> 139 us
  waiting for transfers between devices: 319 us -> 308 us
    ppermute x125 -> x124, waiting for transfers between devices: 318 us -> 308 us  [swap(): return lax.ppermute(values, axis, [(i, i ^ mask) for i in range(size)])]
    unnamed x346 -> x354, local copies, waits for them, and re-layouts: 59.4 us -> 66.7 us
    ppermute x125 -> x124, starting transfers between devices: 135 us -> 128 us  [swap(): return lax.ppermute(values, axis, [(i, i ^ mask) for i in range(size)])]
  transfers between devices with their start and end apart: 129 -> 127, of which waited for: 60 -> 60; matrix products, arithmetic and copies ran while one was open for 19% -> 20% of each run, Pallas kernels for 24% -> 24%
where the time goes in v13:
time: 1040 us; the launch traced here: 1020 us
  waiting for transfers between devices  308 us (30%)
  Pallas kernels  255 us (25%)
  local copies, waits for them, and re-layouts  152 us (15%)
  starting transfers between devices  139 us (13%)
  other arithmetic  111 us (11%)
  matrix products  47.9 us (5%)
    ppermute x124, waiting for transfers between devices, swap(): return lax.ppermute(values, axis, [(i, i ^ mask) for i in range(size)])  308 us
    ppermute x124, starting transfers between devices, swap(): return lax.ppermute(values, axis, [(i, i ^ mask) for i in range(size)])  128 us
    pallas_call x2, Pallas kernels, run_experts(): pl.pallas_call(partial(expert_kernel, in_places, down_places), grid=(step...  118 us
    unnamed x354, local copies, waits for them, and re-layouts  66.7 us
    pallas_call x6, Pallas kernels, products(): pl.pallas_call(product_kernel, grid_spec=pltpu.PrefetchScalarGridSpec(num...  60.5 us
    pallas_call x1, Pallas kernels, attention_backward(): pl.pallas_call(partial(backward_kernel, span), grid=(heads, length // row...  28.3 us
    pallas_call x1, Pallas kernels, attention_forward(): pl.pallas_call(partial(forward_kernel, span), grid=(heads, length // rows...  21.6 us
  transfers between devices with their start and end apart: 127, of which 60 were waited for; matrix products, arithmetic and copies ran while one was open for 20% of the time, Pallas kernels for 24%

profile of v13, /device:TPU:0, one launch (start us, length us, event | category | flops | bytes accessed | tf_op | source)
XLA Modules:
  0.0 1024.2 jit_solution(13802124763509353992)
XLA Ops:
  30.4 8.6 collective-permute-done.4
  71.1 12.8 %collective-permute-done.7 = bf16[8,64,768]{2,1,0:T(8,128)(2,1)} collective-permute-done((bf16[8,64,768]{2,1,0:T(8,128)(2,1)S(1)}, bf16[8,64,768]{2,1,0:T(8,128)(2,1)}, u32[]{:S(2)}, u32[]{:S(2)}) %collective-permute-start.7) | collective-permute-done | bytes 786464 | tf_op jit(solution)/shard_map/ppermute | solution.py:42
  100.0 14.3 %collective-permute-done.12 = bf16[128,2048]{1,0:T(8,128)(2,1)} collective-permute-done((bf16[128,2048]{1,0:T(8,128)(2,1)S(1)}, bf16[128,2048]{1,0:T(8,128)(2,1)}, u32[]{:S(2)}, u32[]{:S(2)}) %collective-permute-start.12) | collective-permute-done | bytes 524320 | tf_op jit(solution)/shard_map/ppermute | solution.py:42
  128.5 12.6 %project.1 = (bf16[1024,2048]{1,0:T(8,128)(2,1)}, bf16[1024,2048]{1,0:T(8,128)(2,1)}, f32[2048,256]{1,0:T(8,128)S(1)}, f32[2048,256]{1,0:T(8,128)S(1)}, bf16[204...) custom-call(s32[1]{0:T(128)} %bitcast.1.me_ref, bf16[1024,2048]{1,0:T(8,128)(2,1)} %constant_dynamic-update-slice_fusion.even_ref, ...), custom_call_target="tpu_custom_call" | custom-call | flops 6442450944 | bytes 25165824 | tf_op jit(solution)/shard_map/project/pallas_call | solution.py:437
  171.7 10.7 %collective-permute-done.22 = f32[2,2048]{1,0:T(2,128)S(1)} collective-permute-done((f32[2,2048]{1,0:T(2,128)S(1)}, f32[2,2048]{1,0:T(2,128)S(1)}, u32[]{:S(2)}, u32[]{:S(2)}) %collective-permute-start.22) | collective-permute-done | bytes 16416 | tf_op jit(solution)/shard_map/ppermute | solution.py:42
  204.6 21.6 %attend.1 = (bf16[2048,256]{1,0:T(8,128)(2,1)S(1)}, f32[2,1,2048]{2,1,0:T(1,128)S(1)}) custom-call(bf16[2048,256]{1,0:T(8,128)(2,1)S(1)} %get-tuple-element.370.q_ref, bf16[2048,256]{1,0:T(8,128)(2,1)S(1)} %get-tuple-element.371.k_ref, bf16[2048,256]{1,0:T(8,128)(2,1)S(1)} %copy-done.20, s32[1,2048]{1,0:T(1,128)S(1)} %copy-done.14, s32[2048,1]{1,0:T(8,128)S(1)} %copy-done.9), custom_call_target="tpu_custom_call" | custom-call | flops 2684354560 | bytes 4194304 | tf_op jit(solution)/shard_map/attend/pallas_call | solution.py:336
  279.4 6.0 collective-permute-done.37.refs_18_
  306.7 10.7 %collective-permute-done.45.refs_12_ = bf16[2,128,1024]{2,1,0:T(8,128)(2,1)S(1)} collective-permute-done((bf16[2,128,1024]{2,1,0:T(8,128)(2,1)}, bf16[2,128,1024]{2,1,0:T(8,128)(2,1)S(1)}, u32[]{:S(2)}, u32[]{:S(2)}) %collective-permute-start.45) | collective-permute-done | bytes 524320 | tf_op jit(solution)/shard_map/ppermute | solution.py:42
  332.2 10.5 %collective-permute-done.49.refs_19_ = bf16[2,64,2048]{2,1,0:T(8,128)(2,1)S(1)} collective-permute-done((bf16[2,64,2048]{2,1,0:T(8,128)(2,1)S(1)}, bf16[2,64,2048]{2,1,0:T(8,128)(2,1)S(1)}, u32[]{:S(2)}, u32[]{:S(2)}) %collective-permute-start.49) | collective-permute-done | bytes 524320 | tf_op jit(solution)/shard_map/ppermute | solution.py:42
  349.1 22.8 %collective-permute-done.56.refs_9_ = bf16[2,128,1024]{2,1,0:T(8,128)(2,1)S(1)} collective-permute-done((bf16[2,128,1024]{2,1,0:T(8,128)(2,1)S(1)}, bf16[2,128,1024]{2,1,0:T(8,128)(2,1)S(1)}, u32[]{:S(2)}, u32[]{:S(2)}) %collective-permute-start.56) | collective-permute-done | bytes 524320 | tf_op jit(solution)/shard_map/ppermute | solution.py:42
  385.2 7.3 collective-permute-done.61.refs_13_
  392.5 11.1 %collective-permute-done.59.refs_21_ = bf16[2,64,2048]{2,1,0:T(8,128)(2,1)S(1)} collective-permute-done((bf16[2,64,2048]{2,1,0:T(8,128)(2,1)S(1)}, bf16[2,64,2048]{2,1,0:T(8,128)(2,1)S(1)}, u32[]{:S(2)}, u32[]{:S(2)}) %collective-permute-start.59) | collective-permute-done | bytes 524320 | tf_op jit(solution)/shard_map/ppermute | solution.py:42
  411.4 59.4 %experts.2 = (bf16[1024,2048]{1,0:T(8,128)(2,1)}, bf16[1024,2048]{1,0:T(8,128)(2,1)}, bf16[1024,2048]{1,0:T(8,128)(2,1)}, bf16[1024,2048]{1,0:T(8,128)(2,1)}, f3...) custom-call(s32[2]{0:T(128)} %pad_add_fusion.first_ref, ...), custom_call_target="tpu_custom_call" | custom-call | flops 38654705664 | bytes 62914560 | tf_op jit(solution)/shard_map/experts/pallas_call | solution.py:732
  471.4 59.1 %experts.3 = (bf16[1024,2048]{1,0:T(8,128)(2,1)}, bf16[1024,2048]{1,0:T(8,128)(2,1)}, bf16[1024,2048]{1,0:T(8,128)(2,1)}, bf16[1024,2048]{1,0:T(8,128)(2,1)}, f3...) custom-call(s32[2]{0:T(128)} %pad_add_fusion.first_ref, ...), custom_call_target="tpu_custom_call", output_to_operand_aliasing={{6}: (30, {}), {7}: (31, {}), {8}: (32, {}), {9}: (33, {})} | custom-call | flops 38654705664 | bytes 62914560 | tf_op jit(solution)/shard_map/experts/pallas_call | solution.py:732
  535.0 8.1 all_to_all.27
  548.1 9.7 in_products.4
  572.2 11.0 %down_products.2 = bf16[2,256,2048]{2,1,0:T(8,128)(2,1)} custom-call(s32[1]{0:T(128)} %bitcast.25.me_ref, bf16[2,2304,512]{2,1,0:T(8,128)(2,1)} %get-tuple-element.544.left_ref, bf16[2,2304,2048]{2,1,0:T(8,128)(2,1)} %get-tuple-element.518.right_ref), custom_call_target="tpu_custom_call" | custom-call | flops 4831838208 | bytes 21233664 | tf_op jit(solution)/shard_map/down_products/pallas_call | solution.py:769
  583.2 8.9 collective-permute-done.70
  608.6 9.3 in_products.5
  618.5 11.2 %collective-permute-done.75 = bf16[128,2048]{1,0:T(8,128)(2,1)} collective-permute-done((bf16[128,2048]{1,0:T(8,128)(2,1)}, bf16[128,2048]{1,0:T(8,128)(2,1)}, u32[]{:S(2)}, u32[]{:S(2)}) %collective-permute-start.75) | collective-permute-done | bytes 524320 | tf_op jit(solution)/shard_map/ppermute | solution.py:42
  644.0 9.9 in_products.6
  653.9 8.8 collective-permute-done.80
  682.4 11.0 %down_products.3 = bf16[2,256,2048]{2,1,0:T(8,128)(2,1)} custom-call(s32[1]{0:T(128)} %bitcast.25.me_ref, bf16[2,2304,512]{2,1,0:T(8,128)(2,1)} %get-tuple-element.544.left_ref, bf16[2,2304,2048]{2,1,0:T(8,128)(2,1)} %get-tuple-element.518.right_ref), custom_call_target="tpu_custom_call" | custom-call | flops 4831838208 | bytes 21233664 | tf_op jit(solution)/shard_map/down_products/pallas_call | solution.py:769
  694.4 8.4 collective-permute-done.83
  706.1 7.2 collective-permute-done.85
  726.0 13.8 %collective-permute-done.89 = bf16[2,64,2048]{2,1,0:T(8,128)(2,1)S(1)} collective-permute-done((bf16[2,64,2048]{2,1,0:T(8,128)(2,1)S(1)}, bf16[2,64,2048]{2,1,0:T(8,128)(2,1)S(1)}, u32[]{:S(2)}, u32[]{:S(2)}) %collective-permute-start.89) | collective-permute-done | bytes 524320 | tf_op jit(solution)/shard_map/ppermute | solution.py:42
  748.0 28.3 %attend_back.1 = (bf16[2048,256]{1,0:T(8,128)(2,1)S(1)}, bf16[2048,256]{1,0:T(8,128)(2,1)S(1)}, bf16[2048,256]{1,0:T(8,128)(2,1)S(1)}) custom-call(bf16[2048,256]{1,0:T(8,128)(2,1)S(1)} %copy-done.16, bf16[2048,256]{1,0:T(8,128)(2,1)S(1)} %copy-done.18, bf16[2048,256]{1,0:T(8,128)(2,1)} %copy-done.19, bf16[2048,256]{1,0:T(8,128)(2,1)} %bitcast.365, ...), custom_call_target="tpu_custom_call" | custom-call | flops 6710886400 | bytes 7340032 | tf_op jit(solution)/shard_map/attend_back/pallas_call | solution.py:368
  840.8 15.6 %collective-permute-done.103 = bf16[128,2048]{1,0:T(8,128)(2,1)S(1)} collective-permute-done((bf16[128,2048]{1,0:T(8,128)(2,1)S(1)}, bf16[128,2048]{1,0:T(8,128)(2,1)S(1)}, u32[]{:S(2)}, u32[]{:S(2)}) %collective-permute-start.103) | collective-permute-done | bytes 524320 | tf_op jit(solution)/shard_map/ppermute | solution.py:42
  908.2 9.6 in_products.7
  917.7 7.4 collective-permute-done.112
  946.4 16.1 %collective-permute-done.113 = bf16[1,8,64,512]{3,2,1,0:T(8,128)(2,1)S(1)} collective-permute-done((bf16[1,8,64,512]{3,2,1,0:T(8,128)(2,1)S(1)}, bf16[1,8,64,512]{3,2,1,0:T(8,128)(2,1)S(1)}, u32[]{:S(2)}, u32[]{:S(2)}) %collective-permute-start.113) | collective-permute-done | bytes 524320 | tf_op jit(solution)/shard_map/ppermute | solution.py:42
  988.1 10.7 %collective-permute-done.118 = bf16[128,2048]{1,0:T(8,128)(2,1)} collective-permute-done((bf16[128,2048]{1,0:T(8,128)(2,1)}, bf16[128,2048]{1,0:T(8,128)(2,1)}, u32[]{:S(2)}, u32[]{:S(2)}) %collective-permute-start.118) | collective-permute-done | bytes 524320 | tf_op jit(solution)/shard_map/ppermute | solution.py:42
  (824 shorter events, 548.3 us)
Async XLA Ops:
  20.1 29.5 %collective-permute-start.2 = (bf16[2,256,1024]{2,1,0:T(8,128)(2,1)S(1)}, bf16[2,256,1024]{2,1,0:T(8,128)(2,1)}, u32[]{:S(2)}, u32[]{:S(2)}) collective-permute-start(bf16[2,256,1024]{2,1,0:T(8,128)(2,1)S(1)} %pad_maximum_fusion.5.refs_0_), channel_id=1, source_target_pairs={{0,1},{1,0},{2,3},{3,2},{4,5},{5,4},{6,7},{7,6},{8,9},{9,8},{10,11... | collective-permute-start | bytes 3145736 | tf_op jit(solution)/shard_map/ppermute | solution.py:42
  49.6 39.5 %collective-permute-start.10 = (bf16[256,2048]{1,0:T(8,128)(2,1)S(1)}, bf16[256,2048]{1,0:T(8,128)(2,1)S(1)}, u32[]{:S(2)}, u32[]{:S(2)}) collective-permute-start(bf16[256,2048]{1,0:T(8,128)(2,1)S(1)} %bitcast.329), channel_id=1, source_target_pairs={{0,16},{4,20},{8,24},{12,28},{16,0},{20,4},{24,8},{28,12},{1,17},{... | collective-permute-start | bytes 3145736 | tf_op jit(solution)/shard_map/ppermute | solution.py:42
  51.1 38.0 %collective-permute-start.9 = (bf16[256,2048]{1,0:T(8,128)(2,1)S(1)}, bf16[256,2048]{1,0:T(8,128)(2,1)}, u32[]{:S(2)}, u32[]{:S(2)}) collective-permute-start(bf16[256,2048]{1,0:T(8,128)(2,1)S(1)} %bitcast.330), channel_id=1, source_target_pairs={{0,8},{4,12},{8,0},{12,4},{16,24},{20,28},{24,16},{28,20},{1,9},{5... | collective-permute-start | bytes 3145736 | tf_op jit(solution)/shard_map/ppermute | solution.py:42
  52.6 31.3 %collective-permute-start.7 = (bf16[8,64,768]{2,1,0:T(8,128)(2,1)S(1)}, bf16[8,64,768]{2,1,0:T(8,128)(2,1)}, u32[]{:S(2)}, u32[]{:S(2)}) collective-permute-start(bf16[8,64,768]{2,1,0:T(8,128)(2,1)S(1)} %all-to-all-done), channel_id=1, source_target_pairs={{0,1},{1,0},{2,3},{3,2},{4,5},{5,4},{6,7},{7,6},{8,9},{9,8},{10,11... | collective-permute-start | bytes 2359304 | tf_op jit(solution)/shard_map/ppermute | solution.py:42
  55.0 34.1 %collective-permute-start.8 = (bf16[8,64,768]{2,1,0:T(8,128)(2,1)S(1)}, bf16[8,64,768]{2,1,0:T(8,128)(2,1)}, u32[]{:S(2)}, u32[]{:S(2)}) collective-permute-start(bf16[8,64,768]{2,1,0:T(8,128)(2,1)S(1)} %all-to-all-done), channel_id=1, source_target_pairs={{0,2},{1,3},{2,0},{3,1},{4,6},{5,7},{6,4},{7,5},{8,10},{9,11},{10,... | collective-permute-start | bytes 2359304 | tf_op jit(solution)/shard_map/ppermute | solution.py:42
  157.2 35.1 %collective-permute-start.24 = (bf16[256,2048]{1,0:T(8,128)(2,1)}, bf16[256,2048]{1,0:T(8,128)(2,1)}, u32[]{:S(2)}, u32[]{:S(2)}) collective-permute-start(bf16[256,2048]{1,0:T(8,128)(2,1)} %bitcast.18), channel_id=1, source_target_pairs={{0,8},{4,12},{8,0},{12,4},{16,24},{20,28},{24,16},{28,20},{1,9},{5... | collective-permute-start | bytes 3145736 | tf_op jit(solution)/shard_map/ppermute | solution.py:42
  158.2 34.1 %collective-permute-start.25 = (bf16[256,2048]{1,0:T(8,128)(2,1)}, bf16[256,2048]{1,0:T(8,128)(2,1)}, u32[]{:S(2)}, u32[]{:S(2)}) collective-permute-start(bf16[256,2048]{1,0:T(8,128)(2,1)} %bitcast.18), channel_id=1, source_target_pairs={{0,16},{4,20},{8,24},{12,28},{16,0},{20,4},{24,8},{28,12},{1,17},{... | collective-permute-start | bytes 3145736 | tf_op jit(solution)/shard_map/ppermute | solution.py:42
  188.2 59.9 %collective-permute-start.34 = (bf16[128,2048]{1,0:T(8,128)(2,1)}, bf16[128,2048]{1,0:T(8,128)(2,1)}, u32[]{:S(2)}, u32[]{:S(2)}) collective-permute-start(bf16[128,2048]{1,0:T(8,128)(2,1)} %slice.574), channel_id=1, source_target_pairs={{0,16},{4,20},{8,24},{12,28},{16,0},{20,4},{24,8},{28,12},{1,17},{... | collective-permute-start | bytes 1572872 | tf_op jit(solution)/shard_map/ppermute | solution.py:42
  192.3 34.9 %collective-permute-start.31 = (bf16[2,128,1024]{2,1,0:T(8,128)(2,1)S(1)}, bf16[2,128,1024]{2,1,0:T(8,128)(2,1)S(1)}, u32[]{:S(2)}, u32[]{:S(2)}) collective-permute-start(bf16[2,128,1024]{2,1,0:T(8,128)(2,1)S(1)} %copy-done.97), channel_id=1, source_target_pairs={{0,1},{1,0},{2,3},{3,2},{4,5},{5,4},{6,7},{7,6},{8,9},{9,8},{10,11... | collective-permute-start | bytes 1572872 | tf_op jit(solution)/shard_map/ppermute | solution.py:42
  192.4 35.6 %collective-permute-start.30 = (bf16[2,128,1024]{2,1,0:T(8,128)(2,1)S(1)}, bf16[2,128,1024]{2,1,0:T(8,128)(2,1)S(1)}, u32[]{:S(2)}, u32[]{:S(2)}) collective-permute-start(bf16[2,128,1024]{2,1,0:T(8,128)(2,1)S(1)} %copy-done.100), channel_id=1, source_target_pairs={{0,2},{1,3},{2,0},{3,1},{4,6},{5,7},{6,4},{7,5},{8,10},{9,11},{10,... | collective-permute-start | bytes 1572872 | tf_op jit(solution)/shard_map/ppermute | solution.py:42
  196.6 31.4 %collective-permute-start.28 = (bf16[128,2048]{1,0:T(8,128)(2,1)S(1)}, bf16[128,2048]{1,0:T(8,128)(2,1)}, u32[]{:S(2)}, u32[]{:S(2)}) collective-permute-start(bf16[128,2048]{1,0:T(8,128)(2,1)S(1)} %slice.572), channel_id=1, source_target_pairs={{0,16},{4,20},{8,24},{12,28},{16,0},{20,4},{24,8},{28,12},{1,17},{... | collective-permute-start | bytes 1572872 | tf_op jit(solution)/shard_map/ppermute | solution.py:42
  198.6 29.4 %collective-permute-start.29 = (bf16[128,2048]{1,0:T(8,128)(2,1)S(1)}, bf16[128,2048]{1,0:T(8,128)(2,1)}, u32[]{:S(2)}, u32[]{:S(2)}) collective-permute-start(bf16[128,2048]{1,0:T(8,128)(2,1)S(1)} %slice.573), channel_id=1, source_target_pairs={{0,8},{4,12},{8,0},{12,4},{16,24},{20,28},{24,16},{28,20},{1,9},{5... | collective-permute-start | bytes 1572872 | tf_op jit(solution)/shard_map/ppermute | solution.py:42
  240.6 30.6 %collective-permute-start.36 = (bf16[1024,2048]{1,0:T(8,128)(2,1)}, bf16[1024,2048]{1,0:T(8,128)(2,1)}, u32[]{:S(2)}, u32[]{:S(2)}) collective-permute-start(bf16[1024,2048]{1,0:T(8,128)(2,1)} %constant_dynamic-update-slice_fusion.13), channel_id=1, source_target_pairs={{0,4},{4,0},{8,12},{12,8},{16,20},{20,16},{24,28},{28,24},{1,5},{5... | collective-permute-start | bytes 12582920 | tf_op jit(solution)/shard_map/ppermute | solution.py:42
  256.0 29.4 %collective-permute-start.41 = (bf16[1024,2048]{1,0:T(8,128)(2,1)}, bf16[1024,2048]{1,0:T(8,128)(2,1)}, u32[]{:S(2)}, u32[]{:S(2)}) collective-permute-start(bf16[1024,2048]{1,0:T(8,128)(2,1)} %constant_dynamic-update-slice_fusion.20.ua_ref), channel_id=1, source_target_pairs={{0,4},{4,0},{8,12},{12,8},{16,20},{20,16},{24,28},{28,24},{1,5},{5... | collective-permute-start | bytes 12582920 | tf_op jit(solution)/shard_map/ppermute | solution.py:42
  288.5 29.9 %collective-permute-start.42 = (bf16[256,2048]{1,0:T(8,128)(2,1)}, bf16[256,2048]{1,0:T(8,128)(2,1)}, u32[]{:S(2)}, u32[]{:S(2)}) collective-permute-start(bf16[256,2048]{1,0:T(8,128)(2,1)} %multiply_convert_fusion), channel_id=1, source_target_pairs={{0,8},{4,12},{8,0},{12,4},{16,24},{20,28},{24,16},{28,20},{1,9},{5... | collective-permute-start | bytes 3145736 | tf_op jit(solution)/shard_map/ppermute | solution.py:42
  289.6 28.7 %collective-permute-start.43 = (bf16[256,2048]{1,0:T(8,128)(2,1)}, bf16[256,2048]{1,0:T(8,128)(2,1)}, u32[]{:S(2)}, u32[]{:S(2)}) collective-permute-start(bf16[256,2048]{1,0:T(8,128)(2,1)} %multiply_convert_fusion), channel_id=1, source_target_pairs={{0,16},{4,20},{8,24},{12,28},{16,0},{20,4},{24,8},{28,12},{1,17},{... | collective-permute-start | bytes 3145736 | tf_op jit(solution)/shard_map/ppermute | solution.py:42
  297.9 29.2 %collective-permute-start.50 = (bf16[128,2048]{1,0:T(8,128)(2,1)S(1)}, bf16[128,2048]{1,0:T(8,128)(2,1)S(1)}, u32[]{:S(2)}, u32[]{:S(2)}) collective-permute-start(bf16[128,2048]{1,0:T(8,128)(2,1)S(1)} %slice.588), channel_id=1, source_target_pairs={{0,16},{4,20},{8,24},{12,28},{16,0},{20,4},{24,8},{28,12},{1,17},{... | collective-permute-start | bytes 1572872 | tf_op jit(solution)/shard_map/ppermute | solution.py:42
  406.1 64.6 %collective-permute-start.62 = (bf16[1024,2048]{1,0:T(8,128)(2,1)}, bf16[1024,2048]{1,0:T(8,128)(2,1)}, u32[]{:S(2)}, u32[]{:S(2)}) collective-permute-start(bf16[1024,2048]{1,0:T(8,128)(2,1)} %constant_dynamic-update-slice_fusion.51.xa_ref), channel_id=1, source_target_pairs={{0,4},{4,0},{8,12},{12,8},{16,20},{20,16},{24,28},{28,24},{1,5},{5... | collective-permute-start | bytes 12582920 | tf_op jit(solution)/shard_map/ppermute | solution.py:42
  470.8 59.7 %collective-permute-start.63 = (bf16[1024,2048]{1,0:T(8,128)(2,1)}, bf16[1024,2048]{1,0:T(8,128)(2,1)}, u32[]{:S(2)}, u32[]{:S(2)}) collective-permute-start(bf16[1024,2048]{1,0:T(8,128)(2,1)} %get-tuple-element.489), channel_id=1, source_target_pairs={{0,4},{4,0},{8,12},{12,8},{16,20},{20,16},{24,28},{28,24},{1,5},{5... | collective-permute-start | bytes 12582920 | tf_op jit(solution)/shard_map/ppermute | solution.py:42
  471.4 59.2 %collective-permute-start.64 = (bf16[1024,2048]{1,0:T(8,128)(2,1)}, bf16[1024,2048]{1,0:T(8,128)(2,1)}, u32[]{:S(2)}, u32[]{:S(2)}) collective-permute-start(bf16[1024,2048]{1,0:T(8,128)(2,1)} %get-tuple-element.490), channel_id=1, source_target_pairs={{0,4},{4,0},{8,12},{12,8},{16,20},{20,16},{24,28},{28,24},{1,5},{5... | collective-permute-start | bytes 12582920 | tf_op jit(solution)/shard_map/ppermute | solution.py:42
  672.2 30.6 %collective-permute-start.81 = (bf16[256,2048]{1,0:T(8,128)(2,1)}, bf16[256,2048]{1,0:T(8,128)(2,1)S(1)}, u32[]{:S(2)}, u32[]{:S(2)}) collective-permute-start(bf16[256,2048]{1,0:T(8,128)(2,1)} %get-tuple-element.701), channel_id=1, source_target_pairs={{0,8},{4,12},{8,0},{12,4},{16,24},{20,28},{24,16},{28,20},{1,9},{5... | collective-permute-start | bytes 3145736 | tf_op jit(solution)/shard_map/ppermute | solution.py:42
  673.7 29.2 %collective-permute-start.82 = (bf16[256,2048]{1,0:T(8,128)(2,1)}, bf16[256,2048]{1,0:T(8,128)(2,1)S(1)}, u32[]{:S(2)}, u32[]{:S(2)}) collective-permute-start(bf16[256,2048]{1,0:T(8,128)(2,1)} %get-tuple-element.701), channel_id=1, source_target_pairs={{0,16},{4,20},{8,24},{12,28},{16,0},{20,4},{24,8},{28,12},{1,17},{... | collective-permute-start | bytes 3145736 | tf_op jit(solution)/shard_map/ppermute | solution.py:42
  741.7 36.0 %collective-permute-start.91 = (bf16[2,128,2048]{2,1,0:T(8,128)(2,1)S(1)}, bf16[2,128,2048]{2,1,0:T(8,128)(2,1)S(1)}, u32[]{:S(2)}, u32[]{:S(2)}) collective-permute-start(bf16[2,128,2048]{2,1,0:T(8,128)(2,1)S(1)} %concatenate.251), channel_id=1, source_target_pairs={{0,1},{1,0},{2,3},{3,2},{4,5},{5,4},{6,7},{7,6},{8,9},{9,8},{10,11... | collective-permute-start | bytes 3145736 | tf_op jit(solution)/shard_map/ppermute | solution.py:42
  741.8 34.5 %collective-permute-start.90 = (bf16[2,128,1024]{2,1,0:T(8,128)(2,1)S(1)}, bf16[2,128,1024]{2,1,0:T(8,128)(2,1)S(1)}, u32[]{:S(2)}, u32[]{:S(2)}) collective-permute-start(bf16[2,128,1024]{2,1,0:T(8,128)(2,1)S(1)} %copy-done.90), channel_id=1, source_target_pairs={{0,2},{1,3},{2,0},{3,1},{4,6},{5,7},{6,4},{7,5},{8,10},{9,11},{10,... | collective-permute-start | bytes 1572872 | tf_op jit(solution)/shard_map/ppermute | solution.py:42
  746.7 29.6 %collective-permute-start.92 = (bf16[128,2048]{1,0:T(8,128)(2,1)}, bf16[128,2048]{1,0:T(8,128)(2,1)S(1)}, u32[]{:S(2)}, u32[]{:S(2)}) collective-permute-start(bf16[128,2048]{1,0:T(8,128)(2,1)} %get-tuple-element.559), channel_id=1, source_target_pairs={{0,16},{4,20},{8,24},{12,28},{16,0},{20,4},{24,8},{28,12},{1,17},{... | collective-permute-start | bytes 1572872 | tf_op jit(solution)/shard_map/ppermute | solution.py:42
  783.4 33.2 %collective-permute-start.97 = (bf16[256,2048]{1,0:T(8,128)(2,1)S(1)}, bf16[256,2048]{1,0:T(8,128)(2,1)S(1)}, u32[]{:S(2)}, u32[]{:S(2)}) collective-permute-start(bf16[256,2048]{1,0:T(8,128)(2,1)S(1)} %pad_maximum_fusion.14), channel_id=1, source_target_pairs={{0,8},{4,12},{8,0},{12,4},{16,24},{20,28},{24,16},{28,20},{1,9},{5... | collective-permute-start | bytes 3145736 | tf_op jit(solution)/shard_map/ppermute | solution.py:42
  783.9 33.7 %collective-permute-start.98 = (bf16[256,2048]{1,0:T(8,128)(2,1)S(1)}, bf16[256,2048]{1,0:T(8,128)(2,1)}, u32[]{:S(2)}, u32[]{:S(2)}) collective-permute-start(bf16[256,2048]{1,0:T(8,128)(2,1)S(1)} %pad_maximum_fusion.15), channel_id=1, source_target_pairs={{0,16},{4,20},{8,24},{12,28},{16,0},{20,4},{24,8},{28,12},{1,17},{... | collective-permute-start | bytes 3145736 | tf_op jit(solution)/shard_map/ppermute | solution.py:42
  826.3 30.3 %collective-permute-start.101 = (bf16[1024,2048]{1,0:T(8,128)(2,1)}, bf16[1024,2048]{1,0:T(8,128)(2,1)}, u32[]{:S(2)}, u32[]{:S(2)}) collective-permute-start(bf16[1024,2048]{1,0:T(8,128)(2,1)} %convolution_convert_fusion.2), channel_id=1, source_target_pairs={{0,4},{4,0},{8,12},{12,8},{16,20},{20,16},{24,28},{28,24},{1,5},{5... | collective-permute-start | bytes 12582920 | tf_op jit(solution)/shard_map/ppermute | solution.py:42
  932.1 32.7 %collective-permute-start.116 = (bf16[2,256,1024]{2,1,0:T(8,128)(2,1)S(1)}, bf16[2,256,1024]{2,1,0:T(8,128)(2,1)}, u32[]{:S(2)}, u32[]{:S(2)}) collective-permute-start(bf16[2,256,1024]{2,1,0:T(8,128)(2,1)S(1)} %get-tuple-element.611), channel_id=1, source_target_pairs={{0,1},{1,0},{2,3},{3,2},{4,5},{5,4},{6,7},{7,6},{8,9},{9,8},{10,11... | collective-permute-start | bytes 3145736 | tf_op jit(solution)/shard_map/ppermute | solution.py:42
  934.9 29.9 %collective-permute-start.114 = (bf16[256,2048]{1,0:T(8,128)(2,1)S(1)}, bf16[256,2048]{1,0:T(8,128)(2,1)S(1)}, u32[]{:S(2)}, u32[]{:S(2)}) collective-permute-start(bf16[256,2048]{1,0:T(8,128)(2,1)S(1)} %pad_maximum_fusion.19), channel_id=1, source_target_pairs={{0,8},{4,12},{8,0},{12,4},{16,24},{20,28},{24,16},{28,20},{1,9},{5... | collective-permute-start | bytes 3145736 | tf_op jit(solution)/shard_map/ppermute | solution.py:42
  968.0 31.7 %collective-permute-start.119 = (bf16[2,256,1024]{2,1,0:T(8,128)(2,1)}, bf16[2,256,1024]{2,1,0:T(8,128)(2,1)}, u32[]{:S(2)}, u32[]{:S(2)}) collective-permute-start(bf16[2,256,1024]{2,1,0:T(8,128)(2,1)} %get-tuple-element.620), channel_id=1, source_target_pairs={{0,1},{1,0},{2,3},{3,2},{4,5},{5,4},{6,7},{7,6},{8,9},{9,8},{10,11... | collective-permute-start | bytes 3145736 | tf_op jit(solution)/shard_map/ppermute | solution.py:42
  969.0 29.7 %collective-permute-start.118 = (bf16[128,2048]{1,0:T(8,128)(2,1)}, bf16[128,2048]{1,0:T(8,128)(2,1)}, u32[]{:S(2)}, u32[]{:S(2)}) collective-permute-start(bf16[128,2048]{1,0:T(8,128)(2,1)} %get-tuple-element.619), channel_id=1, source_target_pairs={{0,2},{1,3},{2,0},{3,1},{4,6},{5,7},{6,4},{7,5},{8,10},{9,11},{10,... | collective-permute-start | bytes 1572872 | tf_op jit(solution)/shard_map/ppermute | solution.py:42
  (237 other events, 3194.2 us)

commit v14 on v13

--- a/solution.py
+++ b/solution.py
@@ -947,8 +947,11 @@
     out_more = gather_more(own_output, out_first, S)
     far.append(far_part(1, query_low))
     near_own.append(near_swap(own_quarters[3], query_low))
+    down = [near_swap(down_rows[0], query_low)]
     attended, lse = attention_forward(query_low, key_low, value_low, seg_row, seg_col)
-    attended, out_more, far[1], near_own[2] = tie(attended, out_more, far[1], near_own[2])
+    attended, out_more, far[1], near_own[2], down[0] = tie(
+        attended, out_more, far[1], near_own[2], down[0]
+    )
     attended_blocks = attended.reshape(S, T, C)
     come = lax.all_to_all(attended_blocks, "seq", split_axis=0, concat_axis=0, tiled=True)
     out_even, out_odd = gather_end(own_output, out_first, out_more, S)
@@ -958,15 +961,15 @@
     come, far[2], near_far[0], own_up_more = tie(come, far[2], near_far[0], own_up_more)
     own_u = gather_end(upstream_low, own_up_first, own_up_more, S)
     near_far.append(near_swap(far[1], come))
-    down = [near_swap(down_rows[0], come)]
+    down.append(near_swap(down_rows[1], come))
     partner_up_first = gather_first(after(partner_up, come), S)
     come = relative(come, s).transpose(1, 0, 2).reshape(T, D)
     residual = inputs + matmul(come[:, : D // 2], out_even) + matmul(come[:, D // 2 :], out_odd)
     moe_factor = rms_factor(residual)
     residual_n = residual * moe_factor
     second_low = (residual_n * gain_moe).astype(BF16)
-    second_low, down[0], near_far[1], partner_up_first, own_u = tie(
-        second_low, down[0], near_far[1], partner_up_first, own_u
+    second_low, down[1], near_far[1], partner_up_first, own_u = tie(
+        second_low, down[1], near_far[1], partner_up_first, own_u
     )
 
     own_first = gather_first(second_low, S)
@@ -985,22 +988,21 @@
     )
     own_more = gather_more(second_low, own_first, S)
     partner_low.append(far_swap(second_low[half_rows:], own_first))
-    down.append(near_swap(down_rows[1], own_first))
+    down.append(near_swap(down_rows[2], own_first))
     partner_up_more = gather_more(after(partner_up, own_first), partner_up_first, S)
-    own_more, partner_low[1], down[1], partner_up_more = tie(
-        own_more, partner_low[1], down[1], partner_up_more
+    own_more, partner_low[1], down[2], partner_up_more = tie(
+        own_more, partner_low[1], down[2], partner_up_more
     )
     partner_low = jnp.concatenate(partner_low, 0)
     own_x = gather_end(second_low, own_first, own_more, S)
     partner_first = gather_first(after(partner_low, own_more), S)
-    down.append(near_swap(down_rows[2], own_more))
+    down.append(near_swap(down_rows[3], own_more))
     far.append(far_part(3, own_more))
-    partner_first, down[2], own_x, far[3] = tie(partner_first, down[2], own_x, far[3])
+    partner_first, down[3], own_x, far[3] = tie(partner_first, down[3], own_x, far[3])
     other_u = gather_end(after(partner_up, partner_first), partner_up_first, partner_up_more, S)
     partner_more = gather_more(partner_low, partner_first, S)
-    down.append(near_swap(down_rows[3], partner_first))
     near_far.append(near_swap(far[3], partner_first))
-    partner_more, down[3], other_u, near_far[3] = tie(partner_more, down[3], other_u, near_far[3])
+    partner_more, other_u, near_far[3] = tie(partner_more, other_u, near_far[3])
     other_x = gather_end(partner_low, partner_first, partner_more, S)
     in_pieces = []
     for r in range(F):

time: 1040 us -> 1030 us (level)
  waiting for transfers between devices: 308 us -> 294 us
    ppermute x124, waiting for transfers between devices: 308 us -> 294 us  [swap(): return lax.ppermute(values, axis, [(i, i ^ mask) for i in range(size)])]
  transfers between devices with their start and end apart: 127 -> 127, of which waited for: 60 -> 59; matrix products, arithmetic and copies ran while one was open for 20% -> 21% of each run, Pallas kernels for 24% -> 24%
where the time goes in v14:
time: 1030 us; the launch traced here: 1010 us
  waiting for transfers between devices  294 us (29%)
  Pallas kernels  255 us (25%)
  local copies, waits for them, and re-layouts  152 us (15%)
  starting transfers between devices  143 us (14%)
  other arithmetic  111 us (11%)
  matrix products  48 us (5%)
    ppermute x124, waiting for transfers between devices, swap(): return lax.ppermute(values, axis, [(i, i ^ mask) for i in range(size)])  294 us
    ppermute x124, starting transfers between devices, swap(): return lax.ppermute(values, axis, [(i, i ^ mask) for i in range(size)])  131 us
    pallas_call x2, Pallas kernels, run_experts(): pl.pallas_call(partial(expert_kernel, in_places, down_places), grid=(step...  118 us
    unnamed x354, local copies, waits for them, and re-layouts  66.4 us
    pallas_call x6, Pallas kernels, products(): pl.pallas_call(product_kernel, grid_spec=pltpu.PrefetchScalarGridSpec(num...  60.1 us
    pallas_call x1, Pallas kernels, attention_backward(): pl.pallas_call(partial(backward_kernel, span), grid=(heads, length // row...  28.3 us
    pallas_call x1, Pallas kernels, attention_forward(): pl.pallas_call(partial(forward_kernel, span), grid=(heads, length // rows...  21.6 us
  transfers between devices with their start and end apart: 127, of which 59 were waited for; matrix products, arithmetic and copies ran while one was open for 21% of the time, Pallas kernels for 24%

profile of v14, /device:TPU:0, one launch (start us, length us, event | category | flops | bytes accessed | tf_op | source)
XLA Modules:
  0.0 1012.2 jit_solution(14839209281409257348)
XLA Ops:
  30.4 8.6 collective-permute-done.4
  71.1 12.8 %collective-permute-done.7 = bf16[8,64,768]{2,1,0:T(8,128)(2,1)} collective-permute-done((bf16[8,64,768]{2,1,0:T(8,128)(2,1)S(1)}, bf16[8,64,768]{2,1,0:T(8,128)(2,1)}, u32[]{:S(2)}, u32[]{:S(2)}) %collective-permute-start.7) | collective-permute-done | bytes 786464 | tf_op jit(solution)/shard_map/ppermute | solution.py:42
  100.0 14.3 %collective-permute-done.12 = bf16[128,2048]{1,0:T(8,128)(2,1)} collective-permute-done((bf16[128,2048]{1,0:T(8,128)(2,1)S(1)}, bf16[128,2048]{1,0:T(8,128)(2,1)}, u32[]{:S(2)}, u32[]{:S(2)}) %collective-permute-start.12) | collective-permute-done | bytes 524320 | tf_op jit(solution)/shard_map/ppermute | solution.py:42
  128.5 12.6 %project.1 = (bf16[1024,2048]{1,0:T(8,128)(2,1)}, bf16[1024,2048]{1,0:T(8,128)(2,1)}, f32[2048,256]{1,0:T(8,128)S(1)}, f32[2048,256]{1,0:T(8,128)S(1)}, bf16[204...) custom-call(s32[1]{0:T(128)} %bitcast.1.me_ref, bf16[1024,2048]{1,0:T(8,128)(2,1)} %constant_dynamic-update-slice_fusion.even_ref, ...), custom_call_target="tpu_custom_call" | custom-call | flops 6442450944 | bytes 25165824 | tf_op jit(solution)/shard_map/project/pallas_call | solution.py:437
  171.7 10.7 %collective-permute-done.22 = f32[2,2048]{1,0:T(2,128)S(1)} collective-permute-done((f32[2,2048]{1,0:T(2,128)S(1)}, f32[2,2048]{1,0:T(2,128)S(1)}, u32[]{:S(2)}, u32[]{:S(2)}) %collective-permute-start.22) | collective-permute-done | bytes 16416 | tf_op jit(solution)/shard_map/ppermute | solution.py:42
  203.8 21.6 %attend.1 = (bf16[2048,256]{1,0:T(8,128)(2,1)S(1)}, f32[2,1,2048]{2,1,0:T(1,128)S(1)}) custom-call(bf16[2048,256]{1,0:T(8,128)(2,1)S(1)} %get-tuple-element.370.q_ref, bf16[2048,256]{1,0:T(8,128)(2,1)S(1)} %get-tuple-element.371.k_ref, bf16[2048,256]{1,0:T(8,128)(2,1)S(1)} %copy-done.20, s32[1,2048]{1,0:T(1,128)S(1)} %copy-done.14, s32[2048,1]{1,0:T(8,128)S(1)} %copy-done.9), custom_call_target="tpu_custom_call" | custom-call | flops 2684354560 | bytes 4194304 | tf_op jit(solution)/shard_map/attend/pallas_call | solution.py:336
  280.8 6.0 collective-permute-done.38.refs_19_
  307.5 10.2 %collective-permute-done.46.refs_12_ = bf16[2,128,1024]{2,1,0:T(8,128)(2,1)S(1)} collective-permute-done((bf16[2,128,1024]{2,1,0:T(8,128)(2,1)}, bf16[2,128,1024]{2,1,0:T(8,128)(2,1)S(1)}, u32[]{:S(2)}, u32[]{:S(2)}) %collective-permute-start.46) | collective-permute-done | bytes 524320 | tf_op jit(solution)/shard_map/ppermute | solution.py:42
  333.5 9.9 collective-permute-done.50.refs_20_
  350.5 22.8 %collective-permute-done.57.refs_9_ = bf16[2,128,1024]{2,1,0:T(8,128)(2,1)S(1)} collective-permute-done((bf16[2,128,1024]{2,1,0:T(8,128)(2,1)S(1)}, bf16[2,128,1024]{2,1,0:T(8,128)(2,1)S(1)}, u32[]{:S(2)}, u32[]{:S(2)}) %collective-permute-start.57) | collective-permute-done | bytes 524320 | tf_op jit(solution)/shard_map/ppermute | solution.py:42
  383.8 10.1 collective-permute-done.61.refs_13_
  402.0 59.4 %experts.2 = (bf16[1024,2048]{1,0:T(8,128)(2,1)}, bf16[1024,2048]{1,0:T(8,128)(2,1)}, bf16[1024,2048]{1,0:T(8,128)(2,1)}, bf16[1024,2048]{1,0:T(8,128)(2,1)}, f3...) custom-call(s32[2]{0:T(128)} %pad_add_fusion.first_ref, ...), custom_call_target="tpu_custom_call" | custom-call | flops 38654705664 | bytes 62914560 | tf_op jit(solution)/shard_map/experts/pallas_call | solution.py:732
  462.1 59.1 %experts.3 = (bf16[1024,2048]{1,0:T(8,128)(2,1)}, bf16[1024,2048]{1,0:T(8,128)(2,1)}, bf16[1024,2048]{1,0:T(8,128)(2,1)}, bf16[1024,2048]{1,0:T(8,128)(2,1)}, f3...) custom-call(s32[2]{0:T(128)} %pad_add_fusion.first_ref, ...), custom_call_target="tpu_custom_call", output_to_operand_aliasing={{6}: (30, {}), {7}: (31, {}), {8}: (32, {}), {9}: (33, {})} | custom-call | flops 38654705664 | bytes 62914560 | tf_op jit(solution)/shard_map/experts/pallas_call | solution.py:732
  525.6 7.4 all_to_all.27
  540.0 9.3 in_products.4
  562.5 11.0 %down_products.2 = bf16[2,256,2048]{2,1,0:T(8,128)(2,1)} custom-call(s32[1]{0:T(128)} %bitcast.25.me_ref, bf16[2,2304,512]{2,1,0:T(8,128)(2,1)} %get-tuple-element.544.left_ref, bf16[2,2304,2048]{2,1,0:T(8,128)(2,1)} %get-tuple-element.518.right_ref), custom_call_target="tpu_custom_call" | custom-call | flops 4831838208 | bytes 21233664 | tf_op jit(solution)/shard_map/down_products/pallas_call | solution.py:769
  573.5 8.0 collective-permute-done.70
  598.5 9.3 in_products.5
  607.8 10.0 collective-permute-done.75
  632.9 9.9 in_products.6
  642.8 8.0 collective-permute-done.80
  670.2 11.0 %down_products.3 = bf16[2,256,2048]{2,1,0:T(8,128)(2,1)} custom-call(s32[1]{0:T(128)} %bitcast.25.me_ref, bf16[2,2304,512]{2,1,0:T(8,128)(2,1)} %get-tuple-element.544.left_ref, bf16[2,2304,2048]{2,1,0:T(8,128)(2,1)} %get-tuple-element.518.right_ref), custom_call_target="tpu_custom_call" | custom-call | flops 4831838208 | bytes 21233664 | tf_op jit(solution)/shard_map/down_products/pallas_call | solution.py:769
  681.3 8.4 collective-permute-done.83
  693.7 6.5 collective-permute-done.85
  713.2 13.3 %collective-permute-done.89 = bf16[2,64,2048]{2,1,0:T(8,128)(2,1)S(1)} collective-permute-done((bf16[2,64,2048]{2,1,0:T(8,128)(2,1)S(1)}, bf16[2,64,2048]{2,1,0:T(8,128)(2,1)S(1)}, u32[]{:S(2)}, u32[]{:S(2)}) %collective-permute-start.89) | collective-permute-done | bytes 524320 | tf_op jit(solution)/shard_map/ppermute | solution.py:42
  735.7 28.3 %attend_back.1 = (bf16[2048,256]{1,0:T(8,128)(2,1)S(1)}, bf16[2048,256]{1,0:T(8,128)(2,1)S(1)}, bf16[2048,256]{1,0:T(8,128)(2,1)S(1)}) custom-call(bf16[2048,256]{1,0:T(8,128)(2,1)S(1)} %copy-done.16, bf16[2048,256]{1,0:T(8,128)(2,1)S(1)} %copy-done.18, bf16[2048,256]{1,0:T(8,128)(2,1)} %copy-done.19, bf16[2048,256]{1,0:T(8,128)(2,1)} %bitcast.365, ...), custom_call_target="tpu_custom_call" | custom-call | flops 6710886400 | bytes 7340032 | tf_op jit(solution)/shard_map/attend_back/pallas_call | solution.py:368
  789.1 5.9 collective-permute-done.95
  828.7 15.6 %collective-permute-done.103 = bf16[128,2048]{1,0:T(8,128)(2,1)S(1)} collective-permute-done((bf16[128,2048]{1,0:T(8,128)(2,1)S(1)}, bf16[128,2048]{1,0:T(8,128)(2,1)S(1)}, u32[]{:S(2)}, u32[]{:S(2)}) %collective-permute-start.103) | collective-permute-done | bytes 524320 | tf_op jit(solution)/shard_map/ppermute | solution.py:42
  896.1 9.6 in_products.7
  905.7 6.9 collective-permute-done.112
  933.2 17.3 %collective-permute-done.113 = bf16[1,8,64,512]{3,2,1,0:T(8,128)(2,1)S(1)} collective-permute-done((bf16[1,8,64,512]{3,2,1,0:T(8,128)(2,1)S(1)}, bf16[1,8,64,512]{3,2,1,0:T(8,128)(2,1)S(1)}, u32[]{:S(2)}, u32[]{:S(2)}) %collective-permute-start.113) | collective-permute-done | bytes 524320 | tf_op jit(solution)/shard_map/ppermute | solution.py:42
  975.4 11.3 %collective-permute-done.118 = bf16[128,2048]{1,0:T(8,128)(2,1)} collective-permute-done((bf16[128,2048]{1,0:T(8,128)(2,1)}, bf16[128,2048]{1,0:T(8,128)(2,1)}, u32[]{:S(2)}, u32[]{:S(2)}) %collective-permute-start.118) | collective-permute-done | bytes 524320 | tf_op jit(solution)/shard_map/ppermute | solution.py:42
  (824 shorter events, 543.5 us)
Async XLA Ops:
  20.1 29.5 %collective-permute-start.2 = (bf16[2,256,1024]{2,1,0:T(8,128)(2,1)S(1)}, bf16[2,256,1024]{2,1,0:T(8,128)(2,1)}, u32[]{:S(2)}, u32[]{:S(2)}) collective-permute-start(bf16[2,256,1024]{2,1,0:T(8,128)(2,1)S(1)} %pad_maximum_fusion.5.refs_0_), channel_id=1, source_target_pairs={{0,1},{1,0},{2,3},{3,2},{4,5},{5,4},{6,7},{7,6},{8,9},{9,8},{10,11... | collective-permute-start | bytes 3145736 | tf_op jit(solution)/shard_map/ppermute | solution.py:42
  49.6 39.5 %collective-permute-start.10 = (bf16[256,2048]{1,0:T(8,128)(2,1)S(1)}, bf16[256,2048]{1,0:T(8,128)(2,1)S(1)}, u32[]{:S(2)}, u32[]{:S(2)}) collective-permute-start(bf16[256,2048]{1,0:T(8,128)(2,1)S(1)} %bitcast.329), channel_id=1, source_target_pairs={{0,16},{4,20},{8,24},{12,28},{16,0},{20,4},{24,8},{28,12},{1,17},{... | collective-permute-start | bytes 3145736 | tf_op jit(solution)/shard_map/ppermute | solution.py:42
  51.1 38.0 %collective-permute-start.9 = (bf16[256,2048]{1,0:T(8,128)(2,1)S(1)}, bf16[256,2048]{1,0:T(8,128)(2,1)}, u32[]{:S(2)}, u32[]{:S(2)}) collective-permute-start(bf16[256,2048]{1,0:T(8,128)(2,1)S(1)} %bitcast.330), channel_id=1, source_target_pairs={{0,8},{4,12},{8,0},{12,4},{16,24},{20,28},{24,16},{28,20},{1,9},{5... | collective-permute-start | bytes 3145736 | tf_op jit(solution)/shard_map/ppermute | solution.py:42
  52.6 31.3 %collective-permute-start.7 = (bf16[8,64,768]{2,1,0:T(8,128)(2,1)S(1)}, bf16[8,64,768]{2,1,0:T(8,128)(2,1)}, u32[]{:S(2)}, u32[]{:S(2)}) collective-permute-start(bf16[8,64,768]{2,1,0:T(8,128)(2,1)S(1)} %all-to-all-done), channel_id=1, source_target_pairs={{0,1},{1,0},{2,3},{3,2},{4,5},{5,4},{6,7},{7,6},{8,9},{9,8},{10,11... | collective-permute-start | bytes 2359304 | tf_op jit(solution)/shard_map/ppermute | solution.py:42
  55.0 34.1 %collective-permute-start.8 = (bf16[8,64,768]{2,1,0:T(8,128)(2,1)S(1)}, bf16[8,64,768]{2,1,0:T(8,128)(2,1)}, u32[]{:S(2)}, u32[]{:S(2)}) collective-permute-start(bf16[8,64,768]{2,1,0:T(8,128)(2,1)S(1)} %all-to-all-done), channel_id=1, source_target_pairs={{0,2},{1,3},{2,0},{3,1},{4,6},{5,7},{6,4},{7,5},{8,10},{9,11},{10,... | collective-permute-start | bytes 2359304 | tf_op jit(solution)/shard_map/ppermute | solution.py:42
  157.2 33.6 %collective-permute-start.24 = (bf16[256,2048]{1,0:T(8,128)(2,1)}, bf16[256,2048]{1,0:T(8,128)(2,1)}, u32[]{:S(2)}, u32[]{:S(2)}) collective-permute-start(bf16[256,2048]{1,0:T(8,128)(2,1)} %bitcast.18), channel_id=1, source_target_pairs={{0,8},{4,12},{8,0},{12,4},{16,24},{20,28},{24,16},{28,20},{1,9},{5... | collective-permute-start | bytes 3145736 | tf_op jit(solution)/shard_map/ppermute | solution.py:42
  158.2 32.6 %collective-permute-start.25 = (bf16[256,2048]{1,0:T(8,128)(2,1)}, bf16[256,2048]{1,0:T(8,128)(2,1)}, u32[]{:S(2)}, u32[]{:S(2)}) collective-permute-start(bf16[256,2048]{1,0:T(8,128)(2,1)} %bitcast.18), channel_id=1, source_target_pairs={{0,16},{4,20},{8,24},{12,28},{16,0},{20,4},{24,8},{28,12},{1,17},{... | collective-permute-start | bytes 3145736 | tf_op jit(solution)/shard_map/ppermute | solution.py:42
  190.8 35.6 %collective-permute-start.32 = (bf16[2,64,2048]{2,1,0:T(8,128)(2,1)S(1)}, bf16[2,64,2048]{2,1,0:T(8,128)(2,1)S(1)}, u32[]{:S(2)}, u32[]{:S(2)}) collective-permute-start(bf16[2,64,2048]{2,1,0:T(8,128)(2,1)S(1)} %copy-done.107), channel_id=1, source_target_pairs={{0,1},{1,0},{2,3},{3,2},{4,5},{5,4},{6,7},{7,6},{8,9},{9,8},{10,11... | collective-permute-start | bytes 1572872 | tf_op jit(solution)/shard_map/ppermute | solution.py:42
  191.6 36.4 %collective-permute-start.31 = (bf16[2,128,1024]{2,1,0:T(8,128)(2,1)S(1)}, bf16[2,128,1024]{2,1,0:T(8,128)(2,1)S(1)}, u32[]{:S(2)}, u32[]{:S(2)}) collective-permute-start(bf16[2,128,1024]{2,1,0:T(8,128)(2,1)S(1)} %copy-done.97), channel_id=1, source_target_pairs={{0,1},{1,0},{2,3},{3,2},{4,5},{5,4},{6,7},{7,6},{8,9},{9,8},{10,11... | collective-permute-start | bytes 1572872 | tf_op jit(solution)/shard_map/ppermute | solution.py:42
  192.9 35.5 %collective-permute-start.30 = (bf16[2,128,1024]{2,1,0:T(8,128)(2,1)S(1)}, bf16[2,128,1024]{2,1,0:T(8,128)(2,1)S(1)}, u32[]{:S(2)}, u32[]{:S(2)}) collective-permute-start(bf16[2,128,1024]{2,1,0:T(8,128)(2,1)S(1)} %copy-done.100), channel_id=1, source_target_pairs={{0,2},{1,3},{2,0},{3,1},{4,6},{5,7},{6,4},{7,5},{8,10},{9,11},{10,... | collective-permute-start | bytes 1572872 | tf_op jit(solution)/shard_map/ppermute | solution.py:42
  195.8 32.6 %collective-permute-start.28 = (bf16[128,2048]{1,0:T(8,128)(2,1)S(1)}, bf16[128,2048]{1,0:T(8,128)(2,1)}, u32[]{:S(2)}, u32[]{:S(2)}) collective-permute-start(bf16[128,2048]{1,0:T(8,128)(2,1)S(1)} %slice.572), channel_id=1, source_target_pairs={{0,16},{4,20},{8,24},{12,28},{16,0},{20,4},{24,8},{28,12},{1,17},{... | collective-permute-start | bytes 1572872 | tf_op jit(solution)/shard_map/ppermute | solution.py:42
  198.5 29.9 %collective-permute-start.29 = (bf16[128,2048]{1,0:T(8,128)(2,1)S(1)}, bf16[128,2048]{1,0:T(8,128)(2,1)}, u32[]{:S(2)}, u32[]{:S(2)}) collective-permute-start(bf16[128,2048]{1,0:T(8,128)(2,1)S(1)} %slice.573), channel_id=1, source_target_pairs={{0,8},{4,12},{8,0},{12,4},{16,24},{20,28},{24,16},{28,20},{1,9},{5... | collective-permute-start | bytes 1572872 | tf_op jit(solution)/shard_map/ppermute | solution.py:42
  240.7 31.8 %collective-permute-start.37 = (bf16[1024,2048]{1,0:T(8,128)(2,1)}, bf16[1024,2048]{1,0:T(8,128)(2,1)}, u32[]{:S(2)}, u32[]{:S(2)}) collective-permute-start(bf16[1024,2048]{1,0:T(8,128)(2,1)} %constant_dynamic-update-slice_fusion.13), channel_id=1, source_target_pairs={{0,4},{4,0},{8,12},{12,8},{16,20},{20,16},{24,28},{28,24},{1,5},{5... | collective-permute-start | bytes 12582920 | tf_op jit(solution)/shard_map/ppermute | solution.py:42
  256.6 30.2 %collective-permute-start.42 = (bf16[1024,2048]{1,0:T(8,128)(2,1)}, bf16[1024,2048]{1,0:T(8,128)(2,1)}, u32[]{:S(2)}, u32[]{:S(2)}) collective-permute-start(bf16[1024,2048]{1,0:T(8,128)(2,1)} %constant_dynamic-update-slice_fusion.20.ua_ref), channel_id=1, source_target_pairs={{0,4},{4,0},{8,12},{12,8},{16,20},{20,16},{24,28},{28,24},{1,5},{5... | collective-permute-start | bytes 12582920 | tf_op jit(solution)/shard_map/ppermute | solution.py:42
  289.9 29.6 %collective-permute-start.43 = (bf16[256,2048]{1,0:T(8,128)(2,1)}, bf16[256,2048]{1,0:T(8,128)(2,1)}, u32[]{:S(2)}, u32[]{:S(2)}) collective-permute-start(bf16[256,2048]{1,0:T(8,128)(2,1)} %multiply_convert_fusion), channel_id=1, source_target_pairs={{0,8},{4,12},{8,0},{12,4},{16,24},{20,28},{24,16},{28,20},{1,9},{5... | collective-permute-start | bytes 3145736 | tf_op jit(solution)/shard_map/ppermute | solution.py:42
  298.6 29.8 %collective-permute-start.51 = (bf16[128,2048]{1,0:T(8,128)(2,1)S(1)}, bf16[128,2048]{1,0:T(8,128)(2,1)S(1)}, u32[]{:S(2)}, u32[]{:S(2)}) collective-permute-start(bf16[128,2048]{1,0:T(8,128)(2,1)S(1)} %slice.588), channel_id=1, source_target_pairs={{0,16},{4,20},{8,24},{12,28},{16,0},{20,4},{24,8},{28,12},{1,17},{... | collective-permute-start | bytes 1572872 | tf_op jit(solution)/shard_map/ppermute | solution.py:42
  345.2 29.3 %collective-permute-start.56 = (bf16[1024,2048]{1,0:T(8,128)(2,1)S(1)}, bf16[1024,2048]{1,0:T(8,128)(2,1)S(1)}, u32[]{:S(2)}, u32[]{:S(2)}) collective-permute-start(bf16[1024,2048]{1,0:T(8,128)(2,1)S(1)} %constant_dynamic-update-slice_fusion.41.xa_ref), channel_id=1, source_target_pairs={{0,4},{4,0},{8,12},{12,8},{16,20},{20,16},{24,28},{28,24},{1,5},{5... | collective-permute-start | bytes 12582920 | tf_op jit(solution)/shard_map/ppermute | solution.py:42
  396.8 64.6 %collective-permute-start.62 = (bf16[1024,2048]{1,0:T(8,128)(2,1)}, bf16[1024,2048]{1,0:T(8,128)(2,1)}, u32[]{:S(2)}, u32[]{:S(2)}) collective-permute-start(bf16[1024,2048]{1,0:T(8,128)(2,1)} %constant_dynamic-update-slice_fusion.51.xa_ref), channel_id=1, source_target_pairs={{0,4},{4,0},{8,12},{12,8},{16,20},{20,16},{24,28},{28,24},{1,5},{5... | collective-permute-start | bytes 12582920 | tf_op jit(solution)/shard_map/ppermute | solution.py:42
  461.5 59.8 %collective-permute-start.63 = (bf16[1024,2048]{1,0:T(8,128)(2,1)}, bf16[1024,2048]{1,0:T(8,128)(2,1)}, u32[]{:S(2)}, u32[]{:S(2)}) collective-permute-start(bf16[1024,2048]{1,0:T(8,128)(2,1)} %get-tuple-element.489), channel_id=1, source_target_pairs={{0,4},{4,0},{8,12},{12,8},{16,20},{20,16},{24,28},{28,24},{1,5},{5... | collective-permute-start | bytes 12582920 | tf_op jit(solution)/shard_map/ppermute | solution.py:42
  462.1 59.2 %collective-permute-start.64 = (bf16[1024,2048]{1,0:T(8,128)(2,1)}, bf16[1024,2048]{1,0:T(8,128)(2,1)}, u32[]{:S(2)}, u32[]{:S(2)}) collective-permute-start(bf16[1024,2048]{1,0:T(8,128)(2,1)} %get-tuple-element.490), channel_id=1, source_target_pairs={{0,4},{4,0},{8,12},{12,8},{16,20},{20,16},{24,28},{28,24},{1,5},{5... | collective-permute-start | bytes 12582920 | tf_op jit(solution)/shard_map/ppermute | solution.py:42
  660.2 29.5 %collective-permute-start.81 = (bf16[256,2048]{1,0:T(8,128)(2,1)}, bf16[256,2048]{1,0:T(8,128)(2,1)S(1)}, u32[]{:S(2)}, u32[]{:S(2)}) collective-permute-start(bf16[256,2048]{1,0:T(8,128)(2,1)} %get-tuple-element.701), channel_id=1, source_target_pairs={{0,8},{4,12},{8,0},{12,4},{16,24},{20,28},{24,16},{28,20},{1,9},{5... | collective-permute-start | bytes 3145736 | tf_op jit(solution)/shard_map/ppermute | solution.py:42
  728.9 36.0 %collective-permute-start.91 = (bf16[2,128,2048]{2,1,0:T(8,128)(2,1)S(1)}, bf16[2,128,2048]{2,1,0:T(8,128)(2,1)S(1)}, u32[]{:S(2)}, u32[]{:S(2)}) collective-permute-start(bf16[2,128,2048]{2,1,0:T(8,128)(2,1)S(1)} %concatenate.251), channel_id=1, source_target_pairs={{0,1},{1,0},{2,3},{3,2},{4,5},{5,4},{6,7},{7,6},{8,9},{9,8},{10,11... | collective-permute-start | bytes 3145736 | tf_op jit(solution)/shard_map/ppermute | solution.py:42
  728.9 35.1 %collective-permute-start.90 = (bf16[2,128,1024]{2,1,0:T(8,128)(2,1)S(1)}, bf16[2,128,1024]{2,1,0:T(8,128)(2,1)S(1)}, u32[]{:S(2)}, u32[]{:S(2)}) collective-permute-start(bf16[2,128,1024]{2,1,0:T(8,128)(2,1)S(1)} %copy-done.90), channel_id=1, source_target_pairs={{0,2},{1,3},{2,0},{3,1},{4,6},{5,7},{6,4},{7,5},{8,10},{9,11},{10,... | collective-permute-start | bytes 1572872 | tf_op jit(solution)/shard_map/ppermute | solution.py:42
  733.4 30.6 %collective-permute-start.92 = (bf16[128,2048]{1,0:T(8,128)(2,1)}, bf16[128,2048]{1,0:T(8,128)(2,1)S(1)}, u32[]{:S(2)}, u32[]{:S(2)}) collective-permute-start(bf16[128,2048]{1,0:T(8,128)(2,1)} %get-tuple-element.559), channel_id=1, source_target_pairs={{0,16},{4,20},{8,24},{12,28},{16,0},{20,4},{24,8},{28,12},{1,17},{... | collective-permute-start | bytes 1572872 | tf_op jit(solution)/shard_map/ppermute | solution.py:42
  734.4 29.6 %collective-permute-start.93 = (bf16[128,2048]{1,0:T(8,128)(2,1)}, bf16[128,2048]{1,0:T(8,128)(2,1)}, u32[]{:S(2)}, u32[]{:S(2)}) collective-permute-start(bf16[128,2048]{1,0:T(8,128)(2,1)} %get-tuple-element.560), channel_id=1, source_target_pairs={{0,8},{4,12},{8,0},{12,4},{16,24},{20,28},{24,16},{28,20},{1,9},{5... | collective-permute-start | bytes 1572872 | tf_op jit(solution)/shard_map/ppermute | solution.py:42
  770.5 33.6 %collective-permute-start.97 = (bf16[256,2048]{1,0:T(8,128)(2,1)S(1)}, bf16[256,2048]{1,0:T(8,128)(2,1)S(1)}, u32[]{:S(2)}, u32[]{:S(2)}) collective-permute-start(bf16[256,2048]{1,0:T(8,128)(2,1)S(1)} %pad_maximum_fusion.14), channel_id=1, source_target_pairs={{0,8},{4,12},{8,0},{12,4},{16,24},{20,28},{24,16},{28,20},{1,9},{5... | collective-permute-start | bytes 3145736 | tf_op jit(solution)/shard_map/ppermute | solution.py:42
  771.8 33.4 %collective-permute-start.98 = (bf16[256,2048]{1,0:T(8,128)(2,1)S(1)}, bf16[256,2048]{1,0:T(8,128)(2,1)}, u32[]{:S(2)}, u32[]{:S(2)}) collective-permute-start(bf16[256,2048]{1,0:T(8,128)(2,1)S(1)} %pad_maximum_fusion.15), channel_id=1, source_target_pairs={{0,16},{4,20},{8,24},{12,28},{16,0},{20,4},{24,8},{28,12},{1,17},{... | collective-permute-start | bytes 3145736 | tf_op jit(solution)/shard_map/ppermute | solution.py:42
  813.9 30.6 %collective-permute-start.101 = (bf16[1024,2048]{1,0:T(8,128)(2,1)}, bf16[1024,2048]{1,0:T(8,128)(2,1)}, u32[]{:S(2)}, u32[]{:S(2)}) collective-permute-start(bf16[1024,2048]{1,0:T(8,128)(2,1)} %convolution_convert_fusion.2), channel_id=1, source_target_pairs={{0,4},{4,0},{8,12},{12,8},{16,20},{20,16},{24,28},{28,24},{1,5},{5... | collective-permute-start | bytes 12582920 | tf_op jit(solution)/shard_map/ppermute | solution.py:42
  920.1 32.7 %collective-permute-start.116 = (bf16[2,256,1024]{2,1,0:T(8,128)(2,1)S(1)}, bf16[2,256,1024]{2,1,0:T(8,128)(2,1)}, u32[]{:S(2)}, u32[]{:S(2)}) collective-permute-start(bf16[2,256,1024]{2,1,0:T(8,128)(2,1)S(1)} %get-tuple-element.611), channel_id=1, source_target_pairs={{0,1},{1,0},{2,3},{3,2},{4,5},{5,4},{6,7},{7,6},{8,9},{9,8},{10,11... | collective-permute-start | bytes 3145736 | tf_op jit(solution)/shard_map/ppermute | solution.py:42
  922.8 29.9 %collective-permute-start.114 = (bf16[256,2048]{1,0:T(8,128)(2,1)S(1)}, bf16[256,2048]{1,0:T(8,128)(2,1)S(1)}, u32[]{:S(2)}, u32[]{:S(2)}) collective-permute-start(bf16[256,2048]{1,0:T(8,128)(2,1)S(1)} %pad_maximum_fusion.19), channel_id=1, source_target_pairs={{0,8},{4,12},{8,0},{12,4},{16,24},{20,28},{24,16},{28,20},{1,9},{5... | collective-permute-start | bytes 3145736 | tf_op jit(solution)/shard_map/ppermute | solution.py:42
  956.0 31.7 %collective-permute-start.119 = (bf16[2,256,1024]{2,1,0:T(8,128)(2,1)}, bf16[2,256,1024]{2,1,0:T(8,128)(2,1)}, u32[]{:S(2)}, u32[]{:S(2)}) collective-permute-start(bf16[2,256,1024]{2,1,0:T(8,128)(2,1)} %get-tuple-element.620), channel_id=1, source_target_pairs={{0,1},{1,0},{2,3},{3,2},{4,5},{5,4},{6,7},{7,6},{8,9},{9,8},{10,11... | collective-permute-start | bytes 3145736 | tf_op jit(solution)/shard_map/ppermute | solution.py:42
  957.0 29.8 %collective-permute-start.118 = (bf16[128,2048]{1,0:T(8,128)(2,1)}, bf16[128,2048]{1,0:T(8,128)(2,1)}, u32[]{:S(2)}, u32[]{:S(2)}) collective-permute-start(bf16[128,2048]{1,0:T(8,128)(2,1)} %get-tuple-element.619), channel_id=1, source_target_pairs={{0,2},{1,3},{2,0},{3,1},{4,6},{5,7},{6,4},{7,5},{8,10},{9,11},{10,... | collective-permute-start | bytes 1572872 | tf_op jit(solution)/shard_map/ppermute | solution.py:42
  (237 other events, 3141.5 us)
